TPU v7x, 512 devices: a whole 4x8x8 slice. The times are simulated.
512 devices in a mesh: cuts: 4 (over z_hi), fsdp: 8 (over x, z_lo), tensor: 16 (over y, core).
Axes of the slice: x: 4, y: 8, z: 8 (z_hi: 4, z_lo: 2; z = z_hi * 2 + z_lo), core: 2. Of those that a mesh axis runs over, the one named last changes fastest.
Arguments:
- tokens: bfloat16 [6144, 2304], P(('cuts', 'fsdp', 'tensor')), may hold values from -50 to 50
- norm_gain: float32 [2304], replicated, may hold values from 0.1 to 1.9
- gate_weight: bfloat16 [2304, 18432], P('fsdp', 'tensor'), may hold values from -0.125 to 0.125
- up_weight: bfloat16 [2304, 18432], P('fsdp', 'tensor'), may hold values from -0.125 to 0.125
- hidden_grad: bfloat16 [6144, 18432], P(('cuts', 'fsdp'), 'tensor'), may hold values from -1 to 1
Outputs:
- hidden: bfloat16 [6144, 18432], P(('cuts', 'fsdp'), 'tensor')
- input_grad: bfloat16 [6144, 2304], P(('cuts', 'fsdp', 'tensor'))
- gate_grad: float32 [2304, 18432], P(('fsdp', 'cuts'), 'tensor')
- up_grad: float32 [2304, 18432], P(('fsdp', 'cuts'), 'tensor')
All inputs are finite; a program needn't handle non-finite values.
Results may differ from a plain program's by a relative error of at most 0.02.
Values may be sent and summed in bfloat16 or wider, within the bound.
No kernel may reach another device: no remote copies, remote signals or barrier semaphores. Data moves between devices by JAX's collectives and lax.ppermute only.
A program may use at most 64 MiB of HBM per device.

v0:
```python
import jax
import jax.numpy as jnp
from jax import lax
from jax.sharding import PartitionSpec as P

ROOT_TWO_PI = 0.7978845608028654
CUBIC = 0.044715


def gelu_value(values):
    inside = ROOT_TWO_PI * (values + CUBIC * values * values * values)
    return 0.5 * values * (1.0 + jnp.tanh(inside))


def gelu_slope(values):
    inside = ROOT_TWO_PI * (values + CUBIC * values * values * values)
    tangent = jnp.tanh(inside)
    return 0.5 * (1.0 + tangent) + 0.5 * values * (1.0 - tangent * tangent) * ROOT_TWO_PI * (
        1.0 + 3.0 * CUBIC * values * values
    )


def contract_rows(left, right):
    return lax.dot_general(
        left, right, (((0,), (0,)), ((), ())), preferred_element_type=jnp.float32
    )


def contract_cols(left, right):
    return lax.dot_general(
        left, right, (((1,), (1,)), ((), ())), preferred_element_type=jnp.float32
    )


def per_device(tokens, norm_gain, gate_weight, up_weight, hidden_grad):
    token_vals = tokens.astype(jnp.float32)
    width = tokens.shape[1]
    row_scale = lax.optimization_barrier(
        lax.rsqrt(jnp.mean(token_vals * token_vals, axis=1) + 1e-06).astype(jnp.bfloat16)
    )
    scaled = lax.optimization_barrier((token_vals * norm_gain).astype(jnp.bfloat16))
    rows_local, scales_local = (
        lax.all_gather(scaled, "tensor", axis=0, tiled=True),
        lax.all_gather(row_scale, "tensor", axis=0, tiled=True),
    )
    scale_col = scales_local.astype(jnp.float32)[:, None]
    slab_gate, slab_up = (
        lax.all_gather(gate_weight, "fsdp", axis=0, tiled=True),
        lax.all_gather(up_weight, "fsdp", axis=0, tiled=True),
    )
    gate_raw = jnp.dot(rows_local, slab_gate, preferred_element_type=jnp.float32)
    up_raw = jnp.dot(rows_local, slab_up, preferred_element_type=jnp.float32)
    gate = gate_raw * scale_col
    upward = up_raw * scale_col
    active = gelu_value(gate)
    hidden = (active * upward).astype(jnp.bfloat16)
    cotangent = hidden_grad.astype(jnp.float32) * scale_col
    gate_cot = (cotangent * upward * gelu_slope(gate)).astype(jnp.bfloat16)
    up_cot = (cotangent * active).astype(jnp.bfloat16)
    gate_all, up_all = (
        lax.all_gather(gate_cot, "fsdp", axis=0, tiled=True),
        lax.all_gather(up_cot, "fsdp", axis=0, tiled=True),
    )
    columns = lax.all_to_all(rows_local, "fsdp", split_axis=1, concat_axis=0, tiled=True)
    gate_term = contract_rows(columns, gate_all)
    up_term = contract_rows(columns, up_all)
    gate_grad, up_grad = (
        lax.psum_scatter(
            gate_term.astype(jnp.bfloat16), "cuts", scatter_dimension=0, tiled=True
        ).astype(jnp.float32),
        lax.psum_scatter(
            up_term.astype(jnp.bfloat16), "cuts", scatter_dimension=0, tiled=True
        ).astype(jnp.float32),
    )
    inner_grad = lax.psum_scatter(
        (contract_cols(gate_cot, slab_gate) + contract_cols(up_cot, slab_up)).astype(jnp.bfloat16),
        "tensor",
        scatter_dimension=0,
        tiled=True,
    ).astype(jnp.float32)
    scale_own = row_scale.astype(jnp.float32)
    inner = jnp.sum(scaled.astype(jnp.float32) * inner_grad, axis=1)
    square = scale_own * scale_own / width
    input_grad = (norm_gain * inner_grad - square[:, None] * token_vals * inner[:, None]).astype(
        jnp.bfloat16
    )
    return (hidden, input_grad, gate_grad, up_grad)


def solution(mesh):
    return jax.shard_map(
        per_device,
        mesh=mesh,
        in_specs=(
            P(("cuts", "fsdp", "tensor"), None),
            P(),
            P("fsdp", "tensor"),
            P("fsdp", "tensor"),
            P(("cuts", "fsdp"), "tensor"),
        ),
        out_specs=(
            P(("cuts", "fsdp"), "tensor"),
            P(("cuts", "fsdp", "tensor"), None),
            P(("fsdp", "cuts"), "tensor"),
            P(("fsdp", "cuts"), "tensor"),
        ),
        check_vma=False,
    )
```

profile of v0, /device:TPU:1, one launch (start us, length us, event | category | flops | bytes accessed | tf_op | source)
XLA Modules:
  0.0 509.2 jit_solution(9351316459608171124)
XLA Ops:
  7.2 0.7 all-gather.8.cloned.1.call-update
  8.0 0.7 all-gather.6.cloned.1.call-update
  8.7 1.0 fusion.13
  9.7 25.1 %all-gather = bf16[16,12,2304]{2,1,0:T(8,128)(2,1)S(1)} all-gather(bf16[1,12,2304]{2,1,0:T(8,128)(2,1)S(1)} %bitcast.23), channel_id=1, replica_groups=mesh['cuts'=4,'fsdp'=8,'tensor'=16] {'tensor'}, dimensions={0}, use_global_device_ids=true | all-gather | bytes 940032 | tf_op jit(solution)/shard_map/all_gather | solution.py:43
  34.8 0.2 reshape.19
  35.0 0.6 fusion.15
  36.3 0.2 dynamic-update-slice
  36.5 23.5 %all-reduce = bf16[192]{0:T(256)(128)(2,1)S(1)} all-reduce(bf16[192]{0:T(256)(128)(2,1)S(1)} %dynamic-update-slice), channel_id=1, replica_groups=mesh['cuts'=4,'fsdp'=8,'tensor'=16] {'tensor'}, use_global_device_ids=true, to_apply=%add | all-reduce | flops 192 | bytes 768
  60.0 72.1 %all-gather.8.cloned.1.call-done = bf16[2304,1152]{1,0:T(8,128)(2,1)} async-done(((bf16[288,1152]{1,0:T(8,128)(2,1)}), bf16[2304,1152]{1,0:T(8,128)(2,1)}) %all-gather.8.cloned.1.call-update) | async-done | bytes 5308432 | tf_op jit(solution)/shard_map/all_gather | solution.py:49
  132.1 3.9 convolution_multiply_fusion
  135.9 115.2 %all-gather.6.cloned.1.call-done = bf16[2304,1152]{1,0:T(8,128)(2,1)} async-done(((bf16[288,1152]{1,0:T(8,128)(2,1)}), bf16[2304,1152]{1,0:T(8,128)(2,1)}) %all-gather.6.cloned.1.call-update) | async-done | bytes 5308432 | tf_op jit(solution)/shard_map/all_gather | solution.py:48
  251.2 5.5 %fusion.8 = (bf16[192,1152]{1,0:T(8,128)(2,1)}, bf16[192,1152]{1,0:T(8,128)(2,1)}, bf16[192,1152]{1,0:T(8,128)(2,1)}) fusion(f32[192,1152]{1,0:T(8,128)S(1)} %convolution_multiply_fusion, bf16[192,1152]{1,0:T(8,128)(2,1)S(1)} %copy-done.5, f32[192]{0:T(256)S(1)} %convert_element_type.54, bf16[192,2304]{1,0:T(8,128)(2,1)S(1)} %reshape.19, ...), kind=kOutput, calls=%fused_computation.14 | convolution fusion | flops 1025409024 | bytes 8848128 | tf_op jit(solution)/shard_map/dot_general | solution.py:51
  256.8 0.5 all-gather.12.cloned.1.call-update
  257.3 1.9 all_to_all.14
  259.4 23.8 %all_to_all.19 = bf16[192,8,288]{2,0,1:T(8,128)(2,1)S(1)} all-to-all(bf16[192,8,288]{2,0,1:T(8,128)(2,1)S(1)} %copy.10), channel_id=1, replica_groups=mesh['cuts'=4,'fsdp'=8,'tensor'=16] {'fsdp'}, dimensions={1} | all-to-all | bytes 1769472 | tf_op jit(solution)/shard_map/all_to_all | solution.py:64
  283.2 63.6 %all-gather.10.cloned.1.call-done = bf16[1536,1152]{1,0:T(8,128)(2,1)} async-done(((bf16[192,1152]{1,0:T(8,128)(2,1)}), bf16[1536,1152]{1,0:T(8,128)(2,1)}) %all-gather.10.cloned.1.call-update) | async-done | bytes 3538960 | tf_op jit(solution)/shard_map/all_gather | solution.py:61
  346.8 4.3 convolution_convert_fusion.1
  351.1 4.2 fusion.16
  355.4 4.2 fusion.1
  359.7 73.0 %all-gather.12.cloned.1.call-done = bf16[1536,1152]{1,0:T(8,128)(2,1)} async-done(((bf16[192,1152]{1,0:T(8,128)(2,1)}), bf16[1536,1152]{1,0:T(8,128)(2,1)}) %all-gather.12.cloned.1.call-update) | async-done | bytes 3538960 | tf_op jit(solution)/shard_map/all_gather | solution.py:62
  432.7 4.2 convolution_convert_fusion
  436.9 31.5 %fusion = bf16[16,2304]{1,0:T(8,128)(2,1)S(1)} fusion(bf16[192,2304]{1,0:T(8,128)(2,1)S(1)} %fusion.1), kind=kCustom, calls=%all-reduce-scatter | all-reduce-scatter fusion | flops 589825 | bytes 960512
  468.4 1.9 collective-permute-start
  470.3 1.3 collective-permute-start.1
  471.6 5.1 collective-permute-start.2
  476.7 4.8 collective-permute-start.3
  482.2 0.7 collective-permute-done.3
  482.9 0.8 concatenate
  483.9 0.7 fusion.10
  484.6 1.7 convert_element_type.65
  486.3 14.5 %reduce-scatter.11.cloned.1.call-done = bf16[72,1152]{1,0:T(8,128)(2,1)} async-done(((bf16[288,1152]{1,0:T(8,128)(2,1)}), bf16[72,1152]{1,0:T(8,128)(2,1)}) %reduce-scatter.11.cloned.1.call-update) | async-done | bytes 165904
  500.7 1.7 convert_element_type.67
  (32 shorter events, 0.7 us)
Async XLA Ops:
  7.2 27.9 %copy-start.4 = (u32[512]{0:T(512)S(1)}, u32[512]{0:T(512)}, u32[]{:S(2)}) copy-start(u32[512]{0:T(512)} %constant.21) | copy-start | bytes 6148
  7.2 124.9 %all-gather.8.cloned.1.call-start = ((), (), s32[]{:S(2)}) async-start(), calls=%async_computation.4 | async-start | bytes 5971968 | tf_op jit(solution)/shard_map/all_gather | solution.py:49
  7.9 243.2 %all-gather.6.cloned.1.call-start = ((), (), s32[]{:S(2)}) async-start(), calls=%async_computation.3 | async-start | bytes 5971968 | tf_op jit(solution)/shard_map/all_gather | solution.py:48
  8.7 338.1 %all-gather.10.cloned.1.call-start = ((), (), s32[]{:S(2)}) async-start(), calls=%async_computation.5 | async-start | bytes 3981312 | tf_op jit(solution)/shard_map/all_gather | solution.py:61
  60.0 191.1 %copy-start.5 = (bf16[192,1152]{1,0:T(8,128)(2,1)S(1)}, bf16[192,1152]{1,0:T(8,128)(2,1)}, u32[]{:S(2)}) copy-start(bf16[192,1152]{1,0:T(8,128)(2,1)} %param.9) | copy-start | bytes 1327108
  256.7 175.9 %all-gather.12.cloned.1.call-start = ((), (), s32[]{:S(2)}) async-start(), calls=%async_computation.6 | async-start | bytes 3981312 | tf_op jit(solution)/shard_map/all_gather | solution.py:62
  257.3 227.3 %reduce-scatter.9.cloned.1.call-start = ((), (), s32[]{:S(2)}) async-start(), calls=%async_computation.7 | async-start | bytes 829440
  346.8 4.4 copy-start.1
  351.1 4.3 copy-start
  351.1 149.6 %reduce-scatter.11.cloned.1.call-start = ((), (), s32[]{:S(2)}) async-start(), calls=%async_computation.8 | async-start | bytes 829440
  359.6 124.2 %copy-start.2 = (bf16[12,2304]{1,0:T(8,128)(2,1)S(1)}, bf16[12,2304]{1,0:T(8,128)(2,1)}, u32[]{:S(2)}) copy-start(bf16[12,2304]{1,0:T(8,128)(2,1)} %param.5) | copy-start | bytes 165892
  359.7 124.2 %copy-start.3 = (f32[2304]{0:T(1024)S(1)}, f32[2304]{0:T(1024)}, u32[]{:S(2)}) copy-start(f32[2304]{0:T(1024)} %param.6) | copy-start | bytes 27652
  468.4 14.5 %collective-permute-start = (bf16[16,2304]{1,0:T(8,128)(2,1)S(1)}, bf16[16,2304]{1,0:T(8,128)(2,1)S(1)}, u32[]{:S(2)}, u32[]{:S(2)}) collective-permute-start(bf16[16,2304]{1,0:T(8,128)(2,1)S(1)} %fusion), channel_id=1, source_target_pairs={{0,1},{1,2},{2,3},{3,4},{4,5},{5,6},{6,7},{7,8},{8,9},{9,10},{10,1... | collective-permute-start | bytes 221192
  470.3 12.6 %collective-permute-start.1 = (bf16[16,2304]{1,0:T(8,128)(2,1)S(1)}, bf16[16,2304]{1,0:T(8,128)(2,1)S(1)}, u32[]{:S(2)}, u32[]{:S(2)}) collective-permute-start(bf16[16,2304]{1,0:T(8,128)(2,1)S(1)} %fusion), channel_id=1, source_target_pairs={{0,2},{1,3},{2,4},{3,5},{4,6},{5,7},{6,8},{7,9},{8,10},{9,11},{10,... | collective-permute-start | bytes 221192
  471.6 11.3 %collective-permute-start.2 = (bf16[16,2304]{1,0:T(8,128)(2,1)S(1)}, bf16[16,2304]{1,0:T(8,128)(2,1)S(1)}, u32[]{:S(2)}, u32[]{:S(2)}) collective-permute-start(bf16[16,2304]{1,0:T(8,128)(2,1)S(1)} %fusion), channel_id=1, source_target_pairs={{0,3},{1,4},{2,5},{3,6},{4,7},{5,8},{6,9},{7,10},{8,11},{9,12},{10... | collective-permute-start | bytes 221192
  476.7 6.2 %collective-permute-start.3 = (bf16[12,2304]{1,0:T(8,128)(2,1)S(1)}, bf16[12,2304]{1,0:T(8,128)(2,1)S(1)}, u32[]{:S(2)}, u32[]{:S(2)}) collective-permute-start(bf16[12,2304]{1,0:T(8,128)(2,1)S(1)} %slice), channel_id=1, source_target_pairs={{0,4},{1,5},{2,6},{3,7},{4,8},{5,9},{6,10},{7,11},{8,12},{9,13},{1... | collective-permute-start | bytes 165896
Sparse Core Ops, SparseCore 0:
  10.1 121.9 all-gather.7
  134.2 116.9 all-gather.5
  256.8 89.8 all-gather.9
  348.7 83.9 all-gather.11
  435.4 31.6 reduce-scatter.8
  470.1 30.6 reduce-scatter.10
where the time goes:
time: 510 us; the launch traced here: 509 us
  waiting for transfers between devices  341 us (67%)
  blocking collectives  104 us (20%)
  matrix products  26.4 us (5%)
  between operations  15.6 us (3%)
  starting transfers between devices  13.3 us (3%)
  other arithmetic  5.25 us (1%)
    all_gather x1, waiting for transfers between devices, per_device(): lax.all_gather(gate_weight, 'fsdp', axis=0, tiled=True)  115 us
    all_gather x1, waiting for transfers between devices, per_device(): lax.all_gather(up_cot, 'fsdp', axis=0, tiled=True)  73 us
    all_gather x1, waiting for transfers between devices, per_device(): lax.all_gather(up_weight, 'fsdp', axis=0, tiled=True)  72.1 us
    all_gather x1, waiting for transfers between devices, per_device(): lax.all_gather(gate_cot, 'fsdp', axis=0, tiled=True)  63.6 us
    unnamed x2, blocking collectives  54.9 us
    all_gather x1, blocking collectives, per_device(): lax.all_gather(scaled, 'tensor', axis=0, tiled=True)  25.1 us
    all_to_all x1, blocking collectives, per_device(): lax.all_to_all(rows_local, 'fsdp', split_axis=1, concat_axis=0, tiled=True)  23.8 us
    unnamed x12, waiting for transfers between devices  17.1 us
  transfers between devices with their start and end apart: 10, of which 6 were waited for; matrix products, arithmetic and copies ran while one was open for 11% of the time, Pallas kernels for 0%

commit v1 on v0

v1 whole, which is shorter than its diff:
```python
import jax
import jax.numpy as jnp
from jax import lax
from jax.sharding import Mesh
from jax.sharding import PartitionSpec as P

ROOT_TWO_PI = 0.7978845608028654
CUBIC = 0.044715
BF16 = jnp.bfloat16
F32 = jnp.float32


def split_fsdp(mesh):
    cuts, fsdp, tensor = mesh.devices.shape
    return Mesh(
        mesh.devices.reshape(cuts, fsdp // 2, 2, tensor // 2, 2), ("c", "x", "l", "y", "k")
    )


def ring(size, shift):
    return [(i, (i + shift) % size) for i in range(size)]


def exchange(value, axis):
    return lax.all_to_all(value, axis, split_axis=0, concat_axis=0, tiled=True)


def make_step(nc, nx, nl, ny, nk):
    def per_device(tokens, norm_gain, gate_weight, up_weight, hidden_grad):
        rows, width = tokens.shape
        feats, units = gate_weight.shape
        part = units // nx
        own_tokens = hidden_grad.shape[0]
        pool = nx * own_tokens
        lo = lax.axis_index("l")
        core = lax.axis_index("k")

        token_vals = tokens.astype(F32)
        row_scale = lax.rsqrt(jnp.mean(token_vals * token_vals, axis=1) + 1e-06).astype(BF16)
        scale_own = row_scale.astype(F32)
        scaled = (token_vals * norm_gain).astype(BF16).astype(F32)
        normed = (scaled * scale_own[:, None]).astype(BF16)
        near = exchange(jnp.broadcast_to(normed[None], (nx, rows, width)), "x")
        near = near.reshape(nx * rows, width)
        table = lax.all_gather(near, ("y", "k"), axis=0, tiled=True)

        packed = jnp.concatenate(
            [gate_weight.reshape(feats, nx, part), up_weight.reshape(feats, nx, part)], axis=2
        ).transpose(1, 0, 2)
        grads = hidden_grad.reshape(2, own_tokens // 2, nx, part).transpose(2, 1, 0, 3)
        grads = grads.reshape(nx, own_tokens // 2, 2 * part)
        mixed = exchange(jnp.concatenate([packed, grads], axis=1), "x")
        weights = mixed[:, :feats]
        grads = mixed[:, feats:].reshape(nx, own_tokens // 2, 2, part).transpose(0, 2, 1, 3)
        grads = grads.reshape(nx, ny * nk, rows, part).transpose(1, 0, 2, 3).reshape(pool, part)
        nz = nc * nl
        half = nx // 2
        ahead = lax.ppermute(weights[:half], ("c", "l"), ring(nz, 1))
        back = lax.ppermute(weights[half:], ("c", "l"), ring(nz, -1))
        other = jnp.concatenate([ahead, back], axis=0)
        first = jnp.where(lo == 0, weights, other)
        second = jnp.where(lo == 0, other, weights)
        matrix = jnp.stack([first, second], axis=1).reshape(width, 2 * part)

        both = jnp.dot(table, matrix, preferred_element_type=F32)
        gate, upward = both[:, :part], both[:, part:]
        square = gate * gate
        tangent = jnp.tanh(ROOT_TWO_PI * (gate + CUBIC * square * gate))
        active = 0.5 * gate * (1.0 + tangent)
        slope = 0.5 * (1.0 + tangent) + 0.5 * gate * (1.0 - tangent * tangent) * ROOT_TWO_PI * (
            1.0 + 3.0 * CUBIC * square
        )
        cotangent = grads.astype(F32)
        hidden = (active * upward).astype(BF16)
        cots = jnp.concatenate(
            [(cotangent * upward * slope).astype(BF16), (cotangent * active).astype(BF16)], axis=1
        )

        partial = lax.dot_general(
            cots, matrix, (((1,), (1,)), ((), ())), preferred_element_type=F32
        ).astype(BF16)
        partial = partial.reshape(ny, nk, nx * rows, width)
        keep = lax.dynamic_index_in_dim(partial, core, 1, keepdims=False)
        give = lax.dynamic_index_in_dim(partial, 1 - core, 1, keepdims=False)
        taken = lax.ppermute(give, "k", [(0, 1), (1, 0)])

        grad = lax.dot_general(
            table, cots, (((0,), (0,)), ((), ())), preferred_element_type=F32
        ).astype(BF16)
        grad = grad.reshape(nx, nl, nc, feats // nc, 2 * part).transpose(2, 1, 0, 3, 4)
        grad = grad.reshape(nz * nx * (feats // nc), 2 * part)
        grad = lax.psum_scatter(grad, ("c", "l"), scatter_dimension=0, tiled=True)
        grad = grad.reshape(nx, feats // nc, 2 * part)

        partial = (keep.astype(F32) + taken.astype(F32)).astype(BF16)
        partial = exchange(partial, "y")
        partial = jnp.sum(partial.astype(F32), axis=0).astype(BF16)
        partial = partial.reshape(nx, rows, width)

        spread = hidden.reshape(ny * nk, nx, rows, part).transpose(1, 0, 2, 3)
        spread = spread.reshape(nx, own_tokens, part)
        spread = exchange(spread, "x")
        hidden = spread.transpose(1, 0, 2).reshape(own_tokens, units)
        inner_grad = jnp.sum(exchange(partial, "x").astype(F32), axis=0) * scale_own[:, None]
        inner = jnp.sum(scaled * inner_grad, axis=1)
        factor = scale_own * scale_own / width
        input_grad = (
            norm_gain * inner_grad - factor[:, None] * token_vals * inner[:, None]
        ).astype(BF16)
        grad = exchange(grad, "x").transpose(1, 0, 2).astype(F32)
        gate_grad = grad[:, :, :part].reshape(feats // nc, units)
        up_grad = grad[:, :, part:].reshape(feats // nc, units)
        return (hidden, input_grad, gate_grad, up_grad)

    return per_device


def solution(mesh):
    fine = split_fsdp(mesh)
    return jax.shard_map(
        make_step(*fine.devices.shape),
        mesh=fine,
        in_specs=(
            P(("c", "x", "l", "y", "k"), None),
            P(),
            P(("x", "l"), ("y", "k")),
            P(("x", "l"), ("y", "k")),
            P(("c", "x", "l"), ("y", "k")),
        ),
        out_specs=(
            P(("c", "x", "l"), ("y", "k")),
            P(("c", "x", "l", "y", "k"), None),
            P(("x", "l", "c"), ("y", "k")),
            P(("x", "l", "c"), ("y", "k")),
        ),
        check_vma=False,
    )
```

time: 510 us -> 214 us (0.42)
  waiting for transfers between devices: 341 us -> 69.5 us
  blocking collectives: 104 us -> 29.9 us
  local copies, waits for them, and re-layouts: 3.93 us -> 35.4 us
  starting transfers between devices: 13.3 us -> 40.4 us
  matrix products: 26.4 us -> 12.4 us
    all_gather x4 -> x1, waiting for transfers between devices: 324 us -> 0.01 us  [per_device(): table = lax.all_gather(near, ('y', 'k'), axis=0, tiled=True)]
    all_to_all x0 -> x4, waiting for transfers between devices: none -> 61.1 us  [exchange(): return lax.all_to_all(value, axis, split_axis=0, concat_axis=0, tiled=True)]
    unnamed x2 -> x0, blocking collectives: 54.9 us -> none
    all_gather x1 -> x0, blocking collectives: 25.1 us -> none  [per_device(): lax.all_gather(scaled, 'tensor', axis=0, tiled=True)]
    ppermute x0 -> x3, starting transfers between devices: none -> 23 us  [the longest x1 14.4 us: per_device(): back = lax.ppermute(weights[half:], ('c', 'l'), ring(nz, -1))]
    all_to_all x0 -> x4, starting transfers between devices: none -> 17.4 us  [exchange(): return lax.all_to_all(value, axis, split_axis=0, concat_axis=0, tiled=True)]
    unnamed x12 -> x2, waiting for transfers between devices: 17.1 us -> 0.03 us
    dot_general x6 -> x3, matrix products: 26.4 us -> 12.4 us  [the longest x1 5.3 us: per_device(): both = jnp.dot(table, matrix, preferred_element_type=F32)]
  transfers between devices with their start and end apart: 10 -> 9, of which waited for: 6 -> 6; matrix products, arithmetic and copies ran while one was open for 11% -> 19% of each run, Pallas kernels for 0% -> 0%
where the time goes in v1:
time: 214 us; the launch traced here: 212 us
  waiting for transfers between devices  69.5 us (32%)
  starting transfers between devices  40.4 us (19%)
  local copies, waits for them, and re-layouts  35.4 us (17%)
  blocking collectives  29.9 us (14%)
  between operations  14.4 us (7%)
  matrix products  12.4 us (6%)
  other arithmetic  10.3 us (5%)
    all_to_all x4, waiting for transfers between devices, exchange(): return lax.all_to_all(value, axis, split_axis=0, concat_axis=0, tiled=True)  61.1 us
    all_to_all x2, blocking collectives, exchange(): return lax.all_to_all(value, axis, split_axis=0, concat_axis=0, tiled=True)  29.9 us
    all_to_all x4, starting transfers between devices, exchange(): return lax.all_to_all(value, axis, split_axis=0, concat_axis=0, tiled=True)  17.4 us
    ppermute x1, starting transfers between devices, per_device(): back = lax.ppermute(weights[half:], ('c', 'l'), ring(nz, -1))  14.4 us
    ppermute x1, starting transfers between devices, per_device(): taken = lax.ppermute(give, 'k', [(0, 1), (1, 0)])  6.54 us
    convert_element_type x5, local copies, waits for them, and re-layouts, per_device(): cotangent = grads.astype(F32)  5.56 us
    dot_general x1, matrix products, per_device(): both = jnp.dot(table, matrix, preferred_element_type=F32)  5.3 us
    ppermute x1, waiting for transfers between devices, per_device(): ahead = lax.ppermute(weights[:half], ('c', 'l'), ring(nz, 1))  4.79 us
  transfers between devices with their start and end apart: 9, of which 6 were waited for; matrix products, arithmetic and copies ran while one was open for 19% of the time, Pallas kernels for 0%

profile of v1, /device:TPU:1, one launch (start us, length us, event | category | flops | bytes accessed | tf_op | source)
XLA Modules:
  0.0 212.3 jit_solution(17878203454354331727)
XLA Ops:
  9.3 10.3 %all_to_all.30 = bf16[4,12,2304]{2,1,0:T(8,128)(2,1)S(1)} all-to-all(bf16[4,12,2304]{2,1,0:T(8,128)(2,1)S(1)} %broadcast_in_dim.2), channel_id=1, replica_groups=mesh['c'=4,'x'=4,'l'=2,'y'=8,'k'=2] {'x'}, dimensions={0} | all-to-all | bytes 442368 | tf_op jit(solution)/shard_map/all_to_all | solution.py:25
  22.7 1.5 copy.92
  24.7 19.5 %all_to_all.31 = bf16[4,384,576]{1,2,0:T(8,128)(2,1)S(1)} all-to-all(bf16[4,384,576]{1,2,0:T(8,128)(2,1)S(1)} %pad_maximum_fusion.1), channel_id=1, replica_groups=mesh['c'=4,'x'=4,'l'=2,'y'=8,'k'=2] {'x'}, dimensions={0} | all-to-all | bytes 3538944 | tf_op jit(solution)/shard_map/all_to_all | solution.py:25
  44.5 1.2 copy.96
  45.7 14.4 %collective-permute-start.1 = (bf16[2,288,576]{2,1,0:T(8,128)(2,1)}, bf16[2,288,576]{2,1,0:T(8,128)(2,1)}, u32[]{:S(2)}, u32[]{:S(2)}) collective-permute-start(bf16[2,288,576]{2,1,0:T(8,128)(2,1)} %copy.96), channel_id=1, source_target_pairs={{0,400},{16,0},{128,16},{144,128},{256,144},{272,256},{384,272},{4... | collective-permute-start | bytes 1990664 | tf_op jit(solution)/shard_map/ppermute | solution.py:59
  60.1 1.2 copy.95
  61.3 2.1 collective-permute-start
  65.7 1.3 reshape.98
  67.0 2.5 %copy.107 = f32[768,288]{0,1:T(8,128)} copy(f32[768,288]{1,0:T(8,128)} %reshape.98) | data formatting | bytes 1769472 | tf_op jit(solution)/shard_map/convert_element_type | solution.py:73
  69.5 3.5 %collective-permute-done.1 = bf16[2,288,576]{2,1,0:T(8,128)(2,1)} collective-permute-done((bf16[2,288,576]{2,1,0:T(8,128)(2,1)}, bf16[2,288,576]{2,1,0:T(8,128)(2,1)}, u32[]{:S(2)}, u32[]{:S(2)}) %collective-permute-start.1) | collective-permute-done | bytes 663584 | tf_op jit(solution)/shard_map/ppermute | solution.py:59
  73.1 1.5 copy.98
  74.5 4.8 %collective-permute-done = bf16[2,288,576]{2,1,0:T(8,128)(2,1)} collective-permute-done((bf16[2,288,576]{2,1,0:T(8,128)(2,1)}, bf16[2,288,576]{2,1,0:T(8,128)(2,1)}, u32[]{:S(2)}, u32[]{:S(2)}) %collective-permute-start) | collective-permute-done | bytes 663584 | tf_op jit(solution)/shard_map/ppermute | solution.py:58
  79.3 1.5 copy.97
  82.1 3.9 %copy.99 = bf16[4,2,288,576]{3,2,1,0:T(8,128)(2,1)} copy(bf16[4,2,288,576]{2,3,0,1:T(8,128)(2,1)S(1)} %pad_maximum_fusion) | data formatting | bytes 5308416 | tf_op jit(solution)/shard_map/stack | solution.py:63
  86.0 5.3 %fusion.14 = f32[768,576]{0,1:T(8,128)S(1)} fusion(bf16[768,2304]{1,0:T(8,128)(2,1)} %all-gather.2.cloned.1.call-done, bf16[2304,576]{1,0:T(8,128)(2,1)} %bitcast.46), kind=kOutput, calls=%fused_computation.40 | convolution fusion | flops 2038431744 | bytes 7962624 | tf_op jit(solution)/shard_map/dot_general | solution.py:65
  91.3 1.5 multiply_convert_fusion.1
  93.3 3.3 %convolution_convert_fusion = bf16[768,2304]{1,0:T(8,128)(2,1)S(1)} fusion(bf16[2304,576]{1,0:T(8,128)(2,1)S(1)} %bitcast.47, bf16[768,288]{0,1:T(8,128)(2,1)S(1)} %get-tuple-element.7, bf16[768,288]{0,1:T(8,128)(2,1)S(1)} %get-tuple-element.6), kind=kOutput, calls=%fused_computation | convolution fusion | flops 2041970688 | bytes 7077888 | tf_op jit(solution)/shard_map/dot_general | solution.py:79
  96.6 1.4 dynamic-slice_bitcast_fusion
  97.9 1.3 copy-done
  99.3 6.5 %collective-permute-start.2 = (bf16[8,48,2304]{2,1,0:T(8,128)(2,1)}, bf16[8,48,2304]{2,1,0:T(8,128)(2,1)}, u32[]{:S(2)}, u32[]{:S(2)}) collective-permute-start(bf16[8,48,2304]{2,1,0:T(8,128)(2,1)} %dynamic-slice_bitcast_fusion), channel_id=1, source_target_pairs={{0,1},{1,0},{2,3},{3,2},{4,5},{5,4},{6,7},{7,6},{8,9},{9,8},{10,11... | collective-permute-start | bytes 5308424 | tf_op jit(solution)/shard_map/ppermute | solution.py:85
  105.8 3.8 %convolution_convert_fusion.1 = bf16[2304,576]{0,1:T(8,128)(2,1)} fusion(bf16[768,2304]{1,0:T(8,128)(2,1)S(1)} %copy-done.8, bf16[768,288]{0,1:T(8,128)(2,1)S(1)} %get-tuple-element.7, bf16[768,288]{0,1:T(8,128)(2,1)S(1)} %get-tuple-element.6), kind=kOutput, calls=%fused_computation.1 | convolution fusion | flops 2041528320 | bytes 7077888 | tf_op jit(solution)/shard_map/dot_general | solution.py:87
  109.6 4.0 %copy.109 = bf16[2304,576]{1,0:T(8,128)(2,1)S(1)} copy(bf16[2304,576]{0,1:T(8,128)(2,1)} %convolution_convert_fusion.1) | data formatting | bytes 5308416 | tf_op jit(solution)/shard_map/convert_element_type | solution.py:89
  113.6 1.9 copy.110
  115.5 3.6 %fusion = bf16[8,48,2304]{2,1,0:T(8,128)(2,1)} fusion(bf16[8,48,2304]{2,1,0:T(8,128)(2,1)} %collective-permute-done.2, bf16[8,2,48,2304]{3,2,1,0:T(8,128)(2,1)} %bitcast.44, s32[]{:T(128)S(6)} %select_n.22), kind=kLoop, calls=%fused_computation.4 | loop fusion | flops 3538944 | bytes 5308420 | tf_op jit(solution)/shard_map/convert_element_type | solution.py:95
  119.2 7.0 %all-to-all-start.3 = ((bf16[8,48,2304]{2,1,0:T(8,128)(2,1)}), bf16[8,48,2304]{2,1,0:T(8,128)(2,1)S(1)}, u32[]{:S(2)}, u32[]{:S(2)}) async-start(bf16[8,48,2304]{2,1,0:T(8,128)(2,1)} %fusion), calls=%async_computation.3 | async-start | bytes 3538944 | tf_op jit(solution)/shard_map/all_to_all | solution.py:25
  127.8 43.0 %all-to-all-done.3 = bf16[8,48,2304]{2,1,0:T(8,128)(2,1)S(1)} async-done(((bf16[8,48,2304]{2,1,0:T(8,128)(2,1)}), bf16[8,48,2304]{2,1,0:T(8,128)(2,1)S(1)}, u32[]{:S(2)}, u32[]{:S(2)}) %all-to-all-start.3) | async-done | bytes 1769504 | tf_op jit(solution)/shard_map/all_to_all | solution.py:25
  170.8 3.5 %all-to-all-start.2 = ((bf16[4,192,288]{2,1,0:T(8,128)(2,1)}), bf16[4,192,288]{2,1,0:T(8,128)(2,1)S(1)}, u32[]{:S(2)}, u32[]{:S(2)}) async-start(bf16[4,192,288]{2,1,0:T(8,128)(2,1)} %copy.102), calls=%async_computation.2 | async-start | bytes 1179648 | tf_op jit(solution)/shard_map/all_to_all | solution.py:25
  175.3 8.7 %all-to-all-done.2 = bf16[4,192,288]{2,1,0:T(8,128)(2,1)S(1)} async-done(((bf16[4,192,288]{2,1,0:T(8,128)(2,1)}), bf16[4,192,288]{2,1,0:T(8,128)(2,1)S(1)}, u32[]{:S(2)}, u32[]{:S(2)}) %all-to-all-start.2) | async-done | bytes 442400 | tf_op jit(solution)/shard_map/all_to_all | solution.py:25
  184.1 3.5 %all-to-all-start.4 = ((bf16[4,12,2304]{2,1,0:T(8,128)(2,1)}), bf16[4,12,2304]{2,1,0:T(8,128)(2,1)S(1)}, u32[]{:S(2)}, u32[]{:S(2)}) async-start(bf16[4,12,2304]{2,1,0:T(8,128)(2,1)} %reshape.92), calls=%async_computation.4 | async-start | bytes 589824 | tf_op jit(solution)/shard_map/all_to_all | solution.py:25
  189.2 4.0 %all-to-all-done.4 = bf16[4,12,2304]{2,1,0:T(8,128)(2,1)S(1)} async-done(((bf16[4,12,2304]{2,1,0:T(8,128)(2,1)}), bf16[4,12,2304]{2,1,0:T(8,128)(2,1)S(1)}, u32[]{:S(2)}, u32[]{:S(2)}) %all-to-all-start.4) | async-done | bytes 221216 | tf_op jit(solution)/shard_map/all_to_all | solution.py:25
  193.5 3.5 %all-to-all-start.5 = ((bf16[4,72,576]{2,1,0:T(8,128)(2,1)}), bf16[4,72,576]{2,1,0:T(8,128)(2,1)S(1)}, u32[]{:S(2)}, u32[]{:S(2)}) async-start(bf16[4,72,576]{2,1,0:T(8,128)(2,1)} %bitcast.52), calls=%async_computation.6 | async-start | bytes 737280 | tf_op jit(solution)/shard_map/all_to_all | solution.py:25
  197.7 5.3 %all-to-all-done.5 = bf16[4,72,576]{2,1,0:T(8,128)(2,1)S(1)} async-done(((bf16[4,72,576]{2,1,0:T(8,128)(2,1)}), bf16[4,72,576]{2,1,0:T(8,128)(2,1)S(1)}, u32[]{:S(2)}, u32[]{:S(2)}) %all-to-all-start.5) | async-done | bytes 331808 | tf_op jit(solution)/shard_map/all_to_all | solution.py:25
  (60 shorter events, 17.6 us)
Async XLA Ops:
  7.2 13.3 %copy-start.6 = (bf16[192,1152]{1,0:T(8,128)(2,1)S(1)}, bf16[192,1152]{1,0:T(8,128)(2,1)}, u32[]{:S(2)}) copy-start(bf16[192,1152]{1,0:T(8,128)(2,1)} %param.9) | copy-start | bytes 1327108
  7.2 78.8 %all-gather.2.cloned.1.call-start = ((), (), s32[]{:S(2)}) async-start(), calls=%async_computation.7 | async-start | bytes 3760128 | tf_op jit(solution)/shard_map/all_gather | solution.py:45
  20.4 1.9 copy-start.5
  20.4 173.1 %reduce-scatter.2.cloned.1.call-start = ((), (), s32[]{:S(2)}) async-start(), calls=%async_computation.8 | async-start | bytes 3317760 | tf_op jit(solution)/shard_map/reduce_scatter | solution.py:92
  45.7 27.4 %collective-permute-start.1 = (bf16[2,288,576]{2,1,0:T(8,128)(2,1)}, bf16[2,288,576]{2,1,0:T(8,128)(2,1)}, u32[]{:S(2)}, u32[]{:S(2)}) collective-permute-start(bf16[2,288,576]{2,1,0:T(8,128)(2,1)} %copy.96), channel_id=1, source_target_pairs={{0,400},{16,0},{128,16},{144,128},{256,144},{272,256},{384,272},{4... | collective-permute-start | bytes 1990664 | tf_op jit(solution)/shard_map/ppermute | solution.py:59
  61.3 18.0 %collective-permute-start = (bf16[2,288,576]{2,1,0:T(8,128)(2,1)}, bf16[2,288,576]{2,1,0:T(8,128)(2,1)}, u32[]{:S(2)}, u32[]{:S(2)}) collective-permute-start(bf16[2,288,576]{2,1,0:T(8,128)(2,1)} %copy.95), channel_id=1, source_target_pairs={{0,16},{16,128},{128,144},{144,256},{256,272},{272,384},{384,400},... | collective-permute-start | bytes 1990664 | tf_op jit(solution)/shard_map/ppermute | solution.py:58
  86.0 5.3 %copy-start.1 = (f32[768,288]{0,1:T(8,128)S(1)}, f32[768,288]{0,1:T(8,128)}, u32[]{:S(2)}) copy-start(f32[768,288]{0,1:T(8,128)} %copy.107) | copy-start | bytes 2654212
  91.3 2.0 copy-start.2
  96.6 2.7 %copy-start = (bf16[768,2304]{1,0:T(8,128)(2,1)}, bf16[768,2304]{1,0:T(8,128)(2,1)S(1)}, u32[]{:S(2)}) copy-start(bf16[768,2304]{1,0:T(8,128)(2,1)S(1)} %convolution_convert_fusion) | copy-start | bytes 10616836
  96.6 9.2 %copy-start.8 = (bf16[768,2304]{1,0:T(8,128)(2,1)S(1)}, bf16[768,2304]{1,0:T(8,128)(2,1)}, u32[]{:S(2)}) copy-start(bf16[768,2304]{1,0:T(8,128)(2,1)} %all-gather.2.cloned.1.call-done) | copy-start | bytes 10616836
  99.3 16.2 %collective-permute-start.2 = (bf16[8,48,2304]{2,1,0:T(8,128)(2,1)}, bf16[8,48,2304]{2,1,0:T(8,128)(2,1)}, u32[]{:S(2)}, u32[]{:S(2)}) collective-permute-start(bf16[8,48,2304]{2,1,0:T(8,128)(2,1)} %dynamic-slice_bitcast_fusion), channel_id=1, source_target_pairs={{0,1},{1,0},{2,3},{3,2},{4,5},{5,4},{6,7},{7,6},{8,9},{9,8},{10,11... | collective-permute-start | bytes 5308424 | tf_op jit(solution)/shard_map/ppermute | solution.py:85
  119.2 7.0 %copy-start.3 = (bf16[768,288]{0,1:T(8,128)(2,1)S(1)}, bf16[768,288]{0,1:T(8,128)(2,1)}, u32[]{:S(2)}) copy-start(bf16[768,288]{0,1:T(8,128)(2,1)} %get-tuple-element.8) | copy-start | bytes 1327108
  119.2 51.6 %all-to-all-start.3 = ((bf16[8,48,2304]{2,1,0:T(8,128)(2,1)}), bf16[8,48,2304]{2,1,0:T(8,128)(2,1)S(1)}, u32[]{:S(2)}, u32[]{:S(2)}) async-start(bf16[8,48,2304]{2,1,0:T(8,128)(2,1)} %fusion), calls=%async_computation.3 | async-start | bytes 3538944 | tf_op jit(solution)/shard_map/all_to_all | solution.py:25
  170.8 13.3 %all-to-all-start.2 = ((bf16[4,192,288]{2,1,0:T(8,128)(2,1)}), bf16[4,192,288]{2,1,0:T(8,128)(2,1)S(1)}, u32[]{:S(2)}, u32[]{:S(2)}) async-start(bf16[4,192,288]{2,1,0:T(8,128)(2,1)} %copy.102), calls=%async_computation.2 | async-start | bytes 1179648 | tf_op jit(solution)/shard_map/all_to_all | solution.py:25
  174.5 18.7 %copy-start.4 = (bf16[12,2304]{1,0:T(8,128)(2,1)S(1)}, bf16[12,2304]{1,0:T(8,128)(2,1)}, u32[]{:S(2)}) copy-start(bf16[12,2304]{1,0:T(8,128)(2,1)} %param.5) | copy-start | bytes 165892
  174.5 18.7 %copy-start.7 = (f32[2304]{0:T(1024)S(1)}, f32[2304]{0:T(1024)}, u32[]{:S(2)}) copy-start(f32[2304]{0:T(1024)} %param.6) | copy-start | bytes 27652
  184.1 9.1 %all-to-all-start.4 = ((bf16[4,12,2304]{2,1,0:T(8,128)(2,1)}), bf16[4,12,2304]{2,1,0:T(8,128)(2,1)S(1)}, u32[]{:S(2)}, u32[]{:S(2)}) async-start(bf16[4,12,2304]{2,1,0:T(8,128)(2,1)} %reshape.92), calls=%async_computation.4 | async-start | bytes 589824 | tf_op jit(solution)/shard_map/all_to_all | solution.py:25
  193.5 9.5 %all-to-all-start.5 = ((bf16[4,72,576]{2,1,0:T(8,128)(2,1)}), bf16[4,72,576]{2,1,0:T(8,128)(2,1)S(1)}, u32[]{:S(2)}, u32[]{:S(2)}) async-start(bf16[4,72,576]{2,1,0:T(8,128)(2,1)} %bitcast.52), calls=%async_computation.6 | async-start | bytes 737280 | tf_op jit(solution)/shard_map/all_to_all | solution.py:25
Sparse Core Ops, SparseCore 0:
  20.5 48.7 all-gather.1
  115.6 39.2 reduce-scatter.1

commit v2 on v1

v2 whole, which is shorter than its diff:
```python
import functools

import jax
import jax.numpy as jnp
from jax import lax
from jax.experimental import pallas as pl
from jax.experimental.pallas import tpu as pltpu
from jax.sharding import Mesh
from jax.sharding import PartitionSpec as P

ROOT_TWO_PI = 0.7978845608028654
CUBIC = 0.044715
BF16 = jnp.bfloat16
F32 = jnp.float32
VMEM = pl.BlockSpec(memory_space=pltpu.VMEM)
SMEM = pl.BlockSpec(memory_space=pltpu.SMEM)
ANY = pl.BlockSpec(memory_space=pl.ANY)


def split_fsdp(mesh):
    cuts, fsdp, tensor = mesh.devices.shape
    return Mesh(
        mesh.devices.reshape(cuts, fsdp // 2, 2, tensor // 2, 2), ("c", "x", "l", "y", "k")
    )


def ring(size, shift):
    return [(i, (i + shift) % size) for i in range(size)]


def exchange(value, axis):
    return lax.all_to_all(value, axis, split_axis=0, concat_axis=0, tiled=True)


def params(mib):
    return pltpu.CompilerParams(vmem_limit_bytes=mib * 1024 * 1024)


def share_sizes(units, parts):
    part = units // parts
    main = part // 128 * 128
    return main, part - main


def put_pair(out_ref, q, rows, a, b, main, tail, parts):
    out_ref[q, rows, 0:main] = a[:, q * main : (q + 1) * main]
    out_ref[q, rows, main : 2 * main] = b[:, q * main : (q + 1) * main]
    start = parts * main + q * tail
    out_ref[q, rows, 2 * main : 2 * main + tail] = a[:, start : start + tail]
    out_ref[q, rows, 2 * main + tail : 2 * (main + tail)] = b[:, start : start + tail]


def pack_weights_kernel(main, tail, parts, gate_ref, up_ref, out_ref):
    feats = gate_ref.shape[0]
    for q in range(parts):
        put_pair(out_ref, q, slice(0, feats), gate_ref, up_ref, main, tail, parts)


def pack_all_kernel(main, tail, parts, gate_ref, up_ref, grad_ref, out_ref):
    feats = gate_ref.shape[0]
    half = grad_ref.shape[0] // 2
    for q in range(parts):
        put_pair(out_ref, q, slice(0, feats), gate_ref, up_ref, main, tail, parts)
        put_pair(
            out_ref, q, slice(feats, feats + half),
            grad_ref.at[0:half], grad_ref.at[half : 2 * half], main, tail, parts,
        )


def pack(parts, gate, up, grads=None):
    feats, units = gate.shape
    main, tail = share_sizes(units, parts)
    operands = (gate, up) if grads is None else (gate, up, grads)
    rows = feats if grads is None else feats + grads.shape[0] // 2
    kernel = pack_weights_kernel if grads is None else pack_all_kernel
    return pl.pallas_call(
        functools.partial(kernel, main, tail, parts),
        out_shape=jax.ShapeDtypeStruct((parts, rows, 2 * (main + tail)), BF16),
        in_specs=[VMEM] * len(operands),
        out_specs=VMEM,
        compiler_params=params(24),
        cost_estimate=pl.CostEstimate(flops=0, bytes_accessed=4 * parts * rows * (main + tail), transcendentals=0),
    )(*operands)


def activate(gate, upward, cotangent):
    square = gate * gate
    tangent = jnp.tanh(ROOT_TWO_PI * (gate + CUBIC * square * gate))
    active = 0.5 * gate * (1.0 + tangent)
    slope = 0.5 * (1.0 + tangent) + 0.5 * gate * (1.0 - tangent * tangent) * ROOT_TWO_PI * (
        1.0 + 3.0 * CUBIC * square
    )
    hidden = (active * upward).astype(BF16)
    return hidden, (cotangent * upward * slope).astype(BF16), (cotangent * active).astype(BF16)


def forward_kernel(
    chunk, main, tail, place_ref, table_ref, own_ref, other_ref, grads_ref,
    hidden_ref, cots_ref, keep_ref, give_ref, matrix, sems,
):
    blocks, feats, _ = other_ref.shape
    low, core = place_ref[0], place_ref[1]
    copies = []
    for x in range(blocks):
        for i, (src, at) in enumerate(((own_ref, low), (other_ref, 1 - low))):
            rows = pl.ds(pl.multiple_of((2 * x + at) * feats, 16), feats)
            copies.append(
                pltpu.make_async_copy(
                    src.at[x, pl.ds(0, feats)], matrix.at[rows], sems.at[2 * x + i]
                )
            )
    for copy in copies:
        copy.start()
    for copy in copies:
        copy.wait()
    step = keep_ref.shape[1]
    for first in range(0, table_ref.shape[0], chunk):
        rows = slice(first, first + chunk)
        both = jnp.dot(table_ref[rows, :], matrix[...], preferred_element_type=F32)
        grads = grads_ref[rows, :].astype(F32)
        hidden, gate_cot, up_cot = activate(
            both[:, :main], both[:, main : 2 * main], grads[:, :main]
        )
        hidden_ref[rows, :main] = hidden
        cots_ref[rows, :main] = gate_cot
        cots_ref[rows, main : 2 * main] = up_cot
        rest = both[:, 2 * main :]
        hidden, gate_cot, up_cot = activate(rest[:, :tail], rest[:, tail:], grads[:, main:])
        hidden_ref[rows, main:] = hidden
        cots_ref[rows, 2 * main : 2 * main + tail] = gate_cot
        cots_ref[rows, 2 * main + tail :] = up_cot
        partial = lax.dot_general(
            cots_ref[rows, :], matrix[...], (((1,), (1,)), ((), ())), preferred_element_type=F32
        )
        for j in range(chunk // (2 * step)):
            even = partial[2 * j * step : (2 * j + 1) * step]
            odd = partial[(2 * j + 1) * step : (2 * j + 2) * step]
            y = first // (2 * step) + j
            keep_ref[y] = jnp.where(core == 0, even, odd).astype(BF16)
            give_ref[y] = jnp.where(core == 0, odd, even).astype(BF16)


def forward(place, table, own, other, grads, ny, chunk):
    pool, width = table.shape
    pair = other.shape[2]
    part = pair // 2
    main = part // 128 * 128
    step = pool // (2 * ny)
    return pl.pallas_call(
        functools.partial(forward_kernel, chunk, main, part - main),
        out_shape=(
            jax.ShapeDtypeStruct((pool, part), BF16),
            jax.ShapeDtypeStruct((pool, pair), BF16),
            jax.ShapeDtypeStruct((ny, step, width), BF16),
            jax.ShapeDtypeStruct((ny, step, width), BF16),
        ),
        in_specs=[SMEM, VMEM, ANY, ANY, VMEM],
        out_specs=(VMEM, VMEM, VMEM, VMEM),
        scratch_shapes=[
            pltpu.VMEM((width, pair), BF16),
            pltpu.SemaphoreType.DMA((2 * other.shape[0],)),
        ],
        compiler_params=params(48),
        cost_estimate=pl.CostEstimate(
            flops=4 * pool * width * pair, bytes_accessed=2 * (2 * pool * width + width * pair), transcendentals=0
        ),
    )(place, table, own, other, grads)


def gradient_kernel(tile, nx, nl, nc, table_ref, cots_ref, out_ref, total):
    width = table_ref.shape[1]
    for first in range(0, width, tile):
        total[first : first + tile, :] = lax.dot_general(
            table_ref[:, first : first + tile], cots_ref[...], (((0,), (0,)), ((), ())),
            preferred_element_type=F32,
        )
    piece = width // (nx * nl * nc)
    block = nx * piece
    for c in range(nc):
        for l in range(nl):
            found = [
                total[((x * nl + l) * nc + c) * piece : ((x * nl + l) * nc + c + 1) * piece, :]
                for x in range(nx)
            ]
            z = c * nl + l
            out_ref[z * block : (z + 1) * block, :] = jnp.concatenate(found, axis=0).astype(BF16)


def gradient(table, cots, nx, nl, nc, tile):
    pool, width = table.shape
    pair = cots.shape[1]
    return pl.pallas_call(
        functools.partial(gradient_kernel, tile, nx, nl, nc),
        out_shape=jax.ShapeDtypeStruct((width, pair), BF16),
        in_specs=[VMEM, VMEM],
        out_specs=VMEM,
        scratch_shapes=[pltpu.VMEM((width, pair), F32)],
        compiler_params=params(48),
        cost_estimate=pl.CostEstimate(
            flops=2 * pool * width * pair, bytes_accessed=2 * (pool * width + width * pair), transcendentals=0
        ),
    )(table, cots)


def swap_over_x(pieces, nx):
    me = lax.axis_index("x")
    got = [lax.dynamic_index_in_dim(pieces, me, 0, keepdims=False)]
    for shift in range(1, nx):
        piece = lax.dynamic_index_in_dim(pieces, lax.rem(me + shift, nx), 0, keepdims=False)
        got.append(lax.ppermute(piece, "x", ring(nx, shift)))
    return got


def make_step(nc, nx, nl, ny, nk):
    def per_device(tokens, norm_gain, gate_weight, up_weight, hidden_grad):
        rows, width = tokens.shape
        feats, units = gate_weight.shape
        main, tail = share_sizes(units, nx)
        part = main + tail
        own_tokens = hidden_grad.shape[0]
        half = own_tokens // 2
        pool = nx * own_tokens
        nz = nc * nl
        place = jnp.stack([lax.axis_index("l"), lax.axis_index("k")]).astype(jnp.int32)

        token_vals = tokens.astype(F32)
        row_scale = lax.rsqrt(jnp.mean(token_vals * token_vals, axis=1) + 1e-06).astype(BF16)
        scale_own = row_scale.astype(F32)
        scaled = (token_vals * norm_gain).astype(BF16).astype(F32)
        normed = (scaled * scale_own[:, None]).astype(BF16)
        near = exchange(jnp.broadcast_to(normed[None], (nx, rows, width)), "x")
        near = near.reshape(nx * rows, width)
        table = lax.all_gather(near, ("y", "k"), axis=0, tiled=True)

        other_gate = lax.ppermute(gate_weight, ("c", "l"), ring(nz, 1))
        other_up = lax.ppermute(up_weight, ("c", "l"), ring(nz, -1))
        own = exchange(pack(nx, gate_weight, up_weight, hidden_grad), "x")
        other = exchange(pack(nx, other_gate, other_up), "x")
        grads = own[:, feats:]
        grads = jnp.stack(
            [
                jnp.concatenate(
                    [
                        grads[:, :, h * main : (h + 1) * main],
                        grads[:, :, 2 * main + h * tail : 2 * main + (h + 1) * tail],
                    ],
                    axis=2,
                )
                for h in range(2)
            ],
            axis=1,
        )
        grads = grads.reshape(nx, ny * nk, rows, part).transpose(1, 0, 2, 3).reshape(pool, part)

        hidden, cots, keep, give = forward(place, table, own, other, grads, ny, pool // 2)
        taken = lax.ppermute(give, "k", [(0, 1), (1, 0)])
        grad = gradient(table, cots, nx, nl, nc, width // 3)
        grad = lax.psum_scatter(grad, ("c", "l"), scatter_dimension=0, tiled=True)
        grad = grad.reshape(nx, feats // nc, 2 * part)

        partial = (keep.astype(F32) + taken.astype(F32)).astype(BF16)
        partial = exchange(partial, "y")
        partial = jnp.sum(partial.astype(F32), axis=0).astype(BF16).reshape(nx, rows, width)
        inner_grad = sum(piece.astype(F32) for piece in swap_over_x(partial, nx))
        inner_grad = inner_grad * scale_own[:, None]
        inner = jnp.sum(scaled * inner_grad, axis=1)
        factor = scale_own * scale_own / width
        input_grad = (
            norm_gain * inner_grad - factor[:, None] * token_vals * inner[:, None]
        ).astype(BF16)

        def ordered(pieces):
            me = lax.axis_index("x")
            stacked = jnp.stack(pieces)
            return [
                lax.dynamic_index_in_dim(stacked, lax.rem(me - q + nx, nx), 0, keepdims=False)
                for q in range(nx)
            ]

        spread = hidden.reshape(ny * nk, nx, rows, part).transpose(1, 0, 2, 3)
        spread = ordered(swap_over_x(spread.reshape(nx, own_tokens, part), nx))
        hidden = jnp.concatenate(
            [p[:, :main] for p in spread] + [p[:, main:] for p in spread], axis=1
        )
        grad = [p.astype(F32) for p in ordered(swap_over_x(grad, nx))]
        gate_grad = jnp.concatenate(
            [p[:, :main] for p in grad] + [p[:, 2 * main : 2 * main + tail] for p in grad], axis=1
        )
        up_grad = jnp.concatenate(
            [p[:, main : 2 * main] for p in grad] + [p[:, 2 * main + tail :] for p in grad], axis=1
        )
        return (hidden, input_grad, gate_grad, up_grad)

    return per_device


def solution(mesh):
    fine = split_fsdp(mesh)
    return jax.shard_map(
        make_step(*fine.devices.shape),
        mesh=fine,
        in_specs=(
            P(("c", "x", "l", "y", "k"), None),
            P(),
            P(("x", "l"), ("y", "k")),
            P(("x", "l"), ("y", "k")),
            P(("c", "x", "l"), ("y", "k")),
        ),
        out_specs=(
            P(("c", "x", "l"), ("y", "k")),
            P(("c", "x", "l", "y", "k"), None),
            P(("x", "l", "c"), ("y", "k")),
            P(("x", "l", "c"), ("y", "k")),
        ),
        check_vma=False,
    )
```

time: 214 us -> 191 us (0.89)
  Pallas kernels: 0 us -> 20.3 us
  blocking collectives: 29.9 us -> 10.3 us
  starting transfers between devices: 40.4 us -> 57.1 us
  waiting for transfers between devices: 69.5 us -> 56.8 us
  matrix products: 12.4 us -> 0 us
  local copies, waits for them, and re-layouts: 35.4 us -> 23 us
  other arithmetic: 10.3 us -> 7.75 us
    all_to_all x4 -> x3, waiting for transfers between devices: 61.1 us -> 32.5 us  [exchange(): return lax.all_to_all(value, axis, split_axis=0, concat_axis=0, tiled=True)]
    pallas_call x0 -> x4, Pallas kernels: none -> 20.3 us  [the longest x1 11.7 us: forward(): pl.pallas_call(functools.partial(forward_kernel, chunk, main, part - main...]
    all_to_all x2 -> x1, blocking collectives: 29.9 us -> 10.3 us  [exchange(): return lax.all_to_all(value, axis, split_axis=0, concat_axis=0, tiled=True)]
    ppermute x2 -> x11, starting transfers between devices: 16.4 us -> 35.9 us  [the longest x9 23.2 us: swap_over_x(): got.append(lax.ppermute(piece, 'x', ring(nx, shift)))]
    ppermute x2 -> x11, waiting for transfers between devices: 8.33 us -> 24.2 us  [the longest x9 12.2 us: swap_over_x(): got.append(lax.ppermute(piece, 'x', ring(nx, shift)))]
    dot_general x3 -> x0, matrix products: 12.4 us -> none  [the longest x1 5.3 us: per_device(): both = jnp.dot(table, matrix, preferred_element_type=F32)]
    convert_element_type x7 -> x0, local copies, waits for them, and re-layouts: 9.9 us -> none  [the longest x5 5.56 us: per_device(): cotangent = grads.astype(F32)]
    reshape x8 -> x2, local copies, waits for them, and re-layouts: 6.52 us -> 2.21 us  [the longest x1 2.16 us: per_device(): grads.reshape(nx, ny * nk, rows, part).transpose(1, 0, 2, 3)]
  transfers between devices with their start and end apart: 9 -> 17, of which waited for: 6 -> 9; matrix products, arithmetic and copies ran while one was open for 19% -> 11% of each run, Pallas kernels for 0% -> 5%
where the time goes in v2:
time: 191 us; the launch traced here: 190 us
  starting transfers between devices  57.1 us (30%)
  waiting for transfers between devices  56.8 us (30%)
  local copies, waits for them, and re-layouts  23 us (12%)
  Pallas kernels  20.3 us (11%)
  between operations  14.5 us (8%)
  blocking collectives  10.3 us (5%)
  other arithmetic  7.75 us (4%)
    all_to_all x3, waiting for transfers between devices, exchange(): return lax.all_to_all(value, axis, split_axis=0, concat_axis=0, tiled=True)  32.5 us
    ppermute x9, starting transfers between devices, swap_over_x(): got.append(lax.ppermute(piece, 'x', ring(nx, shift)))  23.2 us
    all_to_all x3, starting transfers between devices, exchange(): return lax.all_to_all(value, axis, split_axis=0, concat_axis=0, tiled=True)  14.4 us
    ppermute x9, waiting for transfers between devices, swap_over_x(): got.append(lax.ppermute(piece, 'x', ring(nx, shift)))  12.2 us
    pallas_call x1, Pallas kernels, forward(): pl.pallas_call(functools.partial(forward_kernel, chunk, main, part - main...  11.7 us
    ppermute x1, waiting for transfers between devices, per_device(): other_gate = lax.ppermute(gate_weight, ('c', 'l'), ring(nz, 1))  11.2 us
    all_to_all x1, blocking collectives, exchange(): return lax.all_to_all(value, axis, split_axis=0, concat_axis=0, tiled=True)  10.3 us
    ppermute x1, starting transfers between devices, per_device(): other_up = lax.ppermute(up_weight, ('c', 'l'), ring(nz, -1))  8.59 us
  transfers between devices with their start and end apart: 17, of which 9 were waited for; matrix products, arithmetic and copies ran while one was open for 11% of the time, Pallas kernels for 5%

profile of v2, /device:TPU:1, one launch (start us, length us, event | category | flops | bytes accessed | tf_op | source)
XLA Modules:
  0.0 189.9 jit_solution(13071848100218570120)
XLA Ops:
  9.4 10.3 %all_to_all.20 = bf16[4,12,2304]{2,1,0:T(8,128)(2,1)S(1)} all-to-all(bf16[4,12,2304]{2,1,0:T(8,128)(2,1)S(1)} %broadcast_in_dim.2), channel_id=1, replica_groups=mesh['c'=4,'x'=4,'l'=2,'y'=8,'k'=2] {'x'}, dimensions={0} | all-to-all | bytes 442368 | tf_op jit(solution)/shard_map/all_to_all | solution.py:32
  21.9 2.4 %copy.18 = bf16[4,384,576]{1,2,0:T(8,128)(2,1)} copy(bf16[4,384,576]{2,1,0:T(8,128)(2,1)S(1)} %shard_map.84) | data formatting | bytes 3538944 | tf_op jit(solution)/shard_map/pallas_call | solution.py:76
  24.3 3.6 %all-to-all-start.1 = ((bf16[4,384,576]{1,2,0:T(8,128)(2,1)}), bf16[4,384,576]{1,2,0:T(8,128)(2,1)S(1)}, u32[]{:S(2)}, u32[]{:S(2)}) async-start(bf16[4,384,576]{1,2,0:T(8,128)(2,1)} %copy.18), calls=%async_computation.1 | async-start | bytes 3538944 | tf_op jit(solution)/shard_map/all_to_all | solution.py:32
  27.9 4.1 %collective-permute-start = (bf16[288,1152]{1,0:T(8,128)(2,1)S(1)}, bf16[288,1152]{1,0:T(8,128)(2,1)S(1)}, u32[]{:S(2)}, u32[]{:S(2)}) collective-permute-start(bf16[288,1152]{1,0:T(8,128)(2,1)S(1)} %copy-done), channel_id=1, source_target_pairs={{0,16},{16,128},{128,144},{144,256},{256,272},{272,384},{384,400},... | collective-permute-start | bytes 1990664 | tf_op jit(solution)/shard_map/ppermute | solution.py:235
  32.0 8.6 %collective-permute-start.1 = (bf16[288,1152]{1,0:T(8,128)(2,1)S(1)}, bf16[288,1152]{1,0:T(8,128)(2,1)S(1)}, u32[]{:S(2)}, u32[]{:S(2)}) collective-permute-start(bf16[288,1152]{1,0:T(8,128)(2,1)S(1)} %copy-done.1), channel_id=1, source_target_pairs={{0,400},{16,0},{128,16},{144,128},{256,144},{272,256},{384,272},{4... | collective-permute-start | bytes 1990664 | tf_op jit(solution)/shard_map/ppermute | solution.py:236
  40.6 11.2 %collective-permute-done.gate_ref = bf16[288,1152]{1,0:T(8,128)(2,1)S(1)} collective-permute-done((bf16[288,1152]{1,0:T(8,128)(2,1)S(1)}, bf16[288,1152]{1,0:T(8,128)(2,1)S(1)}, u32[]{:S(2)}, u32[]{:S(2)}) %collective-permute-start) | collective-permute-done | bytes 663584 | tf_op jit(solution)/shard_map/ppermute | solution.py:235
  54.0 3.9 %all-to-all-start.2 = ((bf16[4,288,576]{2,1,0:T(8,128)(2,1)}), bf16[4,288,576]{2,1,0:T(8,128)(2,1)S(1)}, u32[]{:S(2)}, u32[]{:S(2)}) async-start(bf16[4,288,576]{2,1,0:T(8,128)(2,1)} %shard_map.85), calls=%async_computation.2 | async-start | bytes 2949120 | tf_op jit(solution)/shard_map/all_to_all | solution.py:32
  59.4 2.1 %copy.19 = bf16[4,2,96,288]{3,0,2,1:T(4,128)(2,1)} copy(bf16[4,2,96,288]{2,3,0,1:T(8,128)(2,1)} %pad_maximum_fusion) | data formatting | bytes 884736 | tf_op jit(solution)/shard_map/stack | solution.py:240
  61.5 2.1 %copy.20 = bf16[16,4,12,288]{3,2,1,0:T(8,128)(2,1)} copy(bf16[16,4,12,288]{3,1,2,0:T(4,128)(2,1)} %bitcast.72) | data formatting | bytes 884736 | tf_op jit(solution)/shard_map/transpose | solution.py:253
  63.6 2.2 %reshape.55.grads_ref = bf16[768,288]{1,0:T(8,128)(2,1)} reshape(bf16[16,4,12,288]{3,2,1,0:T(8,128)(2,1)} %copy.20) | data formatting | bytes 884736 | tf_op jit(solution)/shard_map/reshape | solution.py:253
  65.8 2.4 %copy.21.own_ref = bf16[4,384,576]{2,1,0:T(8,128)(2,1)} copy(bf16[4,384,576]{1,2,0:T(8,128)(2,1)S(1)} %all-to-all-done.1) | data formatting | bytes 3538944 | tf_op jit(solution)/shard_map/all_to_all | solution.py:32
  68.2 5.5 %all-to-all-done.2.other_ref = bf16[4,288,576]{2,1,0:T(8,128)(2,1)S(1)} async-done(((bf16[4,288,576]{2,1,0:T(8,128)(2,1)}), bf16[4,288,576]{2,1,0:T(8,128)(2,1)S(1)}, u32[]{:S(2)}, u32[]{:S(2)}) %all-to-all-start.2) | async-done | bytes 1327136 | tf_op jit(solution)/shard_map/all_to_all | solution.py:32
  74.8 11.7 %shard_map.86 = (bf16[768,288]{1,0:T(8,128)(2,1)S(1)}, bf16[768,576]{1,0:T(8,128)(2,1)S(1)}, bf16[8,48,2304]{2,1,0:T(8,128)(2,1)S(1)}, bf16[8,48,2304]{2,1,0:T(8,128)(2,1)}) custom-call(s32[2]{0:T(128)S(1)} %pad_add_fusion.place_ref, bf16[768,2304]{1,0:T(8,128)(2,1)} %all-gather.2.cloned.1.call-done.table_ref, bf16[4,384,576]{2,1,0:T(8,128)(2,1)} %copy.21.own_ref, ...), custom_call_target="tpu_custom_call" | custom-call | flops 4076863488 | bytes 9732096 | tf_op jit(solution)/shard_map/pallas_call | solution.py:149
  87.4 6.8 %collective-permute-start.5 = (bf16[8,48,2304]{2,1,0:T(8,128)(2,1)}, bf16[8,48,2304]{2,1,0:T(8,128)(2,1)S(1)}, u32[]{:S(2)}, u32[]{:S(2)}) collective-permute-start(bf16[8,48,2304]{2,1,0:T(8,128)(2,1)} %get-tuple-element.10), channel_id=1, source_target_pairs={{0,1},{1,0},{2,3},{3,2},{4,5},{5,4},{6,7},{7,6},{8,9},{9,8},{10,11... | collective-permute-start | bytes 5308424 | tf_op jit(solution)/shard_map/ppermute | solution.py:256
  94.2 6.8 %shard_map.87 = bf16[2304,576]{1,0:T(8,128)(2,1)} custom-call(bf16[768,2304]{1,0:T(8,128)(2,1)} %all-gather.2.cloned.1.call-done.table_ref, bf16[768,576]{1,0:T(8,128)(2,1)S(1)} %get-tuple-element.11.cots_ref), custom_call_target="tpu_custom_call" | custom-call | flops 2038431744 | bytes 6193152 | tf_op jit(solution)/shard_map/pallas_call | solution.py:192
  101.0 1.6 add_convert_fusion
  102.6 7.0 %all-to-all-start.3 = ((bf16[8,48,2304]{2,1,0:T(8,128)(2,1)}), bf16[8,48,2304]{2,1,0:T(8,128)(2,1)S(1)}, u32[]{:S(2)}, u32[]{:S(2)}) async-start(bf16[8,48,2304]{2,1,0:T(8,128)(2,1)} %add_convert_fusion), calls=%async_computation.3 | async-start | bytes 3538944 | tf_op jit(solution)/shard_map/all_to_all | solution.py:32
  111.3 2.8 %collective-permute-start.4 = (bf16[192,288]{1,0:T(8,128)(2,1)S(1)}, bf16[192,288]{1,0:T(8,128)(2,1)S(1)}, u32[]{:S(2)}, u32[]{:S(2)}) collective-permute-start(bf16[192,288]{1,0:T(8,128)(2,1)S(1)} %bitcast.82), channel_id=1, source_target_pairs={{0,96},{32,0},{64,32},{96,64},{1,97},{33,1},{65,33},{97,65},{2,98}... | collective-permute-start | bytes 331784 | tf_op jit(solution)/shard_map/ppermute | solution.py:210
  114.1 3.1 %collective-permute-start.3 = (bf16[192,288]{1,0:T(8,128)(2,1)S(1)}, bf16[192,288]{1,0:T(8,128)(2,1)S(1)}, u32[]{:S(2)}, u32[]{:S(2)}) collective-permute-start(bf16[192,288]{1,0:T(8,128)(2,1)S(1)} %bitcast.84), channel_id=1, source_target_pairs={{0,64},{32,96},{64,0},{96,32},{1,65},{33,97},{65,1},{97,33},{2,66}... | collective-permute-start | bytes 331784 | tf_op jit(solution)/shard_map/ppermute | solution.py:210
  117.2 1.9 %collective-permute-start.2 = (bf16[192,288]{1,0:T(8,128)(2,1)S(1)}, bf16[192,288]{1,0:T(8,128)(2,1)S(1)}, u32[]{:S(2)}, u32[]{:S(2)}) collective-permute-start(bf16[192,288]{1,0:T(8,128)(2,1)S(1)} %bitcast.86), channel_id=1, source_target_pairs={{0,32},{32,64},{64,96},{96,0},{1,33},{33,65},{65,97},{97,1},{2,34}... | collective-permute-start | bytes 331784 | tf_op jit(solution)/shard_map/ppermute | solution.py:210
  119.4 2.9 %collective-permute-done.3 = bf16[192,288]{1,0:T(8,128)(2,1)S(1)} collective-permute-done((bf16[192,288]{1,0:T(8,128)(2,1)S(1)}, bf16[192,288]{1,0:T(8,128)(2,1)S(1)}, u32[]{:S(2)}, u32[]{:S(2)}) %collective-permute-start.3) | collective-permute-done | bytes 110624 | tf_op jit(solution)/shard_map/ppermute | solution.py:210
  122.5 2.9 %collective-permute-done.2 = bf16[192,288]{1,0:T(8,128)(2,1)S(1)} collective-permute-done((bf16[192,288]{1,0:T(8,128)(2,1)S(1)}, bf16[192,288]{1,0:T(8,128)(2,1)S(1)}, u32[]{:S(2)}, u32[]{:S(2)}) %collective-permute-start.2) | collective-permute-done | bytes 110624 | tf_op jit(solution)/shard_map/ppermute | solution.py:210
  125.7 1.5 pad_maximum_fusion.1
  127.2 27.1 %all-to-all-done.3 = bf16[8,48,2304]{2,1,0:T(8,128)(2,1)S(1)} async-done(((bf16[8,48,2304]{2,1,0:T(8,128)(2,1)}), bf16[8,48,2304]{2,1,0:T(8,128)(2,1)S(1)}, u32[]{:S(2)}, u32[]{:S(2)}) %all-to-all-start.3) | async-done | bytes 1769504 | tf_op jit(solution)/shard_map/all_to_all | solution.py:32
  154.6 2.8 %collective-permute-start.8 = (bf16[12,2304]{1,0:T(8,128)(2,1)S(1)}, bf16[12,2304]{1,0:T(8,128)(2,1)S(1)}, u32[]{:S(2)}, u32[]{:S(2)}) collective-permute-start(bf16[12,2304]{1,0:T(8,128)(2,1)S(1)} %get-tuple-element.33), channel_id=1, source_target_pairs={{0,96},{32,0},{64,32},{96,64},{1,97},{33,1},{65,33},{97,65},{2,98}... | collective-permute-start | bytes 165896 | tf_op jit(solution)/shard_map/ppermute | solution.py:210
  157.4 3.1 %collective-permute-start.7 = (bf16[12,2304]{1,0:T(8,128)(2,1)S(1)}, bf16[12,2304]{1,0:T(8,128)(2,1)S(1)}, u32[]{:S(2)}, u32[]{:S(2)}) collective-permute-start(bf16[12,2304]{1,0:T(8,128)(2,1)S(1)} %get-tuple-element.34), channel_id=1, source_target_pairs={{0,64},{32,96},{64,0},{96,32},{1,65},{33,97},{65,1},{97,33},{2,66}... | collective-permute-start | bytes 165896 | tf_op jit(solution)/shard_map/ppermute | solution.py:210
  160.5 1.9 %collective-permute-start.6 = (bf16[12,2304]{1,0:T(8,128)(2,1)S(1)}, bf16[12,2304]{1,0:T(8,128)(2,1)S(1)}, u32[]{:S(2)}, u32[]{:S(2)}) collective-permute-start(bf16[12,2304]{1,0:T(8,128)(2,1)S(1)} %get-tuple-element.32), channel_id=1, source_target_pairs={{0,32},{32,64},{64,96},{96,0},{1,33},{33,65},{65,97},{97,1},{2,34}... | collective-permute-start | bytes 165896 | tf_op jit(solution)/shard_map/ppermute | solution.py:210
  164.8 2.0 %collective-permute-done.6 = bf16[12,2304]{1,0:T(8,128)(2,1)S(1)} collective-permute-done((bf16[12,2304]{1,0:T(8,128)(2,1)S(1)}, bf16[12,2304]{1,0:T(8,128)(2,1)S(1)}, u32[]{:S(2)}, u32[]{:S(2)}) %collective-permute-start.6) | collective-permute-done | bytes 55328 | tf_op jit(solution)/shard_map/ppermute | solution.py:210
  168.1 2.6 %collective-permute-start.11 = (bf16[72,576]{1,0:T(8,128)(2,1)S(1)}, bf16[72,576]{1,0:T(8,128)(2,1)S(1)}, u32[]{:S(2)}, u32[]{:S(2)}) collective-permute-start(bf16[72,576]{1,0:T(8,128)(2,1)S(1)} %get-tuple-element.29), channel_id=1, source_target_pairs={{0,96},{32,0},{64,32},{96,64},{1,97},{33,1},{65,33},{97,65},{2,98}... | collective-permute-start | bytes 248840 | tf_op jit(solution)/shard_map/ppermute | solution.py:210
  170.7 2.5 %collective-permute-start.10 = (bf16[72,576]{1,0:T(8,128)(2,1)S(1)}, bf16[72,576]{1,0:T(8,128)(2,1)S(1)}, u32[]{:S(2)}, u32[]{:S(2)}) collective-permute-start(bf16[72,576]{1,0:T(8,128)(2,1)S(1)} %get-tuple-element.30), channel_id=1, source_target_pairs={{0,64},{32,96},{64,0},{96,32},{1,65},{33,97},{65,1},{97,33},{2,66}... | collective-permute-start | bytes 248840 | tf_op jit(solution)/shard_map/ppermute | solution.py:210
  173.2 2.5 %collective-permute-start.9 = (bf16[72,576]{1,0:T(8,128)(2,1)S(1)}, bf16[72,576]{1,0:T(8,128)(2,1)S(1)}, u32[]{:S(2)}, u32[]{:S(2)}) collective-permute-start(bf16[72,576]{1,0:T(8,128)(2,1)S(1)} %get-tuple-element.31), channel_id=1, source_target_pairs={{0,32},{32,64},{64,96},{96,0},{1,33},{33,65},{65,97},{97,1},{2,34}... | collective-permute-start | bytes 248840 | tf_op jit(solution)/shard_map/ppermute | solution.py:210
  177.5 3.3 %collective-permute-done.9 = bf16[72,576]{1,0:T(8,128)(2,1)S(1)} collective-permute-done((bf16[72,576]{1,0:T(8,128)(2,1)S(1)}, bf16[72,576]{1,0:T(8,128)(2,1)S(1)}, u32[]{:S(2)}, u32[]{:S(2)}) %collective-permute-start.9) | collective-permute-done | bytes 82976 | tf_op jit(solution)/shard_map/ppermute | solution.py:210
  (83 shorter events, 20.3 us)
Async XLA Ops:
  7.2 13.3 %copy-start = (bf16[288,1152]{1,0:T(8,128)(2,1)S(1)}, bf16[288,1152]{1,0:T(8,128)(2,1)}, u32[]{:S(2)}) copy-start(bf16[288,1152]{1,0:T(8,128)(2,1)} %gate_ref.1) | copy-start | bytes 1990660
  7.2 13.3 %copy-start.1 = (bf16[288,1152]{1,0:T(8,128)(2,1)S(1)}, bf16[288,1152]{1,0:T(8,128)(2,1)}, u32[]{:S(2)}) copy-start(bf16[288,1152]{1,0:T(8,128)(2,1)} %up_ref.1) | copy-start | bytes 1990660
  7.2 66.5 %all-gather.2.cloned.1.call-start = ((), (), s32[]{:S(2)}) async-start(), calls=%async_computation.5 | async-start | bytes 3760128 | tf_op jit(solution)/shard_map/all_gather | solution.py:233
  20.5 1.0 copy-start.5
  24.3 29.8 %all-to-all-start.1 = ((bf16[4,384,576]{1,2,0:T(8,128)(2,1)}), bf16[4,384,576]{1,2,0:T(8,128)(2,1)S(1)}, u32[]{:S(2)}, u32[]{:S(2)}) async-start(bf16[4,384,576]{1,2,0:T(8,128)(2,1)} %copy.18), calls=%async_computation.1 | async-start | bytes 3538944 | tf_op jit(solution)/shard_map/all_to_all | solution.py:32
  27.9 23.9 %collective-permute-start = (bf16[288,1152]{1,0:T(8,128)(2,1)S(1)}, bf16[288,1152]{1,0:T(8,128)(2,1)S(1)}, u32[]{:S(2)}, u32[]{:S(2)}) collective-permute-start(bf16[288,1152]{1,0:T(8,128)(2,1)S(1)} %copy-done), channel_id=1, source_target_pairs={{0,16},{16,128},{128,144},{144,256},{256,272},{272,384},{384,400},... | collective-permute-start | bytes 1990664 | tf_op jit(solution)/shard_map/ppermute | solution.py:235
  32.0 20.6 %collective-permute-start.1 = (bf16[288,1152]{1,0:T(8,128)(2,1)S(1)}, bf16[288,1152]{1,0:T(8,128)(2,1)S(1)}, u32[]{:S(2)}, u32[]{:S(2)}) collective-permute-start(bf16[288,1152]{1,0:T(8,128)(2,1)S(1)} %copy-done.1), channel_id=1, source_target_pairs={{0,400},{16,0},{128,16},{144,128},{256,144},{272,256},{384,272},{4... | collective-permute-start | bytes 1990664 | tf_op jit(solution)/shard_map/ppermute | solution.py:236
  54.0 19.7 %all-to-all-start.2 = ((bf16[4,288,576]{2,1,0:T(8,128)(2,1)}), bf16[4,288,576]{2,1,0:T(8,128)(2,1)S(1)}, u32[]{:S(2)}, u32[]{:S(2)}) async-start(bf16[4,288,576]{2,1,0:T(8,128)(2,1)} %shard_map.85), calls=%async_computation.2 | async-start | bytes 2949120 | tf_op jit(solution)/shard_map/all_to_all | solution.py:32
  57.9 109.1 %reduce-scatter.2.cloned.1.call-start = ((), (), s32[]{:S(2)}) async-start(), calls=%async_computation.6 | async-start | bytes 3317760 | tf_op jit(solution)/shard_map/reduce_scatter | solution.py:258
  73.7 1.1 copy-start.4
  86.5 0.9 copy-start.2
  87.4 13.6 %collective-permute-start.5 = (bf16[8,48,2304]{2,1,0:T(8,128)(2,1)}, bf16[8,48,2304]{2,1,0:T(8,128)(2,1)S(1)}, u32[]{:S(2)}, u32[]{:S(2)}) collective-permute-start(bf16[8,48,2304]{2,1,0:T(8,128)(2,1)} %get-tuple-element.10), channel_id=1, source_target_pairs={{0,1},{1,0},{2,3},{3,2},{4,5},{5,4},{6,7},{7,6},{8,9},{9,8},{10,11... | collective-permute-start | bytes 5308424 | tf_op jit(solution)/shard_map/ppermute | solution.py:256
  102.6 7.0 %copy-start.3 = (bf16[768,288]{1,0:T(8,128)(2,1)S(1)}, bf16[768,288]{1,0:T(8,128)(2,1)}, u32[]{:S(2)}) copy-start(bf16[768,288]{1,0:T(8,128)(2,1)} %copy-done.2) | copy-start | bytes 1327108
  102.6 51.6 %all-to-all-start.3 = ((bf16[8,48,2304]{2,1,0:T(8,128)(2,1)}), bf16[8,48,2304]{2,1,0:T(8,128)(2,1)S(1)}, u32[]{:S(2)}, u32[]{:S(2)}) async-start(bf16[8,48,2304]{2,1,0:T(8,128)(2,1)} %add_convert_fusion), calls=%async_computation.3 | async-start | bytes 3538944 | tf_op jit(solution)/shard_map/all_to_all | solution.py:32
  111.3 7.9 %collective-permute-start.4 = (bf16[192,288]{1,0:T(8,128)(2,1)S(1)}, bf16[192,288]{1,0:T(8,128)(2,1)S(1)}, u32[]{:S(2)}, u32[]{:S(2)}) collective-permute-start(bf16[192,288]{1,0:T(8,128)(2,1)S(1)} %bitcast.82), channel_id=1, source_target_pairs={{0,96},{32,0},{64,32},{96,64},{1,97},{33,1},{65,33},{97,65},{2,98}... | collective-permute-start | bytes 331784 | tf_op jit(solution)/shard_map/ppermute | solution.py:210
  114.1 8.2 %collective-permute-start.3 = (bf16[192,288]{1,0:T(8,128)(2,1)S(1)}, bf16[192,288]{1,0:T(8,128)(2,1)S(1)}, u32[]{:S(2)}, u32[]{:S(2)}) collective-permute-start(bf16[192,288]{1,0:T(8,128)(2,1)S(1)} %bitcast.84), channel_id=1, source_target_pairs={{0,64},{32,96},{64,0},{96,32},{1,65},{33,97},{65,1},{97,33},{2,66}... | collective-permute-start | bytes 331784 | tf_op jit(solution)/shard_map/ppermute | solution.py:210
  117.2 8.3 %collective-permute-start.2 = (bf16[192,288]{1,0:T(8,128)(2,1)S(1)}, bf16[192,288]{1,0:T(8,128)(2,1)S(1)}, u32[]{:S(2)}, u32[]{:S(2)}) collective-permute-start(bf16[192,288]{1,0:T(8,128)(2,1)S(1)} %bitcast.86), channel_id=1, source_target_pairs={{0,32},{32,64},{64,96},{96,0},{1,33},{33,65},{65,97},{97,1},{2,34}... | collective-permute-start | bytes 331784 | tf_op jit(solution)/shard_map/ppermute | solution.py:210
  154.6 10.2 %collective-permute-start.8 = (bf16[12,2304]{1,0:T(8,128)(2,1)S(1)}, bf16[12,2304]{1,0:T(8,128)(2,1)S(1)}, u32[]{:S(2)}, u32[]{:S(2)}) collective-permute-start(bf16[12,2304]{1,0:T(8,128)(2,1)S(1)} %get-tuple-element.33), channel_id=1, source_target_pairs={{0,96},{32,0},{64,32},{96,64},{1,97},{33,1},{65,33},{97,65},{2,98}... | collective-permute-start | bytes 165896 | tf_op jit(solution)/shard_map/ppermute | solution.py:210
  157.4 7.4 %collective-permute-start.7 = (bf16[12,2304]{1,0:T(8,128)(2,1)S(1)}, bf16[12,2304]{1,0:T(8,128)(2,1)S(1)}, u32[]{:S(2)}, u32[]{:S(2)}) collective-permute-start(bf16[12,2304]{1,0:T(8,128)(2,1)S(1)} %get-tuple-element.34), channel_id=1, source_target_pairs={{0,64},{32,96},{64,0},{96,32},{1,65},{33,97},{65,1},{97,33},{2,66}... | collective-permute-start | bytes 165896 | tf_op jit(solution)/shard_map/ppermute | solution.py:210
  160.5 6.3 %collective-permute-start.6 = (bf16[12,2304]{1,0:T(8,128)(2,1)S(1)}, bf16[12,2304]{1,0:T(8,128)(2,1)S(1)}, u32[]{:S(2)}, u32[]{:S(2)}) collective-permute-start(bf16[12,2304]{1,0:T(8,128)(2,1)S(1)} %get-tuple-element.32), channel_id=1, source_target_pairs={{0,32},{32,64},{64,96},{96,0},{1,33},{33,65},{65,97},{97,1},{2,34}... | collective-permute-start | bytes 165896 | tf_op jit(solution)/shard_map/ppermute | solution.py:210
  163.7 3.1 %copy-start.6 = (bf16[12,2304]{1,0:T(8,128)(2,1)S(1)}, bf16[12,2304]{1,0:T(8,128)(2,1)}, u32[]{:S(2)}) copy-start(bf16[12,2304]{1,0:T(8,128)(2,1)} %param.5) | copy-start | bytes 165892
  163.7 3.1 %copy-start.7 = (f32[2304]{0:T(1024)S(1)}, f32[2304]{0:T(1024)}, u32[]{:S(2)}) copy-start(f32[2304]{0:T(1024)} %param.6) | copy-start | bytes 27652
  168.1 8.4 %collective-permute-start.11 = (bf16[72,576]{1,0:T(8,128)(2,1)S(1)}, bf16[72,576]{1,0:T(8,128)(2,1)S(1)}, u32[]{:S(2)}, u32[]{:S(2)}) collective-permute-start(bf16[72,576]{1,0:T(8,128)(2,1)S(1)} %get-tuple-element.29), channel_id=1, source_target_pairs={{0,96},{32,0},{64,32},{96,64},{1,97},{33,1},{65,33},{97,65},{2,98}... | collective-permute-start | bytes 248840 | tf_op jit(solution)/shard_map/ppermute | solution.py:210
  170.7 6.8 %collective-permute-start.10 = (bf16[72,576]{1,0:T(8,128)(2,1)S(1)}, bf16[72,576]{1,0:T(8,128)(2,1)S(1)}, u32[]{:S(2)}, u32[]{:S(2)}) collective-permute-start(bf16[72,576]{1,0:T(8,128)(2,1)S(1)} %get-tuple-element.30), channel_id=1, source_target_pairs={{0,64},{32,96},{64,0},{96,32},{1,65},{33,97},{65,1},{97,33},{2,66}... | collective-permute-start | bytes 248840 | tf_op jit(solution)/shard_map/ppermute | solution.py:210
  173.2 7.6 %collective-permute-start.9 = (bf16[72,576]{1,0:T(8,128)(2,1)S(1)}, bf16[72,576]{1,0:T(8,128)(2,1)S(1)}, u32[]{:S(2)}, u32[]{:S(2)}) collective-permute-start(bf16[72,576]{1,0:T(8,128)(2,1)S(1)} %get-tuple-element.31), channel_id=1, source_target_pairs={{0,32},{32,64},{64,96},{96,0},{1,33},{33,65},{65,97},{97,1},{2,34}... | collective-permute-start | bytes 248840 | tf_op jit(solution)/shard_map/ppermute | solution.py:210
Sparse Core Ops, SparseCore 0:
  20.6 48.7 all-gather.1
  101.1 42.5 reduce-scatter.1

commit v3 on v2

--- a/solution.py
+++ b/solution.py
@@ -94,12 +94,32 @@
     return hidden, (cotangent * upward * slope).astype(BF16), (cotangent * active).astype(BF16)
 
 
+def split_index(value, size, top):
+    factor = (1 << 20) // size + 1
+    assert all(i * factor >> 20 == i // size for i in range(top))
+    high = (value * factor) >> 20
+    return high, value - high * size
+
+
+def shuffle(pool, outer, inner, rows):
+    index = lax.broadcasted_iota(jnp.int32, (pool, 1), 0)
+    high, rest = split_index(index, inner * rows, pool)
+    mid, low = split_index(rest, rows, inner * rows)
+    source = mid * (outer * rows) + high * rows + low
+    columns = lax.broadcasted_iota(jnp.int32, (pool, pool), 1)
+    return (columns == source).astype(F32).astype(BF16)
+
+
 def forward_kernel(
-    chunk, main, tail, place_ref, table_ref, own_ref, other_ref, grads_ref,
-    hidden_ref, cots_ref, keep_ref, give_ref, matrix, sems,
+    chunk, main, tail, rows_each, place_ref, table_any, own_ref, other_ref,
+    hidden_ref, cots_ref, keep_ref, give_ref, table_ref, matrix, raw, grads_ref, found, sems,
 ):
     blocks, feats, _ = other_ref.shape
+    pool = table_ref.shape[0]
+    half = raw.shape[1]
     low, core = place_ref[0], place_ref[1]
+    grads_copy = pltpu.make_async_copy(own_ref.at[:, pl.ds(feats, half)], raw, sems.at[2 * blocks])
+    grads_copy.start()
     copies = []
     for x in range(blocks):
         for i, (src, at) in enumerate(((own_ref, low), (other_ref, 1 - low))):
@@ -109,24 +129,44 @@
                     src.at[x, pl.ds(0, feats)], matrix.at[rows], sems.at[2 * x + i]
                 )
             )
+    tables = [
+        pltpu.make_async_copy(
+            table_any.at[pl.ds(first, chunk)], table_ref.at[pl.ds(first, chunk)],
+            sems.at[2 * blocks + 1 + first // chunk],
+        )
+        for first in range(0, pool, chunk)
+    ]
+    tables[0].start()
     for copy in copies:
         copy.start()
+    for copy in tables[1:]:
+        copy.start()
+    groups = pool // (blocks * rows_each)
+    forth = shuffle(pool, groups, blocks, rows_each)
+    back = shuffle(pool, blocks, groups, rows_each)
+    grads_copy.wait()
+    for x in range(blocks):
+        for h in range(2):
+            rows = slice((2 * x + h) * half, (2 * x + h + 1) * half)
+            grads_ref[rows, :main] = raw[x, :, h * main : (h + 1) * main]
+            grads_ref[rows, main:] = raw[x, :, 2 * main + h * tail : 2 * main + (h + 1) * tail]
     for copy in copies:
         copy.wait()
     step = keep_ref.shape[1]
-    for first in range(0, table_ref.shape[0], chunk):
+    for first in range(0, pool, chunk):
         rows = slice(first, first + chunk)
+        tables[first // chunk].wait()
         both = jnp.dot(table_ref[rows, :], matrix[...], preferred_element_type=F32)
-        grads = grads_ref[rows, :].astype(F32)
+        grads = jnp.dot(forth[rows, :], grads_ref[...], preferred_element_type=F32)
         hidden, gate_cot, up_cot = activate(
             both[:, :main], both[:, main : 2 * main], grads[:, :main]
         )
-        hidden_ref[rows, :main] = hidden
+        found[rows, :main] = hidden
         cots_ref[rows, :main] = gate_cot
         cots_ref[rows, main : 2 * main] = up_cot
         rest = both[:, 2 * main :]
         hidden, gate_cot, up_cot = activate(rest[:, :tail], rest[:, tail:], grads[:, main:])
-        hidden_ref[rows, main:] = hidden
+        found[rows, main:] = hidden
         cots_ref[rows, 2 * main : 2 * main + tail] = gate_cot
         cots_ref[rows, 2 * main + tail :] = up_cot
         partial = lax.dot_general(
@@ -138,33 +178,44 @@
             y = first // (2 * step) + j
             keep_ref[y] = jnp.where(core == 0, even, odd).astype(BF16)
             give_ref[y] = jnp.where(core == 0, odd, even).astype(BF16)
-
-
-def forward(place, table, own, other, grads, ny, chunk):
+    spread = jnp.dot(back, found[...], preferred_element_type=F32).astype(BF16)
+    for x in range(blocks):
+        for h in range(2):
+            rows = slice((2 * x + h) * half, (2 * x + h + 1) * half)
+            hidden_ref[x, :, h * main : (h + 1) * main] = spread[rows, :main]
+            hidden_ref[x, :, 2 * main + h * tail : 2 * main + (h + 1) * tail] = spread[rows, main:]
+
+
+def forward(place, table, own, other, ny, rows_each, chunk):
     pool, width = table.shape
-    pair = other.shape[2]
+    blocks, feats, pair = other.shape
     part = pair // 2
     main = part // 128 * 128
     step = pool // (2 * ny)
+    half = own.shape[1] - feats
     return pl.pallas_call(
-        functools.partial(forward_kernel, chunk, main, part - main),
+        functools.partial(forward_kernel, chunk, main, part - main, rows_each),
         out_shape=(
-            jax.ShapeDtypeStruct((pool, part), BF16),
+            jax.ShapeDtypeStruct((blocks, half, pair), BF16),
             jax.ShapeDtypeStruct((pool, pair), BF16),
             jax.ShapeDtypeStruct((ny, step, width), BF16),
             jax.ShapeDtypeStruct((ny, step, width), BF16),
         ),
-        in_specs=[SMEM, VMEM, ANY, ANY, VMEM],
+        in_specs=[SMEM, ANY, ANY, ANY],
         out_specs=(VMEM, VMEM, VMEM, VMEM),
         scratch_shapes=[
+            pltpu.VMEM((pool, width), BF16),
             pltpu.VMEM((width, pair), BF16),
-            pltpu.SemaphoreType.DMA((2 * other.shape[0],)),
+            pltpu.VMEM((blocks, half, pair), BF16),
+            pltpu.VMEM((pool, part), BF16),
+            pltpu.VMEM((pool, part), BF16),
+            pltpu.SemaphoreType.DMA((2 * blocks + 1 + pool // chunk,)),
         ],
         compiler_params=params(48),
         cost_estimate=pl.CostEstimate(
             flops=4 * pool * width * pair, bytes_accessed=2 * (2 * pool * width + width * pair), transcendentals=0
         ),
-    )(place, table, own, other, grads)
+    )(place, table, own, other)
 
 
 def gradient_kernel(tile, nx, nl, nc, table_ref, cots_ref, out_ref, total):
@@ -211,84 +262,148 @@
     return got
 
 
+def row_scale_of(token_vals):
+    mean = jnp.mean(token_vals * token_vals, axis=1, keepdims=True)
+    return lax.rsqrt(mean + 1e-06).astype(BF16).astype(F32)
+
+
+def normalise_kernel(tokens_ref, gain_ref, out_ref):
+    token_vals = tokens_ref[...].astype(F32)
+    scaled = (token_vals * gain_ref[...]).astype(BF16).astype(F32)
+    normed = (scaled * row_scale_of(token_vals)).astype(BF16)
+    for i in range(out_ref.shape[0]):
+        out_ref[i] = normed
+
+
+def normalise(tokens, gain, copies):
+    return pl.pallas_call(
+        normalise_kernel,
+        out_shape=jax.ShapeDtypeStruct((copies, *tokens.shape), BF16),
+        in_specs=[VMEM, VMEM],
+        out_specs=VMEM,
+        compiler_params=params(8),
+    )(tokens, gain)
+
+
+def gather_kernel(nx, rows, wide, thin, sums_ref, grad_ref, out_ref):
+    total = sums_ref[0].astype(F32)
+    for i in range(1, sums_ref.shape[0]):
+        total = total + sums_ref[i].astype(F32)
+    grad = grad_ref[...].astype(F32)
+    piece = grad.shape[0] // nx
+    pad = jnp.zeros((16 - rows, wide + thin), F32)
+    for x in range(nx):
+        mine = total[x * rows : (x + 1) * rows]
+        for j in range(nx):
+            start = nx * wide + j * thin
+            both = jnp.concatenate(
+                [mine[:, j * wide : (j + 1) * wide], mine[:, start : start + thin]], axis=1
+            )
+            out_ref[x, 16 * j : 16 * j + 16, :] = jnp.concatenate([both, pad], axis=0).astype(BF16)
+        out_ref[x, 16 * nx :, :] = grad[x * piece : (x + 1) * piece].astype(BF16)
+
+
+def finish_kernel(main, tail, wide, thin, got_ref, tokens_ref, gain_ref, input_ref, gate_ref, up_ref):
+    nx = got_ref.shape[0]
+    rows, width = tokens_ref.shape
+    found = [
+        sum(got_ref[x, 16 * j : 16 * j + 16, :].astype(F32) for x in range(nx))[:rows]
+        for j in range(nx)
+    ]
+    token_vals = tokens_ref[...].astype(F32)
+    scale = row_scale_of(token_vals)
+    gain = gain_ref[...]
+    scaled = (token_vals * gain).astype(BF16).astype(F32)
+    inner_grad = (
+        jnp.concatenate([f[:, :wide] for f in found] + [f[:, wide:] for f in found], axis=1) * scale
+    )
+    inner = jnp.sum(scaled * inner_grad, axis=1, keepdims=True)
+    factor = scale * scale / width
+    input_ref[...] = (gain * inner_grad - factor * token_vals * inner).astype(BF16)
+    for q in range(nx):
+        grad = got_ref[q, 16 * nx :, :].astype(F32)
+        start = nx * main + q * tail
+        gate_ref[:, q * main : (q + 1) * main] = grad[:, :main]
+        gate_ref[:, start : start + tail] = grad[:, 2 * main : 2 * main + tail]
+        up_ref[:, q * main : (q + 1) * main] = grad[:, main : 2 * main]
+        up_ref[:, start : start + tail] = grad[:, 2 * main + tail :]
+
+
+def spread_kernel(main, tail, place_ref, got_ref, out_ref):
+    nx, half, _ = got_ref.shape
+    me = place_ref[2]
+    for q in range(nx):
+        source = lax.rem(me - q + nx, nx)
+        start = nx * main + q * tail
+        for h in range(2):
+            rows = slice(h * half, (h + 1) * half)
+            out_ref[rows, q * main : (q + 1) * main] = got_ref[source, :, h * main : (h + 1) * main]
+            out_ref[rows, start : start + tail] = got_ref[
+                source, :, 2 * main + h * tail : 2 * main + (h + 1) * tail
+            ]
+
+
 def make_step(nc, nx, nl, ny, nk):
     def per_device(tokens, norm_gain, gate_weight, up_weight, hidden_grad):
         rows, width = tokens.shape
         feats, units = gate_weight.shape
         main, tail = share_sizes(units, nx)
-        part = main + tail
+        wide, thin = share_sizes(width, nx)
+        pair = 2 * (main + tail)
         own_tokens = hidden_grad.shape[0]
-        half = own_tokens // 2
         pool = nx * own_tokens
         nz = nc * nl
-        place = jnp.stack([lax.axis_index("l"), lax.axis_index("k")]).astype(jnp.int32)
-
-        token_vals = tokens.astype(F32)
-        row_scale = lax.rsqrt(jnp.mean(token_vals * token_vals, axis=1) + 1e-06).astype(BF16)
-        scale_own = row_scale.astype(F32)
-        scaled = (token_vals * norm_gain).astype(BF16).astype(F32)
-        normed = (scaled * scale_own[:, None]).astype(BF16)
-        near = exchange(jnp.broadcast_to(normed[None], (nx, rows, width)), "x")
-        near = near.reshape(nx * rows, width)
-        table = lax.all_gather(near, ("y", "k"), axis=0, tiled=True)
+        place = jnp.stack([lax.axis_index("l"), lax.axis_index("k"), lax.axis_index("x")])
+        place = place.astype(jnp.int32)
+        gain = norm_gain.reshape(1, width)
 
         other_gate = lax.ppermute(gate_weight, ("c", "l"), ring(nz, 1))
         other_up = lax.ppermute(up_weight, ("c", "l"), ring(nz, -1))
+
+        near = exchange(normalise(tokens, gain, nx), "x").reshape(nx * rows, width)
+        table = lax.all_gather(near, ("y", "k"), axis=0, tiled=True)
+
+        gate_weight, up_weight, hidden_grad, other_gate, other_up = lax.optimization_barrier(
+            (gate_weight, up_weight, hidden_grad, other_gate, other_up)
+        )
         own = exchange(pack(nx, gate_weight, up_weight, hidden_grad), "x")
         other = exchange(pack(nx, other_gate, other_up), "x")
-        grads = own[:, feats:]
-        grads = jnp.stack(
-            [
-                jnp.concatenate(
-                    [
-                        grads[:, :, h * main : (h + 1) * main],
-                        grads[:, :, 2 * main + h * tail : 2 * main + (h + 1) * tail],
-                    ],
-                    axis=2,
-                )
-                for h in range(2)
-            ],
-            axis=1,
-        )
-        grads = grads.reshape(nx, ny * nk, rows, part).transpose(1, 0, 2, 3).reshape(pool, part)
-
-        hidden, cots, keep, give = forward(place, table, own, other, grads, ny, pool // 2)
+
+        hidden, cots, keep, give = forward(place, table, own, other, ny, rows, pool // 2)
         taken = lax.ppermute(give, "k", [(0, 1), (1, 0)])
         grad = gradient(table, cots, nx, nl, nc, width // 3)
         grad = lax.psum_scatter(grad, ("c", "l"), scatter_dimension=0, tiled=True)
-        grad = grad.reshape(nx, feats // nc, 2 * part)
 
         partial = (keep.astype(F32) + taken.astype(F32)).astype(BF16)
         partial = exchange(partial, "y")
-        partial = jnp.sum(partial.astype(F32), axis=0).astype(BF16).reshape(nx, rows, width)
-        inner_grad = sum(piece.astype(F32) for piece in swap_over_x(partial, nx))
-        inner_grad = inner_grad * scale_own[:, None]
-        inner = jnp.sum(scaled * inner_grad, axis=1)
-        factor = scale_own * scale_own / width
-        input_grad = (
-            norm_gain * inner_grad - factor[:, None] * token_vals * inner[:, None]
-        ).astype(BF16)
-
-        def ordered(pieces):
-            me = lax.axis_index("x")
-            stacked = jnp.stack(pieces)
-            return [
-                lax.dynamic_index_in_dim(stacked, lax.rem(me - q + nx, nx), 0, keepdims=False)
-                for q in range(nx)
-            ]
-
-        spread = hidden.reshape(ny * nk, nx, rows, part).transpose(1, 0, 2, 3)
-        spread = ordered(swap_over_x(spread.reshape(nx, own_tokens, part), nx))
-        hidden = jnp.concatenate(
-            [p[:, :main] for p in spread] + [p[:, main:] for p in spread], axis=1
-        )
-        grad = [p.astype(F32) for p in ordered(swap_over_x(grad, nx))]
-        gate_grad = jnp.concatenate(
-            [p[:, :main] for p in grad] + [p[:, 2 * main : 2 * main + tail] for p in grad], axis=1
-        )
-        up_grad = jnp.concatenate(
-            [p[:, main : 2 * main] for p in grad] + [p[:, 2 * main + tail :] for p in grad], axis=1
-        )
+
+        hidden = jnp.stack(swap_over_x(hidden, nx))
+        hidden = pl.pallas_call(
+            functools.partial(spread_kernel, main, tail),
+            out_shape=jax.ShapeDtypeStruct((own_tokens, units), BF16),
+            in_specs=[SMEM, VMEM],
+            out_specs=VMEM,
+            compiler_params=params(8),
+        )(place, hidden)
+        last = pl.pallas_call(
+            functools.partial(gather_kernel, nx, rows, wide, thin),
+            out_shape=jax.ShapeDtypeStruct((nx, 16 * nx + feats // nc, pair), BF16),
+            in_specs=[VMEM, VMEM],
+            out_specs=VMEM,
+            compiler_params=params(24),
+        )(partial, grad)
+        last = exchange(last, "x")
+        input_grad, gate_grad, up_grad = pl.pallas_call(
+            functools.partial(finish_kernel, main, tail, wide, thin),
+            out_shape=(
+                jax.ShapeDtypeStruct((rows, width), BF16),
+                jax.ShapeDtypeStruct((feats // nc, units), F32),
+                jax.ShapeDtypeStruct((feats // nc, units), F32),
+            ),
+            in_specs=[VMEM, VMEM, VMEM],
+            out_specs=(VMEM, VMEM, VMEM),
+            compiler_params=params(16),
+        )(last, tokens, gain)
         return (hidden, input_grad, gate_grad, up_grad)
 
     return per_device

time: 191 us -> 202 us (1.058)
  blocking collectives: 10.3 us -> 61.7 us
  starting transfers between devices: 57.1 us -> 40.3 us
  local copies, waits for them, and re-layouts: 23 us -> 11.8 us
  waiting for transfers between devices: 56.8 us -> 49.5 us
  other arithmetic: 7.75 us -> 0.58 us
  Pallas kernels: 20.3 us -> 23.6 us
    all_to_all x1 -> x2, blocking collectives: 10.3 us -> 61.7 us  [exchange(): return lax.all_to_all(value, axis, split_axis=0, concat_axis=0, tiled=True)]
    ppermute x9 -> x3, starting transfers between devices: 23.2 us -> 9.47 us  [swap_over_x(): got.append(lax.ppermute(piece, 'x', ring(nx, shift)))]
    ppermute x9 -> x3, waiting for transfers between devices: 12.2 us -> 6.89 us  [swap_over_x(): got.append(lax.ppermute(piece, 'x', ring(nx, shift)))]
    pallas_call x0 -> x4, Pallas kernels: none -> 3.81 us  [the longest x1 1.45 us: per_device(): pl.pallas_call(functools.partial(spread_kernel, main, tail), out_shape=ja...]
    all_to_all x3, starting transfers between devices: 14.4 us -> 10.7 us  [exchange(): return lax.all_to_all(value, axis, split_axis=0, concat_axis=0, tiled=True)]
    another operation x4 -> x0, local copies, waits for them, and re-layouts: 2.77 us -> none  [the longest x1 2.08 us: per_device(): jnp.stack([jnp.concatenate([grads[:, :, h * main:(h + 1) * main], grads[:...]
    another operation x5 -> x2, other arithmetic: 2.72 us -> 0.17 us  [the longest x1 0.1 us: per_device(): hidden = jnp.stack(swap_over_x(hidden, nx))]
    concatenate x3 -> x0, local copies, waits for them, and re-layouts: 2.55 us -> none  [the longest x1 0.89 us: per_device(): jnp.concatenate([p[:, :main] for p in spread] + [p[:, main:] for p in spr...]
  transfers between devices with their start and end apart: 17 -> 11, of which waited for: 9 -> 7; matrix products, arithmetic and copies ran while one was open for 11% -> 3% of each run, Pallas kernels for 5% -> 5%
where the time goes in v3:
time: 202 us
  blocking collectives  61.7 us (31%)
  waiting for transfers between devices  49.5 us (25%)
  starting transfers between devices  40.3 us (20%)
  Pallas kernels  23.6 us (12%)
  between operations  14.3 us (7%)
  local copies, waits for them, and re-layouts  11.8 us (6%)
    all_to_all x2, blocking collectives, exchange(): return lax.all_to_all(value, axis, split_axis=0, concat_axis=0, tiled=True)  61.7 us
    all_to_all x3, waiting for transfers between devices, exchange(): return lax.all_to_all(value, axis, split_axis=0, concat_axis=0, tiled=True)  31 us
    ppermute x1, waiting for transfers between devices, per_device(): other_gate = lax.ppermute(gate_weight, ('c', 'l'), ring(nz, 1))  11.4 us
    pallas_call x1, Pallas kernels, forward(): pl.pallas_call(functools.partial(forward_kernel, chunk, main, part - main...  11.1 us
    all_to_all x3, starting transfers between devices, exchange(): return lax.all_to_all(value, axis, split_axis=0, concat_axis=0, tiled=True)  10.7 us
    ppermute x3, starting transfers between devices, swap_over_x(): got.append(lax.ppermute(piece, 'x', ring(nx, shift)))  9.47 us
    ppermute x1, starting transfers between devices, per_device(): other_up = lax.ppermute(up_weight, ('c', 'l'), ring(nz, -1))  8.59 us
    ppermute x1, starting transfers between devices, per_device(): taken = lax.ppermute(give, 'k', [(0, 1), (1, 0)])  7.32 us
  transfers between devices with their start and end apart: 11, of which 7 were waited for; matrix products, arithmetic and copies ran while one was open for 3% of the time, Pallas kernels for 5%

profile of v3, /device:TPU:1, one launch (start us, length us, event | category | flops | bytes accessed | tf_op | source)
XLA Modules:
  0.0 201.7 jit_solution(17430149830123425072)
XLA Ops:
  7.2 0.8 reshape.14.gain_ref
  8.0 0.9 copy-done.10
  9.1 10.3 %all_to_all.25 = bf16[4,12,2304]{2,1,0:T(8,128)(2,1)S(1)} all-to-all(bf16[4,12,2304]{2,1,0:T(8,128)(2,1)S(1)} %shard_map.84), channel_id=1, replica_groups=mesh['c'=4,'x'=4,'l'=2,'y'=8,'k'=2] {'x'}, dimensions={0} | all-to-all | bytes 442368 | tf_op jit(solution)/shard_map/all_to_all | solution.py:32
  20.2 4.1 %collective-permute-start = (bf16[288,1152]{1,0:T(8,128)(2,1)}, bf16[288,1152]{1,0:T(8,128)(2,1)S(1)}, u32[]{:S(2)}, u32[]{:S(2)}) collective-permute-start(bf16[288,1152]{1,0:T(8,128)(2,1)} %gate_ref), channel_id=1, source_target_pairs={{0,16},{16,128},{128,144},{144,256},{256,272},{272,384},{384,400},... | collective-permute-start | bytes 1990664 | tf_op jit(solution)/shard_map/ppermute | solution.py:360
  24.3 8.6 %collective-permute-start.1 = (bf16[288,1152]{1,0:T(8,128)(2,1)}, bf16[288,1152]{1,0:T(8,128)(2,1)S(1)}, u32[]{:S(2)}, u32[]{:S(2)}) collective-permute-start(bf16[288,1152]{1,0:T(8,128)(2,1)} %up_ref), channel_id=1, source_target_pairs={{0,400},{16,0},{128,16},{144,128},{256,144},{272,256},{384,272},{4... | collective-permute-start | bytes 1990664 | tf_op jit(solution)/shard_map/ppermute | solution.py:361
  32.9 11.4 %collective-permute-done.gate_ref = bf16[288,1152]{1,0:T(8,128)(2,1)S(1)} collective-permute-done((bf16[288,1152]{1,0:T(8,128)(2,1)}, bf16[288,1152]{1,0:T(8,128)(2,1)S(1)}, u32[]{:S(2)}, u32[]{:S(2)}) %collective-permute-start) | collective-permute-done | bytes 663584 | tf_op jit(solution)/shard_map/ppermute | solution.py:360
  44.3 0.8 copy-done.2
  45.2 0.8 copy-done.4
  46.1 1.0 copy-done.8
  47.5 2.4 %copy.9 = bf16[4,384,576]{1,2,0:T(8,128)(2,1)} copy(bf16[4,384,576]{2,1,0:T(8,128)(2,1)S(1)} %shard_map.85) | data formatting | bytes 3538944 | tf_op jit(solution)/shard_map/pallas_call | solution.py:76
  49.9 3.7 %all-to-all-start.1 = ((bf16[4,384,576]{1,2,0:T(8,128)(2,1)}), bf16[4,384,576]{1,2,0:T(8,128)(2,1)S(1)}, u32[]{:S(2)}, u32[]{:S(2)}) async-start(bf16[4,384,576]{1,2,0:T(8,128)(2,1)} %copy.9), calls=%async_computation.1 | async-start | bytes 3538944 | tf_op jit(solution)/shard_map/all_to_all | solution.py:32
  53.6 1.5 shard_map.86
  55.1 18.2 %all-to-all-done.1 = bf16[4,384,576]{1,2,0:T(8,128)(2,1)S(1)} async-done(((bf16[4,384,576]{1,2,0:T(8,128)(2,1)}), bf16[4,384,576]{1,2,0:T(8,128)(2,1)S(1)}, u32[]{:S(2)}, u32[]{:S(2)}) %all-to-all-start.1) | async-done | bytes 1769504 | tf_op jit(solution)/shard_map/all_to_all | solution.py:32
  73.3 3.6 %all-to-all-start.2 = ((bf16[4,288,576]{2,1,0:T(8,128)(2,1)}), bf16[4,288,576]{2,1,0:T(8,128)(2,1)S(1)}, u32[]{:S(2)}, u32[]{:S(2)}) async-start(bf16[4,288,576]{2,1,0:T(8,128)(2,1)} %shard_map.86), calls=%async_computation.2 | async-start | bytes 2949120 | tf_op jit(solution)/shard_map/all_to_all | solution.py:32
  77.0 2.4 %copy.10.own_ref = bf16[4,384,576]{2,1,0:T(8,128)(2,1)} copy(bf16[4,384,576]{1,2,0:T(8,128)(2,1)S(1)} %all-to-all-done.1) | data formatting | bytes 3538944 | tf_op jit(solution)/shard_map/all_to_all | solution.py:32
  79.4 12.8 %all-to-all-done.2.other_ref = bf16[4,288,576]{2,1,0:T(8,128)(2,1)S(1)} async-done(((bf16[4,288,576]{2,1,0:T(8,128)(2,1)}), bf16[4,288,576]{2,1,0:T(8,128)(2,1)S(1)}, u32[]{:S(2)}, u32[]{:S(2)}) %all-to-all-start.2) | async-done | bytes 1327136 | tf_op jit(solution)/shard_map/all_to_all | solution.py:32
  92.2 11.1 %shard_map.87 = (bf16[4,96,576]{2,1,0:T(8,128)(2,1)S(1)}, bf16[768,576]{1,0:T(8,128)(2,1)S(1)}, bf16[8,48,2304]{2,1,0:T(8,128)(2,1)S(1)}, bf16[8,48,2304]{2,1,0:T(8,128)(2,1)}) custom-call(s32[3]{0:T(128)S(1)} %pad_add_fusion.place_ref, bf16[768,2304]{1,0:T(8,128)(2,1)} %all-gather.2.cloned.1.call-done.table_any.table_ref, ...), custom_call_target="tpu_custom_call" | custom-call | flops 4076863488 | bytes 9732096 | tf_op jit(solution)/shard_map/pallas_call | solution.py:196
  103.3 0.8 copy-done.6
  104.1 7.3 %collective-permute-start.5 = (bf16[8,48,2304]{2,1,0:T(8,128)(2,1)}, bf16[8,48,2304]{2,1,0:T(8,128)(2,1)S(1)}, u32[]{:S(2)}, u32[]{:S(2)}) collective-permute-start(bf16[8,48,2304]{2,1,0:T(8,128)(2,1)} %get-tuple-element.23), channel_id=1, source_target_pairs={{0,1},{1,0},{2,3},{3,2},{4,5},{5,4},{6,7},{7,6},{8,9},{9,8},{10,11... | collective-permute-start | bytes 5308424 | tf_op jit(solution)/shard_map/ppermute | solution.py:373
  111.4 6.8 %shard_map.89 = bf16[2304,576]{1,0:T(8,128)(2,1)} custom-call(bf16[768,2304]{1,0:T(8,128)(2,1)} %all-gather.2.cloned.1.call-done.table_any.table_ref, bf16[768,576]{1,0:T(8,128)(2,1)S(1)} %get-tuple-element.24.cots_ref), custom_call_target="tpu_custom_call" | custom-call | flops 2038431744 | bytes 6193152 | tf_op jit(solution)/shard_map/pallas_call | solution.py:243
  118.7 51.3 %all_to_all.26.sums_ref = bf16[8,48,2304]{2,1,0:T(8,128)(2,1)S(1)} all-to-all(bf16[8,48,2304]{2,1,0:T(8,128)(2,1)S(1)} %add_convert_fusion), channel_id=1, replica_groups=mesh['c'=4,'x'=4,'l'=2,'y'=8,'k'=2] {'y'}, dimensions={0} | all-to-all | bytes 3538944 | tf_op jit(solution)/shard_map/all_to_all | solution.py:32
  170.1 1.0 copy-done.9
  171.1 1.2 shard_map.90
  172.3 3.5 %all-to-all-start.4 = ((bf16[4,136,576]{2,1,0:T(8,128)(2,1)}), bf16[4,136,576]{2,1,0:T(8,128)(2,1)S(1)}, u32[]{:S(2)}, u32[]{:S(2)}) async-start(bf16[4,136,576]{2,1,0:T(8,128)(2,1)} %shard_map.90), calls=%async_computation.5 | async-start | bytes 1392640 | tf_op jit(solution)/shard_map/all_to_all | solution.py:32
  175.9 4.5 %collective-permute-start.4 = (bf16[96,576]{1,0:T(8,128)(2,1)S(1)}, bf16[96,576]{1,0:T(8,128)(2,1)S(1)}, u32[]{:S(2)}, u32[]{:S(2)}) collective-permute-start(bf16[96,576]{1,0:T(8,128)(2,1)S(1)} %get-tuple-element.29), channel_id=1, source_target_pairs={{0,96},{32,0},{64,32},{96,64},{1,97},{33,1},{65,33},{97,65},{2,98}... | collective-permute-start | bytes 331784 | tf_op jit(solution)/shard_map/ppermute | solution.py:261
  180.4 2.5 %collective-permute-start.3 = (bf16[96,576]{1,0:T(8,128)(2,1)S(1)}, bf16[96,576]{1,0:T(8,128)(2,1)S(1)}, u32[]{:S(2)}, u32[]{:S(2)}) collective-permute-start(bf16[96,576]{1,0:T(8,128)(2,1)S(1)} %get-tuple-element.30), channel_id=1, source_target_pairs={{0,64},{32,96},{64,0},{96,32},{1,65},{33,97},{65,1},{97,33},{2,66}... | collective-permute-start | bytes 331784 | tf_op jit(solution)/shard_map/ppermute | solution.py:261
  182.9 2.5 %collective-permute-start.2 = (bf16[96,576]{1,0:T(8,128)(2,1)S(1)}, bf16[96,576]{1,0:T(8,128)(2,1)S(1)}, u32[]{:S(2)}, u32[]{:S(2)}) collective-permute-start(bf16[96,576]{1,0:T(8,128)(2,1)S(1)} %get-tuple-element.31), channel_id=1, source_target_pairs={{0,32},{32,64},{64,96},{96,0},{1,33},{33,65},{65,97},{97,1},{2,34}... | collective-permute-start | bytes 331784 | tf_op jit(solution)/shard_map/ppermute | solution.py:261
  185.4 2.5 %collective-permute-done.4 = bf16[96,576]{1,0:T(8,128)(2,1)S(1)} collective-permute-done((bf16[96,576]{1,0:T(8,128)(2,1)S(1)}, bf16[96,576]{1,0:T(8,128)(2,1)S(1)}, u32[]{:S(2)}, u32[]{:S(2)}) %collective-permute-start.4) | collective-permute-done | bytes 110624 | tf_op jit(solution)/shard_map/ppermute | solution.py:261
  187.9 1.5 collective-permute-done.3
  189.4 2.9 %collective-permute-done.2 = bf16[96,576]{1,0:T(8,128)(2,1)S(1)} collective-permute-done((bf16[96,576]{1,0:T(8,128)(2,1)S(1)}, bf16[96,576]{1,0:T(8,128)(2,1)S(1)}, u32[]{:S(2)}, u32[]{:S(2)}) %collective-permute-start.2) | collective-permute-done | bytes 110624 | tf_op jit(solution)/shard_map/ppermute | solution.py:261
  192.4 1.5 shard_map.88
  193.8 1.0 shard_map.91
  (34 shorter events, 2.1 us)
Async XLA Ops:
  7.2 38.9 %copy-start = (bf16[288,1152]{1,0:T(8,128)(2,1)S(1)}, bf16[288,1152]{1,0:T(8,128)(2,1)}, u32[]{:S(2)}) copy-start(bf16[288,1152]{1,0:T(8,128)(2,1)} %gate_ref) | copy-start | bytes 1990660
  7.2 38.9 %copy-start.1 = (bf16[288,1152]{1,0:T(8,128)(2,1)S(1)}, bf16[288,1152]{1,0:T(8,128)(2,1)}, u32[]{:S(2)}) copy-start(bf16[288,1152]{1,0:T(8,128)(2,1)} %up_ref) | copy-start | bytes 1990660
  7.2 85.0 %all-gather.2.cloned.1.call-start = ((), (), s32[]{:S(2)}) async-start(), calls=%async_computation.6 | async-start | bytes 3760128 | tf_op jit(solution)/shard_map/all_gather | solution.py:364
  8.0 0.9 copy-start.10
  20.2 24.1 %collective-permute-start = (bf16[288,1152]{1,0:T(8,128)(2,1)}, bf16[288,1152]{1,0:T(8,128)(2,1)S(1)}, u32[]{:S(2)}, u32[]{:S(2)}) collective-permute-start(bf16[288,1152]{1,0:T(8,128)(2,1)} %gate_ref), channel_id=1, source_target_pairs={{0,16},{16,128},{128,144},{144,256},{256,272},{272,384},{384,400},... | collective-permute-start | bytes 1990664 | tf_op jit(solution)/shard_map/ppermute | solution.py:360
  24.3 20.9 %collective-permute-start.1 = (bf16[288,1152]{1,0:T(8,128)(2,1)}, bf16[288,1152]{1,0:T(8,128)(2,1)S(1)}, u32[]{:S(2)}, u32[]{:S(2)}) collective-permute-start(bf16[288,1152]{1,0:T(8,128)(2,1)} %up_ref), channel_id=1, source_target_pairs={{0,400},{16,0},{128,16},{144,128},{256,144},{272,256},{384,272},{4... | collective-permute-start | bytes 1990664 | tf_op jit(solution)/shard_map/ppermute | solution.py:361
  44.3 0.8 copy-start.2
  45.2 0.8 copy-start.4
  46.1 1.0 copy-start.8
  49.9 3.7 %copy-start.3 = (bf16[288,1152]{1,0:T(8,128)(2,1)S(1)}, bf16[288,1152]{1,0:T(8,128)(2,1)}, u32[]{:S(2)}) copy-start(bf16[288,1152]{1,0:T(8,128)(2,1)} %copy-done.2) | copy-start | bytes 1990660
  49.9 3.7 %copy-start.5 = (bf16[288,1152]{1,0:T(8,128)(2,1)S(1)}, bf16[288,1152]{1,0:T(8,128)(2,1)}, u32[]{:S(2)}) copy-start(bf16[288,1152]{1,0:T(8,128)(2,1)} %copy-done.4) | copy-start | bytes 1990660
  49.9 23.4 %all-to-all-start.1 = ((bf16[4,384,576]{1,2,0:T(8,128)(2,1)}), bf16[4,384,576]{1,2,0:T(8,128)(2,1)S(1)}, u32[]{:S(2)}, u32[]{:S(2)}) async-start(bf16[4,384,576]{1,2,0:T(8,128)(2,1)} %copy.9), calls=%async_computation.1 | async-start | bytes 3538944 | tf_op jit(solution)/shard_map/all_to_all | solution.py:32
  73.3 18.9 %all-to-all-start.2 = ((bf16[4,288,576]{2,1,0:T(8,128)(2,1)}), bf16[4,288,576]{2,1,0:T(8,128)(2,1)S(1)}, u32[]{:S(2)}, u32[]{:S(2)}) async-start(bf16[4,288,576]{2,1,0:T(8,128)(2,1)} %shard_map.86), calls=%async_computation.2 | async-start | bytes 2949120 | tf_op jit(solution)/shard_map/all_to_all | solution.py:32
  76.9 93.2 %reduce-scatter.2.cloned.1.call-start = ((), (), s32[]{:S(2)}) async-start(), calls=%async_computation.7 | async-start | bytes 3317760 | tf_op jit(solution)/shard_map/reduce_scatter | solution.py:375
  103.3 0.8 copy-start.6
  104.1 14.2 %collective-permute-start.5 = (bf16[8,48,2304]{2,1,0:T(8,128)(2,1)}, bf16[8,48,2304]{2,1,0:T(8,128)(2,1)S(1)}, u32[]{:S(2)}, u32[]{:S(2)}) collective-permute-start(bf16[8,48,2304]{2,1,0:T(8,128)(2,1)} %get-tuple-element.23), channel_id=1, source_target_pairs={{0,1},{1,0},{2,3},{3,2},{4,5},{5,4},{6,7},{7,6},{8,9},{9,8},{10,11... | collective-permute-start | bytes 5308424 | tf_op jit(solution)/shard_map/ppermute | solution.py:373
  170.1 5.8 %copy-start.7 = (bf16[4,96,576]{2,1,0:T(8,128)(2,1)S(1)}, bf16[4,96,576]{2,1,0:T(8,128)(2,1)}, u32[]{:S(2)}) copy-start(bf16[4,96,576]{2,1,0:T(8,128)(2,1)} %copy-done.6) | copy-start | bytes 1327108
  170.1 1.0 copy-start.9
  172.3 21.5 %all-to-all-start.4 = ((bf16[4,136,576]{2,1,0:T(8,128)(2,1)}), bf16[4,136,576]{2,1,0:T(8,128)(2,1)S(1)}, u32[]{:S(2)}, u32[]{:S(2)}) async-start(bf16[4,136,576]{2,1,0:T(8,128)(2,1)} %shard_map.90), calls=%async_computation.5 | async-start | bytes 1392640 | tf_op jit(solution)/shard_map/all_to_all | solution.py:32
  175.8 18.0 %copy-start.11 = (bf16[12,2304]{1,0:T(8,128)(2,1)S(1)}, bf16[12,2304]{1,0:T(8,128)(2,1)}, u32[]{:S(2)}) copy-start(bf16[12,2304]{1,0:T(8,128)(2,1)} %tokens_ref.3) | copy-start | bytes 165892
  175.9 12.0 %collective-permute-start.4 = (bf16[96,576]{1,0:T(8,128)(2,1)S(1)}, bf16[96,576]{1,0:T(8,128)(2,1)S(1)}, u32[]{:S(2)}, u32[]{:S(2)}) collective-permute-start(bf16[96,576]{1,0:T(8,128)(2,1)S(1)} %get-tuple-element.29), channel_id=1, source_target_pairs={{0,96},{32,0},{64,32},{96,64},{1,97},{33,1},{65,33},{97,65},{2,98}... | collective-permute-start | bytes 331784 | tf_op jit(solution)/shard_map/ppermute | solution.py:261
  180.4 9.0 %collective-permute-start.3 = (bf16[96,576]{1,0:T(8,128)(2,1)S(1)}, bf16[96,576]{1,0:T(8,128)(2,1)S(1)}, u32[]{:S(2)}, u32[]{:S(2)}) collective-permute-start(bf16[96,576]{1,0:T(8,128)(2,1)S(1)} %get-tuple-element.30), channel_id=1, source_target_pairs={{0,64},{32,96},{64,0},{96,32},{1,65},{33,97},{65,1},{97,33},{2,66}... | collective-permute-start | bytes 331784 | tf_op jit(solution)/shard_map/ppermute | solution.py:261
  182.9 9.4 %collective-permute-start.2 = (bf16[96,576]{1,0:T(8,128)(2,1)S(1)}, bf16[96,576]{1,0:T(8,128)(2,1)S(1)}, u32[]{:S(2)}, u32[]{:S(2)}) collective-permute-start(bf16[96,576]{1,0:T(8,128)(2,1)S(1)} %get-tuple-element.31), channel_id=1, source_target_pairs={{0,32},{32,64},{64,96},{96,0},{1,33},{33,65},{65,97},{97,1},{2,34}... | collective-permute-start | bytes 331784 | tf_op jit(solution)/shard_map/ppermute | solution.py:261
Sparse Core Ops, SparseCore 0:
  20.3 48.7 all-gather.1
  118.4 42.2 reduce-scatter.1

commit v4 on v3

--- a/solution.py
+++ b/solution.py
@@ -26,6 +26,12 @@
 
 def ring(size, shift):
     return [(i, (i + shift) % size) for i in range(size)]
+
+
+def both_ways(size):
+    return [(2 * i, 2 * ((i + 1) % size)) for i in range(size)] + [
+        (2 * i + 1, 2 * ((i - 1) % size) + 1) for i in range(size)
+    ]
 
 
 def exchange(value, axis):
@@ -71,7 +77,7 @@
     feats, units = gate.shape
     main, tail = share_sizes(units, parts)
     operands = (gate, up) if grads is None else (gate, up, grads)
-    rows = feats if grads is None else feats + grads.shape[0] // 2
+    rows = feats if grads is None else feats + grads.shape[0] // 2 + 16
     kernel = pack_weights_kernel if grads is None else pack_all_kernel
     return pl.pallas_call(
         functools.partial(kernel, main, tail, parts),
@@ -117,7 +123,8 @@
     blocks, feats, _ = other_ref.shape
     pool = table_ref.shape[0]
     half = raw.shape[1]
-    low, core = place_ref[0], place_ref[1]
+    low, core, me = place_ref[0], place_ref[1], place_ref[3]
+    chain = keep_ref.shape[0]
     grads_copy = pltpu.make_async_copy(own_ref.at[:, pl.ds(feats, half)], raw, sems.at[2 * blocks])
     grads_copy.start()
     copies = []
@@ -172,12 +179,21 @@
         partial = lax.dot_general(
             cots_ref[rows, :], matrix[...], (((1,), (1,)), ((), ())), preferred_element_type=F32
         )
-        for j in range(chunk // (2 * step)):
-            even = partial[2 * j * step : (2 * j + 1) * step]
-            odd = partial[(2 * j + 1) * step : (2 * j + 2) * step]
-            y = first // (2 * step) + j
-            keep_ref[y] = jnp.where(core == 0, even, odd).astype(BF16)
-            give_ref[y] = jnp.where(core == 0, odd, even).astype(BF16)
+        for j in range(chunk // step):
+            block = partial[j * step : (j + 1) * step].astype(BF16)
+            ahead = lax.rem(first // step + j - me + 2 * chain, 2 * chain)
+            right = ahead < chain
+            slot = jnp.where(right, chain - 1 - ahead, ahead - chain)
+            kept = right == (core == 0)
+
+            @pl.when(kept)
+            def _():
+                keep_ref[slot] = block
+
+            @pl.when(jnp.logical_not(kept))
+            def _():
+                give_ref[slot] = block
+
     spread = jnp.dot(back, found[...], preferred_element_type=F32).astype(BF16)
     for x in range(blocks):
         for h in range(2):
@@ -186,20 +202,19 @@
             hidden_ref[x, :, 2 * main + h * tail : 2 * main + (h + 1) * tail] = spread[rows, main:]
 
 
-def forward(place, table, own, other, ny, rows_each, chunk):
+def forward(place, table, own, other, ny, rows_each, half, chunk):
     pool, width = table.shape
     blocks, feats, pair = other.shape
     part = pair // 2
     main = part // 128 * 128
-    step = pool // (2 * ny)
-    half = own.shape[1] - feats
+    step = pool // ny
     return pl.pallas_call(
         functools.partial(forward_kernel, chunk, main, part - main, rows_each),
         out_shape=(
             jax.ShapeDtypeStruct((blocks, half, pair), BF16),
             jax.ShapeDtypeStruct((pool, pair), BF16),
-            jax.ShapeDtypeStruct((ny, step, width), BF16),
-            jax.ShapeDtypeStruct((ny, step, width), BF16),
+            jax.ShapeDtypeStruct((ny // 2, step, width), BF16),
+            jax.ShapeDtypeStruct((ny // 2, step, width), BF16),
         ),
         in_specs=[SMEM, ANY, ANY, ANY],
         out_specs=(VMEM, VMEM, VMEM, VMEM),
@@ -285,10 +300,9 @@
     )(tokens, gain)
 
 
-def gather_kernel(nx, rows, wide, thin, sums_ref, grad_ref, out_ref):
-    total = sums_ref[0].astype(F32)
-    for i in range(1, sums_ref.shape[0]):
-        total = total + sums_ref[i].astype(F32)
+def gather_kernel(nx, rows, wide, thin, place_ref, near_ref, far_ref, sums_ref, grad_ref, out_ref):
+    mine = sums_ref[0 : near_ref.shape[0], :].astype(F32)
+    total = near_ref[...].astype(F32) + jnp.where(place_ref[1] == 0, mine, far_ref[...].astype(F32))
     grad = grad_ref[...].astype(F32)
     piece = grad.shape[0] // nx
     pad = jnp.zeros((16 - rows, wide + thin), F32)
@@ -353,29 +367,43 @@
         own_tokens = hidden_grad.shape[0]
         pool = nx * own_tokens
         nz = nc * nl
-        place = jnp.stack([lax.axis_index("l"), lax.axis_index("k"), lax.axis_index("x")])
-        place = place.astype(jnp.int32)
+        place = jnp.stack([lax.axis_index(name) for name in ("l", "k", "x", "y")]).astype(jnp.int32)
         gain = norm_gain.reshape(1, width)
-
-        other_gate = lax.ppermute(gate_weight, ("c", "l"), ring(nz, 1))
-        other_up = lax.ppermute(up_weight, ("c", "l"), ring(nz, -1))
 
         near = exchange(normalise(tokens, gain, nx), "x").reshape(nx * rows, width)
         table = lax.all_gather(near, ("y", "k"), axis=0, tiled=True)
 
-        gate_weight, up_weight, hidden_grad, other_gate, other_up = lax.optimization_barrier(
-            (gate_weight, up_weight, hidden_grad, other_gate, other_up)
+        other = exchange(
+            lax.ppermute(pack(nx, gate_weight, up_weight), ("c", "l", "k"), both_ways(nz)), "x"
         )
         own = exchange(pack(nx, gate_weight, up_weight, hidden_grad), "x")
-        other = exchange(pack(nx, other_gate, other_up), "x")
-
-        hidden, cots, keep, give = forward(place, table, own, other, ny, rows, pool // 2)
+
+        hidden, cots, keep, give = forward(
+            place, table, own, other, ny, rows, own_tokens // 2, pool // 2
+        )
         taken = lax.ppermute(give, "k", [(0, 1), (1, 0)])
         grad = gradient(table, cots, nx, nl, nc, width // 3)
+        taken, grad = lax.optimization_barrier((taken, grad))
         grad = lax.psum_scatter(grad, ("c", "l"), scatter_dimension=0, tiled=True)
 
-        partial = (keep.astype(F32) + taken.astype(F32)).astype(BF16)
-        partial = exchange(partial, "y")
+        def term(i):
+            return keep[i].astype(F32) + taken[i].astype(F32)
+
+        partial = term(0).astype(BF16)
+        for i in range(1, ny // 2):
+            partial = lax.ppermute(partial, ("y", "k"), both_ways(ny))
+            partial = (partial.astype(F32) + term(i)).astype(BF16)
+        step = partial.shape[0] // 2
+        lower, upper = partial[:step], partial[step:]
+        core = lax.axis_index("k")
+        near = lax.ppermute(
+            jnp.where(core == 0, upper, lower), ("y", "k"),
+            [(2 * y, 2 * y + 1) for y in range(ny)]
+            + [(2 * y + 1, 2 * ((y - 1) % ny)) for y in range(ny)],
+        )
+        far = lax.ppermute(
+            upper, ("y", "k"), [(2 * y + 1, 2 * ((y - 1) % ny) + 1) for y in range(ny)]
+        )
 
         hidden = jnp.stack(swap_over_x(hidden, nx))
         hidden = pl.pallas_call(
@@ -388,10 +416,10 @@
         last = pl.pallas_call(
             functools.partial(gather_kernel, nx, rows, wide, thin),
             out_shape=jax.ShapeDtypeStruct((nx, 16 * nx + feats // nc, pair), BF16),
-            in_specs=[VMEM, VMEM],
+            in_specs=[SMEM, VMEM, VMEM, VMEM, VMEM],
             out_specs=VMEM,
             compiler_params=params(24),
-        )(partial, grad)
+        )(place, near, far, partial, grad)
         last = exchange(last, "x")
         input_grad, gate_grad, up_grad = pl.pallas_call(
             functools.partial(finish_kernel, main, tail, wide, thin),

time: 202 us -> 184 us (0.911)
  blocking collectives: 61.7 us -> 10.3 us
  starting transfers between devices: 40.3 us -> 64 us
  waiting for transfers between devices: 49.5 us -> 57.1 us
  local copies, waits for them, and re-layouts: 11.8 us -> 7.01 us
  other arithmetic: 0.58 us -> 4.88 us
    all_to_all x2 -> x1, blocking collectives: 61.7 us -> 10.3 us  [exchange(): return lax.all_to_all(value, axis, split_axis=0, concat_axis=0, tiled=True)]
    ppermute x2 -> x6, waiting for transfers between devices: 11.5 us -> 36.7 us  [the longest x1 16.3 us: per_device(): lax.ppermute(pack(nx, gate_weight, up_weight), ('c', 'l', 'k'), both_ways...]
    ppermute x2 -> x6, starting transfers between devices: 12.7 us -> 33.7 us  [the longest x3 15.6 us: per_device(): partial = lax.ppermute(partial, ('y', 'k'), both_ways(ny))]
    all_to_all x3, waiting for transfers between devices: 31 us -> 15.2 us  [exchange(): return lax.all_to_all(value, axis, split_axis=0, concat_axis=0, tiled=True)]
    convert_element_type x1 -> x4, other arithmetic: 0.4 us -> 4.67 us  [the longest x3 3.55 us: per_device(): partial = (partial.astype(F32) + term(i)).astype(BF16)]
    all_to_all x1 -> x0, local copies, waits for them, and re-layouts: 2.4 us -> none  [exchange(): return lax.all_to_all(value, axis, split_axis=0, concat_axis=0, tiled=True)]
    pallas_call x1 -> x0, local copies, waits for them, and re-layouts: 2.36 us -> none  [pack(): pl.pallas_call(functools.partial(kernel, main, tail, parts), out_shape=ja...]
    unnamed x24 -> x16, local copies, waits for them, and re-layouts: 5.48 us -> 5.41 us
  transfers between devices with their start and end apart: 11 -> 15, of which waited for: 7 -> 8; matrix products, arithmetic and copies ran while one was open for 3% -> 3% of each run, Pallas kernels for 5% -> 6%
where the time goes in v4:
time: 184 us; the launch traced here: 182 us
  starting transfers between devices  64 us (35%)
  waiting for transfers between devices  57.1 us (31%)
  Pallas kernels  24.5 us (13%)
  between operations  14.3 us (8%)
  blocking collectives  10.3 us (6%)
  local copies, waits for them, and re-layouts  7.01 us (4%)
  other arithmetic  4.88 us (3%)
    ppermute x1, waiting for transfers between devices, per_device(): lax.ppermute(pack(nx, gate_weight, up_weight), ('c', 'l', 'k'), both_ways...  16.3 us
    ppermute x3, waiting for transfers between devices, per_device(): partial = lax.ppermute(partial, ('y', 'k'), both_ways(ny))  15.7 us
    ppermute x3, starting transfers between devices, per_device(): partial = lax.ppermute(partial, ('y', 'k'), both_ways(ny))  15.6 us
    all_to_all x3, waiting for transfers between devices, exchange(): return lax.all_to_all(value, axis, split_axis=0, concat_axis=0, tiled=True)  15.2 us
    all_to_all x3, starting transfers between devices, exchange(): return lax.all_to_all(value, axis, split_axis=0, concat_axis=0, tiled=True)  12.1 us
    pallas_call x1, Pallas kernels, forward(): pl.pallas_call(functools.partial(forward_kernel, chunk, main, part - main...  11.5 us
    ppermute x1, starting transfers between devices, per_device(): lax.ppermute(pack(nx, gate_weight, up_weight), ('c', 'l', 'k'), both_ways...  10.8 us
    ppermute x3, starting transfers between devices, swap_over_x(): got.append(lax.ppermute(piece, 'x', ring(nx, shift)))  10.7 us
  transfers between devices with their start and end apart: 15, of which 8 were waited for; matrix products, arithmetic and copies ran while one was open for 3% of the time, Pallas kernels for 6%

profile of v4, /device:TPU:1, one launch (start us, length us, event | category | flops | bytes accessed | tf_op | source)
XLA Modules:
  0.0 182.1 jit_solution(15136755607149698831)
XLA Ops:
  9.1 10.3 %all_to_all.20 = bf16[4,12,2304]{2,1,0:T(8,128)(2,1)S(1)} all-to-all(bf16[4,12,2304]{2,1,0:T(8,128)(2,1)S(1)} %shard_map.84), channel_id=1, replica_groups=mesh['c'=4,'x'=4,'l'=2,'y'=8,'k'=2] {'x'}, dimensions={0} | all-to-all | bytes 442368 | tf_op jit(solution)/shard_map/all_to_all | solution.py:38
  21.2 1.7 shard_map.85
  22.9 4.4 %all-to-all-start.1 = ((bf16[4,400,576]{2,1,0:T(8,128)(2,1)}), bf16[4,400,576]{2,1,0:T(8,128)(2,1)}, u32[]{:S(2)}, u32[]{:S(2)}) async-start(bf16[4,400,576]{2,1,0:T(8,128)(2,1)} %shard_map.85), calls=%async_computation.1 | async-start | bytes 4096000 | tf_op jit(solution)/shard_map/all_to_all | solution.py:38
  27.7 10.8 %collective-permute-start = (bf16[4,288,576]{2,1,0:T(8,128)(2,1)S(1)}, bf16[4,288,576]{2,1,0:T(8,128)(2,1)}, u32[]{:S(2)}, u32[]{:S(2)}) collective-permute-start(bf16[4,288,576]{2,1,0:T(8,128)(2,1)S(1)} %shard_map.86), channel_id=1, source_target_pairs={{0,16},{16,128},{128,144},{144,256},{256,272},{272,384},{384,400},... | collective-permute-start | bytes 3981320 | tf_op jit(solution)/shard_map/ppermute | solution.py:377
  38.5 16.3 %collective-permute-done = bf16[4,288,576]{2,1,0:T(8,128)(2,1)} collective-permute-done((bf16[4,288,576]{2,1,0:T(8,128)(2,1)S(1)}, bf16[4,288,576]{2,1,0:T(8,128)(2,1)}, u32[]{:S(2)}, u32[]{:S(2)}) %collective-permute-start) | collective-permute-done | bytes 1327136 | tf_op jit(solution)/shard_map/ppermute | solution.py:377
  54.7 4.2 %all-to-all-start.2 = ((bf16[4,288,576]{2,1,0:T(8,128)(2,1)}), bf16[4,288,576]{2,1,0:T(8,128)(2,1)S(1)}, u32[]{:S(2)}, u32[]{:S(2)}) async-start(bf16[4,288,576]{2,1,0:T(8,128)(2,1)} %collective-permute-done), calls=%async_computation.2 | async-start | bytes 2949120 | tf_op jit(solution)/shard_map/all_to_all | solution.py:38
  59.0 15.2 %all-to-all-done.2.other_ref = bf16[4,288,576]{2,1,0:T(8,128)(2,1)S(1)} async-done(((bf16[4,288,576]{2,1,0:T(8,128)(2,1)}), bf16[4,288,576]{2,1,0:T(8,128)(2,1)S(1)}, u32[]{:S(2)}, u32[]{:S(2)}) %all-to-all-start.2) | async-done | bytes 1327136 | tf_op jit(solution)/shard_map/all_to_all | solution.py:38
  74.2 1.1 copy-done.2
  75.3 1.4 copy-done.3
  76.7 11.5 %shard_map.87 = (bf16[4,96,576]{2,1,0:T(8,128)(2,1)S(1)}, bf16[768,576]{1,0:T(8,128)(2,1)S(1)}, bf16[4,96,2304]{2,1,0:T(8,128)(2,1)S(1)}, bf16[4,96,2304]{2,1,0:T(8,128)(2,1)}) custom-call(s32[4]{0:T(128)S(1)} %pad_add_fusion.place_ref, bf16[768,2304]{1,0:T(8,128)(2,1)} %all-gather.2.cloned.1.call-done.table_any.table_ref, ...), custom_call_target="tpu_custom_call" | custom-call | flops 4076863488 | bytes 9732096 | tf_op jit(solution)/shard_map/pallas_call | solution.py:211
  88.2 7.5 %collective-permute-start.4 = (bf16[4,96,2304]{2,1,0:T(8,128)(2,1)}, bf16[4,96,2304]{2,1,0:T(8,128)(2,1)}, u32[]{:S(2)}, u32[]{:S(2)}) collective-permute-start(bf16[4,96,2304]{2,1,0:T(8,128)(2,1)} %get-tuple-element.15), channel_id=1, source_target_pairs={{0,1},{1,0},{2,3},{3,2},{4,5},{5,4},{6,7},{7,6},{8,9},{9,8},{10,11... | collective-permute-start | bytes 5308424 | tf_op jit(solution)/shard_map/ppermute | solution.py:384
  95.7 6.8 %shard_map.89 = bf16[2304,576]{1,0:T(8,128)(2,1)} custom-call(bf16[768,2304]{1,0:T(8,128)(2,1)} %all-gather.2.cloned.1.call-done.table_any.table_ref, bf16[768,576]{1,0:T(8,128)(2,1)S(1)} %get-tuple-element.16.cots_ref), custom_call_target="tpu_custom_call" | custom-call | flops 2038431744 | bytes 6193152 | tf_op jit(solution)/shard_map/pallas_call | solution.py:258
  103.7 5.1 %collective-permute-start.5 = (bf16[96,2304]{1,0:T(8,128)(2,1)S(1)}, bf16[96,2304]{1,0:T(8,128)(2,1)S(1)}, u32[]{:S(2)}, u32[]{:S(2)}) collective-permute-start(bf16[96,2304]{1,0:T(8,128)(2,1)S(1)} %fusion.3), channel_id=1, source_target_pairs={{0,2},{2,4},{4,6},{6,8},{8,10},{10,12},{12,14},{14,0},{1,15},{3,1}... | collective-permute-start | bytes 1327112 | tf_op jit(solution)/shard_map/ppermute | solution.py:394
  108.8 5.2 %collective-permute-done.5 = bf16[96,2304]{1,0:T(8,128)(2,1)S(1)} collective-permute-done((bf16[96,2304]{1,0:T(8,128)(2,1)S(1)}, bf16[96,2304]{1,0:T(8,128)(2,1)S(1)}, u32[]{:S(2)}, u32[]{:S(2)}) %collective-permute-start.5) | collective-permute-done | bytes 442400 | tf_op jit(solution)/shard_map/ppermute | solution.py:394
  114.0 1.2 fusion.2
  115.2 5.1 %collective-permute-start.6 = (bf16[96,2304]{1,0:T(8,128)(2,1)S(1)}, bf16[96,2304]{1,0:T(8,128)(2,1)S(1)}, u32[]{:S(2)}, u32[]{:S(2)}) collective-permute-start(bf16[96,2304]{1,0:T(8,128)(2,1)S(1)} %fusion.2), channel_id=1, source_target_pairs={{0,2},{2,4},{4,6},{6,8},{8,10},{10,12},{12,14},{14,0},{1,15},{3,1}... | collective-permute-start | bytes 1327112 | tf_op jit(solution)/shard_map/ppermute | solution.py:394
  120.3 5.2 %collective-permute-done.6 = bf16[96,2304]{1,0:T(8,128)(2,1)S(1)} collective-permute-done((bf16[96,2304]{1,0:T(8,128)(2,1)S(1)}, bf16[96,2304]{1,0:T(8,128)(2,1)S(1)}, u32[]{:S(2)}, u32[]{:S(2)}) %collective-permute-start.6) | collective-permute-done | bytes 442400 | tf_op jit(solution)/shard_map/ppermute | solution.py:394
  125.5 1.2 fusion.1
  126.7 5.4 %collective-permute-start.7 = (bf16[96,2304]{1,0:T(8,128)(2,1)S(1)}, bf16[96,2304]{1,0:T(8,128)(2,1)S(1)}, u32[]{:S(2)}, u32[]{:S(2)}) collective-permute-start(bf16[96,2304]{1,0:T(8,128)(2,1)S(1)} %fusion.1), channel_id=1, source_target_pairs={{0,2},{2,4},{4,6},{6,8},{8,10},{10,12},{12,14},{14,0},{1,15},{3,1}... | collective-permute-start | bytes 1327112 | tf_op jit(solution)/shard_map/ppermute | solution.py:394
  132.1 5.2 %collective-permute-done.7 = bf16[96,2304]{1,0:T(8,128)(2,1)S(1)} collective-permute-done((bf16[96,2304]{1,0:T(8,128)(2,1)S(1)}, bf16[96,2304]{1,0:T(8,128)(2,1)S(1)}, u32[]{:S(2)}, u32[]{:S(2)}) %collective-permute-start.7) | collective-permute-done | bytes 442400 | tf_op jit(solution)/shard_map/ppermute | solution.py:394
  137.3 1.2 fusion.sums_ref
  138.6 4.3 %collective-permute-start.8 = (bf16[48,2304]{1,0:T(8,128)(2,1)S(1)}, bf16[48,2304]{1,0:T(8,128)(2,1)S(1)}, u32[]{:S(2)}, u32[]{:S(2)}) collective-permute-start(bf16[48,2304]{1,0:T(8,128)(2,1)S(1)} %get-tuple-element.27), channel_id=1, source_target_pairs={{0,1},{2,3},{4,5},{6,7},{8,9},{10,11},{12,13},{14,15},{1,14},{3,0}... | collective-permute-start | bytes 663560 | tf_op jit(solution)/shard_map/ppermute | solution.py:399
  142.8 3.1 %collective-permute-start.9 = (bf16[48,2304]{1,0:T(8,128)(2,1)S(1)}, bf16[48,2304]{1,0:T(8,128)(2,1)S(1)}, u32[]{:S(2)}, u32[]{:S(2)}) collective-permute-start(bf16[48,2304]{1,0:T(8,128)(2,1)S(1)} %get-tuple-element.26), channel_id=1, source_target_pairs={{1,15},{3,1},{5,3},{7,5},{9,7},{11,9},{13,11},{15,13},{17,31},{19,... | collective-permute-start | bytes 663560 | tf_op jit(solution)/shard_map/ppermute | solution.py:404
  145.9 4.7 %collective-permute-done.9.far_ref = bf16[48,2304]{1,0:T(8,128)(2,1)S(1)} collective-permute-done((bf16[48,2304]{1,0:T(8,128)(2,1)S(1)}, bf16[48,2304]{1,0:T(8,128)(2,1)S(1)}, u32[]{:S(2)}, u32[]{:S(2)}) %collective-permute-start.9) | collective-permute-done | bytes 221216 | tf_op jit(solution)/shard_map/ppermute | solution.py:404
  151.6 1.5 shard_map.90
  153.2 3.5 %all-to-all-start.3 = ((bf16[4,136,576]{2,1,0:T(8,128)(2,1)}), bf16[4,136,576]{2,1,0:T(8,128)(2,1)S(1)}, u32[]{:S(2)}, u32[]{:S(2)}) async-start(bf16[4,136,576]{2,1,0:T(8,128)(2,1)} %shard_map.90), calls=%async_computation.4 | async-start | bytes 1392640 | tf_op jit(solution)/shard_map/all_to_all | solution.py:38
  156.8 3.3 %collective-permute-start.1 = (bf16[96,576]{1,0:T(8,128)(2,1)S(1)}, bf16[96,576]{1,0:T(8,128)(2,1)S(1)}, u32[]{:S(2)}, u32[]{:S(2)}) collective-permute-start(bf16[96,576]{1,0:T(8,128)(2,1)S(1)} %get-tuple-element.25), channel_id=1, source_target_pairs={{0,32},{32,64},{64,96},{96,0},{1,33},{33,65},{65,97},{97,1},{2,34}... | collective-permute-start | bytes 331784 | tf_op jit(solution)/shard_map/ppermute | solution.py:276
  160.1 4.3 %collective-permute-start.2 = (bf16[96,576]{1,0:T(8,128)(2,1)S(1)}, bf16[96,576]{1,0:T(8,128)(2,1)S(1)}, u32[]{:S(2)}, u32[]{:S(2)}) collective-permute-start(bf16[96,576]{1,0:T(8,128)(2,1)S(1)} %get-tuple-element.24), channel_id=1, source_target_pairs={{0,64},{32,96},{64,0},{96,32},{1,65},{33,97},{65,1},{97,33},{2,66}... | collective-permute-start | bytes 331784 | tf_op jit(solution)/shard_map/ppermute | solution.py:276
  164.4 3.1 %collective-permute-start.3 = (bf16[96,576]{1,0:T(8,128)(2,1)S(1)}, bf16[96,576]{1,0:T(8,128)(2,1)S(1)}, u32[]{:S(2)}, u32[]{:S(2)}) collective-permute-start(bf16[96,576]{1,0:T(8,128)(2,1)S(1)} %get-tuple-element.23), channel_id=1, source_target_pairs={{0,96},{32,0},{64,32},{96,64},{1,97},{33,1},{65,33},{97,65},{2,98}... | collective-permute-start | bytes 331784 | tf_op jit(solution)/shard_map/ppermute | solution.py:276
  167.5 2.2 %collective-permute-done.1 = bf16[96,576]{1,0:T(8,128)(2,1)S(1)} collective-permute-done((bf16[96,576]{1,0:T(8,128)(2,1)S(1)}, bf16[96,576]{1,0:T(8,128)(2,1)S(1)}, u32[]{:S(2)}, u32[]{:S(2)}) %collective-permute-start.1) | collective-permute-done | bytes 110624 | tf_op jit(solution)/shard_map/ppermute | solution.py:276
  169.7 3.0 %collective-permute-done.2 = bf16[96,576]{1,0:T(8,128)(2,1)S(1)} collective-permute-done((bf16[96,576]{1,0:T(8,128)(2,1)S(1)}, bf16[96,576]{1,0:T(8,128)(2,1)S(1)}, u32[]{:S(2)}, u32[]{:S(2)}) %collective-permute-start.2) | collective-permute-done | bytes 110624 | tf_op jit(solution)/shard_map/ppermute | solution.py:276
  172.8 1.5 shard_map.88
  (35 shorter events, 7.4 us)
Async XLA Ops:
  7.2 13.0 %copy-start = (bf16[288,1152]{1,0:T(8,128)(2,1)S(1)}, bf16[288,1152]{1,0:T(8,128)(2,1)}, u32[]{:S(2)}) copy-start(bf16[288,1152]{1,0:T(8,128)(2,1)} %gate_ref.3) | copy-start | bytes 1990660
  7.2 13.0 %copy-start.1 = (bf16[288,1152]{1,0:T(8,128)(2,1)S(1)}, bf16[288,1152]{1,0:T(8,128)(2,1)}, u32[]{:S(2)}) copy-start(bf16[288,1152]{1,0:T(8,128)(2,1)} %up_ref.3) | copy-start | bytes 1990660
  7.2 68.2 %all-gather.2.cloned.1.call-start = ((), (), s32[]{:S(2)}) async-start(), calls=%async_computation.5 | async-start | bytes 3760128 | tf_op jit(solution)/shard_map/all_gather | solution.py:374
  8.0 0.9 copy-start.6
  20.2 1.0 copy-start.4
  22.9 31.8 %all-to-all-start.1 = ((bf16[4,400,576]{2,1,0:T(8,128)(2,1)}), bf16[4,400,576]{2,1,0:T(8,128)(2,1)}, u32[]{:S(2)}, u32[]{:S(2)}) async-start(bf16[4,400,576]{2,1,0:T(8,128)(2,1)} %shard_map.85), calls=%async_computation.1 | async-start | bytes 4096000 | tf_op jit(solution)/shard_map/all_to_all | solution.py:38
  27.7 27.1 %collective-permute-start = (bf16[4,288,576]{2,1,0:T(8,128)(2,1)S(1)}, bf16[4,288,576]{2,1,0:T(8,128)(2,1)}, u32[]{:S(2)}, u32[]{:S(2)}) collective-permute-start(bf16[4,288,576]{2,1,0:T(8,128)(2,1)S(1)} %shard_map.86), channel_id=1, source_target_pairs={{0,16},{16,128},{128,144},{144,256},{256,272},{272,384},{384,400},... | collective-permute-start | bytes 3981320 | tf_op jit(solution)/shard_map/ppermute | solution.py:377
  54.7 19.4 %all-to-all-start.2 = ((bf16[4,288,576]{2,1,0:T(8,128)(2,1)}), bf16[4,288,576]{2,1,0:T(8,128)(2,1)S(1)}, u32[]{:S(2)}, u32[]{:S(2)}) async-start(bf16[4,288,576]{2,1,0:T(8,128)(2,1)} %collective-permute-done), calls=%async_computation.2 | async-start | bytes 2949120 | tf_op jit(solution)/shard_map/all_to_all | solution.py:38
  58.9 91.7 %reduce-scatter.2.cloned.1.call-start = ((), (), s32[]{:S(2)}) async-start(), calls=%async_computation.6 | async-start | bytes 3317760 | tf_op jit(solution)/shard_map/reduce_scatter | solution.py:387
  74.2 1.1 copy-start.2
  75.3 1.4 copy-start.3
  88.2 14.3 %collective-permute-start.4 = (bf16[4,96,2304]{2,1,0:T(8,128)(2,1)}, bf16[4,96,2304]{2,1,0:T(8,128)(2,1)}, u32[]{:S(2)}, u32[]{:S(2)}) collective-permute-start(bf16[4,96,2304]{2,1,0:T(8,128)(2,1)} %get-tuple-element.15), channel_id=1, source_target_pairs={{0,1},{1,0},{2,3},{3,2},{4,5},{5,4},{6,7},{7,6},{8,9},{9,8},{10,11... | collective-permute-start | bytes 5308424 | tf_op jit(solution)/shard_map/ppermute | solution.py:384
  103.7 10.3 %collective-permute-start.5 = (bf16[96,2304]{1,0:T(8,128)(2,1)S(1)}, bf16[96,2304]{1,0:T(8,128)(2,1)S(1)}, u32[]{:S(2)}, u32[]{:S(2)}) collective-permute-start(bf16[96,2304]{1,0:T(8,128)(2,1)S(1)} %fusion.3), channel_id=1, source_target_pairs={{0,2},{2,4},{4,6},{6,8},{8,10},{10,12},{12,14},{14,0},{1,15},{3,1}... | collective-permute-start | bytes 1327112 | tf_op jit(solution)/shard_map/ppermute | solution.py:394
  115.2 10.3 %collective-permute-start.6 = (bf16[96,2304]{1,0:T(8,128)(2,1)S(1)}, bf16[96,2304]{1,0:T(8,128)(2,1)S(1)}, u32[]{:S(2)}, u32[]{:S(2)}) collective-permute-start(bf16[96,2304]{1,0:T(8,128)(2,1)S(1)} %fusion.2), channel_id=1, source_target_pairs={{0,2},{2,4},{4,6},{6,8},{8,10},{10,12},{12,14},{14,0},{1,15},{3,1}... | collective-permute-start | bytes 1327112 | tf_op jit(solution)/shard_map/ppermute | solution.py:394
  126.7 10.7 %collective-permute-start.7 = (bf16[96,2304]{1,0:T(8,128)(2,1)S(1)}, bf16[96,2304]{1,0:T(8,128)(2,1)S(1)}, u32[]{:S(2)}, u32[]{:S(2)}) collective-permute-start(bf16[96,2304]{1,0:T(8,128)(2,1)S(1)} %fusion.1), channel_id=1, source_target_pairs={{0,2},{2,4},{4,6},{6,8},{8,10},{10,12},{12,14},{14,0},{1,15},{3,1}... | collective-permute-start | bytes 1327112 | tf_op jit(solution)/shard_map/ppermute | solution.py:394
  138.6 7.4 %collective-permute-start.8 = (bf16[48,2304]{1,0:T(8,128)(2,1)S(1)}, bf16[48,2304]{1,0:T(8,128)(2,1)S(1)}, u32[]{:S(2)}, u32[]{:S(2)}) collective-permute-start(bf16[48,2304]{1,0:T(8,128)(2,1)S(1)} %get-tuple-element.27), channel_id=1, source_target_pairs={{0,1},{2,3},{4,5},{6,7},{8,9},{10,11},{12,13},{14,15},{1,14},{3,0}... | collective-permute-start | bytes 663560 | tf_op jit(solution)/shard_map/ppermute | solution.py:399
  142.8 7.8 %collective-permute-start.9 = (bf16[48,2304]{1,0:T(8,128)(2,1)S(1)}, bf16[48,2304]{1,0:T(8,128)(2,1)S(1)}, u32[]{:S(2)}, u32[]{:S(2)}) collective-permute-start(bf16[48,2304]{1,0:T(8,128)(2,1)S(1)} %get-tuple-element.26), channel_id=1, source_target_pairs={{1,15},{3,1},{5,3},{7,5},{9,7},{11,9},{13,11},{15,13},{17,31},{19,... | collective-permute-start | bytes 663560 | tf_op jit(solution)/shard_map/ppermute | solution.py:404
  150.6 1.0 copy-start.5
  153.2 21.1 %all-to-all-start.3 = ((bf16[4,136,576]{2,1,0:T(8,128)(2,1)}), bf16[4,136,576]{2,1,0:T(8,128)(2,1)S(1)}, u32[]{:S(2)}, u32[]{:S(2)}) async-start(bf16[4,136,576]{2,1,0:T(8,128)(2,1)} %shard_map.90), calls=%async_computation.4 | async-start | bytes 1392640 | tf_op jit(solution)/shard_map/all_to_all | solution.py:38
  156.7 17.6 %copy-start.7 = (bf16[12,2304]{1,0:T(8,128)(2,1)S(1)}, bf16[12,2304]{1,0:T(8,128)(2,1)}, u32[]{:S(2)}) copy-start(bf16[12,2304]{1,0:T(8,128)(2,1)} %tokens_ref.3) | copy-start | bytes 165892
  156.8 12.9 %collective-permute-start.1 = (bf16[96,576]{1,0:T(8,128)(2,1)S(1)}, bf16[96,576]{1,0:T(8,128)(2,1)S(1)}, u32[]{:S(2)}, u32[]{:S(2)}) collective-permute-start(bf16[96,576]{1,0:T(8,128)(2,1)S(1)} %get-tuple-element.25), channel_id=1, source_target_pairs={{0,32},{32,64},{64,96},{96,0},{1,33},{33,65},{65,97},{97,1},{2,34}... | collective-permute-start | bytes 331784 | tf_op jit(solution)/shard_map/ppermute | solution.py:276
  160.1 12.6 %collective-permute-start.2 = (bf16[96,576]{1,0:T(8,128)(2,1)S(1)}, bf16[96,576]{1,0:T(8,128)(2,1)S(1)}, u32[]{:S(2)}, u32[]{:S(2)}) collective-permute-start(bf16[96,576]{1,0:T(8,128)(2,1)S(1)} %get-tuple-element.24), channel_id=1, source_target_pairs={{0,64},{32,96},{64,0},{96,32},{1,65},{33,97},{65,1},{97,33},{2,66}... | collective-permute-start | bytes 331784 | tf_op jit(solution)/shard_map/ppermute | solution.py:276
  164.4 8.3 %collective-permute-start.3 = (bf16[96,576]{1,0:T(8,128)(2,1)S(1)}, bf16[96,576]{1,0:T(8,128)(2,1)S(1)}, u32[]{:S(2)}, u32[]{:S(2)}) collective-permute-start(bf16[96,576]{1,0:T(8,128)(2,1)S(1)} %get-tuple-element.23), channel_id=1, source_target_pairs={{0,96},{32,0},{64,32},{96,64},{1,97},{33,1},{65,33},{97,65},{2,98}... | collective-permute-start | bytes 331784 | tf_op jit(solution)/shard_map/ppermute | solution.py:276
Sparse Core Ops, SparseCore 0:
  20.3 48.7 all-gather.1
  102.7 43.4 reduce-scatter.1

commit v5 on v4

--- a/solution.py
+++ b/solution.py
@@ -57,9 +57,9 @@
 
 
 def pack_weights_kernel(main, tail, parts, gate_ref, up_ref, out_ref):
-    feats = gate_ref.shape[0]
+    rows = slice(0, out_ref.shape[1])
     for q in range(parts):
-        put_pair(out_ref, q, slice(0, feats), gate_ref, up_ref, main, tail, parts)
+        put_pair(out_ref, q, rows, gate_ref.at[rows], up_ref.at[rows], main, tail, parts)
 
 
 def pack_all_kernel(main, tail, parts, gate_ref, up_ref, grad_ref, out_ref):
@@ -77,7 +77,7 @@
     feats, units = gate.shape
     main, tail = share_sizes(units, parts)
     operands = (gate, up) if grads is None else (gate, up, grads)
-    rows = feats if grads is None else feats + grads.shape[0] // 2 + 16
+    rows = feats // 2 if grads is None else feats + grads.shape[0] // 2 + 16
     kernel = pack_weights_kernel if grads is None else pack_all_kernel
     return pl.pallas_call(
         functools.partial(kernel, main, tail, parts),
@@ -117,29 +117,33 @@
 
 
 def forward_kernel(
-    chunk, main, tail, rows_each, place_ref, table_any, own_ref, other_ref,
-    hidden_ref, cots_ref, keep_ref, give_ref, table_ref, matrix, raw, grads_ref, found, sems,
+    chunk, main, tail, rows_each, place_ref, table_any, own_ref, early_ref, late_ref,
+    hidden_ref, cots_ref, keep_ref, give_ref, table_ref, mine, theirs, raw, grads_ref, found, sems,
 ):
-    blocks, feats, _ = other_ref.shape
-    pool = table_ref.shape[0]
+    blocks, cut, _ = early_ref.shape
+    feats = cut + late_ref.shape[1]
+    pool, width = table_ref.shape
     half = raw.shape[1]
     low, core, me = place_ref[0], place_ref[1], place_ref[3]
     chain = keep_ref.shape[0]
-    grads_copy = pltpu.make_async_copy(own_ref.at[:, pl.ds(feats, half)], raw, sems.at[2 * blocks])
+    near_cols = pl.ds(pl.multiple_of(low * (width // 2), 128), width // 2)
+    far_cols = pl.ds(pl.multiple_of((1 - low) * (width // 2), 128), width // 2)
+    grads_copy = pltpu.make_async_copy(own_ref.at[:, pl.ds(feats, half)], raw, sems.at[3 * blocks])
     grads_copy.start()
     copies = []
     for x in range(blocks):
-        for i, (src, at) in enumerate(((own_ref, low), (other_ref, 1 - low))):
-            rows = pl.ds(pl.multiple_of((2 * x + at) * feats, 16), feats)
+        for i, (src, dst, first, size) in enumerate((
+            (own_ref, mine, 0, feats), (early_ref, theirs, 0, cut), (late_ref, theirs, cut, feats - cut)
+        )):
             copies.append(
                 pltpu.make_async_copy(
-                    src.at[x, pl.ds(0, feats)], matrix.at[rows], sems.at[2 * x + i]
+                    src.at[x, pl.ds(0, size)], dst.at[pl.ds(x * feats + first, size)], sems.at[3 * x + i]
                 )
             )
     tables = [
         pltpu.make_async_copy(
             table_any.at[pl.ds(first, chunk)], table_ref.at[pl.ds(first, chunk)],
-            sems.at[2 * blocks + 1 + first // chunk],
+            sems.at[3 * blocks + 1 + first // chunk],
         )
         for first in range(0, pool, chunk)
     ]
@@ -163,7 +167,8 @@
     for first in range(0, pool, chunk):
         rows = slice(first, first + chunk)
         tables[first // chunk].wait()
-        both = jnp.dot(table_ref[rows, :], matrix[...], preferred_element_type=F32)
+        both = jnp.dot(table_ref[rows, near_cols], mine[...], preferred_element_type=F32)
+        both = both + jnp.dot(table_ref[rows, far_cols], theirs[...], preferred_element_type=F32)
         grads = jnp.dot(forth[rows, :], grads_ref[...], preferred_element_type=F32)
         hidden, gate_cot, up_cot = activate(
             both[:, :main], both[:, main : 2 * main], grads[:, :main]
@@ -176,23 +181,24 @@
         found[rows, main:] = hidden
         cots_ref[rows, 2 * main : 2 * main + tail] = gate_cot
         cots_ref[rows, 2 * main + tail :] = up_cot
-        partial = lax.dot_general(
-            cots_ref[rows, :], matrix[...], (((1,), (1,)), ((), ())), preferred_element_type=F32
-        )
-        for j in range(chunk // step):
-            block = partial[j * step : (j + 1) * step].astype(BF16)
-            ahead = lax.rem(first // step + j - me + 2 * chain, 2 * chain)
-            right = ahead < chain
-            slot = jnp.where(right, chain - 1 - ahead, ahead - chain)
-            kept = right == (core == 0)
-
-            @pl.when(kept)
-            def _():
-                keep_ref[slot] = block
-
-            @pl.when(jnp.logical_not(kept))
-            def _():
-                give_ref[slot] = block
+        for weights, cols in ((mine, near_cols), (theirs, far_cols)):
+            partial = lax.dot_general(
+                cots_ref[rows, :], weights[...], (((1,), (1,)), ((), ())), preferred_element_type=F32
+            )
+            for j in range(chunk // step):
+                block = partial[j * step : (j + 1) * step].astype(BF16)
+                ahead = lax.rem(first // step + j - me + 2 * chain, 2 * chain)
+                right = ahead < chain
+                slot = jnp.where(right, chain - 1 - ahead, ahead - chain)
+                kept = right == (core == 0)
+
+                @pl.when(kept)
+                def _():
+                    keep_ref[slot, :, cols] = block
+
+                @pl.when(jnp.logical_not(kept))
+                def _():
+                    give_ref[slot, :, cols] = block
 
     spread = jnp.dot(back, found[...], preferred_element_type=F32).astype(BF16)
     for x in range(blocks):
@@ -202,9 +208,9 @@
             hidden_ref[x, :, 2 * main + h * tail : 2 * main + (h + 1) * tail] = spread[rows, main:]
 
 
-def forward(place, table, own, other, ny, rows_each, half, chunk):
+def forward(place, table, own, early, late, ny, rows_each, half, chunk):
     pool, width = table.shape
-    blocks, feats, pair = other.shape
+    blocks, _, pair = early.shape
     part = pair // 2
     main = part // 128 * 128
     step = pool // ny
@@ -216,21 +222,22 @@
             jax.ShapeDtypeStruct((ny // 2, step, width), BF16),
             jax.ShapeDtypeStruct((ny // 2, step, width), BF16),
         ),
-        in_specs=[SMEM, ANY, ANY, ANY],
+        in_specs=[SMEM, ANY, ANY, ANY, ANY],
         out_specs=(VMEM, VMEM, VMEM, VMEM),
         scratch_shapes=[
             pltpu.VMEM((pool, width), BF16),
-            pltpu.VMEM((width, pair), BF16),
+            pltpu.VMEM((width // 2, pair), BF16),
+            pltpu.VMEM((width // 2, pair), BF16),
             pltpu.VMEM((blocks, half, pair), BF16),
             pltpu.VMEM((pool, part), BF16),
             pltpu.VMEM((pool, part), BF16),
-            pltpu.SemaphoreType.DMA((2 * blocks + 1 + pool // chunk,)),
+            pltpu.SemaphoreType.DMA((3 * blocks + 1 + pool // chunk,)),
         ],
-        compiler_params=params(48),
+        compiler_params=params(60),
         cost_estimate=pl.CostEstimate(
             flops=4 * pool * width * pair, bytes_accessed=2 * (2 * pool * width + width * pair), transcendentals=0
         ),
-    )(place, table, own, other)
+    )(place, table, own, early, late)
 
 
 def gradient_kernel(tile, nx, nl, nc, table_ref, cots_ref, out_ref, total):
@@ -245,7 +252,7 @@
     for c in range(nc):
         for l in range(nl):
             found = [
-                total[((x * nl + l) * nc + c) * piece : ((x * nl + l) * nc + c + 1) * piece, :]
+                total[((l * nx + x) * nc + c) * piece : ((l * nx + x) * nc + c + 1) * piece, :]
                 for x in range(nx)
             ]
             z = c * nl + l
@@ -282,10 +289,16 @@
     return lax.rsqrt(mean + 1e-06).astype(BF16).astype(F32)
 
 
+def turned(value, outer, inner):
+    size = value.shape[1] // (outer * inner)
+    blocks = [(o * inner + i) * size for i in range(inner) for o in range(outer)]
+    return jnp.concatenate([value[:, at : at + size] for at in blocks], axis=1)
+
+
 def normalise_kernel(tokens_ref, gain_ref, out_ref):
     token_vals = tokens_ref[...].astype(F32)
     scaled = (token_vals * gain_ref[...]).astype(BF16).astype(F32)
-    normed = (scaled * row_scale_of(token_vals)).astype(BF16)
+    normed = turned(scaled * row_scale_of(token_vals), out_ref.shape[0], 2).astype(BF16)
     for i in range(out_ref.shape[0]):
         out_ref[i] = normed
 
@@ -328,9 +341,8 @@
     scale = row_scale_of(token_vals)
     gain = gain_ref[...]
     scaled = (token_vals * gain).astype(BF16).astype(F32)
-    inner_grad = (
-        jnp.concatenate([f[:, :wide] for f in found] + [f[:, wide:] for f in found], axis=1) * scale
-    )
+    inner_grad = jnp.concatenate([f[:, :wide] for f in found] + [f[:, wide:] for f in found], axis=1)
+    inner_grad = turned(inner_grad, 2, nx) * scale
     inner = jnp.sum(scaled * inner_grad, axis=1, keepdims=True)
     factor = scale * scale / width
     input_ref[...] = (gain * inner_grad - factor * token_vals * inner).astype(BF16)
@@ -373,13 +385,13 @@
         near = exchange(normalise(tokens, gain, nx), "x").reshape(nx * rows, width)
         table = lax.all_gather(near, ("y", "k"), axis=0, tiled=True)
 
-        other = exchange(
-            lax.ppermute(pack(nx, gate_weight, up_weight), ("c", "l", "k"), both_ways(nz)), "x"
-        )
+        early = lax.ppermute(pack(nx, gate_weight, up_weight), ("c", "l", "k"), both_ways(nz))
         own = exchange(pack(nx, gate_weight, up_weight, hidden_grad), "x")
+        early = exchange(early, "x")
+        late = lax.ppermute(own[:, feats // 2 : feats], ("c", "l", "k"), both_ways(nz))
 
         hidden, cots, keep, give = forward(
-            place, table, own, other, ny, rows, own_tokens // 2, pool // 2
+            place, table, own, early, late, ny, rows, own_tokens // 2, pool // 2
         )
         taken = lax.ppermute(give, "k", [(0, 1), (1, 0)])
         grad = gradient(table, cots, nx, nl, nc, width // 3)
@@ -413,6 +425,7 @@
             out_specs=VMEM,
             compiler_params=params(8),
         )(place, hidden)
+        hidden, near, far = lax.optimization_barrier((hidden, near, far))
         last = pl.pallas_call(
             functools.partial(gather_kernel, nx, rows, wide, thin),
             out_shape=jax.ShapeDtypeStruct((nx, 16 * nx + feats // nc, pair), BF16),

time: 184 us -> 176 us (0.957)
  waiting for transfers between devices: 57.1 us -> 29 us
  blocking collectives: 10.3 us -> 24.1 us
  local copies, waits for them, and re-layouts: 7.01 us -> 9.43 us
    ppermute x1, waiting for transfers between devices: 16.3 us -> 0.01 us  [per_device(): lax.ppermute(pack(nx, gate_weight, up_weight), ('c', 'l', 'k'), both_ways...]
    ppermute x0 -> x1, starting transfers between devices: none -> 14.7 us  [per_device(): lax.ppermute(own[:, feats // 2:feats], ('c', 'l', 'k'), both_ways(nz))]
    all_to_all x1 -> x2, blocking collectives: 10.3 us -> 24.1 us  [exchange(): return lax.all_to_all(value, axis, split_axis=0, concat_axis=0, tiled=True)]
    ppermute x1, starting transfers between devices: 7.45 us -> 2.1 us  [per_device(): taken = lax.ppermute(give, 'k', [(0, 1), (1, 0)])]
    ppermute x3, waiting for transfers between devices: 15.7 us -> 10.5 us  [per_device(): partial = lax.ppermute(partial, ('y', 'k'), both_ways(ny))]
    ppermute x3, waiting for transfers between devices: 5.2 us -> 0.01 us  [swap_over_x(): got.append(lax.ppermute(piece, 'x', ring(nx, shift)))]
    ppermute x1, waiting for transfers between devices: 4.71 us -> 0.01 us  [per_device(): lax.ppermute(upper, ('y', 'k'), [(2 * y + 1, 2 * ((y - 1) % ny) + 1) for...]
    all_to_all x3 -> x2, starting transfers between devices: 12.1 us -> 7.93 us  [exchange(): return lax.all_to_all(value, axis, split_axis=0, concat_axis=0, tiled=True)]
  transfers between devices with their start and end apart: 15 -> 15, of which waited for: 8 -> 5; matrix products, arithmetic and copies ran while one was open for 3% -> 4% of each run, Pallas kernels for 6% -> 6%
where the time goes in v5:
time: 176 us; the launch traced here: 174 us
  starting transfers between devices  65.2 us (37%)
  waiting for transfers between devices  29 us (16%)
  Pallas kernels  26 us (15%)
  blocking collectives  24.1 us (14%)
  between operations  14.4 us (8%)
  local copies, waits for them, and re-layouts  9.43 us (5%)
  other arithmetic  5.45 us (3%)
    all_to_all x2, blocking collectives, exchange(): return lax.all_to_all(value, axis, split_axis=0, concat_axis=0, tiled=True)  24.1 us
    all_to_all x2, waiting for transfers between devices, exchange(): return lax.all_to_all(value, axis, split_axis=0, concat_axis=0, tiled=True)  17.3 us
    ppermute x3, starting transfers between devices, per_device(): partial = lax.ppermute(partial, ('y', 'k'), both_ways(ny))  15.6 us
    ppermute x1, starting transfers between devices, per_device(): lax.ppermute(own[:, feats // 2:feats], ('c', 'l', 'k'), both_ways(nz))  14.7 us
    pallas_call x1, Pallas kernels, forward(): pl.pallas_call(functools.partial(forward_kernel, chunk, main, part - main...  13.8 us
    ppermute x1, starting transfers between devices, per_device(): lax.ppermute(pack(nx, gate_weight, up_weight), ('c', 'l', 'k'), both_ways...  10.8 us
    ppermute x3, waiting for transfers between devices, per_device(): partial = lax.ppermute(partial, ('y', 'k'), both_ways(ny))  10.5 us
    ppermute x3, starting transfers between devices, swap_over_x(): got.append(lax.ppermute(piece, 'x', ring(nx, shift)))  8.57 us
  transfers between devices with their start and end apart: 15, of which 5 were waited for; matrix products, arithmetic and copies ran while one was open for 4% of the time, Pallas kernels for 6%

profile of v5, /device:TPU:1, one launch (start us, length us, event | category | flops | bytes accessed | tf_op | source)
XLA Modules:
  0.0 173.6 jit_solution(1072554466973857078)
XLA Ops:
  9.1 10.3 %all_to_all.20 = bf16[4,12,2304]{2,1,0:T(8,128)(2,1)S(1)} all-to-all(bf16[4,12,2304]{2,1,0:T(8,128)(2,1)S(1)} %shard_map.84), channel_id=1, replica_groups=mesh['c'=4,'x'=4,'l'=2,'y'=8,'k'=2] {'x'}, dimensions={0} | all-to-all | bytes 442368 | tf_op jit(solution)/shard_map/all_to_all | solution.py:38
  21.3 1.8 %shard_map.85 = bf16[4,400,576]{2,1,0:T(8,128)(2,1)} custom-call(bf16[288,1152]{1,0:T(8,128)(2,1)S(1)} %copy-done, bf16[288,1152]{1,0:T(8,128)(2,1)S(1)} %copy-done.1, bf16[192,1152]{1,0:T(8,128)(2,1)S(1)} %copy-done.2), custom_call_target="tpu_custom_call" | custom-call | bytes 1843200 | tf_op jit(solution)/shard_map/pallas_call | solution.py:82
  23.1 4.4 %all-to-all-start.1 = ((bf16[4,400,576]{2,1,0:T(8,128)(2,1)}), bf16[4,400,576]{2,1,0:T(8,128)(2,1)}, u32[]{:S(2)}, u32[]{:S(2)}) async-start(bf16[4,400,576]{2,1,0:T(8,128)(2,1)} %shard_map.85), calls=%async_computation.1 | async-start | bytes 4096000 | tf_op jit(solution)/shard_map/all_to_all | solution.py:38
  27.7 10.8 %collective-permute-start = (bf16[4,144,576]{2,1,0:T(8,128)(2,1)S(1)}, bf16[4,144,576]{2,1,0:T(8,128)(2,1)}, u32[]{:S(2)}, u32[]{:S(2)}) collective-permute-start(bf16[4,144,576]{2,1,0:T(8,128)(2,1)S(1)} %shard_map.86), channel_id=1, source_target_pairs={{0,16},{16,128},{128,144},{144,256},{256,272},{272,384},{384,400},... | collective-permute-start | bytes 1990664 | tf_op jit(solution)/shard_map/ppermute | solution.py:388
  38.5 8.9 %all-to-all-done.1.own_ref = bf16[4,400,576]{2,1,0:T(8,128)(2,1)} async-done(((bf16[4,400,576]{2,1,0:T(8,128)(2,1)}), bf16[4,400,576]{2,1,0:T(8,128)(2,1)}, u32[]{:S(2)}, u32[]{:S(2)}) %all-to-all-start.1) | async-done | bytes 1843232 | tf_op jit(solution)/shard_map/all_to_all | solution.py:38
  47.4 1.2 slice.44
  48.6 14.7 %collective-permute-start.1 = (bf16[4,144,576]{2,1,0:T(8,128)(2,1)S(1)}, bf16[4,144,576]{2,1,0:T(8,128)(2,1)S(1)}, u32[]{:S(2)}, u32[]{:S(2)}) collective-permute-start(bf16[4,144,576]{2,1,0:T(8,128)(2,1)S(1)} %slice.44), channel_id=1, source_target_pairs={{0,16},{16,128},{128,144},{144,256},{256,272},{272,384},{384,400},... | collective-permute-start | bytes 1990664 | tf_op jit(solution)/shard_map/ppermute | solution.py:391
  63.3 3.5 %all-to-all-start.2 = ((bf16[4,144,576]{2,1,0:T(8,128)(2,1)}), bf16[4,144,576]{2,1,0:T(8,128)(2,1)S(1)}, u32[]{:S(2)}, u32[]{:S(2)}) async-start(bf16[4,144,576]{2,1,0:T(8,128)(2,1)} %collective-permute-done), calls=%async_computation.2 | async-start | bytes 1474560 | tf_op jit(solution)/shard_map/all_to_all | solution.py:38
  67.5 8.4 %all-to-all-done.2.early_ref = bf16[4,144,576]{2,1,0:T(8,128)(2,1)S(1)} async-done(((bf16[4,144,576]{2,1,0:T(8,128)(2,1)}), bf16[4,144,576]{2,1,0:T(8,128)(2,1)S(1)}, u32[]{:S(2)}, u32[]{:S(2)}) %all-to-all-start.2) | async-done | bytes 663584 | tf_op jit(solution)/shard_map/all_to_all | solution.py:38
  77.0 13.8 %shard_map.87 = (bf16[4,96,576]{2,1,0:T(8,128)(2,1)}, bf16[768,576]{1,0:T(8,128)(2,1)}, bf16[4,96,2304]{2,1,0:T(8,128)(2,1)}, bf16[4,96,2304]{2,1,0:T(8,128)(2,1)}) custom-call(s32[4]{0:T(128)} %pad_add_fusion.place_ref, bf16[768,2304]{1,0:T(8,128)(2,1)} %all-gather.2.cloned.1.call-done.table_any.table_ref, bf16[4,400,576]{2,1,0:T(8,128)(2,1)} %all-to-all-done.1.own_ref, ...), custom_call_target="tpu_custom_call" | custom-call | flops 4076863488 | bytes 9732096 | tf_op jit(solution)/shard_map/pallas_call | solution.py:217
  90.8 2.1 %collective-permute-start.5 = (bf16[4,96,2304]{2,1,0:T(8,128)(2,1)}, bf16[4,96,2304]{2,1,0:T(8,128)(2,1)}, u32[]{:S(2)}, u32[]{:S(2)}) collective-permute-start(bf16[4,96,2304]{2,1,0:T(8,128)(2,1)} %get-tuple-element.18), channel_id=1, source_target_pairs={{0,1},{1,0},{2,3},{3,2},{4,5},{5,4},{6,7},{7,6},{8,9},{9,8},{10,11... | collective-permute-start | bytes 5308424 | tf_op jit(solution)/shard_map/ppermute | solution.py:396
  93.0 1.2 copy-done.7
  94.2 6.8 %shard_map.89 = bf16[2304,576]{1,0:T(8,128)(2,1)} custom-call(bf16[768,2304]{1,0:T(8,128)(2,1)} %all-gather.2.cloned.1.call-done.table_any.table_ref, bf16[768,576]{1,0:T(8,128)(2,1)S(1)} %copy-done.7), custom_call_target="tpu_custom_call" | custom-call | flops 2038431744 | bytes 6193152 | tf_op jit(solution)/shard_map/pallas_call | solution.py:265
  101.0 1.4 copy-done.8
  102.5 1.1 fusion.3
  103.6 5.3 %collective-permute-start.6 = (bf16[96,2304]{1,0:T(8,128)(2,1)S(1)}, bf16[96,2304]{1,0:T(8,128)(2,1)S(1)}, u32[]{:S(2)}, u32[]{:S(2)}) collective-permute-start(bf16[96,2304]{1,0:T(8,128)(2,1)S(1)} %fusion.3), channel_id=1, source_target_pairs={{0,2},{2,4},{4,6},{6,8},{8,10},{10,12},{12,14},{14,0},{1,15},{3,1}... | collective-permute-start | bytes 1327112 | tf_op jit(solution)/shard_map/ppermute | solution.py:406
  108.9 5.2 %collective-permute-done.6 = bf16[96,2304]{1,0:T(8,128)(2,1)S(1)} collective-permute-done((bf16[96,2304]{1,0:T(8,128)(2,1)S(1)}, bf16[96,2304]{1,0:T(8,128)(2,1)S(1)}, u32[]{:S(2)}, u32[]{:S(2)}) %collective-permute-start.6) | collective-permute-done | bytes 442400 | tf_op jit(solution)/shard_map/ppermute | solution.py:406
  114.1 1.2 fusion.2
  115.3 5.0 %collective-permute-start.7 = (bf16[96,2304]{1,0:T(8,128)(2,1)S(1)}, bf16[96,2304]{1,0:T(8,128)(2,1)S(1)}, u32[]{:S(2)}, u32[]{:S(2)}) collective-permute-start(bf16[96,2304]{1,0:T(8,128)(2,1)S(1)} %fusion.2), channel_id=1, source_target_pairs={{0,2},{2,4},{4,6},{6,8},{8,10},{10,12},{12,14},{14,0},{1,15},{3,1}... | collective-permute-start | bytes 1327112 | tf_op jit(solution)/shard_map/ppermute | solution.py:406
  120.3 5.2 %collective-permute-done.7 = bf16[96,2304]{1,0:T(8,128)(2,1)S(1)} collective-permute-done((bf16[96,2304]{1,0:T(8,128)(2,1)S(1)}, bf16[96,2304]{1,0:T(8,128)(2,1)S(1)}, u32[]{:S(2)}, u32[]{:S(2)}) %collective-permute-start.7) | collective-permute-done | bytes 442400 | tf_op jit(solution)/shard_map/ppermute | solution.py:406
  125.5 1.2 fusion.1
  126.7 5.3 %collective-permute-start.8 = (bf16[96,2304]{1,0:T(8,128)(2,1)S(1)}, bf16[96,2304]{1,0:T(8,128)(2,1)S(1)}, u32[]{:S(2)}, u32[]{:S(2)}) collective-permute-start(bf16[96,2304]{1,0:T(8,128)(2,1)S(1)} %fusion.1), channel_id=1, source_target_pairs={{0,2},{2,4},{4,6},{6,8},{8,10},{10,12},{12,14},{14,0},{1,15},{3,1}... | collective-permute-start | bytes 1327112 | tf_op jit(solution)/shard_map/ppermute | solution.py:406
  132.1 2.3 %collective-permute-start.2 = (bf16[96,576]{1,0:T(8,128)(2,1)S(1)}, bf16[96,576]{1,0:T(8,128)(2,1)S(1)}, u32[]{:S(2)}, u32[]{:S(2)}) collective-permute-start(bf16[96,576]{1,0:T(8,128)(2,1)S(1)} %get-tuple-element.31), channel_id=1, source_target_pairs={{0,32},{32,64},{64,96},{96,0},{1,33},{33,65},{65,97},{97,1},{2,34}... | collective-permute-start | bytes 331784 | tf_op jit(solution)/shard_map/ppermute | solution.py:283
  134.5 3.8 %collective-permute-start.3 = (bf16[96,576]{1,0:T(8,128)(2,1)S(1)}, bf16[96,576]{1,0:T(8,128)(2,1)S(1)}, u32[]{:S(2)}, u32[]{:S(2)}) collective-permute-start(bf16[96,576]{1,0:T(8,128)(2,1)S(1)} %get-tuple-element.30), channel_id=1, source_target_pairs={{0,64},{32,96},{64,0},{96,32},{1,65},{33,97},{65,1},{97,33},{2,66}... | collective-permute-start | bytes 331784 | tf_op jit(solution)/shard_map/ppermute | solution.py:283
  138.2 2.5 %collective-permute-start.4 = (bf16[96,576]{1,0:T(8,128)(2,1)S(1)}, bf16[96,576]{1,0:T(8,128)(2,1)S(1)}, u32[]{:S(2)}, u32[]{:S(2)}) collective-permute-start(bf16[96,576]{1,0:T(8,128)(2,1)S(1)} %get-tuple-element.29), channel_id=1, source_target_pairs={{0,96},{32,0},{64,32},{96,64},{1,97},{33,1},{65,33},{97,65},{2,98}... | collective-permute-start | bytes 331784 | tf_op jit(solution)/shard_map/ppermute | solution.py:283
  140.7 1.2 fusion.sums_ref
  141.9 1.9 %collective-permute-start.10 = (bf16[48,2304]{1,0:T(8,128)(2,1)S(1)}, bf16[48,2304]{1,0:T(8,128)(2,1)S(1)}, u32[]{:S(2)}, u32[]{:S(2)}) collective-permute-start(bf16[48,2304]{1,0:T(8,128)(2,1)S(1)} %get-tuple-element.32), channel_id=1, source_target_pairs={{1,15},{3,1},{5,3},{7,5},{9,7},{11,9},{13,11},{15,13},{17,31},{19,... | collective-permute-start | bytes 663560 | tf_op jit(solution)/shard_map/ppermute | solution.py:416
  143.9 3.5 %collective-permute-start.9 = (bf16[48,2304]{1,0:T(8,128)(2,1)S(1)}, bf16[48,2304]{1,0:T(8,128)(2,1)S(1)}, u32[]{:S(2)}, u32[]{:S(2)}) collective-permute-start(bf16[48,2304]{1,0:T(8,128)(2,1)S(1)} %get-tuple-element.33), channel_id=1, source_target_pairs={{0,1},{2,3},{4,5},{6,7},{8,9},{10,11},{12,13},{14,15},{1,14},{3,0}... | collective-permute-start | bytes 663560 | tf_op jit(solution)/shard_map/ppermute | solution.py:411
  147.6 1.5 shard_map.88
  149.0 1.2 collective-permute-done.9.near_ref
  152.0 13.8 %all_to_all.21.got_ref = bf16[4,136,576]{2,1,0:T(8,128)(2,1)S(1)} all-to-all(bf16[4,136,576]{2,1,0:T(8,128)(2,1)S(1)} %shard_map.90), channel_id=1, replica_groups=mesh['c'=4,'x'=4,'l'=2,'y'=8,'k'=2] {'x'}, dimensions={0} | all-to-all | bytes 1253376 | tf_op jit(solution)/shard_map/all_to_all | solution.py:38
  165.7 1.0 shard_map.91
  (45 shorter events, 7.6 us)
Async XLA Ops:
  7.2 13.1 %copy-start = (bf16[288,1152]{1,0:T(8,128)(2,1)S(1)}, bf16[288,1152]{1,0:T(8,128)(2,1)}, u32[]{:S(2)}) copy-start(bf16[288,1152]{1,0:T(8,128)(2,1)} %gate_ref.3) | copy-start | bytes 1990660
  7.2 13.1 %copy-start.1 = (bf16[288,1152]{1,0:T(8,128)(2,1)S(1)}, bf16[288,1152]{1,0:T(8,128)(2,1)}, u32[]{:S(2)}) copy-start(bf16[288,1152]{1,0:T(8,128)(2,1)} %up_ref.3) | copy-start | bytes 1990660
  7.2 68.7 %all-gather.2.cloned.1.call-start = ((), (), s32[]{:S(2)}) async-start(), calls=%async_computation.5 | async-start | bytes 3760128 | tf_op jit(solution)/shard_map/all_gather | solution.py:386
  8.0 0.9 copy-start.4
  20.3 1.0 copy-start.2
  23.1 24.3 %all-to-all-start.1 = ((bf16[4,400,576]{2,1,0:T(8,128)(2,1)}), bf16[4,400,576]{2,1,0:T(8,128)(2,1)}, u32[]{:S(2)}, u32[]{:S(2)}) async-start(bf16[4,400,576]{2,1,0:T(8,128)(2,1)} %shard_map.85), calls=%async_computation.1 | async-start | bytes 4096000 | tf_op jit(solution)/shard_map/all_to_all | solution.py:38
  27.7 35.5 %collective-permute-start = (bf16[4,144,576]{2,1,0:T(8,128)(2,1)S(1)}, bf16[4,144,576]{2,1,0:T(8,128)(2,1)}, u32[]{:S(2)}, u32[]{:S(2)}) collective-permute-start(bf16[4,144,576]{2,1,0:T(8,128)(2,1)S(1)} %shard_map.86), channel_id=1, source_target_pairs={{0,16},{16,128},{128,144},{144,256},{256,272},{272,384},{384,400},... | collective-permute-start | bytes 1990664 | tf_op jit(solution)/shard_map/ppermute | solution.py:388
  48.6 27.3 %collective-permute-start.1 = (bf16[4,144,576]{2,1,0:T(8,128)(2,1)S(1)}, bf16[4,144,576]{2,1,0:T(8,128)(2,1)S(1)}, u32[]{:S(2)}, u32[]{:S(2)}) collective-permute-start(bf16[4,144,576]{2,1,0:T(8,128)(2,1)S(1)} %slice.44), channel_id=1, source_target_pairs={{0,16},{16,128},{128,144},{144,256},{256,272},{272,384},{384,400},... | collective-permute-start | bytes 1990664 | tf_op jit(solution)/shard_map/ppermute | solution.py:391
  63.3 12.6 %all-to-all-start.2 = ((bf16[4,144,576]{2,1,0:T(8,128)(2,1)}), bf16[4,144,576]{2,1,0:T(8,128)(2,1)S(1)}, u32[]{:S(2)}, u32[]{:S(2)}) async-start(bf16[4,144,576]{2,1,0:T(8,128)(2,1)} %collective-permute-done), calls=%async_computation.2 | async-start | bytes 1474560 | tf_op jit(solution)/shard_map/all_to_all | solution.py:38
  66.8 83.5 %reduce-scatter.2.cloned.1.call-start = ((), (), s32[]{:S(2)}) async-start(), calls=%async_computation.6 | async-start | bytes 3317760 | tf_op jit(solution)/shard_map/reduce_scatter | solution.py:399
  75.9 0.9 copy-start.9
  75.9 1.1 copy-start.11
  90.8 10.1 %collective-permute-start.5 = (bf16[4,96,2304]{2,1,0:T(8,128)(2,1)}, bf16[4,96,2304]{2,1,0:T(8,128)(2,1)}, u32[]{:S(2)}, u32[]{:S(2)}) collective-permute-start(bf16[4,96,2304]{2,1,0:T(8,128)(2,1)} %get-tuple-element.18), channel_id=1, source_target_pairs={{0,1},{1,0},{2,3},{3,2},{4,5},{5,4},{6,7},{7,6},{8,9},{9,8},{10,11... | collective-permute-start | bytes 5308424 | tf_op jit(solution)/shard_map/ppermute | solution.py:396
  93.0 1.2 copy-start.7
  101.0 1.5 copy-start.8
  103.6 28.5 %copy-start.10 = (bf16[4,96,576]{2,1,0:T(8,128)(2,1)S(1)}, bf16[4,96,576]{2,1,0:T(8,128)(2,1)}, u32[]{:S(2)}) copy-start(bf16[4,96,576]{2,1,0:T(8,128)(2,1)} %get-tuple-element.16) | copy-start | bytes 1327108
  103.6 10.5 %collective-permute-start.6 = (bf16[96,2304]{1,0:T(8,128)(2,1)S(1)}, bf16[96,2304]{1,0:T(8,128)(2,1)S(1)}, u32[]{:S(2)}, u32[]{:S(2)}) collective-permute-start(bf16[96,2304]{1,0:T(8,128)(2,1)S(1)} %fusion.3), channel_id=1, source_target_pairs={{0,2},{2,4},{4,6},{6,8},{8,10},{10,12},{12,14},{14,0},{1,15},{3,1}... | collective-permute-start | bytes 1327112 | tf_op jit(solution)/shard_map/ppermute | solution.py:406
  115.3 10.3 %collective-permute-start.7 = (bf16[96,2304]{1,0:T(8,128)(2,1)S(1)}, bf16[96,2304]{1,0:T(8,128)(2,1)S(1)}, u32[]{:S(2)}, u32[]{:S(2)}) collective-permute-start(bf16[96,2304]{1,0:T(8,128)(2,1)S(1)} %fusion.2), channel_id=1, source_target_pairs={{0,2},{2,4},{4,6},{6,8},{8,10},{10,12},{12,14},{14,0},{1,15},{3,1}... | collective-permute-start | bytes 1327112 | tf_op jit(solution)/shard_map/ppermute | solution.py:406
  126.7 14.0 %collective-permute-start.8 = (bf16[96,2304]{1,0:T(8,128)(2,1)S(1)}, bf16[96,2304]{1,0:T(8,128)(2,1)S(1)}, u32[]{:S(2)}, u32[]{:S(2)}) collective-permute-start(bf16[96,2304]{1,0:T(8,128)(2,1)S(1)} %fusion.1), channel_id=1, source_target_pairs={{0,2},{2,4},{4,6},{6,8},{8,10},{10,12},{12,14},{14,0},{1,15},{3,1}... | collective-permute-start | bytes 1327112 | tf_op jit(solution)/shard_map/ppermute | solution.py:406
  132.1 15.3 %collective-permute-start.2 = (bf16[96,576]{1,0:T(8,128)(2,1)S(1)}, bf16[96,576]{1,0:T(8,128)(2,1)S(1)}, u32[]{:S(2)}, u32[]{:S(2)}) collective-permute-start(bf16[96,576]{1,0:T(8,128)(2,1)S(1)} %get-tuple-element.31), channel_id=1, source_target_pairs={{0,32},{32,64},{64,96},{96,0},{1,33},{33,65},{65,97},{97,1},{2,34}... | collective-permute-start | bytes 331784 | tf_op jit(solution)/shard_map/ppermute | solution.py:283
  134.5 13.0 %collective-permute-start.3 = (bf16[96,576]{1,0:T(8,128)(2,1)S(1)}, bf16[96,576]{1,0:T(8,128)(2,1)S(1)}, u32[]{:S(2)}, u32[]{:S(2)}) collective-permute-start(bf16[96,576]{1,0:T(8,128)(2,1)S(1)} %get-tuple-element.30), channel_id=1, source_target_pairs={{0,64},{32,96},{64,0},{96,32},{1,65},{33,97},{65,1},{97,33},{2,66}... | collective-permute-start | bytes 331784 | tf_op jit(solution)/shard_map/ppermute | solution.py:283
  138.2 9.3 %copy-start.6 = (s32[4]{0:T(128)S(1)}, s32[4]{0:T(128)}, u32[]{:S(2)}) copy-start(s32[4]{0:T(128)} %pad_add_fusion.place_ref) | copy-start | bytes 52
  138.2 9.2 %collective-permute-start.4 = (bf16[96,576]{1,0:T(8,128)(2,1)S(1)}, bf16[96,576]{1,0:T(8,128)(2,1)S(1)}, u32[]{:S(2)}, u32[]{:S(2)}) collective-permute-start(bf16[96,576]{1,0:T(8,128)(2,1)S(1)} %get-tuple-element.29), channel_id=1, source_target_pairs={{0,96},{32,0},{64,32},{96,64},{1,97},{33,1},{65,33},{97,65},{2,98}... | collective-permute-start | bytes 331784 | tf_op jit(solution)/shard_map/ppermute | solution.py:283
  141.9 7.1 %collective-permute-start.10 = (bf16[48,2304]{1,0:T(8,128)(2,1)S(1)}, bf16[48,2304]{1,0:T(8,128)(2,1)S(1)}, u32[]{:S(2)}, u32[]{:S(2)}) collective-permute-start(bf16[48,2304]{1,0:T(8,128)(2,1)S(1)} %get-tuple-element.32), channel_id=1, source_target_pairs={{1,15},{3,1},{5,3},{7,5},{9,7},{11,9},{13,11},{15,13},{17,31},{19,... | collective-permute-start | bytes 663560 | tf_op jit(solution)/shard_map/ppermute | solution.py:416
  143.9 6.4 %collective-permute-start.9 = (bf16[48,2304]{1,0:T(8,128)(2,1)S(1)}, bf16[48,2304]{1,0:T(8,128)(2,1)S(1)}, u32[]{:S(2)}, u32[]{:S(2)}) collective-permute-start(bf16[48,2304]{1,0:T(8,128)(2,1)S(1)} %get-tuple-element.33), channel_id=1, source_target_pairs={{0,1},{2,3},{4,5},{6,7},{8,9},{10,11},{12,13},{14,15},{1,14},{3,0}... | collective-permute-start | bytes 663560 | tf_op jit(solution)/shard_map/ppermute | solution.py:411
  147.6 18.2 %copy-start.5 = (bf16[12,2304]{1,0:T(8,128)(2,1)S(1)}, bf16[12,2304]{1,0:T(8,128)(2,1)}, u32[]{:S(2)}) copy-start(bf16[12,2304]{1,0:T(8,128)(2,1)} %tokens_ref.3) | copy-start | bytes 165892
  150.3 1.0 copy-start.3
Sparse Core Ops, SparseCore 0:
  20.4 48.7 all-gather.1
  101.1 43.4 reduce-scatter.1

commit v6 on v5

--- a/solution.py
+++ b/solution.py
@@ -62,31 +62,38 @@
         put_pair(out_ref, q, rows, gate_ref.at[rows], up_ref.at[rows], main, tail, parts)
 
 
-def pack_all_kernel(main, tail, parts, gate_ref, up_ref, grad_ref, out_ref):
-    feats = gate_ref.shape[0]
+def pack_weights(parts, gate, up, rows):
+    main, tail = share_sizes(gate.shape[1], parts)
+    return pl.pallas_call(
+        functools.partial(pack_weights_kernel, main, tail, parts),
+        out_shape=jax.ShapeDtypeStruct((parts, rows, 2 * (main + tail)), BF16),
+        in_specs=[VMEM, VMEM],
+        out_specs=VMEM,
+        compiler_params=params(16),
+    )(gate, up)
+
+
+def pack_grads_kernel(main, tail, parts, weights_ref, grad_ref, out_ref):
+    cut = weights_ref.shape[1]
     half = grad_ref.shape[0] // 2
+    out_ref[:, 0:cut, :] = weights_ref[...]
     for q in range(parts):
-        put_pair(out_ref, q, slice(0, feats), gate_ref, up_ref, main, tail, parts)
         put_pair(
-            out_ref, q, slice(feats, feats + half),
+            out_ref, q, slice(cut, cut + half),
             grad_ref.at[0:half], grad_ref.at[half : 2 * half], main, tail, parts,
         )
 
 
-def pack(parts, gate, up, grads=None):
-    feats, units = gate.shape
-    main, tail = share_sizes(units, parts)
-    operands = (gate, up) if grads is None else (gate, up, grads)
-    rows = feats // 2 if grads is None else feats + grads.shape[0] // 2 + 16
-    kernel = pack_weights_kernel if grads is None else pack_all_kernel
-    return pl.pallas_call(
-        functools.partial(kernel, main, tail, parts),
+def pack_grads(parts, weights, grads):
+    main, tail = share_sizes(grads.shape[1], parts)
+    rows = weights.shape[1] + grads.shape[0] // 2 + 32
+    return pl.pallas_call(
+        functools.partial(pack_grads_kernel, main, tail, parts),
         out_shape=jax.ShapeDtypeStruct((parts, rows, 2 * (main + tail)), BF16),
-        in_specs=[VMEM] * len(operands),
+        in_specs=[VMEM, VMEM],
         out_specs=VMEM,
-        compiler_params=params(24),
-        cost_estimate=pl.CostEstimate(flops=0, bytes_accessed=4 * parts * rows * (main + tail), transcendentals=0),
-    )(*operands)
+        compiler_params=params(16),
+    )(weights, grads)
 
 
 def activate(gate, upward, cotangent):
@@ -116,74 +123,110 @@
     return (columns == source).astype(F32).astype(BF16)
 
 
+SORTED = 4
+
+
+def sort_grads_kernel(main, tail, cut, rows_each, raw_ref, out_ref):
+    blocks = raw_ref.shape[0]
+    size = SORTED * rows_each
+    half = out_ref.shape[0] // (2 * blocks)
+    order = shuffle(blocks * size, SORTED, blocks, rows_each)
+    for g in range(2 * half // size):
+        h, at = g * size // half, cut + g * size % half
+        found = [raw_ref[x, at : at + size, :] for x in range(blocks)]
+        found = jnp.concatenate(found, axis=0)
+        rows = slice(g * blocks * size, (g + 1) * blocks * size)
+        for lanes, first, width in (
+            (slice(0, main), h * main, main), (slice(main, main + tail), 2 * main + h * tail, tail)
+        ):
+            out_ref[rows, lanes] = jnp.dot(
+                order, found[:, first : first + width], preferred_element_type=F32
+            ).astype(BF16)
+
+
+def sort_grads(raw, cut, own_tokens, rows_each):
+    blocks, _, pair = raw.shape
+    main = pair // 2 // 128 * 128
+    return pl.pallas_call(
+        functools.partial(sort_grads_kernel, main, pair // 2 - main, cut, rows_each),
+        out_shape=jax.ShapeDtypeStruct((blocks * own_tokens, pair // 2), BF16),
+        in_specs=[VMEM],
+        out_specs=VMEM,
+        compiler_params=params(16),
+    )(raw)
+
+
+def sort_hidden_kernel(main, tail, rows_each, found_ref, out_ref):
+    blocks, half, _ = out_ref.shape
+    size = SORTED * rows_each
+    order = shuffle(blocks * size, blocks, SORTED, rows_each)
+    for g in range(2 * half // size):
+        h, at = g * size // half, g * size % half
+        rows = slice(g * blocks * size, (g + 1) * blocks * size)
+        for lanes, first, width in (
+            (slice(0, main), h * main, main), (slice(main, main + tail), 2 * main + h * tail, tail)
+        ):
+            got = jnp.dot(order, found_ref[rows, lanes], preferred_element_type=F32).astype(BF16)
+            for x in range(blocks):
+                out_ref[x, at : at + size, first : first + width] = got[x * size : (x + 1) * size]
+
+
+def sort_hidden(found, blocks, rows_each):
+    pool, part = found.shape
+    main = part // 128 * 128
+    return pl.pallas_call(
+        functools.partial(sort_hidden_kernel, main, part - main, rows_each),
+        out_shape=jax.ShapeDtypeStruct((blocks, pool // blocks // 2, 2 * part), BF16),
+        in_specs=[VMEM],
+        out_specs=VMEM,
+        compiler_params=params(16),
+    )(found)
+
+
 def forward_kernel(
-    chunk, main, tail, rows_each, place_ref, table_any, own_ref, early_ref, late_ref,
-    hidden_ref, cots_ref, keep_ref, give_ref, table_ref, mine, theirs, raw, grads_ref, found, sems,
+    chunk, main, tail, place_ref, table_any, own_ref, early_ref, late_ref, grads_ref,
+    found_ref, cots_ref, keep_ref, give_ref, table_ref, theirs, sems,
 ):
-    blocks, cut, _ = early_ref.shape
-    feats = cut + late_ref.shape[1]
+    blocks, feats, pair = own_ref.shape
+    cut = feats - late_ref.shape[1]
     pool, width = table_ref.shape
-    half = raw.shape[1]
     low, core, me = place_ref[0], place_ref[1], place_ref[3]
-    chain = keep_ref.shape[0]
-    near_cols = pl.ds(pl.multiple_of(low * (width // 2), 128), width // 2)
-    far_cols = pl.ds(pl.multiple_of((1 - low) * (width // 2), 128), width // 2)
-    grads_copy = pltpu.make_async_copy(own_ref.at[:, pl.ds(feats, half)], raw, sems.at[3 * blocks])
-    grads_copy.start()
-    copies = []
-    for x in range(blocks):
-        for i, (src, dst, first, size) in enumerate((
-            (own_ref, mine, 0, feats), (early_ref, theirs, 0, cut), (late_ref, theirs, cut, feats - cut)
-        )):
-            copies.append(
-                pltpu.make_async_copy(
-                    src.at[x, pl.ds(0, size)], dst.at[pl.ds(x * feats + first, size)], sems.at[3 * x + i]
-                )
-            )
+    chain, step, _ = keep_ref.shape
     tables = [
         pltpu.make_async_copy(
             table_any.at[pl.ds(first, chunk)], table_ref.at[pl.ds(first, chunk)],
-            sems.at[3 * blocks + 1 + first // chunk],
+            sems.at[first // chunk],
         )
         for first in range(0, pool, chunk)
     ]
-    tables[0].start()
-    for copy in copies:
+    for copy in tables:
         copy.start()
-    for copy in tables[1:]:
-        copy.start()
-    groups = pool // (blocks * rows_each)
-    forth = shuffle(pool, groups, blocks, rows_each)
-    back = shuffle(pool, blocks, groups, rows_each)
-    grads_copy.wait()
+    near_cols = pl.ds(pl.multiple_of(low * (width // 2), 128), width // 2)
+    far_cols = pl.ds(pl.multiple_of((1 - low) * (width // 2), 128), width // 2)
     for x in range(blocks):
-        for h in range(2):
-            rows = slice((2 * x + h) * half, (2 * x + h + 1) * half)
-            grads_ref[rows, :main] = raw[x, :, h * main : (h + 1) * main]
-            grads_ref[rows, main:] = raw[x, :, 2 * main + h * tail : 2 * main + (h + 1) * tail]
-    for copy in copies:
-        copy.wait()
-    step = keep_ref.shape[1]
+        theirs[x * feats : x * feats + cut, :] = early_ref[x, :cut, :]
+        theirs[x * feats + cut : (x + 1) * feats, :] = late_ref[x]
     for first in range(0, pool, chunk):
         rows = slice(first, first + chunk)
         tables[first // chunk].wait()
-        both = jnp.dot(table_ref[rows, near_cols], mine[...], preferred_element_type=F32)
+        mine = own_ref[...].reshape(blocks * feats, pair)
+        both = jnp.dot(table_ref[rows, near_cols], mine, preferred_element_type=F32)
         both = both + jnp.dot(table_ref[rows, far_cols], theirs[...], preferred_element_type=F32)
-        grads = jnp.dot(forth[rows, :], grads_ref[...], preferred_element_type=F32)
+        grads = grads_ref[rows, :].astype(F32)
         hidden, gate_cot, up_cot = activate(
             both[:, :main], both[:, main : 2 * main], grads[:, :main]
         )
-        found[rows, :main] = hidden
+        found_ref[rows, :main] = hidden
         cots_ref[rows, :main] = gate_cot
         cots_ref[rows, main : 2 * main] = up_cot
         rest = both[:, 2 * main :]
         hidden, gate_cot, up_cot = activate(rest[:, :tail], rest[:, tail:], grads[:, main:])
-        found[rows, main:] = hidden
+        found_ref[rows, main:] = hidden
         cots_ref[rows, 2 * main : 2 * main + tail] = gate_cot
         cots_ref[rows, 2 * main + tail :] = up_cot
-        for weights, cols in ((mine, near_cols), (theirs, far_cols)):
+        for weights, cols in ((mine, near_cols), (theirs[...], far_cols)):
             partial = lax.dot_general(
-                cots_ref[rows, :], weights[...], (((1,), (1,)), ((), ())), preferred_element_type=F32
+                cots_ref[rows, :], weights, (((1,), (1,)), ((), ())), preferred_element_type=F32
             )
             for j in range(chunk // step):
                 block = partial[j * step : (j + 1) * step].astype(BF16)
@@ -200,75 +243,74 @@
                 def _():
                     give_ref[slot, :, cols] = block
 
-    spread = jnp.dot(back, found[...], preferred_element_type=F32).astype(BF16)
-    for x in range(blocks):
-        for h in range(2):
-            rows = slice((2 * x + h) * half, (2 * x + h + 1) * half)
-            hidden_ref[x, :, h * main : (h + 1) * main] = spread[rows, :main]
-            hidden_ref[x, :, 2 * main + h * tail : 2 * main + (h + 1) * tail] = spread[rows, main:]
-
-
-def forward(place, table, own, early, late, ny, rows_each, half, chunk):
+
+def forward(place, table, own, early, late, grads, ny, chunk):
     pool, width = table.shape
-    blocks, _, pair = early.shape
+    _, _, pair = own.shape
     part = pair // 2
     main = part // 128 * 128
     step = pool // ny
     return pl.pallas_call(
-        functools.partial(forward_kernel, chunk, main, part - main, rows_each),
+        functools.partial(forward_kernel, chunk, main, part - main),
         out_shape=(
-            jax.ShapeDtypeStruct((blocks, half, pair), BF16),
+            jax.ShapeDtypeStruct((pool, part), BF16),
             jax.ShapeDtypeStruct((pool, pair), BF16),
             jax.ShapeDtypeStruct((ny // 2, step, width), BF16),
             jax.ShapeDtypeStruct((ny // 2, step, width), BF16),
+            jax.ShapeDtypeStruct((pool, width), BF16),
         ),
-        in_specs=[SMEM, ANY, ANY, ANY, ANY],
-        out_specs=(VMEM, VMEM, VMEM, VMEM),
+        in_specs=[SMEM, ANY, VMEM, VMEM, VMEM, VMEM],
+        out_specs=(VMEM, VMEM, VMEM, VMEM, VMEM),
         scratch_shapes=[
-            pltpu.VMEM((pool, width), BF16),
             pltpu.VMEM((width // 2, pair), BF16),
-            pltpu.VMEM((width // 2, pair), BF16),
-            pltpu.VMEM((blocks, half, pair), BF16),
-            pltpu.VMEM((pool, part), BF16),
-            pltpu.VMEM((pool, part), BF16),
-            pltpu.SemaphoreType.DMA((3 * blocks + 1 + pool // chunk,)),
+            pltpu.SemaphoreType.DMA((pool // chunk,)),
         ],
-        compiler_params=params(60),
+        compiler_params=params(36),
         cost_estimate=pl.CostEstimate(
             flops=4 * pool * width * pair, bytes_accessed=2 * (2 * pool * width + width * pair), transcendentals=0
         ),
-    )(place, table, own, early, late)
-
-
-def gradient_kernel(tile, nx, nl, nc, table_ref, cots_ref, out_ref, total):
+    )(place, table, own, early, late, grads)
+
+
+def gradient_kernel(nx, nl, nc, table_ref, cots_ref, out_any, total, ready, sems):
     width = table_ref.shape[1]
-    for first in range(0, width, tile):
-        total[first : first + tile, :] = lax.dot_general(
-            table_ref[:, first : first + tile], cots_ref[...], (((0,), (0,)), ((), ())),
+    span = width // nl
+    piece = span // (nx * nc)
+    block = nx * piece
+    copies = []
+    for l in range(nl):
+        total[...] = lax.dot_general(
+            table_ref[:, l * span : (l + 1) * span], cots_ref[...], (((0,), (0,)), ((), ())),
             preferred_element_type=F32,
         )
-    piece = width // (nx * nl * nc)
-    block = nx * piece
-    for c in range(nc):
-        for l in range(nl):
-            found = [
-                total[((l * nx + x) * nc + c) * piece : ((l * nx + x) * nc + c + 1) * piece, :]
-                for x in range(nx)
-            ]
+        for c in range(nc):
+            found = [total[(x * nc + c) * piece : (x * nc + c + 1) * piece, :] for x in range(nx)]
             z = c * nl + l
-            out_ref[z * block : (z + 1) * block, :] = jnp.concatenate(found, axis=0).astype(BF16)
-
-
-def gradient(table, cots, nx, nl, nc, tile):
+            ready[z] = jnp.concatenate(found, axis=0).astype(BF16)
+            copies.append(
+                pltpu.make_async_copy(
+                    ready.at[z], out_any.at[pl.ds(z * block, block)], sems.at[z]
+                )
+            )
+            copies[-1].start()
+    for copy in copies:
+        copy.wait()
+
+
+def gradient(table, cots, nx, nl, nc):
     pool, width = table.shape
     pair = cots.shape[1]
     return pl.pallas_call(
-        functools.partial(gradient_kernel, tile, nx, nl, nc),
+        functools.partial(gradient_kernel, nx, nl, nc),
         out_shape=jax.ShapeDtypeStruct((width, pair), BF16),
         in_specs=[VMEM, VMEM],
-        out_specs=VMEM,
-        scratch_shapes=[pltpu.VMEM((width, pair), F32)],
-        compiler_params=params(48),
+        out_specs=ANY,
+        scratch_shapes=[
+            pltpu.VMEM((width // nl, pair), F32),
+            pltpu.VMEM((nl * nc, width // (nl * nc), pair), BF16),
+            pltpu.SemaphoreType.DMA((nl * nc,)),
+        ],
+        compiler_params=params(32),
         cost_estimate=pl.CostEstimate(
             flops=2 * pool * width * pair, bytes_accessed=2 * (pool * width + width * pair), transcendentals=0
         ),
@@ -385,16 +427,20 @@
         near = exchange(normalise(tokens, gain, nx), "x").reshape(nx * rows, width)
         table = lax.all_gather(near, ("y", "k"), axis=0, tiled=True)
 
-        early = lax.ppermute(pack(nx, gate_weight, up_weight), ("c", "l", "k"), both_ways(nz))
-        own = exchange(pack(nx, gate_weight, up_weight, hidden_grad), "x")
-        early = exchange(early, "x")
-        late = lax.ppermute(own[:, feats // 2 : feats], ("c", "l", "k"), both_ways(nz))
-
-        hidden, cots, keep, give = forward(
-            place, table, own, early, late, ny, rows, own_tokens // 2, pool // 2
+        cut = feats // 2
+        early = lax.ppermute(
+            pack_weights(nx, gate_weight, up_weight, cut), ("c", "l", "k"), both_ways(nz)
+        )
+        own = exchange(pack_weights(nx, gate_weight, up_weight, feats), "x")
+        early = exchange(pack_grads(nx, early, hidden_grad), "x")
+        late = lax.ppermute(own[:, cut:], ("c", "l", "k"), both_ways(nz))
+        grads = sort_grads(early, cut, own_tokens, rows)
+
+        found, cots, keep, give, table = forward(
+            place, table, own, early, late, grads, ny, pool // 2
         )
         taken = lax.ppermute(give, "k", [(0, 1), (1, 0)])
-        grad = gradient(table, cots, nx, nl, nc, width // 3)
+        grad = gradient(table, cots, nx, nl, nc)
         taken, grad = lax.optimization_barrier((taken, grad))
         grad = lax.psum_scatter(grad, ("c", "l"), scatter_dimension=0, tiled=True)
 
@@ -417,7 +463,7 @@
             upper, ("y", "k"), [(2 * y + 1, 2 * ((y - 1) % ny) + 1) for y in range(ny)]
         )
 
-        hidden = jnp.stack(swap_over_x(hidden, nx))
+        hidden = jnp.stack(swap_over_x(sort_hidden(found, nx, rows), nx))
         hidden = pl.pallas_call(
             functools.partial(spread_kernel, main, tail),
             out_shape=jax.ShapeDtypeStruct((own_tokens, units), BF16),

time: 176 us -> 169 us (0.960)
  starting transfers between devices: 65.2 us -> 61.4 us
  Pallas kernels: 26 us -> 23 us
  blocking collectives: 24.1 us -> 22.1 us
    all_to_all x2, waiting for transfers between devices: 17.3 us -> 6.43 us  [exchange(): return lax.all_to_all(value, axis, split_axis=0, concat_axis=0, tiled=True)]
    ppermute x2, waiting for transfers between devices: 0.01 us -> 9.38 us  [the longest x1 8.39 us: per_device(): lax.ppermute(pack_weights(nx, gate_weight, up_weight, cut), ('c', 'l', 'k...]
    ppermute x2, starting transfers between devices: 25.4 us -> 17.8 us  [the longest x1 10.8 us: per_device(): lax.ppermute(pack_weights(nx, gate_weight, up_weight, cut), ('c', 'l', 'k...]
    ppermute x3, starting transfers between devices: 8.57 us -> 11 us  [swap_over_x(): got.append(lax.ppermute(piece, 'x', ring(nx, shift)))]
    all_gather x1, waiting for transfers between devices: 0.02 us -> 2.29 us  [per_device(): table = lax.all_gather(near, ('y', 'k'), axis=0, tiled=True)]
    pallas_call x1, Pallas kernels: 13.8 us -> 11.6 us  [forward(): pl.pallas_call(functools.partial(forward_kernel, chunk, main, part - main...]
    all_to_all x2, blocking collectives: 24.1 us -> 22.1 us  [exchange(): return lax.all_to_all(value, axis, split_axis=0, concat_axis=0, tiled=True)]
    ppermute x1, starting transfers between devices: 2.1 us -> 4.02 us  [per_device(): taken = lax.ppermute(give, 'k', [(0, 1), (1, 0)])]
  transfers between devices with their start and end apart: 15 -> 15, of which waited for: 5 -> 7; matrix products, arithmetic and copies ran while one was open for 4% -> 4% of each run, Pallas kernels for 6% -> 6%
where the time goes in v6:
time: 169 us; the launch traced here: 167 us
  starting transfers between devices  61.4 us (36%)
  waiting for transfers between devices  29.9 us (18%)
  Pallas kernels  23 us (14%)
  blocking collectives  22.1 us (13%)
  between operations  14.3 us (8%)
  local copies, waits for them, and re-layouts  11 us (7%)
  other arithmetic  4.89 us (3%)
    all_to_all x2, blocking collectives, exchange(): return lax.all_to_all(value, axis, split_axis=0, concat_axis=0, tiled=True)  22.1 us
    ppermute x3, starting transfers between devices, per_device(): partial = lax.ppermute(partial, ('y', 'k'), both_ways(ny))  15.5 us
    pallas_call x1, Pallas kernels, forward(): pl.pallas_call(functools.partial(forward_kernel, chunk, main, part - main...  11.6 us
    ppermute x3, starting transfers between devices, swap_over_x(): got.append(lax.ppermute(piece, 'x', ring(nx, shift)))  11 us
    ppermute x1, starting transfers between devices, per_device(): lax.ppermute(pack_weights(nx, gate_weight, up_weight, cut), ('c', 'l', 'k...  10.8 us
    ppermute x3, waiting for transfers between devices, per_device(): partial = lax.ppermute(partial, ('y', 'k'), both_ways(ny))  10.5 us
    unnamed x22, local copies, waits for them, and re-layouts  8.48 us
    ppermute x1, waiting for transfers between devices, per_device(): lax.ppermute(pack_weights(nx, gate_weight, up_weight, cut), ('c', 'l', 'k...  8.39 us
  transfers between devices with their start and end apart: 15, of which 7 were waited for; matrix products, arithmetic and copies ran while one was open for 4% of the time, Pallas kernels for 6%

profile of v6, /device:TPU:1, one launch (start us, length us, event | category | flops | bytes accessed | tf_op | source)
XLA Modules:
  0.0 166.7 jit_solution(17970113379889223322)
XLA Ops:
  9.1 10.3 %all_to_all.20 = bf16[4,12,2304]{2,1,0:T(8,128)(2,1)S(1)} all-to-all(bf16[4,12,2304]{2,1,0:T(8,128)(2,1)S(1)} %shard_map.84), channel_id=1, replica_groups=mesh['c'=4,'x'=4,'l'=2,'y'=8,'k'=2] {'x'}, dimensions={0} | all-to-all | bytes 442368 | tf_op jit(solution)/shard_map/all_to_all | solution.py:38
  20.3 1.4 shard_map.85
  21.7 3.7 %all-to-all-start.1 = ((bf16[4,288,576]{2,1,0:T(8,128)(2,1)}), bf16[4,288,576]{2,1,0:T(8,128)(2,1)S(1)}, u32[]{:S(2)}, u32[]{:S(2)}) async-start(bf16[4,288,576]{2,1,0:T(8,128)(2,1)} %shard_map.85), calls=%async_computation.1 | async-start | bytes 2949120 | tf_op jit(solution)/shard_map/all_to_all | solution.py:38
  25.6 10.8 %collective-permute-start = (bf16[4,144,576]{2,1,0:T(8,128)(2,1)S(1)}, bf16[4,144,576]{2,1,0:T(8,128)(2,1)S(1)}, u32[]{:S(2)}, u32[]{:S(2)}) collective-permute-start(bf16[4,144,576]{2,1,0:T(8,128)(2,1)S(1)} %shard_map.86), channel_id=1, source_target_pairs={{0,16},{16,128},{128,144},{144,256},{256,272},{272,384},{384,400},... | collective-permute-start | bytes 1990664 | tf_op jit(solution)/shard_map/ppermute | solution.py:431
  36.4 8.4 %collective-permute-done.weights_ref = bf16[4,144,576]{2,1,0:T(8,128)(2,1)S(1)} collective-permute-done((bf16[4,144,576]{2,1,0:T(8,128)(2,1)S(1)}, bf16[4,144,576]{2,1,0:T(8,128)(2,1)S(1)}, u32[]{:S(2)}, u32[]{:S(2)}) %collective-permute-start) | collective-permute-done | bytes 663584 | tf_op jit(solution)/shard_map/ppermute | solution.py:431
  44.7 1.3 shard_map.87
  46.0 4.2 %all-to-all-start.2 = ((bf16[4,272,576]{2,1,0:T(8,128)(2,1)}), bf16[4,272,576]{2,1,0:T(8,128)(2,1)S(1)}, u32[]{:S(2)}, u32[]{:S(2)}) async-start(bf16[4,272,576]{2,1,0:T(8,128)(2,1)} %shard_map.87), calls=%async_computation.2 | async-start | bytes 2785280 | tf_op jit(solution)/shard_map/all_to_all | solution.py:38
  51.2 7.0 %collective-permute-start.1 = (bf16[4,144,576]{2,1,0:T(8,128)(2,1)}, bf16[4,144,576]{2,1,0:T(8,128)(2,1)}, u32[]{:S(2)}, u32[]{:S(2)}) collective-permute-start(bf16[4,144,576]{2,1,0:T(8,128)(2,1)} %slice.44), channel_id=1, source_target_pairs={{0,16},{16,128},{128,144},{144,256},{256,272},{272,384},{384,400},... | collective-permute-start | bytes 1990664 | tf_op jit(solution)/shard_map/ppermute | solution.py:436
  58.3 6.4 %all-to-all-done.2.raw_ref.early_ref = bf16[4,272,576]{2,1,0:T(8,128)(2,1)S(1)} async-done(((bf16[4,272,576]{2,1,0:T(8,128)(2,1)}), bf16[4,272,576]{2,1,0:T(8,128)(2,1)S(1)}, u32[]{:S(2)}, u32[]{:S(2)}) %all-to-all-start.2) | async-done | bytes 1253408 | tf_op jit(solution)/shard_map/all_to_all | solution.py:38
  66.9 2.3 %all-gather.2.cloned.1.call-done.table_any = bf16[768,2304]{1,0:T(8,128)(2,1)} async-done(((bf16[48,2304]{1,0:T(8,128)(2,1)}), bf16[768,2304]{1,0:T(8,128)(2,1)}) %all-gather.2.cloned.1.call-update) | async-done | bytes 3538960 | tf_op jit(solution)/shard_map/all_gather | solution.py:428
  70.3 2.0 %copy-done.10 = bf16[768,2304]{1,0:T(8,128)(2,1)S(1)} copy-done((bf16[768,2304]{1,0:T(8,128)(2,1)S(1)}, bf16[768,2304]{1,0:T(8,128)(2,1)}, u32[]{:S(2)}) %copy-start.10) | copy-done | bytes 3538968
  72.3 11.6 %shard_map.89 = (bf16[768,288]{1,0:T(8,128)(2,1)S(1)}, bf16[768,576]{1,0:T(8,128)(2,1)S(1)}, bf16[4,96,2304]{2,1,0:T(8,128)(2,1)S(1)}, bf16[4,96,2304]{2,1,0:T(8,128)(2,1)}, bf16[768,2304]{1,0:T(8,128)(2,1)S(1)}) custom-call(s32[4]{0:T(128)S(1)} %pad_add_fusion.place_ref, bf16[768,2304]{1,0:T(8,128)(2,1)S(1)} %copy-done.10, ...), custom_call_target="tpu_custom_call" | custom-call | flops 4076863488 | bytes 9732096 | tf_op jit(solution)/shard_map/pallas_call | solution.py:253
  83.9 1.3 copy-done.2
  85.1 4.0 %collective-permute-start.5 = (bf16[4,96,2304]{2,1,0:T(8,128)(2,1)}, bf16[4,96,2304]{2,1,0:T(8,128)(2,1)}, u32[]{:S(2)}, u32[]{:S(2)}) collective-permute-start(bf16[4,96,2304]{2,1,0:T(8,128)(2,1)} %get-tuple-element.19), channel_id=1, source_target_pairs={{0,1},{1,0},{2,3},{3,2},{4,5},{5,4},{6,7},{7,6},{8,9},{9,8},{10,11... | collective-permute-start | bytes 5308424 | tf_op jit(solution)/shard_map/ppermute | solution.py:442
  89.2 4.4 %shard_map.92 = bf16[2304,576]{1,0:T(8,128)(2,1)} custom-call(bf16[768,2304]{1,0:T(8,128)(2,1)S(1)} %get-tuple-element.20.table_ref, bf16[768,576]{1,0:T(8,128)(2,1)S(1)} %get-tuple-element.21.cots_ref), custom_call_target="tpu_custom_call" | custom-call | flops 2038431744 | bytes 6193152 | tf_op jit(solution)/shard_map/pallas_call | solution.py:303
  93.6 1.4 copy-done.3
  96.1 5.1 %collective-permute-start.6 = (bf16[96,2304]{1,0:T(8,128)(2,1)S(1)}, bf16[96,2304]{1,0:T(8,128)(2,1)S(1)}, u32[]{:S(2)}, u32[]{:S(2)}) collective-permute-start(bf16[96,2304]{1,0:T(8,128)(2,1)S(1)} %fusion.3), channel_id=1, source_target_pairs={{0,2},{2,4},{4,6},{6,8},{8,10},{10,12},{12,14},{14,0},{1,15},{3,1}... | collective-permute-start | bytes 1327112 | tf_op jit(solution)/shard_map/ppermute | solution.py:452
  101.2 5.2 %collective-permute-done.6 = bf16[96,2304]{1,0:T(8,128)(2,1)S(1)} collective-permute-done((bf16[96,2304]{1,0:T(8,128)(2,1)S(1)}, bf16[96,2304]{1,0:T(8,128)(2,1)S(1)}, u32[]{:S(2)}, u32[]{:S(2)}) %collective-permute-start.6) | collective-permute-done | bytes 442400 | tf_op jit(solution)/shard_map/ppermute | solution.py:452
  106.4 1.2 fusion.2
  107.6 5.0 %collective-permute-start.7 = (bf16[96,2304]{1,0:T(8,128)(2,1)S(1)}, bf16[96,2304]{1,0:T(8,128)(2,1)S(1)}, u32[]{:S(2)}, u32[]{:S(2)}) collective-permute-start(bf16[96,2304]{1,0:T(8,128)(2,1)S(1)} %fusion.2), channel_id=1, source_target_pairs={{0,2},{2,4},{4,6},{6,8},{8,10},{10,12},{12,14},{14,0},{1,15},{3,1}... | collective-permute-start | bytes 1327112 | tf_op jit(solution)/shard_map/ppermute | solution.py:452
  112.7 5.2 %collective-permute-done.7 = bf16[96,2304]{1,0:T(8,128)(2,1)S(1)} collective-permute-done((bf16[96,2304]{1,0:T(8,128)(2,1)S(1)}, bf16[96,2304]{1,0:T(8,128)(2,1)S(1)}, u32[]{:S(2)}, u32[]{:S(2)}) %collective-permute-start.7) | collective-permute-done | bytes 442400 | tf_op jit(solution)/shard_map/ppermute | solution.py:452
  117.9 1.2 fusion.1
  119.1 5.4 %collective-permute-start.8 = (bf16[96,2304]{1,0:T(8,128)(2,1)S(1)}, bf16[96,2304]{1,0:T(8,128)(2,1)S(1)}, u32[]{:S(2)}, u32[]{:S(2)}) collective-permute-start(bf16[96,2304]{1,0:T(8,128)(2,1)S(1)} %fusion.1), channel_id=1, source_target_pairs={{0,2},{2,4},{4,6},{6,8},{8,10},{10,12},{12,14},{14,0},{1,15},{3,1}... | collective-permute-start | bytes 1327112 | tf_op jit(solution)/shard_map/ppermute | solution.py:452
  125.0 3.6 %collective-permute-start.2 = (bf16[96,576]{1,0:T(8,128)(2,1)S(1)}, bf16[96,576]{1,0:T(8,128)(2,1)S(1)}, u32[]{:S(2)}, u32[]{:S(2)}) collective-permute-start(bf16[96,576]{1,0:T(8,128)(2,1)S(1)} %get-tuple-element.33), channel_id=1, source_target_pairs={{0,32},{32,64},{64,96},{96,0},{1,33},{33,65},{65,97},{97,1},{2,34}... | collective-permute-start | bytes 331784 | tf_op jit(solution)/shard_map/ppermute | solution.py:325
  128.6 4.3 %collective-permute-start.3 = (bf16[96,576]{1,0:T(8,128)(2,1)S(1)}, bf16[96,576]{1,0:T(8,128)(2,1)S(1)}, u32[]{:S(2)}, u32[]{:S(2)}) collective-permute-start(bf16[96,576]{1,0:T(8,128)(2,1)S(1)} %get-tuple-element.32), channel_id=1, source_target_pairs={{0,64},{32,96},{64,0},{96,32},{1,65},{33,97},{65,1},{97,33},{2,66}... | collective-permute-start | bytes 331784 | tf_op jit(solution)/shard_map/ppermute | solution.py:325
  132.9 3.1 %collective-permute-start.4 = (bf16[96,576]{1,0:T(8,128)(2,1)S(1)}, bf16[96,576]{1,0:T(8,128)(2,1)S(1)}, u32[]{:S(2)}, u32[]{:S(2)}) collective-permute-start(bf16[96,576]{1,0:T(8,128)(2,1)S(1)} %get-tuple-element.31), channel_id=1, source_target_pairs={{0,96},{32,0},{64,32},{96,64},{1,97},{33,1},{65,33},{97,65},{2,98}... | collective-permute-start | bytes 331784 | tf_op jit(solution)/shard_map/ppermute | solution.py:325
  136.0 1.2 fusion.sums_ref
  137.2 1.9 %collective-permute-start.10 = (bf16[48,2304]{1,0:T(8,128)(2,1)S(1)}, bf16[48,2304]{1,0:T(8,128)(2,1)S(1)}, u32[]{:S(2)}, u32[]{:S(2)}) collective-permute-start(bf16[48,2304]{1,0:T(8,128)(2,1)S(1)} %get-tuple-element.34), channel_id=1, source_target_pairs={{1,15},{3,1},{5,3},{7,5},{9,7},{11,9},{13,11},{15,13},{17,31},{19,... | collective-permute-start | bytes 663560 | tf_op jit(solution)/shard_map/ppermute | solution.py:462
  139.2 3.3 %collective-permute-start.9 = (bf16[48,2304]{1,0:T(8,128)(2,1)S(1)}, bf16[48,2304]{1,0:T(8,128)(2,1)S(1)}, u32[]{:S(2)}, u32[]{:S(2)}) collective-permute-start(bf16[48,2304]{1,0:T(8,128)(2,1)S(1)} %get-tuple-element.35), channel_id=1, source_target_pairs={{0,1},{2,3},{4,5},{6,7},{8,9},{10,11},{12,13},{14,15},{1,14},{3,0}... | collective-permute-start | bytes 663560 | tf_op jit(solution)/shard_map/ppermute | solution.py:457
  142.6 1.5 shard_map.91
  144.1 1.2 collective-permute-done.9.near_ref
  147.0 11.8 %all_to_all.21.got_ref = bf16[4,136,576]{2,1,0:T(8,128)(2,1)S(1)} all-to-all(bf16[4,136,576]{2,1,0:T(8,128)(2,1)S(1)} %shard_map.93), channel_id=1, replica_groups=mesh['c'=4,'x'=4,'l'=2,'y'=8,'k'=2] {'x'}, dimensions={0} | all-to-all | bytes 1253376 | tf_op jit(solution)/shard_map/all_to_all | solution.py:38
  (46 shorter events, 11.7 us)
Async XLA Ops:
  7.2 13.1 %copy-start = (bf16[288,1152]{1,0:T(8,128)(2,1)S(1)}, bf16[288,1152]{1,0:T(8,128)(2,1)}, u32[]{:S(2)}) copy-start(bf16[288,1152]{1,0:T(8,128)(2,1)} %gate_ref.3) | copy-start | bytes 1990660
  7.2 13.1 %copy-start.1 = (bf16[288,1152]{1,0:T(8,128)(2,1)S(1)}, bf16[288,1152]{1,0:T(8,128)(2,1)}, u32[]{:S(2)}) copy-start(bf16[288,1152]{1,0:T(8,128)(2,1)} %up_ref.3) | copy-start | bytes 1990660
  7.2 62.0 %all-gather.2.cloned.1.call-start = ((), (), s32[]{:S(2)}) async-start(), calls=%async_computation.5 | async-start | bytes 3760128 | tf_op jit(solution)/shard_map/all_gather | solution.py:428
  8.0 0.9 copy-start.8
  21.7 23.1 %copy-start.6 = (bf16[192,1152]{1,0:T(8,128)(2,1)S(1)}, bf16[192,1152]{1,0:T(8,128)(2,1)}, u32[]{:S(2)}) copy-start(bf16[192,1152]{1,0:T(8,128)(2,1)} %grad_ref.1) | copy-start | bytes 1327108
  21.7 24.3 %all-to-all-start.1 = ((bf16[4,288,576]{2,1,0:T(8,128)(2,1)}), bf16[4,288,576]{2,1,0:T(8,128)(2,1)S(1)}, u32[]{:S(2)}, u32[]{:S(2)}) async-start(bf16[4,288,576]{2,1,0:T(8,128)(2,1)} %shard_map.85), calls=%async_computation.1 | async-start | bytes 2949120 | tf_op jit(solution)/shard_map/all_to_all | solution.py:38
  25.6 19.2 %collective-permute-start = (bf16[4,144,576]{2,1,0:T(8,128)(2,1)S(1)}, bf16[4,144,576]{2,1,0:T(8,128)(2,1)S(1)}, u32[]{:S(2)}, u32[]{:S(2)}) collective-permute-start(bf16[4,144,576]{2,1,0:T(8,128)(2,1)S(1)} %shard_map.86), channel_id=1, source_target_pairs={{0,16},{16,128},{128,144},{144,256},{256,272},{272,384},{384,400},... | collective-permute-start | bytes 1990664 | tf_op jit(solution)/shard_map/ppermute | solution.py:431
  46.0 18.7 %all-to-all-start.2 = ((bf16[4,272,576]{2,1,0:T(8,128)(2,1)}), bf16[4,272,576]{2,1,0:T(8,128)(2,1)S(1)}, u32[]{:S(2)}, u32[]{:S(2)}) async-start(bf16[4,272,576]{2,1,0:T(8,128)(2,1)} %shard_map.87), calls=%async_computation.2 | async-start | bytes 2785280 | tf_op jit(solution)/shard_map/all_to_all | solution.py:38
  50.2 95.1 %reduce-scatter.2.cloned.1.call-start = ((), (), s32[]{:S(2)}) async-start(), calls=%async_computation.6 | async-start | bytes 3317760 | tf_op jit(solution)/shard_map/reduce_scatter | solution.py:445
  51.2 15.7 %collective-permute-start.1 = (bf16[4,144,576]{2,1,0:T(8,128)(2,1)}, bf16[4,144,576]{2,1,0:T(8,128)(2,1)}, u32[]{:S(2)}, u32[]{:S(2)}) collective-permute-start(bf16[4,144,576]{2,1,0:T(8,128)(2,1)} %slice.44), channel_id=1, source_target_pairs={{0,16},{16,128},{128,144},{144,256},{256,272},{272,384},{384,400},... | collective-permute-start | bytes 1990664 | tf_op jit(solution)/shard_map/ppermute | solution.py:436
  65.1 0.8 copy-start.4
  69.2 1.1 copy-start.5
  70.2 2.0 %copy-start.10 = (bf16[768,2304]{1,0:T(8,128)(2,1)S(1)}, bf16[768,2304]{1,0:T(8,128)(2,1)}, u32[]{:S(2)}) copy-start(bf16[768,2304]{1,0:T(8,128)(2,1)} %all-gather.2.cloned.1.call-done.table_any) | copy-start | bytes 10616836
  83.8 1.3 copy-start.2
  85.1 8.4 %collective-permute-start.5 = (bf16[4,96,2304]{2,1,0:T(8,128)(2,1)}, bf16[4,96,2304]{2,1,0:T(8,128)(2,1)}, u32[]{:S(2)}, u32[]{:S(2)}) collective-permute-start(bf16[4,96,2304]{2,1,0:T(8,128)(2,1)} %get-tuple-element.19), channel_id=1, source_target_pairs={{0,1},{1,0},{2,3},{3,2},{4,5},{5,4},{6,7},{7,6},{8,9},{9,8},{10,11... | collective-permute-start | bytes 5308424 | tf_op jit(solution)/shard_map/ppermute | solution.py:442
  93.5 1.5 copy-start.3
  96.1 10.3 %collective-permute-start.6 = (bf16[96,2304]{1,0:T(8,128)(2,1)S(1)}, bf16[96,2304]{1,0:T(8,128)(2,1)S(1)}, u32[]{:S(2)}, u32[]{:S(2)}) collective-permute-start(bf16[96,2304]{1,0:T(8,128)(2,1)S(1)} %fusion.3), channel_id=1, source_target_pairs={{0,2},{2,4},{4,6},{6,8},{8,10},{10,12},{12,14},{14,0},{1,15},{3,1}... | collective-permute-start | bytes 1327112 | tf_op jit(solution)/shard_map/ppermute | solution.py:452
  107.6 10.2 %collective-permute-start.7 = (bf16[96,2304]{1,0:T(8,128)(2,1)S(1)}, bf16[96,2304]{1,0:T(8,128)(2,1)S(1)}, u32[]{:S(2)}, u32[]{:S(2)}) collective-permute-start(bf16[96,2304]{1,0:T(8,128)(2,1)S(1)} %fusion.2), channel_id=1, source_target_pairs={{0,2},{2,4},{4,6},{6,8},{8,10},{10,12},{12,14},{14,0},{1,15},{3,1}... | collective-permute-start | bytes 1327112 | tf_op jit(solution)/shard_map/ppermute | solution.py:452
  119.1 16.9 %collective-permute-start.8 = (bf16[96,2304]{1,0:T(8,128)(2,1)S(1)}, bf16[96,2304]{1,0:T(8,128)(2,1)S(1)}, u32[]{:S(2)}, u32[]{:S(2)}) collective-permute-start(bf16[96,2304]{1,0:T(8,128)(2,1)S(1)} %fusion.1), channel_id=1, source_target_pairs={{0,2},{2,4},{4,6},{6,8},{8,10},{10,12},{12,14},{14,0},{1,15},{3,1}... | collective-permute-start | bytes 1327112 | tf_op jit(solution)/shard_map/ppermute | solution.py:452
  125.0 17.5 %collective-permute-start.2 = (bf16[96,576]{1,0:T(8,128)(2,1)S(1)}, bf16[96,576]{1,0:T(8,128)(2,1)S(1)}, u32[]{:S(2)}, u32[]{:S(2)}) collective-permute-start(bf16[96,576]{1,0:T(8,128)(2,1)S(1)} %get-tuple-element.33), channel_id=1, source_target_pairs={{0,32},{32,64},{64,96},{96,0},{1,33},{33,65},{65,97},{97,1},{2,34}... | collective-permute-start | bytes 331784 | tf_op jit(solution)/shard_map/ppermute | solution.py:325
  128.6 13.9 %collective-permute-start.3 = (bf16[96,576]{1,0:T(8,128)(2,1)S(1)}, bf16[96,576]{1,0:T(8,128)(2,1)S(1)}, u32[]{:S(2)}, u32[]{:S(2)}) collective-permute-start(bf16[96,576]{1,0:T(8,128)(2,1)S(1)} %get-tuple-element.32), channel_id=1, source_target_pairs={{0,64},{32,96},{64,0},{96,32},{1,65},{33,97},{65,1},{97,33},{2,66}... | collective-permute-start | bytes 331784 | tf_op jit(solution)/shard_map/ppermute | solution.py:325
  132.9 9.6 %collective-permute-start.4 = (bf16[96,576]{1,0:T(8,128)(2,1)S(1)}, bf16[96,576]{1,0:T(8,128)(2,1)S(1)}, u32[]{:S(2)}, u32[]{:S(2)}) collective-permute-start(bf16[96,576]{1,0:T(8,128)(2,1)S(1)} %get-tuple-element.31), channel_id=1, source_target_pairs={{0,96},{32,0},{64,32},{96,64},{1,97},{33,1},{65,33},{97,65},{2,98}... | collective-permute-start | bytes 331784 | tf_op jit(solution)/shard_map/ppermute | solution.py:325
  137.2 6.8 %collective-permute-start.10 = (bf16[48,2304]{1,0:T(8,128)(2,1)S(1)}, bf16[48,2304]{1,0:T(8,128)(2,1)S(1)}, u32[]{:S(2)}, u32[]{:S(2)}) collective-permute-start(bf16[48,2304]{1,0:T(8,128)(2,1)S(1)} %get-tuple-element.34), channel_id=1, source_target_pairs={{1,15},{3,1},{5,3},{7,5},{9,7},{11,9},{13,11},{15,13},{17,31},{19,... | collective-permute-start | bytes 663560 | tf_op jit(solution)/shard_map/ppermute | solution.py:462
  139.2 6.2 %collective-permute-start.9 = (bf16[48,2304]{1,0:T(8,128)(2,1)S(1)}, bf16[48,2304]{1,0:T(8,128)(2,1)S(1)}, u32[]{:S(2)}, u32[]{:S(2)}) collective-permute-start(bf16[48,2304]{1,0:T(8,128)(2,1)S(1)} %get-tuple-element.35), channel_id=1, source_target_pairs={{0,1},{2,3},{4,5},{6,7},{8,9},{10,11},{12,13},{14,15},{1,14},{3,0}... | collective-permute-start | bytes 663560 | tf_op jit(solution)/shard_map/ppermute | solution.py:457
  142.6 16.2 %copy-start.9 = (bf16[12,2304]{1,0:T(8,128)(2,1)S(1)}, bf16[12,2304]{1,0:T(8,128)(2,1)}, u32[]{:S(2)}) copy-start(bf16[12,2304]{1,0:T(8,128)(2,1)} %tokens_ref.3) | copy-start | bytes 165892
  145.3 1.0 copy-start.7
Sparse Core Ops, SparseCore 0:
  20.4 48.7 all-gather.1
  93.7 44.1 reduce-scatter.1

commit v7 on v6

--- a/solution.py
+++ b/solution.py
@@ -184,34 +184,26 @@
 
 
 def forward_kernel(
-    chunk, main, tail, place_ref, table_any, own_ref, early_ref, late_ref, grads_ref,
-    found_ref, cots_ref, keep_ref, give_ref, table_ref, theirs, sems,
+    chunk, main, tail, place_ref, table_ref, own_ref, early_ref, late_ref, grads_ref,
+    found_ref, cots_ref, keep_ref, give_ref, matrix,
 ):
     blocks, feats, pair = own_ref.shape
     cut = feats - late_ref.shape[1]
     pool, width = table_ref.shape
     low, core, me = place_ref[0], place_ref[1], place_ref[3]
     chain, step, _ = keep_ref.shape
-    tables = [
-        pltpu.make_async_copy(
-            table_any.at[pl.ds(first, chunk)], table_ref.at[pl.ds(first, chunk)],
-            sems.at[first // chunk],
-        )
-        for first in range(0, pool, chunk)
-    ]
-    for copy in tables:
-        copy.start()
-    near_cols = pl.ds(pl.multiple_of(low * (width // 2), 128), width // 2)
-    far_cols = pl.ds(pl.multiple_of((1 - low) * (width // 2), 128), width // 2)
+    near = low * (width // 2)
+    far = (1 - low) * (width // 2)
     for x in range(blocks):
-        theirs[x * feats : x * feats + cut, :] = early_ref[x, :cut, :]
-        theirs[x * feats + cut : (x + 1) * feats, :] = late_ref[x]
+        for first, size, rows in (
+            (near + x * feats, feats, own_ref[x]),
+            (far + x * feats, cut, early_ref[x, :cut, :]),
+            (far + x * feats + cut, feats - cut, late_ref[x]),
+        ):
+            matrix[pl.ds(pl.multiple_of(first, 16), size), :] = rows
     for first in range(0, pool, chunk):
         rows = slice(first, first + chunk)
-        tables[first // chunk].wait()
-        mine = own_ref[...].reshape(blocks * feats, pair)
-        both = jnp.dot(table_ref[rows, near_cols], mine, preferred_element_type=F32)
-        both = both + jnp.dot(table_ref[rows, far_cols], theirs[...], preferred_element_type=F32)
+        both = jnp.dot(table_ref[rows, :], matrix[...], preferred_element_type=F32)
         grads = grads_ref[rows, :].astype(F32)
         hidden, gate_cot, up_cot = activate(
             both[:, :main], both[:, main : 2 * main], grads[:, :main]
@@ -224,24 +216,23 @@
         found_ref[rows, main:] = hidden
         cots_ref[rows, 2 * main : 2 * main + tail] = gate_cot
         cots_ref[rows, 2 * main + tail :] = up_cot
-        for weights, cols in ((mine, near_cols), (theirs[...], far_cols)):
-            partial = lax.dot_general(
-                cots_ref[rows, :], weights, (((1,), (1,)), ((), ())), preferred_element_type=F32
-            )
-            for j in range(chunk // step):
-                block = partial[j * step : (j + 1) * step].astype(BF16)
-                ahead = lax.rem(first // step + j - me + 2 * chain, 2 * chain)
-                right = ahead < chain
-                slot = jnp.where(right, chain - 1 - ahead, ahead - chain)
-                kept = right == (core == 0)
-
-                @pl.when(kept)
-                def _():
-                    keep_ref[slot, :, cols] = block
-
-                @pl.when(jnp.logical_not(kept))
-                def _():
-                    give_ref[slot, :, cols] = block
+        partial = lax.dot_general(
+            cots_ref[rows, :], matrix[...], (((1,), (1,)), ((), ())), preferred_element_type=F32
+        )
+        for j in range(chunk // step):
+            block = partial[j * step : (j + 1) * step].astype(BF16)
+            ahead = lax.rem(first // step + j - me + 2 * chain, 2 * chain)
+            right = ahead < chain
+            slot = jnp.where(right, chain - 1 - ahead, ahead - chain)
+            kept = right == (core == 0)
+
+            @pl.when(kept)
+            def _():
+                keep_ref[slot] = block
+
+            @pl.when(jnp.logical_not(kept))
+            def _():
+                give_ref[slot] = block
 
 
 def forward(place, table, own, early, late, grads, ny, chunk):
@@ -257,15 +248,11 @@
             jax.ShapeDtypeStruct((pool, pair), BF16),
             jax.ShapeDtypeStruct((ny // 2, step, width), BF16),
             jax.ShapeDtypeStruct((ny // 2, step, width), BF16),
-            jax.ShapeDtypeStruct((pool, width), BF16),
         ),
-        in_specs=[SMEM, ANY, VMEM, VMEM, VMEM, VMEM],
-        out_specs=(VMEM, VMEM, VMEM, VMEM, VMEM),
-        scratch_shapes=[
-            pltpu.VMEM((width // 2, pair), BF16),
-            pltpu.SemaphoreType.DMA((pool // chunk,)),
-        ],
-        compiler_params=params(36),
+        in_specs=[SMEM, VMEM, VMEM, VMEM, VMEM, VMEM],
+        out_specs=(VMEM, VMEM, VMEM, VMEM),
+        scratch_shapes=[pltpu.VMEM((width, pair), BF16)],
+        compiler_params=params(32),
         cost_estimate=pl.CostEstimate(
             flops=4 * pool * width * pair, bytes_accessed=2 * (2 * pool * width + width * pair), transcendentals=0
         ),
@@ -317,15 +304,6 @@
     )(table, cots)
 
 
-def swap_over_x(pieces, nx):
-    me = lax.axis_index("x")
-    got = [lax.dynamic_index_in_dim(pieces, me, 0, keepdims=False)]
-    for shift in range(1, nx):
-        piece = lax.dynamic_index_in_dim(pieces, lax.rem(me + shift, nx), 0, keepdims=False)
-        got.append(lax.ppermute(piece, "x", ring(nx, shift)))
-    return got
-
-
 def row_scale_of(token_vals):
     mean = jnp.mean(token_vals * token_vals, axis=1, keepdims=True)
     return lax.rsqrt(mean + 1e-06).astype(BF16).astype(F32)
@@ -339,7 +317,8 @@
 
 def normalise_kernel(tokens_ref, gain_ref, out_ref):
     token_vals = tokens_ref[...].astype(F32)
-    scaled = (token_vals * gain_ref[...]).astype(BF16).astype(F32)
+    gain = gain_ref[...].reshape(1, tokens_ref.shape[1])
+    scaled = (token_vals * gain).astype(BF16).astype(F32)
     normed = turned(scaled * row_scale_of(token_vals), out_ref.shape[0], 2).astype(BF16)
     for i in range(out_ref.shape[0]):
         out_ref[i] = normed
@@ -381,7 +360,7 @@
     ]
     token_vals = tokens_ref[...].astype(F32)
     scale = row_scale_of(token_vals)
-    gain = gain_ref[...]
+    gain = gain_ref[...].reshape(1, width)
     scaled = (token_vals * gain).astype(BF16).astype(F32)
     inner_grad = jnp.concatenate([f[:, :wide] for f in found] + [f[:, wide:] for f in found], axis=1)
     inner_grad = turned(inner_grad, 2, nx) * scale
@@ -397,17 +376,15 @@
         up_ref[:, start : start + tail] = grad[:, 2 * main + tail :]
 
 
-def spread_kernel(main, tail, place_ref, got_ref, out_ref):
+def spread_kernel(main, tail, got_ref, out_ref):
     nx, half, _ = got_ref.shape
-    me = place_ref[2]
     for q in range(nx):
-        source = lax.rem(me - q + nx, nx)
         start = nx * main + q * tail
         for h in range(2):
             rows = slice(h * half, (h + 1) * half)
-            out_ref[rows, q * main : (q + 1) * main] = got_ref[source, :, h * main : (h + 1) * main]
+            out_ref[rows, q * main : (q + 1) * main] = got_ref[q, :, h * main : (h + 1) * main]
             out_ref[rows, start : start + tail] = got_ref[
-                source, :, 2 * main + h * tail : 2 * main + (h + 1) * tail
+                q, :, 2 * main + h * tail : 2 * main + (h + 1) * tail
             ]
 
 
@@ -422,9 +399,8 @@
         pool = nx * own_tokens
         nz = nc * nl
         place = jnp.stack([lax.axis_index(name) for name in ("l", "k", "x", "y")]).astype(jnp.int32)
-        gain = norm_gain.reshape(1, width)
-
-        near = exchange(normalise(tokens, gain, nx), "x").reshape(nx * rows, width)
+
+        near = exchange(normalise(tokens, norm_gain, nx), "x").reshape(nx * rows, width)
         table = lax.all_gather(near, ("y", "k"), axis=0, tiled=True)
 
         cut = feats // 2
@@ -436,9 +412,7 @@
         late = lax.ppermute(own[:, cut:], ("c", "l", "k"), both_ways(nz))
         grads = sort_grads(early, cut, own_tokens, rows)
 
-        found, cots, keep, give, table = forward(
-            place, table, own, early, late, grads, ny, pool // 2
-        )
+        found, cots, keep, give = forward(place, table, own, early, late, grads, ny, pool)
         taken = lax.ppermute(give, "k", [(0, 1), (1, 0)])
         grad = gradient(table, cots, nx, nl, nc)
         taken, grad = lax.optimization_barrier((taken, grad))
@@ -447,9 +421,12 @@
         def term(i):
             return keep[i].astype(F32) + taken[i].astype(F32)
 
+        hidden = exchange(sort_hidden(found, nx, rows), "x")
         partial = term(0).astype(BF16)
         for i in range(1, ny // 2):
             partial = lax.ppermute(partial, ("y", "k"), both_ways(ny))
+            if i == ny // 2 - 1:
+                partial, hidden = lax.optimization_barrier((partial, hidden))
             partial = (partial.astype(F32) + term(i)).astype(BF16)
         step = partial.shape[0] // 2
         lower, upper = partial[:step], partial[step:]
@@ -463,14 +440,13 @@
             upper, ("y", "k"), [(2 * y + 1, 2 * ((y - 1) % ny) + 1) for y in range(ny)]
         )
 
-        hidden = jnp.stack(swap_over_x(sort_hidden(found, nx, rows), nx))
         hidden = pl.pallas_call(
             functools.partial(spread_kernel, main, tail),
             out_shape=jax.ShapeDtypeStruct((own_tokens, units), BF16),
-            in_specs=[SMEM, VMEM],
+            in_specs=[VMEM],
             out_specs=VMEM,
             compiler_params=params(8),
-        )(place, hidden)
+        )(hidden)
         hidden, near, far = lax.optimization_barrier((hidden, near, far))
         last = pl.pallas_call(
             functools.partial(gather_kernel, nx, rows, wide, thin),
@@ -490,7 +466,7 @@
             in_specs=[VMEM, VMEM, VMEM],
             out_specs=(VMEM, VMEM, VMEM),
             compiler_params=params(16),
-        )(last, tokens, gain)
+        )(last, tokens, norm_gain)
         return (hidden, input_grad, gate_grad, up_grad)
 
     return per_device

time: 169 us -> 170 us (level)
  waiting for transfers between devices: 29.9 us -> 40 us
  starting transfers between devices: 61.4 us -> 53.5 us
    ppermute x3 -> x0, starting transfers between devices: 11 us -> none  [swap_over_x(): got.append(lax.ppermute(piece, 'x', ring(nx, shift)))]
    all_to_all x2 -> x3, waiting for transfers between devices: 6.43 us -> 15.5 us  [exchange(): return lax.all_to_all(value, axis, split_axis=0, concat_axis=0, tiled=True)]
    all_to_all x2 -> x3, starting transfers between devices: 7.89 us -> 12.3 us  [exchange(): return lax.all_to_all(value, axis, split_axis=0, concat_axis=0, tiled=True)]
    ppermute x1, waiting for transfers between devices: 0.01 us -> 1.89 us  [per_device(): lax.ppermute(upper, ('y', 'k'), [(2 * y + 1, 2 * ((y - 1) % ny) + 1) for...]
    unnamed x22 -> x26, local copies, waits for them, and re-layouts: 8.48 us -> 9.3 us
  transfers between devices with their start and end apart: 15 -> 13, of which waited for: 7 -> 9; matrix products, arithmetic and copies ran while one was open for 4% -> 3% of each run, Pallas kernels for 6% -> 6%
where the time goes in v7:
time: 170 us; the launch traced here: 168 us
  starting transfers between devices  53.5 us (31%)
  waiting for transfers between devices  40 us (24%)
  Pallas kernels  22.3 us (13%)
  blocking collectives  21.5 us (13%)
  between operations  14.3 us (8%)
  local copies, waits for them, and re-layouts  11 us (6%)
  other arithmetic  4.91 us (3%)
    all_to_all x2, blocking collectives, exchange(): return lax.all_to_all(value, axis, split_axis=0, concat_axis=0, tiled=True)  21.5 us
    all_to_all x3, waiting for transfers between devices, exchange(): return lax.all_to_all(value, axis, split_axis=0, concat_axis=0, tiled=True)  15.5 us
    ppermute x3, starting transfers between devices, per_device(): partial = lax.ppermute(partial, ('y', 'k'), both_ways(ny))  15.5 us
    all_to_all x3, starting transfers between devices, exchange(): return lax.all_to_all(value, axis, split_axis=0, concat_axis=0, tiled=True)  12.3 us
    ppermute x1, starting transfers between devices, per_device(): lax.ppermute(pack_weights(nx, gate_weight, up_weight, cut), ('c', 'l', 'k...  10.8 us
    pallas_call x1, Pallas kernels, forward(): pl.pallas_call(functools.partial(forward_kernel, chunk, main, part - main...  10.7 us
    ppermute x3, waiting for transfers between devices, per_device(): partial = lax.ppermute(partial, ('y', 'k'), both_ways(ny))  10.5 us
    unnamed x26, local copies, waits for them, and re-layouts  9.3 us
  transfers between devices with their start and end apart: 13, of which 9 were waited for; matrix products, arithmetic and copies ran while one was open for 3% of the time, Pallas kernels for 6%

profile of v7, /device:TPU:1, one launch (start us, length us, event | category | flops | bytes accessed | tf_op | source)
XLA Modules:
  0.0 167.5 jit_solution(11501808388382614706)
XLA Ops:
  9.1 10.3 %all_to_all.25 = bf16[4,12,2304]{2,1,0:T(8,128)(2,1)S(1)} all-to-all(bf16[4,12,2304]{2,1,0:T(8,128)(2,1)S(1)} %shard_map.84), channel_id=1, replica_groups=mesh['c'=4,'x'=4,'l'=2,'y'=8,'k'=2] {'x'}, dimensions={0} | all-to-all | bytes 442368 | tf_op jit(solution)/shard_map/all_to_all | solution.py:38
  20.3 1.4 shard_map.85
  21.7 3.7 %all-to-all-start.1 = ((bf16[4,288,576]{2,1,0:T(8,128)(2,1)}), bf16[4,288,576]{2,1,0:T(8,128)(2,1)S(1)}, u32[]{:S(2)}, u32[]{:S(2)}) async-start(bf16[4,288,576]{2,1,0:T(8,128)(2,1)} %shard_map.85), calls=%async_computation.1 | async-start | bytes 2949120 | tf_op jit(solution)/shard_map/all_to_all | solution.py:38
  25.6 10.8 %collective-permute-start = (bf16[4,144,576]{2,1,0:T(8,128)(2,1)S(1)}, bf16[4,144,576]{2,1,0:T(8,128)(2,1)S(1)}, u32[]{:S(2)}, u32[]{:S(2)}) collective-permute-start(bf16[4,144,576]{2,1,0:T(8,128)(2,1)S(1)} %shard_map.86), channel_id=1, source_target_pairs={{0,16},{16,128},{128,144},{144,256},{256,272},{272,384},{384,400},... | collective-permute-start | bytes 1990664 | tf_op jit(solution)/shard_map/ppermute | solution.py:407
  36.3 8.4 %collective-permute-done.weights_ref = bf16[4,144,576]{2,1,0:T(8,128)(2,1)S(1)} collective-permute-done((bf16[4,144,576]{2,1,0:T(8,128)(2,1)S(1)}, bf16[4,144,576]{2,1,0:T(8,128)(2,1)S(1)}, u32[]{:S(2)}, u32[]{:S(2)}) %collective-permute-start) | collective-permute-done | bytes 663584 | tf_op jit(solution)/shard_map/ppermute | solution.py:407
  44.7 1.3 shard_map.87
  46.0 4.2 %all-to-all-start.2 = ((bf16[4,272,576]{2,1,0:T(8,128)(2,1)}), bf16[4,272,576]{2,1,0:T(8,128)(2,1)S(1)}, u32[]{:S(2)}, u32[]{:S(2)}) async-start(bf16[4,272,576]{2,1,0:T(8,128)(2,1)} %shard_map.87), calls=%async_computation.2 | async-start | bytes 2785280 | tf_op jit(solution)/shard_map/all_to_all | solution.py:38
  51.2 7.0 %collective-permute-start.1 = (bf16[4,144,576]{2,1,0:T(8,128)(2,1)}, bf16[4,144,576]{2,1,0:T(8,128)(2,1)}, u32[]{:S(2)}, u32[]{:S(2)}) collective-permute-start(bf16[4,144,576]{2,1,0:T(8,128)(2,1)} %slice.44), channel_id=1, source_target_pairs={{0,16},{16,128},{128,144},{144,256},{256,272},{272,384},{384,400},... | collective-permute-start | bytes 1990664 | tf_op jit(solution)/shard_map/ppermute | solution.py:412
  58.3 6.4 %all-to-all-done.2.raw_ref.early_ref = bf16[4,272,576]{2,1,0:T(8,128)(2,1)S(1)} async-done(((bf16[4,272,576]{2,1,0:T(8,128)(2,1)}), bf16[4,272,576]{2,1,0:T(8,128)(2,1)S(1)}, u32[]{:S(2)}, u32[]{:S(2)}) %all-to-all-start.2) | async-done | bytes 1253408 | tf_op jit(solution)/shard_map/all_to_all | solution.py:38
  66.9 2.3 %all-gather.2.cloned.1.call-done.table_ref = bf16[768,2304]{1,0:T(8,128)(2,1)} async-done(((bf16[48,2304]{1,0:T(8,128)(2,1)}), bf16[768,2304]{1,0:T(8,128)(2,1)}) %all-gather.2.cloned.1.call-update) | async-done | bytes 3538960 | tf_op jit(solution)/shard_map/all_gather | solution.py:404
  70.2 2.0 %copy-done.12 = bf16[768,2304]{1,0:T(8,128)(2,1)S(1)} copy-done((bf16[768,2304]{1,0:T(8,128)(2,1)S(1)}, bf16[768,2304]{1,0:T(8,128)(2,1)}, u32[]{:S(2)}) %copy-start.12) | copy-done | bytes 3538968
  72.2 10.7 %shard_map.89 = (bf16[768,288]{1,0:T(8,128)(2,1)S(1)}, bf16[768,576]{1,0:T(8,128)(2,1)S(1)}, bf16[4,96,2304]{2,1,0:T(8,128)(2,1)S(1)}, bf16[4,96,2304]{2,1,0:T(8,128)(2,1)}) custom-call(s32[4]{0:T(128)S(1)} %pad_add_fusion.place_ref, bf16[768,2304]{1,0:T(8,128)(2,1)S(1)} %copy-done.12, bf16[4,288,576]{2,1,0:T(8,128)(2,1)S(1)} %all-to-all-done.1.own_ref, ...), custom_call_target="tpu_custom_call" | custom-call | flops 4076863488 | bytes 9732096 | tf_op jit(solution)/shard_map/pallas_call | solution.py:244
  82.9 1.3 copy-done.2
  84.2 4.0 %collective-permute-start.2 = (bf16[4,96,2304]{2,1,0:T(8,128)(2,1)}, bf16[4,96,2304]{2,1,0:T(8,128)(2,1)}, u32[]{:S(2)}, u32[]{:S(2)}) collective-permute-start(bf16[4,96,2304]{2,1,0:T(8,128)(2,1)} %get-tuple-element.19), channel_id=1, source_target_pairs={{0,1},{1,0},{2,3},{3,2},{4,5},{5,4},{6,7},{7,6},{8,9},{9,8},{10,11... | collective-permute-start | bytes 5308424 | tf_op jit(solution)/shard_map/ppermute | solution.py:416
  88.2 4.3 %shard_map.90 = bf16[2304,576]{1,0:T(8,128)(2,1)} custom-call(bf16[768,2304]{1,0:T(8,128)(2,1)S(1)} %copy-done.12, bf16[768,576]{1,0:T(8,128)(2,1)S(1)} %get-tuple-element.20.cots_ref), custom_call_target="tpu_custom_call" | custom-call | flops 2038431744 | bytes 6193152 | tf_op jit(solution)/shard_map/pallas_call | solution.py:290
  92.6 1.4 copy-done.3
  94.0 1.1 fusion.3
  95.2 5.1 %collective-permute-start.3 = (bf16[96,2304]{1,0:T(8,128)(2,1)S(1)}, bf16[96,2304]{1,0:T(8,128)(2,1)S(1)}, u32[]{:S(2)}, u32[]{:S(2)}) collective-permute-start(bf16[96,2304]{1,0:T(8,128)(2,1)S(1)} %fusion.3), channel_id=1, source_target_pairs={{0,2},{2,4},{4,6},{6,8},{8,10},{10,12},{12,14},{14,0},{1,15},{3,1}... | collective-permute-start | bytes 1327112 | tf_op jit(solution)/shard_map/ppermute | solution.py:427
  100.3 5.2 %collective-permute-done.3 = bf16[96,2304]{1,0:T(8,128)(2,1)S(1)} collective-permute-done((bf16[96,2304]{1,0:T(8,128)(2,1)S(1)}, bf16[96,2304]{1,0:T(8,128)(2,1)S(1)}, u32[]{:S(2)}, u32[]{:S(2)}) %collective-permute-start.3) | collective-permute-done | bytes 442400 | tf_op jit(solution)/shard_map/ppermute | solution.py:427
  105.5 1.2 fusion.2
  106.7 5.0 %collective-permute-start.4 = (bf16[96,2304]{1,0:T(8,128)(2,1)S(1)}, bf16[96,2304]{1,0:T(8,128)(2,1)S(1)}, u32[]{:S(2)}, u32[]{:S(2)}) collective-permute-start(bf16[96,2304]{1,0:T(8,128)(2,1)S(1)} %fusion.2), channel_id=1, source_target_pairs={{0,2},{2,4},{4,6},{6,8},{8,10},{10,12},{12,14},{14,0},{1,15},{3,1}... | collective-permute-start | bytes 1327112 | tf_op jit(solution)/shard_map/ppermute | solution.py:427
  111.7 5.2 %collective-permute-done.4 = bf16[96,2304]{1,0:T(8,128)(2,1)S(1)} collective-permute-done((bf16[96,2304]{1,0:T(8,128)(2,1)S(1)}, bf16[96,2304]{1,0:T(8,128)(2,1)S(1)}, u32[]{:S(2)}, u32[]{:S(2)}) %collective-permute-start.4) | collective-permute-done | bytes 442400 | tf_op jit(solution)/shard_map/ppermute | solution.py:427
  116.9 1.2 fusion.1
  118.1 5.4 %collective-permute-start.5 = (bf16[96,2304]{1,0:T(8,128)(2,1)S(1)}, bf16[96,2304]{1,0:T(8,128)(2,1)}, u32[]{:S(2)}, u32[]{:S(2)}) collective-permute-start(bf16[96,2304]{1,0:T(8,128)(2,1)S(1)} %fusion.1), channel_id=1, source_target_pairs={{0,2},{2,4},{4,6},{6,8},{8,10},{10,12},{12,14},{14,0},{1,15},{3,1}... | collective-permute-start | bytes 1327112 | tf_op jit(solution)/shard_map/ppermute | solution.py:427
  123.5 1.2 shard_map.91
  124.8 4.4 %all-to-all-start.3 = ((bf16[4,96,576]{2,1,0:T(8,128)(2,1)}), bf16[4,96,576]{2,1,0:T(8,128)(2,1)S(1)}, u32[]{:S(2)}, u32[]{:S(2)}) async-start(bf16[4,96,576]{2,1,0:T(8,128)(2,1)} %shard_map.91), calls=%async_computation.3 | async-start | bytes 983040 | tf_op jit(solution)/shard_map/all_to_all | solution.py:38
  129.2 9.1 %all-to-all-done.3.got_ref = bf16[4,96,576]{2,1,0:T(8,128)(2,1)S(1)} async-done(((bf16[4,96,576]{2,1,0:T(8,128)(2,1)}), bf16[4,96,576]{2,1,0:T(8,128)(2,1)S(1)}, u32[]{:S(2)}, u32[]{:S(2)}) %all-to-all-start.3) | async-done | bytes 442400 | tf_op jit(solution)/shard_map/all_to_all | solution.py:38
  138.3 1.3 fusion.sums_ref
  139.6 1.9 %collective-permute-start.7 = (bf16[48,2304]{1,0:T(8,128)(2,1)S(1)}, bf16[48,2304]{1,0:T(8,128)(2,1)S(1)}, u32[]{:S(2)}, u32[]{:S(2)}) collective-permute-start(bf16[48,2304]{1,0:T(8,128)(2,1)S(1)} %get-tuple-element.32), channel_id=1, source_target_pairs={{1,15},{3,1},{5,3},{7,5},{9,7},{11,9},{13,11},{15,13},{17,31},{19,... | collective-permute-start | bytes 663560 | tf_op jit(solution)/shard_map/ppermute | solution.py:439
  141.6 1.9 %collective-permute-start.6 = (bf16[48,2304]{1,0:T(8,128)(2,1)S(1)}, bf16[48,2304]{1,0:T(8,128)(2,1)S(1)}, u32[]{:S(2)}, u32[]{:S(2)}) collective-permute-start(bf16[48,2304]{1,0:T(8,128)(2,1)S(1)} %get-tuple-element.33), channel_id=1, source_target_pairs={{0,1},{2,3},{4,5},{6,7},{8,9},{10,11},{12,13},{14,15},{1,14},{3,0}... | collective-permute-start | bytes 663560 | tf_op jit(solution)/shard_map/ppermute | solution.py:434
  144.4 1.9 %collective-permute-done.7.far_ref = bf16[48,2304]{1,0:T(8,128)(2,1)S(1)} collective-permute-done((bf16[48,2304]{1,0:T(8,128)(2,1)S(1)}, bf16[48,2304]{1,0:T(8,128)(2,1)S(1)}, u32[]{:S(2)}, u32[]{:S(2)}) %collective-permute-start.7) | collective-permute-done | bytes 221216 | tf_op jit(solution)/shard_map/ppermute | solution.py:439
  148.5 11.1 %all_to_all.26.got_ref = bf16[4,136,576]{2,1,0:T(8,128)(2,1)S(1)} all-to-all(bf16[4,136,576]{2,1,0:T(8,128)(2,1)S(1)} %shard_map.93), channel_id=1, replica_groups=mesh['c'=4,'x'=4,'l'=2,'y'=8,'k'=2] {'x'}, dimensions={0} | all-to-all | bytes 1253376 | tf_op jit(solution)/shard_map/all_to_all | solution.py:38
  (43 shorter events, 11.3 us)
Async XLA Ops:
  7.2 13.1 %copy-start.1 = (bf16[288,1152]{1,0:T(8,128)(2,1)S(1)}, bf16[288,1152]{1,0:T(8,128)(2,1)}, u32[]{:S(2)}) copy-start(bf16[288,1152]{1,0:T(8,128)(2,1)} %up_ref.3) | copy-start | bytes 1990660
  7.2 13.1 %copy-start = (bf16[288,1152]{1,0:T(8,128)(2,1)S(1)}, bf16[288,1152]{1,0:T(8,128)(2,1)}, u32[]{:S(2)}) copy-start(bf16[288,1152]{1,0:T(8,128)(2,1)} %gate_ref.3) | copy-start | bytes 1990660
  7.2 62.0 %all-gather.2.cloned.1.call-start = ((), (), s32[]{:S(2)}) async-start(), calls=%async_computation.6 | async-start | bytes 3760128 | tf_op jit(solution)/shard_map/all_gather | solution.py:404
  7.2 1.0 copy-start.8
  8.2 0.7 copy-start.10
  21.7 23.1 %copy-start.6 = (bf16[192,1152]{1,0:T(8,128)(2,1)S(1)}, bf16[192,1152]{1,0:T(8,128)(2,1)}, u32[]{:S(2)}) copy-start(bf16[192,1152]{1,0:T(8,128)(2,1)} %grad_ref.1) | copy-start | bytes 1327108
  21.7 24.3 %all-to-all-start.1 = ((bf16[4,288,576]{2,1,0:T(8,128)(2,1)}), bf16[4,288,576]{2,1,0:T(8,128)(2,1)S(1)}, u32[]{:S(2)}, u32[]{:S(2)}) async-start(bf16[4,288,576]{2,1,0:T(8,128)(2,1)} %shard_map.85), calls=%async_computation.1 | async-start | bytes 2949120 | tf_op jit(solution)/shard_map/all_to_all | solution.py:38
  25.6 19.2 %collective-permute-start = (bf16[4,144,576]{2,1,0:T(8,128)(2,1)S(1)}, bf16[4,144,576]{2,1,0:T(8,128)(2,1)S(1)}, u32[]{:S(2)}, u32[]{:S(2)}) collective-permute-start(bf16[4,144,576]{2,1,0:T(8,128)(2,1)S(1)} %shard_map.86), channel_id=1, source_target_pairs={{0,16},{16,128},{128,144},{144,256},{256,272},{272,384},{384,400},... | collective-permute-start | bytes 1990664 | tf_op jit(solution)/shard_map/ppermute | solution.py:407
  46.0 18.7 %all-to-all-start.2 = ((bf16[4,272,576]{2,1,0:T(8,128)(2,1)}), bf16[4,272,576]{2,1,0:T(8,128)(2,1)S(1)}, u32[]{:S(2)}, u32[]{:S(2)}) async-start(bf16[4,272,576]{2,1,0:T(8,128)(2,1)} %shard_map.87), calls=%async_computation.2 | async-start | bytes 2785280 | tf_op jit(solution)/shard_map/all_to_all | solution.py:38
  50.2 96.6 %reduce-scatter.2.cloned.1.call-start = ((), (), s32[]{:S(2)}) async-start(), calls=%async_computation.7 | async-start | bytes 3317760 | tf_op jit(solution)/shard_map/reduce_scatter | solution.py:419
  51.2 15.7 %collective-permute-start.1 = (bf16[4,144,576]{2,1,0:T(8,128)(2,1)}, bf16[4,144,576]{2,1,0:T(8,128)(2,1)}, u32[]{:S(2)}, u32[]{:S(2)}) collective-permute-start(bf16[4,144,576]{2,1,0:T(8,128)(2,1)} %slice.44), channel_id=1, source_target_pairs={{0,16},{16,128},{128,144},{144,256},{256,272},{272,384},{384,400},... | collective-permute-start | bytes 1990664 | tf_op jit(solution)/shard_map/ppermute | solution.py:412
  65.1 0.8 copy-start.4
  69.2 1.1 copy-start.5
  70.2 2.0 %copy-start.12 = (bf16[768,2304]{1,0:T(8,128)(2,1)S(1)}, bf16[768,2304]{1,0:T(8,128)(2,1)}, u32[]{:S(2)}) copy-start(bf16[768,2304]{1,0:T(8,128)(2,1)} %all-gather.2.cloned.1.call-done.table_ref) | copy-start | bytes 10616836
  82.9 1.3 copy-start.2
  84.2 8.4 %collective-permute-start.2 = (bf16[4,96,2304]{2,1,0:T(8,128)(2,1)}, bf16[4,96,2304]{2,1,0:T(8,128)(2,1)}, u32[]{:S(2)}, u32[]{:S(2)}) collective-permute-start(bf16[4,96,2304]{2,1,0:T(8,128)(2,1)} %get-tuple-element.19), channel_id=1, source_target_pairs={{0,1},{1,0},{2,3},{3,2},{4,5},{5,4},{6,7},{7,6},{8,9},{9,8},{10,11... | collective-permute-start | bytes 5308424 | tf_op jit(solution)/shard_map/ppermute | solution.py:416
  92.6 1.5 copy-start.3
  95.2 10.3 %collective-permute-start.3 = (bf16[96,2304]{1,0:T(8,128)(2,1)S(1)}, bf16[96,2304]{1,0:T(8,128)(2,1)S(1)}, u32[]{:S(2)}, u32[]{:S(2)}) collective-permute-start(bf16[96,2304]{1,0:T(8,128)(2,1)S(1)} %fusion.3), channel_id=1, source_target_pairs={{0,2},{2,4},{4,6},{6,8},{8,10},{10,12},{12,14},{14,0},{1,15},{3,1}... | collective-permute-start | bytes 1327112 | tf_op jit(solution)/shard_map/ppermute | solution.py:427
  106.7 10.2 %collective-permute-start.4 = (bf16[96,2304]{1,0:T(8,128)(2,1)S(1)}, bf16[96,2304]{1,0:T(8,128)(2,1)S(1)}, u32[]{:S(2)}, u32[]{:S(2)}) collective-permute-start(bf16[96,2304]{1,0:T(8,128)(2,1)S(1)} %fusion.2), channel_id=1, source_target_pairs={{0,2},{2,4},{4,6},{6,8},{8,10},{10,12},{12,14},{14,0},{1,15},{3,1}... | collective-permute-start | bytes 1327112 | tf_op jit(solution)/shard_map/ppermute | solution.py:427
  118.1 20.2 %collective-permute-start.5 = (bf16[96,2304]{1,0:T(8,128)(2,1)S(1)}, bf16[96,2304]{1,0:T(8,128)(2,1)}, u32[]{:S(2)}, u32[]{:S(2)}) collective-permute-start(bf16[96,2304]{1,0:T(8,128)(2,1)S(1)} %fusion.1), channel_id=1, source_target_pairs={{0,2},{2,4},{4,6},{6,8},{8,10},{10,12},{12,14},{14,0},{1,15},{3,1}... | collective-permute-start | bytes 1327112 | tf_op jit(solution)/shard_map/ppermute | solution.py:427
  124.8 13.5 %all-to-all-start.3 = ((bf16[4,96,576]{2,1,0:T(8,128)(2,1)}), bf16[4,96,576]{2,1,0:T(8,128)(2,1)S(1)}, u32[]{:S(2)}, u32[]{:S(2)}) async-start(bf16[4,96,576]{2,1,0:T(8,128)(2,1)} %shard_map.91), calls=%async_computation.3 | async-start | bytes 983040 | tf_op jit(solution)/shard_map/all_to_all | solution.py:38
  139.6 6.7 %collective-permute-start.7 = (bf16[48,2304]{1,0:T(8,128)(2,1)S(1)}, bf16[48,2304]{1,0:T(8,128)(2,1)S(1)}, u32[]{:S(2)}, u32[]{:S(2)}) collective-permute-start(bf16[48,2304]{1,0:T(8,128)(2,1)S(1)} %get-tuple-element.32), channel_id=1, source_target_pairs={{1,15},{3,1},{5,3},{7,5},{9,7},{11,9},{13,11},{15,13},{17,31},{19,... | collective-permute-start | bytes 663560 | tf_op jit(solution)/shard_map/ppermute | solution.py:439
  141.6 5.2 %collective-permute-start.6 = (bf16[48,2304]{1,0:T(8,128)(2,1)S(1)}, bf16[48,2304]{1,0:T(8,128)(2,1)S(1)}, u32[]{:S(2)}, u32[]{:S(2)}) collective-permute-start(bf16[48,2304]{1,0:T(8,128)(2,1)S(1)} %get-tuple-element.33), channel_id=1, source_target_pairs={{0,1},{2,3},{4,5},{6,7},{8,9},{10,11},{12,13},{14,15},{1,14},{3,0}... | collective-permute-start | bytes 663560 | tf_op jit(solution)/shard_map/ppermute | solution.py:434
  143.5 16.1 %copy-start.9 = (bf16[12,2304]{1,0:T(8,128)(2,1)S(1)}, bf16[12,2304]{1,0:T(8,128)(2,1)}, u32[]{:S(2)}) copy-start(bf16[12,2304]{1,0:T(8,128)(2,1)} %tokens_ref.3) | copy-start | bytes 165892
  143.5 16.1 %copy-start.11 = (f32[2304]{0:T(1024)S(1)}, f32[2304]{0:T(1024)}, u32[]{:S(2)}) copy-start(f32[2304]{0:T(1024)} %gain_ref.3) | copy-start | bytes 27652
  146.8 1.0 copy-start.7
Sparse Core Ops, SparseCore 0:
  20.4 48.7 all-gather.1
  92.7 44.1 reduce-scatter.1

commit v8 on v7

--- a/solution.py
+++ b/solution.py
@@ -191,7 +191,7 @@
     cut = feats - late_ref.shape[1]
     pool, width = table_ref.shape
     low, core, me = place_ref[0], place_ref[1], place_ref[3]
-    chain, step, _ = keep_ref.shape
+    _, chain, step, _ = keep_ref.shape
     near = low * (width // 2)
     far = (1 - low) * (width // 2)
     for x in range(blocks):
@@ -219,20 +219,16 @@
         partial = lax.dot_general(
             cots_ref[rows, :], matrix[...], (((1,), (1,)), ((), ())), preferred_element_type=F32
         )
-        for j in range(chunk // step):
-            block = partial[j * step : (j + 1) * step].astype(BF16)
-            ahead = lax.rem(first // step + j - me + 2 * chain, 2 * chain)
+        for j in range(chunk // (2 * step)):
+            even = partial[2 * j * step : (2 * j + 1) * step]
+            odd = partial[(2 * j + 1) * step : (2 * j + 2) * step]
+            ahead = lax.rem(first // (2 * step) + j - me + 2 * chain, 2 * chain)
             right = ahead < chain
+            side = jnp.where(right, 0, 1)
             slot = jnp.where(right, chain - 1 - ahead, ahead - chain)
-            kept = right == (core == 0)
-
-            @pl.when(kept)
-            def _():
-                keep_ref[slot] = block
-
-            @pl.when(jnp.logical_not(kept))
-            def _():
-                give_ref[slot] = block
+            straight = right == (core == 0)
+            keep_ref[side, slot] = jnp.where(straight, even, odd).astype(BF16)
+            give_ref[side, slot] = jnp.where(straight, odd, even).astype(BF16)
 
 
 def forward(place, table, own, early, late, grads, ny, chunk):
@@ -240,14 +236,14 @@
     _, _, pair = own.shape
     part = pair // 2
     main = part // 128 * 128
-    step = pool // ny
+    step = pool // (2 * ny)
     return pl.pallas_call(
         functools.partial(forward_kernel, chunk, main, part - main),
         out_shape=(
             jax.ShapeDtypeStruct((pool, part), BF16),
             jax.ShapeDtypeStruct((pool, pair), BF16),
-            jax.ShapeDtypeStruct((ny // 2, step, width), BF16),
-            jax.ShapeDtypeStruct((ny // 2, step, width), BF16),
+            jax.ShapeDtypeStruct((2, ny // 2, step, width), BF16),
+            jax.ShapeDtypeStruct((2, ny // 2, step, width), BF16),
         ),
         in_specs=[SMEM, VMEM, VMEM, VMEM, VMEM, VMEM],
         out_specs=(VMEM, VMEM, VMEM, VMEM),
@@ -334,9 +330,8 @@
     )(tokens, gain)
 
 
-def gather_kernel(nx, rows, wide, thin, place_ref, near_ref, far_ref, sums_ref, grad_ref, out_ref):
-    mine = sums_ref[0 : near_ref.shape[0], :].astype(F32)
-    total = near_ref[...].astype(F32) + jnp.where(place_ref[1] == 0, mine, far_ref[...].astype(F32))
+def gather_kernel(nx, rows, wide, thin, right_ref, left_ref, grad_ref, out_ref):
+    total = right_ref[...].astype(F32) + left_ref[...].astype(F32)
     grad = grad_ref[...].astype(F32)
     piece = grad.shape[0] // nx
     pad = jnp.zeros((16 - rows, wide + thin), F32)
@@ -410,6 +405,7 @@
         own = exchange(pack_weights(nx, gate_weight, up_weight, feats), "x")
         early = exchange(pack_grads(nx, early, hidden_grad), "x")
         late = lax.ppermute(own[:, cut:], ("c", "l", "k"), both_ways(nz))
+        table, early = lax.optimization_barrier((table, early))
         grads = sort_grads(early, cut, own_tokens, rows)
 
         found, cots, keep, give = forward(place, table, own, early, late, grads, ny, pool)
@@ -418,26 +414,21 @@
         taken, grad = lax.optimization_barrier((taken, grad))
         grad = lax.psum_scatter(grad, ("c", "l"), scatter_dimension=0, tiled=True)
 
-        def term(i):
-            return keep[i].astype(F32) + taken[i].astype(F32)
+        def term(side, i):
+            return keep[side, i].astype(F32) + taken[side, i].astype(F32)
 
         hidden = exchange(sort_hidden(found, nx, rows), "x")
-        partial = term(0).astype(BF16)
+        right, left = term(0, 0).astype(BF16), term(1, 0).astype(BF16)
         for i in range(1, ny // 2):
-            partial = lax.ppermute(partial, ("y", "k"), both_ways(ny))
+            right = lax.ppermute(right, "y", ring(ny, 1))
+            left = lax.ppermute(left, "y", ring(ny, -1))
             if i == ny // 2 - 1:
-                partial, hidden = lax.optimization_barrier((partial, hidden))
-            partial = (partial.astype(F32) + term(i)).astype(BF16)
-        step = partial.shape[0] // 2
-        lower, upper = partial[:step], partial[step:]
-        core = lax.axis_index("k")
-        near = lax.ppermute(
-            jnp.where(core == 0, upper, lower), ("y", "k"),
-            [(2 * y, 2 * y + 1) for y in range(ny)]
-            + [(2 * y + 1, 2 * ((y - 1) % ny)) for y in range(ny)],
-        )
-        far = lax.ppermute(
-            upper, ("y", "k"), [(2 * y + 1, 2 * ((y - 1) % ny) + 1) for y in range(ny)]
+                right, hidden = lax.optimization_barrier((right, hidden))
+            right = (right.astype(F32) + term(0, i)).astype(BF16)
+            left = (left.astype(F32) + term(1, i)).astype(BF16)
+        left = lax.ppermute(
+            left, ("y", "k"),
+            [(2 * y + k, 2 * ((y - 1) % ny) + 1 - k) for y in range(ny) for k in range(2)],
         )
 
         hidden = pl.pallas_call(
@@ -447,14 +438,14 @@
             out_specs=VMEM,
             compiler_params=params(8),
         )(hidden)
-        hidden, near, far = lax.optimization_barrier((hidden, near, far))
+        hidden, left = lax.optimization_barrier((hidden, left))
         last = pl.pallas_call(
             functools.partial(gather_kernel, nx, rows, wide, thin),
             out_shape=jax.ShapeDtypeStruct((nx, 16 * nx + feats // nc, pair), BF16),
-            in_specs=[SMEM, VMEM, VMEM, VMEM, VMEM],
+            in_specs=[VMEM, VMEM, VMEM],
             out_specs=VMEM,
             compiler_params=params(24),
-        )(place, near, far, partial, grad)
+        )(right, left, grad)
         last = exchange(last, "x")
         input_grad, gate_grad, up_grad = pl.pallas_call(
             functools.partial(finish_kernel, main, tail, wide, thin),

time: 170 us -> 170 us (level); the launches traced: 168 us -> 169 us
  waiting for transfers between devices: 40 us -> 32.2 us
  starting transfers between devices: 53.5 us -> 61.1 us
  blocking collectives: 21.5 us -> 25.5 us
  local copies, waits for them, and re-layouts: 11 us -> 9.12 us
    all_to_all x3, waiting for transfers between devices: 15.5 us -> 6.41 us  [exchange(): return lax.all_to_all(value, axis, split_axis=0, concat_axis=0, tiled=True)]
    ppermute x5 -> x7, starting transfers between devices: 19.4 us -> 27.1 us  [the longest x3 11.6 us: per_device(): left = lax.ppermute(left, 'y', ring(ny, -1))]
    all_to_all x2, blocking collectives: 21.5 us -> 25.5 us  [exchange(): return lax.all_to_all(value, axis, split_axis=0, concat_axis=0, tiled=True)]
    all_gather x1, waiting for transfers between devices: 2.29 us -> 4.48 us  [per_device(): table = lax.all_gather(near, ('y', 'k'), axis=0, tiled=True)]
    unnamed x26 -> x22, local copies, waits for them, and re-layouts: 9.3 us -> 7.43 us
    ppermute x5 -> x7, waiting for transfers between devices: 12.8 us -> 12.8 us  [the longest x3 6.78 us: per_device(): right = lax.ppermute(right, 'y', ring(ny, 1))]
  transfers between devices with their start and end apart: 13 -> 15, of which waited for: 9 -> 8; matrix products, arithmetic and copies ran while one was open for 3% -> 4% of each run, Pallas kernels for 6% -> 6%
where the time goes in v8:
time: 170 us; the launch traced here: 169 us
  starting transfers between devices  61.1 us (36%)
  waiting for transfers between devices  32.2 us (19%)
  blocking collectives  25.5 us (15%)
  Pallas kernels  21.5 us (13%)
  between operations  14.3 us (8%)
  local copies, waits for them, and re-layouts  9.12 us (5%)
  other arithmetic  5.67 us (3%)
    all_to_all x2, blocking collectives, exchange(): return lax.all_to_all(value, axis, split_axis=0, concat_axis=0, tiled=True)  25.5 us
    all_to_all x3, starting transfers between devices, exchange(): return lax.all_to_all(value, axis, split_axis=0, concat_axis=0, tiled=True)  12.4 us
    ppermute x3, starting transfers between devices, per_device(): left = lax.ppermute(left, 'y', ring(ny, -1))  11.6 us
    ppermute x1, starting transfers between devices, per_device(): lax.ppermute(pack_weights(nx, gate_weight, up_weight, cut), ('c', 'l', 'k...  10.8 us
    pallas_call x1, Pallas kernels, forward(): pl.pallas_call(functools.partial(forward_kernel, chunk, main, part - main...  10.4 us
    ppermute x1, waiting for transfers between devices, per_device(): lax.ppermute(pack_weights(nx, gate_weight, up_weight, cut), ('c', 'l', 'k...  8.39 us
    ppermute x1, starting transfers between devices, per_device(): lax.ppermute(left, ('y', 'k'), [(2 * y + k, 2 * ((y - 1) % ny) + 1 - k) f...  8.37 us
    unnamed x22, local copies, waits for them, and re-layouts  7.43 us
  transfers between devices with their start and end apart: 15, of which 8 were waited for; matrix products, arithmetic and copies ran while one was open for 4% of the time, Pallas kernels for 6%

profile of v8, /device:TPU:1, one launch (start us, length us, event | category | flops | bytes accessed | tf_op | source)
XLA Modules:
  0.0 169.2 jit_solution(8189131621202318839)
XLA Ops:
  9.1 10.3 %all_to_all.25 = bf16[4,12,2304]{2,1,0:T(8,128)(2,1)S(1)} all-to-all(bf16[4,12,2304]{2,1,0:T(8,128)(2,1)S(1)} %shard_map.84), channel_id=1, replica_groups=mesh['c'=4,'x'=4,'l'=2,'y'=8,'k'=2] {'x'}, dimensions={0} | all-to-all | bytes 442368 | tf_op jit(solution)/shard_map/all_to_all | solution.py:38
  20.3 1.4 shard_map.87
  21.7 3.7 %all-to-all-start.2 = ((bf16[4,288,576]{2,1,0:T(8,128)(2,1)}), bf16[4,288,576]{2,1,0:T(8,128)(2,1)S(1)}, u32[]{:S(2)}, u32[]{:S(2)}) async-start(bf16[4,288,576]{2,1,0:T(8,128)(2,1)} %shard_map.87), calls=%async_computation.2 | async-start | bytes 2949120 | tf_op jit(solution)/shard_map/all_to_all | solution.py:38
  25.6 10.8 %collective-permute-start = (bf16[4,144,576]{2,1,0:T(8,128)(2,1)S(1)}, bf16[4,144,576]{2,1,0:T(8,128)(2,1)S(1)}, u32[]{:S(2)}, u32[]{:S(2)}) collective-permute-start(bf16[4,144,576]{2,1,0:T(8,128)(2,1)S(1)} %shard_map.85), channel_id=1, source_target_pairs={{0,16},{16,128},{128,144},{144,256},{256,272},{272,384},{384,400},... | collective-permute-start | bytes 1990664 | tf_op jit(solution)/shard_map/ppermute | solution.py:402
  36.4 8.4 %collective-permute-done.weights_ref = bf16[4,144,576]{2,1,0:T(8,128)(2,1)S(1)} collective-permute-done((bf16[4,144,576]{2,1,0:T(8,128)(2,1)S(1)}, bf16[4,144,576]{2,1,0:T(8,128)(2,1)S(1)}, u32[]{:S(2)}, u32[]{:S(2)}) %collective-permute-start) | collective-permute-done | bytes 663584 | tf_op jit(solution)/shard_map/ppermute | solution.py:402
  44.7 1.3 shard_map.86
  46.0 4.2 %all-to-all-start.1 = ((bf16[4,272,576]{2,1,0:T(8,128)(2,1)}), bf16[4,272,576]{2,1,0:T(8,128)(2,1)S(1)}, u32[]{:S(2)}, u32[]{:S(2)}) async-start(bf16[4,272,576]{2,1,0:T(8,128)(2,1)} %shard_map.86), calls=%async_computation.1 | async-start | bytes 2785280 | tf_op jit(solution)/shard_map/all_to_all | solution.py:38
  51.2 7.0 %collective-permute-start.1 = (bf16[4,144,576]{2,1,0:T(8,128)(2,1)}, bf16[4,144,576]{2,1,0:T(8,128)(2,1)}, u32[]{:S(2)}, u32[]{:S(2)}) collective-permute-start(bf16[4,144,576]{2,1,0:T(8,128)(2,1)} %slice.68), channel_id=1, source_target_pairs={{0,16},{16,128},{128,144},{144,256},{256,272},{272,384},{384,400},... | collective-permute-start | bytes 1990664 | tf_op jit(solution)/shard_map/ppermute | solution.py:407
  58.3 6.4 %all-to-all-done.1.raw_ref.early_ref = bf16[4,272,576]{2,1,0:T(8,128)(2,1)S(1)} async-done(((bf16[4,272,576]{2,1,0:T(8,128)(2,1)}), bf16[4,272,576]{2,1,0:T(8,128)(2,1)S(1)}, u32[]{:S(2)}, u32[]{:S(2)}) %all-to-all-start.1) | async-done | bytes 1253408 | tf_op jit(solution)/shard_map/all_to_all | solution.py:38
  64.7 4.5 %all-gather.2.cloned.1.call-done.table_ref = bf16[768,2304]{1,0:T(8,128)(2,1)} async-done(((bf16[48,2304]{1,0:T(8,128)(2,1)}), bf16[768,2304]{1,0:T(8,128)(2,1)}) %all-gather.2.cloned.1.call-update) | async-done | bytes 3538960 | tf_op jit(solution)/shard_map/all_gather | solution.py:399
  69.6 2.0 %copy-done.10 = bf16[768,2304]{1,0:T(8,128)(2,1)S(1)} copy-done((bf16[768,2304]{1,0:T(8,128)(2,1)S(1)}, bf16[768,2304]{1,0:T(8,128)(2,1)}, u32[]{:S(2)}) %copy-start.10) | copy-done | bytes 3538968
  71.6 10.4 %shard_map.89 = (bf16[768,288]{1,0:T(8,128)(2,1)S(1)}, bf16[768,576]{1,0:T(8,128)(2,1)S(1)}, bf16[2,4,48,2304]{3,2,1,0:T(8,128)(2,1)S(1)}, bf16[2,4,48,2304]{3,2,1,0:T(8,128)(2,1)}) custom-call(s32[4]{0:T(128)S(1)} %pad_add_fusion.place_ref, bf16[768,2304]{1,0:T(8,128)(2,1)S(1)} %copy-done.10, bf16[4,288,576]{2,1,0:T(8,128)(2,1)S(1)} %all-to-all-done.2.own_ref, ...), custom_call_target="tpu_custom_call" | custom-call | flops 4076863488 | bytes 9732096 | tf_op jit(solution)/shard_map/pallas_call | solution.py:240
  81.9 1.3 copy-done.2
  83.3 3.7 %collective-permute-start.2 = (bf16[2,4,48,2304]{3,2,1,0:T(8,128)(2,1)}, bf16[2,4,48,2304]{3,2,1,0:T(8,128)(2,1)}, u32[]{:S(2)}, u32[]{:S(2)}) collective-permute-start(bf16[2,4,48,2304]{3,2,1,0:T(8,128)(2,1)} %get-tuple-element.22), channel_id=1, source_target_pairs={{0,1},{1,0},{2,3},{3,2},{4,5},{5,4},{6,7},{7,6},{8,9},{9,8},{10,11... | collective-permute-start | bytes 5308424 | tf_op jit(solution)/shard_map/ppermute | solution.py:412
  86.9 4.3 %shard_map.90 = bf16[2304,576]{1,0:T(8,128)(2,1)} custom-call(bf16[768,2304]{1,0:T(8,128)(2,1)S(1)} %copy-done.10, bf16[768,576]{1,0:T(8,128)(2,1)S(1)} %get-tuple-element.23.cots_ref), custom_call_target="tpu_custom_call" | custom-call | flops 2038431744 | bytes 6193152 | tf_op jit(solution)/shard_map/pallas_call | solution.py:286
  91.3 1.4 copy-done.3
  93.9 5.1 %collective-permute-start.6 = (bf16[48,2304]{1,0:T(8,128)(2,1)S(1)}, bf16[48,2304]{1,0:T(8,128)(2,1)S(1)}, u32[]{:S(2)}, u32[]{:S(2)}) collective-permute-start(bf16[48,2304]{1,0:T(8,128)(2,1)S(1)} %get-tuple-element.40), channel_id=1, source_target_pairs={{0,14},{2,0},{4,2},{6,4},{8,6},{10,8},{12,10},{14,12},{1,15},{3,1}... | collective-permute-start | bytes 663560 | tf_op jit(solution)/shard_map/ppermute | solution.py:424
  99.0 1.9 %collective-permute-start.3 = (bf16[48,2304]{1,0:T(8,128)(2,1)S(1)}, bf16[48,2304]{1,0:T(8,128)(2,1)S(1)}, u32[]{:S(2)}, u32[]{:S(2)}) collective-permute-start(bf16[48,2304]{1,0:T(8,128)(2,1)S(1)} %get-tuple-element.41), channel_id=1, source_target_pairs={{0,2},{2,4},{4,6},{6,8},{8,10},{10,12},{12,14},{14,0},{1,3},{3,5},... | collective-permute-start | bytes 663560 | tf_op jit(solution)/shard_map/ppermute | solution.py:423
  100.9 2.9 %collective-permute-done.6 = bf16[48,2304]{1,0:T(8,128)(2,1)S(1)} collective-permute-done((bf16[48,2304]{1,0:T(8,128)(2,1)S(1)}, bf16[48,2304]{1,0:T(8,128)(2,1)S(1)}, u32[]{:S(2)}, u32[]{:S(2)}) %collective-permute-start.6) | collective-permute-done | bytes 221216 | tf_op jit(solution)/shard_map/ppermute | solution.py:424
  103.8 5.0 %collective-permute-done.3 = bf16[48,2304]{1,0:T(8,128)(2,1)S(1)} collective-permute-done((bf16[48,2304]{1,0:T(8,128)(2,1)S(1)}, bf16[48,2304]{1,0:T(8,128)(2,1)S(1)}, u32[]{:S(2)}, u32[]{:S(2)}) %collective-permute-start.3) | collective-permute-done | bytes 221216 | tf_op jit(solution)/shard_map/ppermute | solution.py:423
  108.8 1.9 %fusion.3 = (bf16[48,2304]{1,0:T(8,128)(2,1)}, bf16[48,2304]{1,0:T(8,128)(2,1)S(1)}) fusion(bf16[48,2304]{1,0:T(8,128)(2,1)S(1)} %collective-permute-done.6, bf16[2,4,48,2304]{3,2,1,0:T(8,128)(2,1)} %collective-permute-done.2, bf16[2,4,48,2304]{3,2,1,0:T(8,128)(2,1)S(1)} %copy-done.3, bf16[48,2304]{1,0:T(8,128)(2,1)S(1)} %collective-permute-done.3), kind=kLoop, calls=%fused_computation.7 | loop fusion | flops 1327104 | bytes 1769472 | tf_op jit(solution)/shard_map/convert_element_type | solution.py:428
  110.7 1.9 %collective-permute-start.7 = (bf16[48,2304]{1,0:T(8,128)(2,1)}, bf16[48,2304]{1,0:T(8,128)(2,1)S(1)}, u32[]{:S(2)}, u32[]{:S(2)}) collective-permute-start(bf16[48,2304]{1,0:T(8,128)(2,1)} %get-tuple-element.38), channel_id=1, source_target_pairs={{0,14},{2,0},{4,2},{6,4},{8,6},{10,8},{12,10},{14,12},{1,15},{3,1}... | collective-permute-start | bytes 663560 | tf_op jit(solution)/shard_map/ppermute | solution.py:424
  112.6 3.4 %collective-permute-start.4 = (bf16[48,2304]{1,0:T(8,128)(2,1)S(1)}, bf16[48,2304]{1,0:T(8,128)(2,1)}, u32[]{:S(2)}, u32[]{:S(2)}) collective-permute-start(bf16[48,2304]{1,0:T(8,128)(2,1)S(1)} %get-tuple-element.39), channel_id=1, source_target_pairs={{0,2},{2,4},{4,6},{6,8},{8,10},{10,12},{12,14},{14,0},{1,3},{3,5},... | collective-permute-start | bytes 663560 | tf_op jit(solution)/shard_map/ppermute | solution.py:423
  117.2 4.5 %all-to-all-start.3 = ((bf16[4,96,576]{2,1,0:T(8,128)(2,1)}), bf16[4,96,576]{2,1,0:T(8,128)(2,1)S(1)}, u32[]{:S(2)}, u32[]{:S(2)}) async-start(bf16[4,96,576]{2,1,0:T(8,128)(2,1)} %shard_map.91), calls=%async_computation.3 | async-start | bytes 983040 | tf_op jit(solution)/shard_map/all_to_all | solution.py:38
  121.8 1.3 fusion.2
  123.1 1.9 %collective-permute-start.5 = (bf16[48,2304]{1,0:T(8,128)(2,1)S(1)}, bf16[48,2304]{1,0:T(8,128)(2,1)S(1)}, u32[]{:S(2)}, u32[]{:S(2)}) collective-permute-start(bf16[48,2304]{1,0:T(8,128)(2,1)S(1)} %get-tuple-element.37), channel_id=1, source_target_pairs={{0,2},{2,4},{4,6},{6,8},{8,10},{10,12},{12,14},{14,0},{1,3},{3,5},... | collective-permute-start | bytes 663560 | tf_op jit(solution)/shard_map/ppermute | solution.py:423
  125.0 4.6 %collective-permute-start.8 = (bf16[48,2304]{1,0:T(8,128)(2,1)S(1)}, bf16[48,2304]{1,0:T(8,128)(2,1)S(1)}, u32[]{:S(2)}, u32[]{:S(2)}) collective-permute-start(bf16[48,2304]{1,0:T(8,128)(2,1)S(1)} %get-tuple-element.36), channel_id=1, source_target_pairs={{0,14},{2,0},{4,2},{6,4},{8,6},{10,8},{12,10},{14,12},{1,15},{3,1}... | collective-permute-start | bytes 663560 | tf_op jit(solution)/shard_map/ppermute | solution.py:424
  129.6 1.8 %collective-permute-done.5 = bf16[48,2304]{1,0:T(8,128)(2,1)S(1)} collective-permute-done((bf16[48,2304]{1,0:T(8,128)(2,1)S(1)}, bf16[48,2304]{1,0:T(8,128)(2,1)S(1)}, u32[]{:S(2)}, u32[]{:S(2)}) %collective-permute-start.5) | collective-permute-done | bytes 221216 | tf_op jit(solution)/shard_map/ppermute | solution.py:423
  132.5 1.2 fusion
  133.7 8.4 %collective-permute-start.9 = (bf16[48,2304]{1,0:T(8,128)(2,1)S(1)}, bf16[48,2304]{1,0:T(8,128)(2,1)S(1)}, u32[]{:S(2)}, u32[]{:S(2)}) collective-permute-start(bf16[48,2304]{1,0:T(8,128)(2,1)S(1)} %get-tuple-element.35), channel_id=1, source_target_pairs={{0,15},{1,14},{2,1},{3,0},{4,3},{5,2},{6,5},{7,4},{8,7},{9,6},{10,... | collective-permute-start | bytes 663560 | tf_op jit(solution)/shard_map/ppermute | solution.py:429
  143.0 2.1 %collective-permute-done.9.left_ref = bf16[48,2304]{1,0:T(8,128)(2,1)S(1)} collective-permute-done((bf16[48,2304]{1,0:T(8,128)(2,1)S(1)}, bf16[48,2304]{1,0:T(8,128)(2,1)S(1)}, u32[]{:S(2)}, u32[]{:S(2)}) %collective-permute-start.9) | collective-permute-done | bytes 221216 | tf_op jit(solution)/shard_map/ppermute | solution.py:429
  146.2 15.1 %all_to_all.26.got_ref = bf16[4,136,576]{2,1,0:T(8,128)(2,1)S(1)} all-to-all(bf16[4,136,576]{2,1,0:T(8,128)(2,1)S(1)} %shard_map.93), channel_id=1, replica_groups=mesh['c'=4,'x'=4,'l'=2,'y'=8,'k'=2] {'x'}, dimensions={0} | all-to-all | bytes 1253376 | tf_op jit(solution)/shard_map/all_to_all | solution.py:38
  (42 shorter events, 10.8 us)
Async XLA Ops:
  7.2 13.1 %copy-start.1 = (bf16[288,1152]{1,0:T(8,128)(2,1)S(1)}, bf16[288,1152]{1,0:T(8,128)(2,1)}, u32[]{:S(2)}) copy-start(bf16[288,1152]{1,0:T(8,128)(2,1)} %up_ref.3) | copy-start | bytes 1990660
  7.2 13.1 %copy-start = (bf16[288,1152]{1,0:T(8,128)(2,1)S(1)}, bf16[288,1152]{1,0:T(8,128)(2,1)}, u32[]{:S(2)}) copy-start(bf16[288,1152]{1,0:T(8,128)(2,1)} %gate_ref.3) | copy-start | bytes 1990660
  7.2 62.0 %all-gather.2.cloned.1.call-start = ((), (), s32[]{:S(2)}) async-start(), calls=%async_computation.6 | async-start | bytes 3760128 | tf_op jit(solution)/shard_map/all_gather | solution.py:399
  7.2 1.0 copy-start.6
  8.2 0.7 copy-start.8
  21.7 23.1 %copy-start.4 = (bf16[192,1152]{1,0:T(8,128)(2,1)S(1)}, bf16[192,1152]{1,0:T(8,128)(2,1)}, u32[]{:S(2)}) copy-start(bf16[192,1152]{1,0:T(8,128)(2,1)} %grad_ref.1) | copy-start | bytes 1327108
  21.7 24.3 %all-to-all-start.2 = ((bf16[4,288,576]{2,1,0:T(8,128)(2,1)}), bf16[4,288,576]{2,1,0:T(8,128)(2,1)S(1)}, u32[]{:S(2)}, u32[]{:S(2)}) async-start(bf16[4,288,576]{2,1,0:T(8,128)(2,1)} %shard_map.87), calls=%async_computation.2 | async-start | bytes 2949120 | tf_op jit(solution)/shard_map/all_to_all | solution.py:38
  25.6 19.2 %collective-permute-start = (bf16[4,144,576]{2,1,0:T(8,128)(2,1)S(1)}, bf16[4,144,576]{2,1,0:T(8,128)(2,1)S(1)}, u32[]{:S(2)}, u32[]{:S(2)}) collective-permute-start(bf16[4,144,576]{2,1,0:T(8,128)(2,1)S(1)} %shard_map.85), channel_id=1, source_target_pairs={{0,16},{16,128},{128,144},{144,256},{256,272},{272,384},{384,400},... | collective-permute-start | bytes 1990664 | tf_op jit(solution)/shard_map/ppermute | solution.py:402
  46.0 18.7 %all-to-all-start.1 = ((bf16[4,272,576]{2,1,0:T(8,128)(2,1)}), bf16[4,272,576]{2,1,0:T(8,128)(2,1)S(1)}, u32[]{:S(2)}, u32[]{:S(2)}) async-start(bf16[4,272,576]{2,1,0:T(8,128)(2,1)} %shard_map.86), calls=%async_computation.1 | async-start | bytes 2785280 | tf_op jit(solution)/shard_map/all_to_all | solution.py:38
  50.2 94.9 %reduce-scatter.2.cloned.1.call-start = ((), (), s32[]{:S(2)}) async-start(), calls=%async_computation.7 | async-start | bytes 3317760 | tf_op jit(solution)/shard_map/reduce_scatter | solution.py:415
  51.2 18.4 %collective-permute-start.1 = (bf16[4,144,576]{2,1,0:T(8,128)(2,1)}, bf16[4,144,576]{2,1,0:T(8,128)(2,1)}, u32[]{:S(2)}, u32[]{:S(2)}) collective-permute-start(bf16[4,144,576]{2,1,0:T(8,128)(2,1)} %slice.68), channel_id=1, source_target_pairs={{0,16},{16,128},{128,144},{144,256},{256,272},{272,384},{384,400},... | collective-permute-start | bytes 1990664 | tf_op jit(solution)/shard_map/ppermute | solution.py:407
  69.6 2.0 %copy-start.10 = (bf16[768,2304]{1,0:T(8,128)(2,1)S(1)}, bf16[768,2304]{1,0:T(8,128)(2,1)}, u32[]{:S(2)}) copy-start(bf16[768,2304]{1,0:T(8,128)(2,1)} %all-gather.2.cloned.1.call-done.table_ref) | copy-start | bytes 10616836
  81.9 1.3 copy-start.2
  83.3 8.0 %collective-permute-start.2 = (bf16[2,4,48,2304]{3,2,1,0:T(8,128)(2,1)}, bf16[2,4,48,2304]{3,2,1,0:T(8,128)(2,1)}, u32[]{:S(2)}, u32[]{:S(2)}) collective-permute-start(bf16[2,4,48,2304]{3,2,1,0:T(8,128)(2,1)} %get-tuple-element.22), channel_id=1, source_target_pairs={{0,1},{1,0},{2,3},{3,2},{4,5},{5,4},{6,7},{7,6},{8,9},{9,8},{10,11... | collective-permute-start | bytes 5308424 | tf_op jit(solution)/shard_map/ppermute | solution.py:412
  91.3 1.5 copy-start.3
  93.9 9.9 %collective-permute-start.6 = (bf16[48,2304]{1,0:T(8,128)(2,1)S(1)}, bf16[48,2304]{1,0:T(8,128)(2,1)S(1)}, u32[]{:S(2)}, u32[]{:S(2)}) collective-permute-start(bf16[48,2304]{1,0:T(8,128)(2,1)S(1)} %get-tuple-element.40), channel_id=1, source_target_pairs={{0,14},{2,0},{4,2},{6,4},{8,6},{10,8},{12,10},{14,12},{1,15},{3,1}... | collective-permute-start | bytes 663560 | tf_op jit(solution)/shard_map/ppermute | solution.py:424
  99.0 9.8 %collective-permute-start.3 = (bf16[48,2304]{1,0:T(8,128)(2,1)S(1)}, bf16[48,2304]{1,0:T(8,128)(2,1)S(1)}, u32[]{:S(2)}, u32[]{:S(2)}) collective-permute-start(bf16[48,2304]{1,0:T(8,128)(2,1)S(1)} %get-tuple-element.41), channel_id=1, source_target_pairs={{0,2},{2,4},{4,6},{6,8},{8,10},{10,12},{12,14},{14,0},{1,3},{3,5},... | collective-permute-start | bytes 663560 | tf_op jit(solution)/shard_map/ppermute | solution.py:423
  110.7 11.1 %collective-permute-start.7 = (bf16[48,2304]{1,0:T(8,128)(2,1)}, bf16[48,2304]{1,0:T(8,128)(2,1)S(1)}, u32[]{:S(2)}, u32[]{:S(2)}) collective-permute-start(bf16[48,2304]{1,0:T(8,128)(2,1)} %get-tuple-element.38), channel_id=1, source_target_pairs={{0,14},{2,0},{4,2},{6,4},{8,6},{10,8},{12,10},{14,12},{1,15},{3,1}... | collective-permute-start | bytes 663560 | tf_op jit(solution)/shard_map/ppermute | solution.py:424
  112.6 9.2 %collective-permute-start.4 = (bf16[48,2304]{1,0:T(8,128)(2,1)S(1)}, bf16[48,2304]{1,0:T(8,128)(2,1)}, u32[]{:S(2)}, u32[]{:S(2)}) collective-permute-start(bf16[48,2304]{1,0:T(8,128)(2,1)S(1)} %get-tuple-element.39), channel_id=1, source_target_pairs={{0,2},{2,4},{4,6},{6,8},{8,10},{10,12},{12,14},{14,0},{1,3},{3,5},... | collective-permute-start | bytes 663560 | tf_op jit(solution)/shard_map/ppermute | solution.py:423
  117.2 12.4 %all-to-all-start.3 = ((bf16[4,96,576]{2,1,0:T(8,128)(2,1)}), bf16[4,96,576]{2,1,0:T(8,128)(2,1)S(1)}, u32[]{:S(2)}, u32[]{:S(2)}) async-start(bf16[4,96,576]{2,1,0:T(8,128)(2,1)} %shard_map.91), calls=%async_computation.3 | async-start | bytes 983040 | tf_op jit(solution)/shard_map/all_to_all | solution.py:38
  123.1 8.3 %collective-permute-start.5 = (bf16[48,2304]{1,0:T(8,128)(2,1)S(1)}, bf16[48,2304]{1,0:T(8,128)(2,1)S(1)}, u32[]{:S(2)}, u32[]{:S(2)}) collective-permute-start(bf16[48,2304]{1,0:T(8,128)(2,1)S(1)} %get-tuple-element.37), channel_id=1, source_target_pairs={{0,2},{2,4},{4,6},{6,8},{8,10},{10,12},{12,14},{14,0},{1,3},{3,5},... | collective-permute-start | bytes 663560 | tf_op jit(solution)/shard_map/ppermute | solution.py:423
  125.0 7.4 %collective-permute-start.8 = (bf16[48,2304]{1,0:T(8,128)(2,1)S(1)}, bf16[48,2304]{1,0:T(8,128)(2,1)S(1)}, u32[]{:S(2)}, u32[]{:S(2)}) collective-permute-start(bf16[48,2304]{1,0:T(8,128)(2,1)S(1)} %get-tuple-element.36), channel_id=1, source_target_pairs={{0,14},{2,0},{4,2},{6,4},{8,6},{10,8},{12,10},{14,12},{1,15},{3,1}... | collective-permute-start | bytes 663560 | tf_op jit(solution)/shard_map/ppermute | solution.py:424
  133.7 27.6 %copy-start.7 = (bf16[12,2304]{1,0:T(8,128)(2,1)S(1)}, bf16[12,2304]{1,0:T(8,128)(2,1)}, u32[]{:S(2)}) copy-start(bf16[12,2304]{1,0:T(8,128)(2,1)} %tokens_ref.3) | copy-start | bytes 165892
  133.7 27.6 %copy-start.9 = (f32[2304]{0:T(1024)S(1)}, f32[2304]{0:T(1024)}, u32[]{:S(2)}) copy-start(f32[2304]{0:T(1024)} %gain_ref.3) | copy-start | bytes 27652
  133.7 11.4 %collective-permute-start.9 = (bf16[48,2304]{1,0:T(8,128)(2,1)S(1)}, bf16[48,2304]{1,0:T(8,128)(2,1)S(1)}, u32[]{:S(2)}, u32[]{:S(2)}) collective-permute-start(bf16[48,2304]{1,0:T(8,128)(2,1)S(1)} %get-tuple-element.35), channel_id=1, source_target_pairs={{0,15},{1,14},{2,1},{3,0},{4,3},{5,2},{6,5},{7,4},{8,7},{9,6},{10,... | collective-permute-start | bytes 663560 | tf_op jit(solution)/shard_map/ppermute | solution.py:429
  145.1 1.0 copy-start.5
Sparse Core Ops, SparseCore 0:
  20.4 48.7 all-gather.1
  91.4 43.9 reduce-scatter.1

commit v9 on v8

--- a/solution.py
+++ b/solution.py
@@ -48,52 +48,56 @@
     return main, part - main
 
 
-def put_pair(out_ref, q, rows, a, b, main, tail, parts):
-    out_ref[q, rows, 0:main] = a[:, q * main : (q + 1) * main]
-    out_ref[q, rows, main : 2 * main] = b[:, q * main : (q + 1) * main]
+def put_pair(out_ref, at, rows, a, b, main, tail, parts, q):
+    out_ref[at, rows, 0:main] = a[:, q * main : (q + 1) * main]
+    out_ref[at, rows, main : 2 * main] = b[:, q * main : (q + 1) * main]
     start = parts * main + q * tail
-    out_ref[q, rows, 2 * main : 2 * main + tail] = a[:, start : start + tail]
-    out_ref[q, rows, 2 * main + tail : 2 * (main + tail)] = b[:, start : start + tail]
-
-
-def pack_weights_kernel(main, tail, parts, gate_ref, up_ref, out_ref):
-    rows = slice(0, out_ref.shape[1])
+    out_ref[at, rows, 2 * main : 2 * main + tail] = a[:, start : start + tail]
+    out_ref[at, rows, 2 * main + tail : 2 * (main + tail)] = b[:, start : start + tail]
+
+
+def pack_weights_kernel(main, tail, parts, gate_ref, up_ref, *out_refs):
+    held, count, _ = out_refs[0].shape
+    rows = slice(0, count)
     for q in range(parts):
-        put_pair(out_ref, q, rows, gate_ref.at[rows], up_ref.at[rows], main, tail, parts)
-
-
-def pack_weights(parts, gate, up, rows):
+        put_pair(
+            out_refs[q // held], q % held, rows, gate_ref.at[rows], up_ref.at[rows], main, tail, parts, q
+        )
+
+
+def pack_weights(parts, gate, up, rows, pieces):
     main, tail = share_sizes(gate.shape[1], parts)
     return pl.pallas_call(
         functools.partial(pack_weights_kernel, main, tail, parts),
-        out_shape=jax.ShapeDtypeStruct((parts, rows, 2 * (main + tail)), BF16),
+        out_shape=(jax.ShapeDtypeStruct((parts // pieces, rows, 2 * (main + tail)), BF16),) * pieces,
         in_specs=[VMEM, VMEM],
-        out_specs=VMEM,
+        out_specs=(VMEM,) * pieces,
         compiler_params=params(16),
     )(gate, up)
 
 
-def pack_grads_kernel(main, tail, parts, weights_ref, grad_ref, out_ref):
-    cut = weights_ref.shape[1]
+def pack_grads_kernel(main, tail, parts, lower_ref, upper_ref, grad_ref, out_ref):
+    held, cut, _ = lower_ref.shape
     half = grad_ref.shape[0] // 2
-    out_ref[:, 0:cut, :] = weights_ref[...]
+    out_ref[:held, 0:cut, :] = lower_ref[...]
+    out_ref[held:, 0:cut, :] = upper_ref[...]
     for q in range(parts):
         put_pair(
             out_ref, q, slice(cut, cut + half),
-            grad_ref.at[0:half], grad_ref.at[half : 2 * half], main, tail, parts,
-        )
-
-
-def pack_grads(parts, weights, grads):
+            grad_ref.at[0:half], grad_ref.at[half : 2 * half], main, tail, parts, q,
+        )
+
+
+def pack_grads(parts, lower, upper, grads):
     main, tail = share_sizes(grads.shape[1], parts)
-    rows = weights.shape[1] + grads.shape[0] // 2 + 32
+    rows = lower.shape[1] + grads.shape[0] // 2 + 32
     return pl.pallas_call(
         functools.partial(pack_grads_kernel, main, tail, parts),
         out_shape=jax.ShapeDtypeStruct((parts, rows, 2 * (main + tail)), BF16),
-        in_specs=[VMEM, VMEM],
+        in_specs=[VMEM, VMEM, VMEM],
         out_specs=VMEM,
         compiler_params=params(16),
-    )(weights, grads)
+    )(lower, upper, grads)
 
 
 def activate(gate, upward, cotangent):
@@ -188,7 +192,8 @@
     found_ref, cots_ref, keep_ref, give_ref, matrix,
 ):
     blocks, feats, pair = own_ref.shape
-    cut = feats - late_ref.shape[1]
+    late = late_ref.shape[1]
+    cut = feats - late
     pool, width = table_ref.shape
     low, core, me = place_ref[0], place_ref[1], place_ref[3]
     _, chain, step, _ = keep_ref.shape
@@ -198,7 +203,7 @@
         for first, size, rows in (
             (near + x * feats, feats, own_ref[x]),
             (far + x * feats, cut, early_ref[x, :cut, :]),
-            (far + x * feats + cut, feats - cut, late_ref[x]),
+            (far + x * feats + cut, late, late_ref[x]),
         ):
             matrix[pl.ds(pl.multiple_of(first, 16), size), :] = rows
     for first in range(0, pool, chunk):
@@ -245,7 +250,7 @@
             jax.ShapeDtypeStruct((2, ny // 2, step, width), BF16),
             jax.ShapeDtypeStruct((2, ny // 2, step, width), BF16),
         ),
-        in_specs=[SMEM, VMEM, VMEM, VMEM, VMEM, VMEM],
+        in_specs=[SMEM] + [VMEM] * 5,
         out_specs=(VMEM, VMEM, VMEM, VMEM),
         scratch_shapes=[pltpu.VMEM((width, pair), BF16)],
         compiler_params=params(32),
@@ -293,7 +298,7 @@
             pltpu.VMEM((nl * nc, width // (nl * nc), pair), BF16),
             pltpu.SemaphoreType.DMA((nl * nc,)),
         ],
-        compiler_params=params(32),
+        compiler_params=params(52),
         cost_estimate=pl.CostEstimate(
             flops=2 * pool * width * pair, bytes_accessed=2 * (pool * width + width * pair), transcendentals=0
         ),
@@ -330,29 +335,50 @@
     )(tokens, gain)
 
 
+def add_terms_kernel(i, keep_ref, taken_ref, *refs):
+    sums, outs = refs[:-2], refs[-2:]
+    for side, out_ref in enumerate(outs):
+        total = keep_ref[side, i].astype(F32) + taken_ref[side, i].astype(F32)
+        if sums:
+            total = total + sums[side][...].astype(F32)
+        out_ref[...] = total.astype(BF16)
+
+
+def add_terms(keep, taken, i, *sums):
+    block = jax.ShapeDtypeStruct(keep.shape[2:], BF16)
+    return pl.pallas_call(
+        functools.partial(add_terms_kernel, i),
+        out_shape=(block, block),
+        in_specs=[VMEM] * (2 + len(sums)),
+        out_specs=(VMEM, VMEM),
+        compiler_params=params(12),
+    )(keep, taken, *sums)
+
+
 def gather_kernel(nx, rows, wide, thin, right_ref, left_ref, grad_ref, out_ref):
     total = right_ref[...].astype(F32) + left_ref[...].astype(F32)
     grad = grad_ref[...].astype(F32)
     piece = grad.shape[0] // nx
-    pad = jnp.zeros((16 - rows, wide + thin), F32)
     for x in range(nx):
         mine = total[x * rows : (x + 1) * rows]
+        found = []
         for j in range(nx):
             start = nx * wide + j * thin
-            both = jnp.concatenate(
-                [mine[:, j * wide : (j + 1) * wide], mine[:, start : start + thin]], axis=1
+            found.append(
+                jnp.concatenate(
+                    [mine[:, j * wide : (j + 1) * wide], mine[:, start : start + thin]], axis=1
+                )
             )
-            out_ref[x, 16 * j : 16 * j + 16, :] = jnp.concatenate([both, pad], axis=0).astype(BF16)
-        out_ref[x, 16 * nx :, :] = grad[x * piece : (x + 1) * piece].astype(BF16)
+        out_ref[x, : nx * rows, : wide + thin] = jnp.concatenate(found, axis=0).astype(BF16)
+        out_ref[x, nx * rows :, : grad.shape[1]] = grad[x * piece : (x + 1) * piece].astype(BF16)
 
 
 def finish_kernel(main, tail, wide, thin, got_ref, tokens_ref, gain_ref, input_ref, gate_ref, up_ref):
     nx = got_ref.shape[0]
     rows, width = tokens_ref.shape
-    found = [
-        sum(got_ref[x, 16 * j : 16 * j + 16, :].astype(F32) for x in range(nx))[:rows]
-        for j in range(nx)
-    ]
+    pair = 2 * (main + tail)
+    total = sum(got_ref[x, : nx * rows, : wide + thin].astype(F32) for x in range(nx))
+    found = [total[j * rows : (j + 1) * rows] for j in range(nx)]
     token_vals = tokens_ref[...].astype(F32)
     scale = row_scale_of(token_vals)
     gain = gain_ref[...].reshape(1, width)
@@ -363,7 +389,7 @@
     factor = scale * scale / width
     input_ref[...] = (gain * inner_grad - factor * token_vals * inner).astype(BF16)
     for q in range(nx):
-        grad = got_ref[q, 16 * nx :, :].astype(F32)
+        grad = got_ref[q, nx * rows :, :pair].astype(F32)
         start = nx * main + q * tail
         gate_ref[:, q * main : (q + 1) * main] = grad[:, :main]
         gate_ref[:, start : start + tail] = grad[:, 2 * main : 2 * main + tail]
@@ -398,34 +424,34 @@
         near = exchange(normalise(tokens, norm_gain, nx), "x").reshape(nx * rows, width)
         table = lax.all_gather(near, ("y", "k"), axis=0, tiled=True)
 
-        cut = feats // 2
-        early = lax.ppermute(
-            pack_weights(nx, gate_weight, up_weight, cut), ("c", "l", "k"), both_ways(nz)
-        )
-        own = exchange(pack_weights(nx, gate_weight, up_weight, feats), "x")
-        early = exchange(pack_grads(nx, early, hidden_grad), "x")
+        def from_other(lower, upper):
+            lower = lax.ppermute(lower, ("c", "l"), ring(nz, 1))
+            return lower, lax.ppermute(upper, ("c", "l"), ring(nz, -1))
+
+        cut, held = feats // 2, nx // 2
+        lower, upper = from_other(*pack_weights(nx, gate_weight, up_weight, cut, 2))
+        own = exchange(pack_weights(nx, gate_weight, up_weight, feats, 1)[0], "x")
+        early = exchange(pack_grads(nx, lower, upper, hidden_grad), "x")
         late = lax.ppermute(own[:, cut:], ("c", "l", "k"), both_ways(nz))
         table, early = lax.optimization_barrier((table, early))
         grads = sort_grads(early, cut, own_tokens, rows)
 
-        found, cots, keep, give = forward(place, table, own, early, late, grads, ny, pool)
+        found, cots, keep, give = forward(
+            place, table, own, early, late, grads, ny, pool
+        )
         taken = lax.ppermute(give, "k", [(0, 1), (1, 0)])
         grad = gradient(table, cots, nx, nl, nc)
         taken, grad = lax.optimization_barrier((taken, grad))
         grad = lax.psum_scatter(grad, ("c", "l"), scatter_dimension=0, tiled=True)
 
-        def term(side, i):
-            return keep[side, i].astype(F32) + taken[side, i].astype(F32)
-
         hidden = exchange(sort_hidden(found, nx, rows), "x")
-        right, left = term(0, 0).astype(BF16), term(1, 0).astype(BF16)
+        right, left = add_terms(keep, taken, 0)
         for i in range(1, ny // 2):
             right = lax.ppermute(right, "y", ring(ny, 1))
             left = lax.ppermute(left, "y", ring(ny, -1))
             if i == ny // 2 - 1:
                 right, hidden = lax.optimization_barrier((right, hidden))
-            right = (right.astype(F32) + term(0, i)).astype(BF16)
-            left = (left.astype(F32) + term(1, i)).astype(BF16)
+            right, left = add_terms(keep, taken, i, right, left)
         left = lax.ppermute(
             left, ("y", "k"),
             [(2 * y + k, 2 * ((y - 1) % ny) + 1 - k) for y in range(ny) for k in range(2)],
@@ -441,7 +467,7 @@
         hidden, left = lax.optimization_barrier((hidden, left))
         last = pl.pallas_call(
             functools.partial(gather_kernel, nx, rows, wide, thin),
-            out_shape=jax.ShapeDtypeStruct((nx, 16 * nx + feats // nc, pair), BF16),
+            out_shape=jax.ShapeDtypeStruct((nx, nx * rows + feats // nc, -(-pair // 128) * 128), BF16),
             in_specs=[VMEM, VMEM, VMEM],
             out_specs=VMEM,
             compiler_params=params(24),

time: 170 us -> 171 us (level)
  Pallas kernels: 21.5 us -> 27.8 us
  other arithmetic: 5.67 us -> 0.08 us
  waiting for transfers between devices: 32.2 us -> 29.5 us
  starting transfers between devices: 61.1 us -> 63.1 us
    convert_element_type x4 -> x0, other arithmetic: 5.59 us -> none  [the longest x2 3.2 us: per_device(): left = (left.astype(F32) + term(1, i)).astype(BF16)]
    pallas_call x0 -> x4, Pallas kernels: none -> 4.08 us  [add_terms(): pl.pallas_call(functools.partial(add_terms_kernel, i), out_shape=(block,...]
    ppermute x3, starting transfers between devices: 7.2 us -> 10.1 us  [per_device(): right = lax.ppermute(right, 'y', ring(ny, 1))]
    ppermute x1 -> x2, waiting for transfers between devices: 8.39 us -> 5.7 us  [the longest x1 4.9 us: from_other(): lower = lax.ppermute(lower, ('c', 'l'), ring(nz, 1))]
    pallas_call x1, Pallas kernels: 4.34 us -> 6.38 us  [gradient(): pl.pallas_call(functools.partial(gradient_kernel, nx, nl, nc), out_shape=...]
    ppermute x1 -> x2, starting transfers between devices: 10.8 us -> 12.7 us  [the longest x1 8.59 us: from_other(): return (lower, lax.ppermute(upper, ('c', 'l'), ring(nz, -1)))]
    unnamed x22 -> x32, local copies, waits for them, and re-layouts: 7.43 us -> 8.96 us
  transfers between devices with their start and end apart: 15 -> 16, of which waited for: 8 -> 9; matrix products, arithmetic and copies ran while one was open for 4% -> 1% of each run, Pallas kernels for 6% -> 9%
where the time goes in v9:
time: 171 us; the launch traced here: 170 us
  starting transfers between devices  63.1 us (37%)
  waiting for transfers between devices  29.5 us (17%)
  Pallas kernels  27.8 us (16%)
  blocking collectives  24.4 us (14%)
  between operations  14.3 us (8%)
  local copies, waits for them, and re-layouts  10.6 us (6%)
    all_to_all x2, blocking collectives, exchange(): return lax.all_to_all(value, axis, split_axis=0, concat_axis=0, tiled=True)  24.4 us
    all_to_all x3, starting transfers between devices, exchange(): return lax.all_to_all(value, axis, split_axis=0, concat_axis=0, tiled=True)  12 us
    ppermute x3, starting transfers between devices, per_device(): left = lax.ppermute(left, 'y', ring(ny, -1))  10.8 us
    pallas_call x1, Pallas kernels, forward(): pl.pallas_call(functools.partial(forward_kernel, chunk, main, part - main...  10.4 us
    ppermute x3, starting transfers between devices, per_device(): right = lax.ppermute(right, 'y', ring(ny, 1))  10.1 us
    unnamed x32, local copies, waits for them, and re-layouts  8.96 us
    ppermute x1, starting transfers between devices, from_other(): return (lower, lax.ppermute(upper, ('c', 'l'), ring(nz, -1)))  8.59 us
    ppermute x1, starting transfers between devices, per_device(): late = lax.ppermute(own[:, cut:], ('c', 'l', 'k'), both_ways(nz))  8.1 us
  transfers between devices with their start and end apart: 16, of which 9 were waited for; matrix products, arithmetic and copies ran while one was open for 1% of the time, Pallas kernels for 9%

profile of v9, /device:TPU:1, one launch (start us, length us, event | category | flops | bytes accessed | tf_op | source)
XLA Modules:
  0.0 169.8 jit_solution(6493008313399394660)
XLA Ops:
  9.1 10.3 %all_to_all.25 = bf16[4,12,2304]{2,1,0:T(8,128)(2,1)S(1)} all-to-all(bf16[4,12,2304]{2,1,0:T(8,128)(2,1)S(1)} %shard_map.84), channel_id=1, replica_groups=mesh['c'=4,'x'=4,'l'=2,'y'=8,'k'=2] {'x'}, dimensions={0} | all-to-all | bytes 442368 | tf_op jit(solution)/shard_map/all_to_all | solution.py:38
  20.3 1.4 shard_map.87
  21.7 3.7 %all-to-all-start.2 = ((bf16[4,288,576]{2,1,0:T(8,128)(2,1)}), bf16[4,288,576]{2,1,0:T(8,128)(2,1)S(1)}, u32[]{:S(2)}, u32[]{:S(2)}) async-start(bf16[4,288,576]{2,1,0:T(8,128)(2,1)} %shard_map.87), calls=%async_computation.2 | async-start | bytes 2949120 | tf_op jit(solution)/shard_map/all_to_all | solution.py:38
  25.6 4.1 %collective-permute-start = (bf16[2,144,576]{2,1,0:T(8,128)(2,1)S(1)}, bf16[2,144,576]{2,1,0:T(8,128)(2,1)S(1)}, u32[]{:S(2)}, u32[]{:S(2)}) collective-permute-start(bf16[2,144,576]{2,1,0:T(8,128)(2,1)S(1)} %get-tuple-element.29), channel_id=1, source_target_pairs={{0,16},{16,128},{128,144},{144,256},{256,272},{272,384},{384,400},... | collective-permute-start | bytes 995336 | tf_op jit(solution)/shard_map/ppermute | solution.py:428
  29.7 8.6 %collective-permute-start.1 = (bf16[2,144,576]{2,1,0:T(8,128)(2,1)S(1)}, bf16[2,144,576]{2,1,0:T(8,128)(2,1)S(1)}, u32[]{:S(2)}, u32[]{:S(2)}) collective-permute-start(bf16[2,144,576]{2,1,0:T(8,128)(2,1)S(1)} %get-tuple-element.30), channel_id=1, source_target_pairs={{0,400},{16,0},{128,16},{144,128},{256,144},{272,256},{384,272},{4... | collective-permute-start | bytes 995336 | tf_op jit(solution)/shard_map/ppermute | solution.py:429
  38.3 4.9 %collective-permute-done.lower_ref = bf16[2,144,576]{2,1,0:T(8,128)(2,1)S(1)} collective-permute-done((bf16[2,144,576]{2,1,0:T(8,128)(2,1)S(1)}, bf16[2,144,576]{2,1,0:T(8,128)(2,1)S(1)}, u32[]{:S(2)}, u32[]{:S(2)}) %collective-permute-start) | collective-permute-done | bytes 331808 | tf_op jit(solution)/shard_map/ppermute | solution.py:428
  44.0 1.2 shard_map.86
  45.3 3.9 %all-to-all-start.1 = ((bf16[4,272,576]{2,1,0:T(8,128)(2,1)}), bf16[4,272,576]{2,1,0:T(8,128)(2,1)S(1)}, u32[]{:S(2)}, u32[]{:S(2)}) async-start(bf16[4,272,576]{2,1,0:T(8,128)(2,1)} %shard_map.86), calls=%async_computation.1 | async-start | bytes 2785280 | tf_op jit(solution)/shard_map/all_to_all | solution.py:38
  50.1 8.1 %collective-permute-start.2 = (bf16[4,144,576]{2,1,0:T(8,128)(2,1)}, bf16[4,144,576]{2,1,0:T(8,128)(2,1)}, u32[]{:S(2)}, u32[]{:S(2)}) collective-permute-start(bf16[4,144,576]{2,1,0:T(8,128)(2,1)} %slice.4), channel_id=1, source_target_pairs={{0,16},{16,128},{128,144},{144,256},{256,272},{272,384},{384,400},... | collective-permute-start | bytes 1990664 | tf_op jit(solution)/shard_map/ppermute | solution.py:435
  58.3 5.8 %all-to-all-done.1.raw_ref.early_ref = bf16[4,272,576]{2,1,0:T(8,128)(2,1)S(1)} async-done(((bf16[4,272,576]{2,1,0:T(8,128)(2,1)}), bf16[4,272,576]{2,1,0:T(8,128)(2,1)S(1)}, u32[]{:S(2)}, u32[]{:S(2)}) %all-to-all-start.1) | async-done | bytes 1253408 | tf_op jit(solution)/shard_map/all_to_all | solution.py:38
  64.1 5.1 %all-gather.2.cloned.1.call-done.table_ref = bf16[768,2304]{1,0:T(8,128)(2,1)} async-done(((bf16[48,2304]{1,0:T(8,128)(2,1)}), bf16[768,2304]{1,0:T(8,128)(2,1)}) %all-gather.2.cloned.1.call-update) | async-done | bytes 3538960 | tf_op jit(solution)/shard_map/all_gather | solution.py:425
  70.6 2.0 %copy-done.15 = bf16[768,2304]{1,0:T(8,128)(2,1)S(1)} copy-done((bf16[768,2304]{1,0:T(8,128)(2,1)S(1)}, bf16[768,2304]{1,0:T(8,128)(2,1)}, u32[]{:S(2)}) %copy-start.15) | copy-done | bytes 3538968
  72.6 10.4 %shard_map.89 = (bf16[768,288]{1,0:T(8,128)(2,1)S(1)}, bf16[768,576]{1,0:T(8,128)(2,1)S(1)}, bf16[2,4,48,2304]{3,2,1,0:T(8,128)(2,1)S(1)}, bf16[2,4,48,2304]{3,2,1,0:T(8,128)(2,1)}) custom-call(s32[4]{0:T(128)S(1)} %pad_add_fusion.place_ref, bf16[768,2304]{1,0:T(8,128)(2,1)S(1)} %copy-done.15, bf16[4,288,576]{2,1,0:T(8,128)(2,1)S(1)} %copy-done.1, ...), custom_call_target="tpu_custom_call" | custom-call | flops 4076863488 | bytes 9732096 | tf_op jit(solution)/shard_map/pallas_call | solution.py:245
  83.8 2.7 %collective-permute-start.3 = (bf16[2,4,48,2304]{3,2,1,0:T(8,128)(2,1)}, bf16[2,4,48,2304]{3,2,1,0:T(8,128)(2,1)S(1)}, u32[]{:S(2)}, u32[]{:S(2)}) collective-permute-start(bf16[2,4,48,2304]{3,2,1,0:T(8,128)(2,1)} %get-tuple-element.34), channel_id=1, source_target_pairs={{0,1},{1,0},{2,3},{3,2},{4,5},{5,4},{6,7},{7,6},{8,9},{9,8},{10,11... | collective-permute-start | bytes 5308424 | tf_op jit(solution)/shard_map/ppermute | solution.py:442
  86.5 6.4 %shard_map.90 = bf16[2304,576]{1,0:T(8,128)(2,1)} custom-call(bf16[768,2304]{1,0:T(8,128)(2,1)} %all-gather.2.cloned.1.call-done.table_ref, bf16[768,576]{1,0:T(8,128)(2,1)S(1)} %get-tuple-element.35.cots_ref), custom_call_target="tpu_custom_call" | custom-call | flops 2038431744 | bytes 6193152 | tf_op jit(solution)/shard_map/pallas_call | solution.py:291
  93.1 3.2 %collective-permute-start.4 = (bf16[48,2304]{1,0:T(8,128)(2,1)S(1)}, bf16[48,2304]{1,0:T(8,128)(2,1)S(1)}, u32[]{:S(2)}, u32[]{:S(2)}) collective-permute-start(bf16[48,2304]{1,0:T(8,128)(2,1)S(1)} %get-tuple-element.37), channel_id=1, source_target_pairs={{0,2},{2,4},{4,6},{6,8},{8,10},{10,12},{12,14},{14,0},{1,3},{3,5},... | collective-permute-start | bytes 663560 | tf_op jit(solution)/shard_map/ppermute | solution.py:450
  96.3 3.9 %collective-permute-start.5 = (bf16[48,2304]{1,0:T(8,128)(2,1)S(1)}, bf16[48,2304]{1,0:T(8,128)(2,1)S(1)}, u32[]{:S(2)}, u32[]{:S(2)}) collective-permute-start(bf16[48,2304]{1,0:T(8,128)(2,1)S(1)} %get-tuple-element.38), channel_id=1, source_target_pairs={{0,14},{2,0},{4,2},{6,4},{8,6},{10,8},{12,10},{14,12},{1,15},{3,1}... | collective-permute-start | bytes 663560 | tf_op jit(solution)/shard_map/ppermute | solution.py:451
  100.2 3.7 %collective-permute-done.4.refs_0_ = bf16[48,2304]{1,0:T(8,128)(2,1)S(1)} collective-permute-done((bf16[48,2304]{1,0:T(8,128)(2,1)S(1)}, bf16[48,2304]{1,0:T(8,128)(2,1)S(1)}, u32[]{:S(2)}, u32[]{:S(2)}) %collective-permute-start.4) | collective-permute-done | bytes 221216 | tf_op jit(solution)/shard_map/ppermute | solution.py:450
  103.9 1.1 collective-permute-done.5.refs_1_
  105.9 3.2 %collective-permute-start.6 = (bf16[48,2304]{1,0:T(8,128)(2,1)}, bf16[48,2304]{1,0:T(8,128)(2,1)}, u32[]{:S(2)}, u32[]{:S(2)}) collective-permute-start(bf16[48,2304]{1,0:T(8,128)(2,1)} %get-tuple-element.39), channel_id=1, source_target_pairs={{0,2},{2,4},{4,6},{6,8},{8,10},{10,12},{12,14},{14,0},{1,3},{3,5},... | collective-permute-start | bytes 663560 | tf_op jit(solution)/shard_map/ppermute | solution.py:450
  109.1 4.1 %collective-permute-start.7 = (bf16[48,2304]{1,0:T(8,128)(2,1)}, bf16[48,2304]{1,0:T(8,128)(2,1)}, u32[]{:S(2)}, u32[]{:S(2)}) collective-permute-start(bf16[48,2304]{1,0:T(8,128)(2,1)} %get-tuple-element.40), channel_id=1, source_target_pairs={{0,14},{2,0},{4,2},{6,4},{8,6},{10,8},{12,10},{14,12},{1,15},{3,1}... | collective-permute-start | bytes 663560 | tf_op jit(solution)/shard_map/ppermute | solution.py:451
  114.4 4.4 %all-to-all-start.3 = ((bf16[4,96,576]{2,1,0:T(8,128)(2,1)}), bf16[4,96,576]{2,1,0:T(8,128)(2,1)}, u32[]{:S(2)}, u32[]{:S(2)}) async-start(bf16[4,96,576]{2,1,0:T(8,128)(2,1)} %copy-done.4), calls=%async_computation.3 | async-start | bytes 983040 | tf_op jit(solution)/shard_map/all_to_all | solution.py:38
  118.8 1.9 %shard_map.93 = (bf16[48,2304]{1,0:T(8,128)(2,1)}, bf16[48,2304]{1,0:T(8,128)(2,1)}) custom-call(bf16[2,4,48,2304]{3,2,1,0:T(8,128)(2,1)S(1)} %get-tuple-element.33.keep_ref, bf16[2,4,48,2304]{3,2,1,0:T(8,128)(2,1)S(1)} %collective-permute-done.3.taken_ref, bf16[48,2304]{1,0:T(8,128)(2,1)} %collective-permute-done.6.refs_0_, ...), custom_call_target="tpu_custom_call" | custom-call | tf_op jit(solution)/shard_map/pallas_call | solution.py:349
  120.7 3.7 %collective-permute-start.8 = (bf16[48,2304]{1,0:T(8,128)(2,1)}, bf16[48,2304]{1,0:T(8,128)(2,1)}, u32[]{:S(2)}, u32[]{:S(2)}) collective-permute-start(bf16[48,2304]{1,0:T(8,128)(2,1)} %get-tuple-element.41), channel_id=1, source_target_pairs={{0,2},{2,4},{4,6},{6,8},{8,10},{10,12},{12,14},{14,0},{1,3},{3,5},... | collective-permute-start | bytes 663560 | tf_op jit(solution)/shard_map/ppermute | solution.py:450
  124.5 2.7 %collective-permute-start.9 = (bf16[48,2304]{1,0:T(8,128)(2,1)}, bf16[48,2304]{1,0:T(8,128)(2,1)}, u32[]{:S(2)}, u32[]{:S(2)}) collective-permute-start(bf16[48,2304]{1,0:T(8,128)(2,1)} %get-tuple-element.45), channel_id=1, source_target_pairs={{0,14},{2,0},{4,2},{6,4},{8,6},{10,8},{12,10},{14,12},{1,15},{3,1}... | collective-permute-start | bytes 663560 | tf_op jit(solution)/shard_map/ppermute | solution.py:451
  127.3 2.3 %collective-permute-done.8.refs_0_ = bf16[48,2304]{1,0:T(8,128)(2,1)} collective-permute-done((bf16[48,2304]{1,0:T(8,128)(2,1)}, bf16[48,2304]{1,0:T(8,128)(2,1)}, u32[]{:S(2)}, u32[]{:S(2)}) %collective-permute-start.8) | collective-permute-done | bytes 221216 | tf_op jit(solution)/shard_map/ppermute | solution.py:450
  129.6 2.2 %collective-permute-done.9.refs_1_ = bf16[48,2304]{1,0:T(8,128)(2,1)} collective-permute-done((bf16[48,2304]{1,0:T(8,128)(2,1)}, bf16[48,2304]{1,0:T(8,128)(2,1)}, u32[]{:S(2)}, u32[]{:S(2)}) %collective-permute-start.9) | collective-permute-done | bytes 221216 | tf_op jit(solution)/shard_map/ppermute | solution.py:451
  131.8 1.2 shard_map.96
  133.7 6.7 %collective-permute-start.10 = (bf16[48,2304]{1,0:T(8,128)(2,1)S(1)}, bf16[48,2304]{1,0:T(8,128)(2,1)S(1)}, u32[]{:S(2)}, u32[]{:S(2)}) collective-permute-start(bf16[48,2304]{1,0:T(8,128)(2,1)S(1)} %get-tuple-element.46), channel_id=1, source_target_pairs={{0,15},{1,14},{2,1},{3,0},{4,3},{5,2},{6,5},{7,4},{8,7},{9,6},{10,... | collective-permute-start | bytes 663560 | tf_op jit(solution)/shard_map/ppermute | solution.py:455
  140.4 1.9 %shard_map.95 = bf16[192,1152]{1,0:T(8,128)(2,1)} custom-call(bf16[4,96,576]{2,1,0:T(8,128)(2,1)} %all-to-all-done.3.got_ref), custom_call_target="tpu_custom_call" | custom-call | tf_op jit(solution)/shard_map/pallas_call | solution.py:460
  142.4 3.5 %collective-permute-done.10.left_ref = bf16[48,2304]{1,0:T(8,128)(2,1)S(1)} collective-permute-done((bf16[48,2304]{1,0:T(8,128)(2,1)S(1)}, bf16[48,2304]{1,0:T(8,128)(2,1)S(1)}, u32[]{:S(2)}, u32[]{:S(2)}) %collective-permute-start.10) | collective-permute-done | bytes 221216 | tf_op jit(solution)/shard_map/ppermute | solution.py:455
  147.9 14.0 %all_to_all.26.got_ref = bf16[4,120,640]{2,1,0:T(8,128)(2,1)S(1)} all-to-all(bf16[4,120,640]{2,1,0:T(8,128)(2,1)S(1)} %shard_map.97), channel_id=1, replica_groups=mesh['c'=4,'x'=4,'l'=2,'y'=8,'k'=2] {'x'}, dimensions={0} | all-to-all | bytes 1228800 | tf_op jit(solution)/shard_map/all_to_all | solution.py:38
  (54 shorter events, 12.9 us)
Async XLA Ops:
  7.2 13.1 %copy-start.3 = (bf16[288,1152]{1,0:T(8,128)(2,1)S(1)}, bf16[288,1152]{1,0:T(8,128)(2,1)}, u32[]{:S(2)}) copy-start(bf16[288,1152]{1,0:T(8,128)(2,1)} %up_ref.3) | copy-start | bytes 1990660
  7.2 13.1 %copy-start.2 = (bf16[288,1152]{1,0:T(8,128)(2,1)S(1)}, bf16[288,1152]{1,0:T(8,128)(2,1)}, u32[]{:S(2)}) copy-start(bf16[288,1152]{1,0:T(8,128)(2,1)} %gate_ref.3) | copy-start | bytes 1990660
  7.2 62.0 %all-gather.2.cloned.1.call-start = ((), (), s32[]{:S(2)}) async-start(), calls=%async_computation.6 | async-start | bytes 3760128 | tf_op jit(solution)/shard_map/all_gather | solution.py:425
  7.2 1.0 copy-start.9
  8.2 0.7 copy-start.13
  21.7 22.3 %copy-start.7 = (bf16[192,1152]{1,0:T(8,128)(2,1)S(1)}, bf16[192,1152]{1,0:T(8,128)(2,1)}, u32[]{:S(2)}) copy-start(bf16[192,1152]{1,0:T(8,128)(2,1)} %grad_ref.1) | copy-start | bytes 1327108
  21.7 23.5 %all-to-all-start.2 = ((bf16[4,288,576]{2,1,0:T(8,128)(2,1)}), bf16[4,288,576]{2,1,0:T(8,128)(2,1)S(1)}, u32[]{:S(2)}, u32[]{:S(2)}) async-start(bf16[4,288,576]{2,1,0:T(8,128)(2,1)} %shard_map.87), calls=%async_computation.2 | async-start | bytes 2949120 | tf_op jit(solution)/shard_map/all_to_all | solution.py:38
  25.6 17.6 %collective-permute-start = (bf16[2,144,576]{2,1,0:T(8,128)(2,1)S(1)}, bf16[2,144,576]{2,1,0:T(8,128)(2,1)S(1)}, u32[]{:S(2)}, u32[]{:S(2)}) collective-permute-start(bf16[2,144,576]{2,1,0:T(8,128)(2,1)S(1)} %get-tuple-element.29), channel_id=1, source_target_pairs={{0,16},{16,128},{128,144},{144,256},{256,272},{272,384},{384,400},... | collective-permute-start | bytes 995336 | tf_op jit(solution)/shard_map/ppermute | solution.py:428
  29.7 14.3 %collective-permute-start.1 = (bf16[2,144,576]{2,1,0:T(8,128)(2,1)S(1)}, bf16[2,144,576]{2,1,0:T(8,128)(2,1)S(1)}, u32[]{:S(2)}, u32[]{:S(2)}) collective-permute-start(bf16[2,144,576]{2,1,0:T(8,128)(2,1)S(1)} %get-tuple-element.30), channel_id=1, source_target_pairs={{0,400},{16,0},{128,16},{144,128},{256,144},{272,256},{384,272},{4... | collective-permute-start | bytes 995336 | tf_op jit(solution)/shard_map/ppermute | solution.py:429
  45.2 4.9 %copy-start = (bf16[4,288,576]{2,1,0:T(8,128)(2,1)}, bf16[4,288,576]{2,1,0:T(8,128)(2,1)S(1)}, u32[]{:S(2)}) copy-start(bf16[4,288,576]{2,1,0:T(8,128)(2,1)S(1)} %all-to-all-done.2.own_ref) | copy-start | bytes 3981316
  45.3 18.8 %all-to-all-start.1 = ((bf16[4,272,576]{2,1,0:T(8,128)(2,1)}), bf16[4,272,576]{2,1,0:T(8,128)(2,1)S(1)}, u32[]{:S(2)}, u32[]{:S(2)}) async-start(bf16[4,272,576]{2,1,0:T(8,128)(2,1)} %shard_map.86), calls=%async_computation.1 | async-start | bytes 2785280 | tf_op jit(solution)/shard_map/all_to_all | solution.py:38
  49.2 96.7 %reduce-scatter.2.cloned.1.call-start = ((), (), s32[]{:S(2)}) async-start(), calls=%async_computation.7 | async-start | bytes 3317760 | tf_op jit(solution)/shard_map/reduce_scatter | solution.py:445
  50.1 19.5 %collective-permute-start.2 = (bf16[4,144,576]{2,1,0:T(8,128)(2,1)}, bf16[4,144,576]{2,1,0:T(8,128)(2,1)}, u32[]{:S(2)}, u32[]{:S(2)}) collective-permute-start(bf16[4,144,576]{2,1,0:T(8,128)(2,1)} %slice.4), channel_id=1, source_target_pairs={{0,16},{16,128},{128,144},{144,256},{256,272},{272,384},{384,400},... | collective-permute-start | bytes 1990664 | tf_op jit(solution)/shard_map/ppermute | solution.py:435
  69.2 1.4 copy-start.1
  70.6 2.0 %copy-start.15 = (bf16[768,2304]{1,0:T(8,128)(2,1)S(1)}, bf16[768,2304]{1,0:T(8,128)(2,1)}, u32[]{:S(2)}) copy-start(bf16[768,2304]{1,0:T(8,128)(2,1)} %all-gather.2.cloned.1.call-done.table_ref) | copy-start | bytes 10616836
  83.0 0.9 copy-start.5
  83.8 9.1 %collective-permute-start.3 = (bf16[2,4,48,2304]{3,2,1,0:T(8,128)(2,1)}, bf16[2,4,48,2304]{3,2,1,0:T(8,128)(2,1)S(1)}, u32[]{:S(2)}, u32[]{:S(2)}) collective-permute-start(bf16[2,4,48,2304]{3,2,1,0:T(8,128)(2,1)} %get-tuple-element.34), channel_id=1, source_target_pairs={{0,1},{1,0},{2,3},{3,2},{4,5},{5,4},{6,7},{7,6},{8,9},{9,8},{10,11... | collective-permute-start | bytes 5308424 | tf_op jit(solution)/shard_map/ppermute | solution.py:442
  93.1 10.9 %collective-permute-start.4 = (bf16[48,2304]{1,0:T(8,128)(2,1)S(1)}, bf16[48,2304]{1,0:T(8,128)(2,1)S(1)}, u32[]{:S(2)}, u32[]{:S(2)}) collective-permute-start(bf16[48,2304]{1,0:T(8,128)(2,1)S(1)} %get-tuple-element.37), channel_id=1, source_target_pairs={{0,2},{2,4},{4,6},{6,8},{8,10},{10,12},{12,14},{14,0},{1,3},{3,5},... | collective-permute-start | bytes 663560 | tf_op jit(solution)/shard_map/ppermute | solution.py:450
  96.3 16.9 %copy-start.6 = (bf16[768,288]{1,0:T(8,128)(2,1)S(1)}, bf16[768,288]{1,0:T(8,128)(2,1)}, u32[]{:S(2)}) copy-start(bf16[768,288]{1,0:T(8,128)(2,1)} %copy-done.5) | copy-start | bytes 1327108
  96.3 8.8 %collective-permute-start.5 = (bf16[48,2304]{1,0:T(8,128)(2,1)S(1)}, bf16[48,2304]{1,0:T(8,128)(2,1)S(1)}, u32[]{:S(2)}, u32[]{:S(2)}) collective-permute-start(bf16[48,2304]{1,0:T(8,128)(2,1)S(1)} %get-tuple-element.38), channel_id=1, source_target_pairs={{0,14},{2,0},{4,2},{6,4},{8,6},{10,8},{12,10},{14,12},{1,15},{3,1}... | collective-permute-start | bytes 663560 | tf_op jit(solution)/shard_map/ppermute | solution.py:451
  105.9 12.9 %collective-permute-start.6 = (bf16[48,2304]{1,0:T(8,128)(2,1)}, bf16[48,2304]{1,0:T(8,128)(2,1)}, u32[]{:S(2)}, u32[]{:S(2)}) collective-permute-start(bf16[48,2304]{1,0:T(8,128)(2,1)} %get-tuple-element.39), channel_id=1, source_target_pairs={{0,2},{2,4},{4,6},{6,8},{8,10},{10,12},{12,14},{14,0},{1,3},{3,5},... | collective-permute-start | bytes 663560 | tf_op jit(solution)/shard_map/ppermute | solution.py:450
  109.1 9.8 %collective-permute-start.7 = (bf16[48,2304]{1,0:T(8,128)(2,1)}, bf16[48,2304]{1,0:T(8,128)(2,1)}, u32[]{:S(2)}, u32[]{:S(2)}) collective-permute-start(bf16[48,2304]{1,0:T(8,128)(2,1)} %get-tuple-element.40), channel_id=1, source_target_pairs={{0,14},{2,0},{4,2},{6,4},{8,6},{10,8},{12,10},{14,12},{1,15},{3,1}... | collective-permute-start | bytes 663560 | tf_op jit(solution)/shard_map/ppermute | solution.py:451
  113.6 0.8 copy-start.4
  114.4 12.9 %all-to-all-start.3 = ((bf16[4,96,576]{2,1,0:T(8,128)(2,1)}), bf16[4,96,576]{2,1,0:T(8,128)(2,1)}, u32[]{:S(2)}, u32[]{:S(2)}) async-start(bf16[4,96,576]{2,1,0:T(8,128)(2,1)} %copy-done.4), calls=%async_computation.3 | async-start | bytes 983040 | tf_op jit(solution)/shard_map/all_to_all | solution.py:38
  120.7 8.8 %collective-permute-start.8 = (bf16[48,2304]{1,0:T(8,128)(2,1)}, bf16[48,2304]{1,0:T(8,128)(2,1)}, u32[]{:S(2)}, u32[]{:S(2)}) collective-permute-start(bf16[48,2304]{1,0:T(8,128)(2,1)} %get-tuple-element.41), channel_id=1, source_target_pairs={{0,2},{2,4},{4,6},{6,8},{8,10},{10,12},{12,14},{14,0},{1,3},{3,5},... | collective-permute-start | bytes 663560 | tf_op jit(solution)/shard_map/ppermute | solution.py:450
  124.5 7.3 %collective-permute-start.9 = (bf16[48,2304]{1,0:T(8,128)(2,1)}, bf16[48,2304]{1,0:T(8,128)(2,1)}, u32[]{:S(2)}, u32[]{:S(2)}) collective-permute-start(bf16[48,2304]{1,0:T(8,128)(2,1)} %get-tuple-element.45), channel_id=1, source_target_pairs={{0,14},{2,0},{4,2},{6,4},{8,6},{10,8},{12,10},{14,12},{1,15},{3,1}... | collective-permute-start | bytes 663560 | tf_op jit(solution)/shard_map/ppermute | solution.py:451
  133.0 0.7 copy-start.11
  133.7 28.3 %copy-start.10 = (bf16[12,2304]{1,0:T(8,128)(2,1)S(1)}, bf16[12,2304]{1,0:T(8,128)(2,1)}, u32[]{:S(2)}) copy-start(bf16[12,2304]{1,0:T(8,128)(2,1)} %tokens_ref.3) | copy-start | bytes 165892
  133.7 28.3 %copy-start.14 = (f32[2304]{0:T(1024)S(1)}, f32[2304]{0:T(1024)}, u32[]{:S(2)}) copy-start(f32[2304]{0:T(1024)} %gain_ref.3) | copy-start | bytes 27652
  133.7 12.2 %collective-permute-start.10 = (bf16[48,2304]{1,0:T(8,128)(2,1)S(1)}, bf16[48,2304]{1,0:T(8,128)(2,1)S(1)}, u32[]{:S(2)}, u32[]{:S(2)}) collective-permute-start(bf16[48,2304]{1,0:T(8,128)(2,1)S(1)} %get-tuple-element.46), channel_id=1, source_target_pairs={{0,15},{1,14},{2,1},{3,0},{4,3},{5,2},{6,5},{7,4},{8,7},{9,6},{10,... | collective-permute-start | bytes 663560 | tf_op jit(solution)/shard_map/ppermute | solution.py:455
  145.9 1.0 copy-start.8
  146.9 0.9 copy-start.12
Sparse Core Ops, SparseCore 0:
  20.4 48.7 all-gather.1
  93.1 44.4 reduce-scatter.1

commit v10 on v7

--- a/solution.py
+++ b/solution.py
@@ -339,25 +339,26 @@
     total = near_ref[...].astype(F32) + jnp.where(place_ref[1] == 0, mine, far_ref[...].astype(F32))
     grad = grad_ref[...].astype(F32)
     piece = grad.shape[0] // nx
-    pad = jnp.zeros((16 - rows, wide + thin), F32)
     for x in range(nx):
         mine = total[x * rows : (x + 1) * rows]
+        found = []
         for j in range(nx):
             start = nx * wide + j * thin
-            both = jnp.concatenate(
-                [mine[:, j * wide : (j + 1) * wide], mine[:, start : start + thin]], axis=1
+            found.append(
+                jnp.concatenate(
+                    [mine[:, j * wide : (j + 1) * wide], mine[:, start : start + thin]], axis=1
+                )
             )
-            out_ref[x, 16 * j : 16 * j + 16, :] = jnp.concatenate([both, pad], axis=0).astype(BF16)
-        out_ref[x, 16 * nx :, :] = grad[x * piece : (x + 1) * piece].astype(BF16)
+        out_ref[x, : nx * rows, : wide + thin] = jnp.concatenate(found, axis=0).astype(BF16)
+        out_ref[x, nx * rows :, : grad.shape[1]] = grad[x * piece : (x + 1) * piece].astype(BF16)
 
 
 def finish_kernel(main, tail, wide, thin, got_ref, tokens_ref, gain_ref, input_ref, gate_ref, up_ref):
     nx = got_ref.shape[0]
     rows, width = tokens_ref.shape
-    found = [
-        sum(got_ref[x, 16 * j : 16 * j + 16, :].astype(F32) for x in range(nx))[:rows]
-        for j in range(nx)
-    ]
+    pair = 2 * (main + tail)
+    total = sum(got_ref[x, : nx * rows, : wide + thin].astype(F32) for x in range(nx))
+    found = [total[j * rows : (j + 1) * rows] for j in range(nx)]
     token_vals = tokens_ref[...].astype(F32)
     scale = row_scale_of(token_vals)
     gain = gain_ref[...].reshape(1, width)
@@ -368,7 +369,7 @@
     factor = scale * scale / width
     input_ref[...] = (gain * inner_grad - factor * token_vals * inner).astype(BF16)
     for q in range(nx):
-        grad = got_ref[q, 16 * nx :, :].astype(F32)
+        grad = got_ref[q, nx * rows :, :pair].astype(F32)
         start = nx * main + q * tail
         gate_ref[:, q * main : (q + 1) * main] = grad[:, :main]
         gate_ref[:, start : start + tail] = grad[:, 2 * main : 2 * main + tail]
@@ -410,6 +411,7 @@
         own = exchange(pack_weights(nx, gate_weight, up_weight, feats), "x")
         early = exchange(pack_grads(nx, early, hidden_grad), "x")
         late = lax.ppermute(own[:, cut:], ("c", "l", "k"), both_ways(nz))
+        table, early = lax.optimization_barrier((table, early))
         grads = sort_grads(early, cut, own_tokens, rows)
 
         found, cots, keep, give = forward(place, table, own, early, late, grads, ny, pool)
@@ -425,9 +427,8 @@
         partial = term(0).astype(BF16)
         for i in range(1, ny // 2):
             partial = lax.ppermute(partial, ("y", "k"), both_ways(ny))
-            if i == ny // 2 - 1:
-                partial, hidden = lax.optimization_barrier((partial, hidden))
             partial = (partial.astype(F32) + term(i)).astype(BF16)
+        partial, hidden = lax.optimization_barrier((partial, hidden))
         step = partial.shape[0] // 2
         lower, upper = partial[:step], partial[step:]
         core = lax.axis_index("k")
@@ -450,7 +451,7 @@
         hidden, near, far = lax.optimization_barrier((hidden, near, far))
         last = pl.pallas_call(
             functools.partial(gather_kernel, nx, rows, wide, thin),
-            out_shape=jax.ShapeDtypeStruct((nx, 16 * nx + feats // nc, pair), BF16),
+            out_shape=jax.ShapeDtypeStruct((nx, nx * rows + feats // nc, -(-pair // 128) * 128), BF16),
             in_specs=[SMEM, VMEM, VMEM, VMEM, VMEM],
             out_specs=VMEM,
             compiler_params=params(24),

time: 170 us -> 167 us (0.982)
  local copies, waits for them, and re-layouts: 11 us -> 9.07 us
    all_gather x1, waiting for transfers between devices: 2.29 us -> 4.47 us  [per_device(): table = lax.all_gather(near, ('y', 'k'), axis=0, tiled=True)]
    unnamed x26 -> x22, local copies, waits for them, and re-layouts: 9.3 us -> 7.4 us
  transfers between devices with their start and end apart: 13 -> 13, of which waited for: 9 -> 8; matrix products, arithmetic and copies ran while one was open for 3% -> 4% of each run, Pallas kernels for 6% -> 6%
where the time goes in v10:
time: 167 us; the launch traced here: 164 us
  starting transfers between devices  53.2 us (32%)
  waiting for transfers between devices  39.9 us (24%)
  Pallas kernels  22.4 us (13%)
  blocking collectives  20.3 us (12%)
  between operations  14.3 us (9%)
  local copies, waits for them, and re-layouts  9.07 us (5%)
  other arithmetic  4.92 us (3%)
    all_to_all x2, blocking collectives, exchange(): return lax.all_to_all(value, axis, split_axis=0, concat_axis=0, tiled=True)  20.3 us
    ppermute x3, starting transfers between devices, per_device(): partial = lax.ppermute(partial, ('y', 'k'), both_ways(ny))  15.5 us
    all_to_all x3, waiting for transfers between devices, exchange(): return lax.all_to_all(value, axis, split_axis=0, concat_axis=0, tiled=True)  14.2 us
    all_to_all x3, starting transfers between devices, exchange(): return lax.all_to_all(value, axis, split_axis=0, concat_axis=0, tiled=True)  12.3 us
    ppermute x1, starting transfers between devices, per_device(): lax.ppermute(pack_weights(nx, gate_weight, up_weight, cut), ('c', 'l', 'k...  10.8 us
    pallas_call x1, Pallas kernels, forward(): pl.pallas_call(functools.partial(forward_kernel, chunk, main, part - main...  10.7 us
    ppermute x3, waiting for transfers between devices, per_device(): partial = lax.ppermute(partial, ('y', 'k'), both_ways(ny))  10.5 us
    ppermute x1, waiting for transfers between devices, per_device(): lax.ppermute(pack_weights(nx, gate_weight, up_weight, cut), ('c', 'l', 'k...  8.39 us
  transfers between devices with their start and end apart: 13, of which 8 were waited for; matrix products, arithmetic and copies ran while one was open for 4% of the time, Pallas kernels for 6%

profile of v10, /device:TPU:1, one launch (start us, length us, event | category | flops | bytes accessed | tf_op | source)
XLA Modules:
  0.0 164.0 jit_solution(3524712369939036781)
XLA Ops:
  9.1 10.3 %all_to_all.25 = bf16[4,12,2304]{2,1,0:T(8,128)(2,1)S(1)} all-to-all(bf16[4,12,2304]{2,1,0:T(8,128)(2,1)S(1)} %shard_map.84), channel_id=1, replica_groups=mesh['c'=4,'x'=4,'l'=2,'y'=8,'k'=2] {'x'}, dimensions={0} | all-to-all | bytes 442368 | tf_op jit(solution)/shard_map/all_to_all | solution.py:38
  20.3 1.4 shard_map.87
  21.7 3.7 %all-to-all-start.2 = ((bf16[4,288,576]{2,1,0:T(8,128)(2,1)}), bf16[4,288,576]{2,1,0:T(8,128)(2,1)S(1)}, u32[]{:S(2)}, u32[]{:S(2)}) async-start(bf16[4,288,576]{2,1,0:T(8,128)(2,1)} %shard_map.87), calls=%async_computation.2 | async-start | bytes 2949120 | tf_op jit(solution)/shard_map/all_to_all | solution.py:38
  25.6 10.8 %collective-permute-start = (bf16[4,144,576]{2,1,0:T(8,128)(2,1)S(1)}, bf16[4,144,576]{2,1,0:T(8,128)(2,1)S(1)}, u32[]{:S(2)}, u32[]{:S(2)}) collective-permute-start(bf16[4,144,576]{2,1,0:T(8,128)(2,1)S(1)} %shard_map.85), channel_id=1, source_target_pairs={{0,16},{16,128},{128,144},{144,256},{256,272},{272,384},{384,400},... | collective-permute-start | bytes 1990664 | tf_op jit(solution)/shard_map/ppermute | solution.py:408
  36.4 8.4 %collective-permute-done.weights_ref = bf16[4,144,576]{2,1,0:T(8,128)(2,1)S(1)} collective-permute-done((bf16[4,144,576]{2,1,0:T(8,128)(2,1)S(1)}, bf16[4,144,576]{2,1,0:T(8,128)(2,1)S(1)}, u32[]{:S(2)}, u32[]{:S(2)}) %collective-permute-start) | collective-permute-done | bytes 663584 | tf_op jit(solution)/shard_map/ppermute | solution.py:408
  44.7 1.3 shard_map.86
  46.0 4.2 %all-to-all-start.1 = ((bf16[4,272,576]{2,1,0:T(8,128)(2,1)}), bf16[4,272,576]{2,1,0:T(8,128)(2,1)S(1)}, u32[]{:S(2)}, u32[]{:S(2)}) async-start(bf16[4,272,576]{2,1,0:T(8,128)(2,1)} %shard_map.86), calls=%async_computation.1 | async-start | bytes 2785280 | tf_op jit(solution)/shard_map/all_to_all | solution.py:38
  51.2 7.0 %collective-permute-start.1 = (bf16[4,144,576]{2,1,0:T(8,128)(2,1)}, bf16[4,144,576]{2,1,0:T(8,128)(2,1)}, u32[]{:S(2)}, u32[]{:S(2)}) collective-permute-start(bf16[4,144,576]{2,1,0:T(8,128)(2,1)} %slice.44), channel_id=1, source_target_pairs={{0,16},{16,128},{128,144},{144,256},{256,272},{272,384},{384,400},... | collective-permute-start | bytes 1990664 | tf_op jit(solution)/shard_map/ppermute | solution.py:413
  58.3 6.4 %all-to-all-done.1.raw_ref.early_ref = bf16[4,272,576]{2,1,0:T(8,128)(2,1)S(1)} async-done(((bf16[4,272,576]{2,1,0:T(8,128)(2,1)}), bf16[4,272,576]{2,1,0:T(8,128)(2,1)S(1)}, u32[]{:S(2)}, u32[]{:S(2)}) %all-to-all-start.1) | async-done | bytes 1253408 | tf_op jit(solution)/shard_map/all_to_all | solution.py:38
  64.7 4.5 %all-gather.2.cloned.1.call-done.table_ref = bf16[768,2304]{1,0:T(8,128)(2,1)} async-done(((bf16[48,2304]{1,0:T(8,128)(2,1)}), bf16[768,2304]{1,0:T(8,128)(2,1)}) %all-gather.2.cloned.1.call-update) | async-done | bytes 3538960 | tf_op jit(solution)/shard_map/all_gather | solution.py:405
  69.6 2.0 %copy-done.10 = bf16[768,2304]{1,0:T(8,128)(2,1)S(1)} copy-done((bf16[768,2304]{1,0:T(8,128)(2,1)S(1)}, bf16[768,2304]{1,0:T(8,128)(2,1)}, u32[]{:S(2)}) %copy-start.10) | copy-done | bytes 3538968
  71.6 10.7 %shard_map.89 = (bf16[768,288]{1,0:T(8,128)(2,1)S(1)}, bf16[768,576]{1,0:T(8,128)(2,1)S(1)}, bf16[4,96,2304]{2,1,0:T(8,128)(2,1)S(1)}, bf16[4,96,2304]{2,1,0:T(8,128)(2,1)}) custom-call(s32[4]{0:T(128)S(1)} %pad_add_fusion.place_ref, bf16[768,2304]{1,0:T(8,128)(2,1)S(1)} %copy-done.10, bf16[4,288,576]{2,1,0:T(8,128)(2,1)S(1)} %all-to-all-done.2.own_ref, ...), custom_call_target="tpu_custom_call" | custom-call | flops 4076863488 | bytes 9732096 | tf_op jit(solution)/shard_map/pallas_call | solution.py:244
  82.2 1.3 copy-done.2
  83.5 3.6 %collective-permute-start.2 = (bf16[4,96,2304]{2,1,0:T(8,128)(2,1)}, bf16[4,96,2304]{2,1,0:T(8,128)(2,1)}, u32[]{:S(2)}, u32[]{:S(2)}) collective-permute-start(bf16[4,96,2304]{2,1,0:T(8,128)(2,1)} %get-tuple-element.23), channel_id=1, source_target_pairs={{0,1},{1,0},{2,3},{3,2},{4,5},{5,4},{6,7},{7,6},{8,9},{9,8},{10,11... | collective-permute-start | bytes 5308424 | tf_op jit(solution)/shard_map/ppermute | solution.py:418
  87.2 4.4 %shard_map.90 = bf16[2304,576]{1,0:T(8,128)(2,1)} custom-call(bf16[768,2304]{1,0:T(8,128)(2,1)S(1)} %copy-done.10, bf16[768,576]{1,0:T(8,128)(2,1)S(1)} %get-tuple-element.24.cots_ref), custom_call_target="tpu_custom_call" | custom-call | flops 2038431744 | bytes 6193152 | tf_op jit(solution)/shard_map/pallas_call | solution.py:290
  91.6 1.4 copy-done.3
  93.0 1.1 fusion.3
  94.1 5.1 %collective-permute-start.3 = (bf16[96,2304]{1,0:T(8,128)(2,1)S(1)}, bf16[96,2304]{1,0:T(8,128)(2,1)S(1)}, u32[]{:S(2)}, u32[]{:S(2)}) collective-permute-start(bf16[96,2304]{1,0:T(8,128)(2,1)S(1)} %fusion.3), channel_id=1, source_target_pairs={{0,2},{2,4},{4,6},{6,8},{8,10},{10,12},{12,14},{14,0},{1,15},{3,1}... | collective-permute-start | bytes 1327112 | tf_op jit(solution)/shard_map/ppermute | solution.py:429
  99.2 5.2 %collective-permute-done.3 = bf16[96,2304]{1,0:T(8,128)(2,1)S(1)} collective-permute-done((bf16[96,2304]{1,0:T(8,128)(2,1)S(1)}, bf16[96,2304]{1,0:T(8,128)(2,1)S(1)}, u32[]{:S(2)}, u32[]{:S(2)}) %collective-permute-start.3) | collective-permute-done | bytes 442400 | tf_op jit(solution)/shard_map/ppermute | solution.py:429
  104.5 1.2 fusion.2
  105.7 5.0 %collective-permute-start.4 = (bf16[96,2304]{1,0:T(8,128)(2,1)S(1)}, bf16[96,2304]{1,0:T(8,128)(2,1)S(1)}, u32[]{:S(2)}, u32[]{:S(2)}) collective-permute-start(bf16[96,2304]{1,0:T(8,128)(2,1)S(1)} %fusion.2), channel_id=1, source_target_pairs={{0,2},{2,4},{4,6},{6,8},{8,10},{10,12},{12,14},{14,0},{1,15},{3,1}... | collective-permute-start | bytes 1327112 | tf_op jit(solution)/shard_map/ppermute | solution.py:429
  110.7 5.2 %collective-permute-done.4 = bf16[96,2304]{1,0:T(8,128)(2,1)S(1)} collective-permute-done((bf16[96,2304]{1,0:T(8,128)(2,1)S(1)}, bf16[96,2304]{1,0:T(8,128)(2,1)S(1)}, u32[]{:S(2)}, u32[]{:S(2)}) %collective-permute-start.4) | collective-permute-done | bytes 442400 | tf_op jit(solution)/shard_map/ppermute | solution.py:429
  115.9 1.2 fusion.1
  117.1 5.4 %collective-permute-start.5 = (bf16[96,2304]{1,0:T(8,128)(2,1)S(1)}, bf16[96,2304]{1,0:T(8,128)(2,1)}, u32[]{:S(2)}, u32[]{:S(2)}) collective-permute-start(bf16[96,2304]{1,0:T(8,128)(2,1)S(1)} %fusion.1), channel_id=1, source_target_pairs={{0,2},{2,4},{4,6},{6,8},{8,10},{10,12},{12,14},{14,0},{1,15},{3,1}... | collective-permute-start | bytes 1327112 | tf_op jit(solution)/shard_map/ppermute | solution.py:429
  122.5 1.2 shard_map.91
  123.7 4.4 %all-to-all-start.3 = ((bf16[4,96,576]{2,1,0:T(8,128)(2,1)}), bf16[4,96,576]{2,1,0:T(8,128)(2,1)S(1)}, u32[]{:S(2)}, u32[]{:S(2)}) async-start(bf16[4,96,576]{2,1,0:T(8,128)(2,1)} %shard_map.91), calls=%async_computation.3 | async-start | bytes 983040 | tf_op jit(solution)/shard_map/all_to_all | solution.py:38
  128.2 1.3 fusion.sums_ref
  129.5 7.8 %all-to-all-done.3.got_ref = bf16[4,96,576]{2,1,0:T(8,128)(2,1)S(1)} async-done(((bf16[4,96,576]{2,1,0:T(8,128)(2,1)}), bf16[4,96,576]{2,1,0:T(8,128)(2,1)S(1)}, u32[]{:S(2)}, u32[]{:S(2)}) %all-to-all-start.3) | async-done | bytes 442400 | tf_op jit(solution)/shard_map/all_to_all | solution.py:38
  137.3 1.9 %collective-permute-start.7 = (bf16[48,2304]{1,0:T(8,128)(2,1)S(1)}, bf16[48,2304]{1,0:T(8,128)(2,1)S(1)}, u32[]{:S(2)}, u32[]{:S(2)}) collective-permute-start(bf16[48,2304]{1,0:T(8,128)(2,1)S(1)} %get-tuple-element.36), channel_id=1, source_target_pairs={{1,15},{3,1},{5,3},{7,5},{9,7},{11,9},{13,11},{15,13},{17,31},{19,... | collective-permute-start | bytes 663560 | tf_op jit(solution)/shard_map/ppermute | solution.py:440
  139.2 1.9 %collective-permute-start.6 = (bf16[48,2304]{1,0:T(8,128)(2,1)S(1)}, bf16[48,2304]{1,0:T(8,128)(2,1)S(1)}, u32[]{:S(2)}, u32[]{:S(2)}) collective-permute-start(bf16[48,2304]{1,0:T(8,128)(2,1)S(1)} %get-tuple-element.37), channel_id=1, source_target_pairs={{0,1},{2,3},{4,5},{6,7},{8,9},{10,11},{12,13},{14,15},{1,14},{3,0}... | collective-permute-start | bytes 663560 | tf_op jit(solution)/shard_map/ppermute | solution.py:435
  142.1 1.9 %collective-permute-done.7.far_ref = bf16[48,2304]{1,0:T(8,128)(2,1)S(1)} collective-permute-done((bf16[48,2304]{1,0:T(8,128)(2,1)S(1)}, bf16[48,2304]{1,0:T(8,128)(2,1)S(1)}, u32[]{:S(2)}, u32[]{:S(2)}) %collective-permute-start.7) | collective-permute-done | bytes 221216 | tf_op jit(solution)/shard_map/ppermute | solution.py:440
  146.1 10.0 %all_to_all.26.got_ref = bf16[4,120,640]{2,1,0:T(8,128)(2,1)S(1)} all-to-all(bf16[4,120,640]{2,1,0:T(8,128)(2,1)S(1)} %shard_map.93), channel_id=1, replica_groups=mesh['c'=4,'x'=4,'l'=2,'y'=8,'k'=2] {'x'}, dimensions={0} | all-to-all | bytes 1228800 | tf_op jit(solution)/shard_map/all_to_all | solution.py:38
  (39 shorter events, 8.4 us)
Async XLA Ops:
  7.2 13.1 %copy-start.1 = (bf16[288,1152]{1,0:T(8,128)(2,1)S(1)}, bf16[288,1152]{1,0:T(8,128)(2,1)}, u32[]{:S(2)}) copy-start(bf16[288,1152]{1,0:T(8,128)(2,1)} %up_ref.3) | copy-start | bytes 1990660
  7.2 13.1 %copy-start = (bf16[288,1152]{1,0:T(8,128)(2,1)S(1)}, bf16[288,1152]{1,0:T(8,128)(2,1)}, u32[]{:S(2)}) copy-start(bf16[288,1152]{1,0:T(8,128)(2,1)} %gate_ref.3) | copy-start | bytes 1990660
  7.2 62.0 %all-gather.2.cloned.1.call-start = ((), (), s32[]{:S(2)}) async-start(), calls=%async_computation.6 | async-start | bytes 3760128 | tf_op jit(solution)/shard_map/all_gather | solution.py:405
  7.2 1.0 copy-start.6
  8.2 0.7 copy-start.8
  21.7 23.1 %copy-start.4 = (bf16[192,1152]{1,0:T(8,128)(2,1)S(1)}, bf16[192,1152]{1,0:T(8,128)(2,1)}, u32[]{:S(2)}) copy-start(bf16[192,1152]{1,0:T(8,128)(2,1)} %grad_ref.1) | copy-start | bytes 1327108
  21.7 24.3 %all-to-all-start.2 = ((bf16[4,288,576]{2,1,0:T(8,128)(2,1)}), bf16[4,288,576]{2,1,0:T(8,128)(2,1)S(1)}, u32[]{:S(2)}, u32[]{:S(2)}) async-start(bf16[4,288,576]{2,1,0:T(8,128)(2,1)} %shard_map.87), calls=%async_computation.2 | async-start | bytes 2949120 | tf_op jit(solution)/shard_map/all_to_all | solution.py:38
  25.6 19.2 %collective-permute-start = (bf16[4,144,576]{2,1,0:T(8,128)(2,1)S(1)}, bf16[4,144,576]{2,1,0:T(8,128)(2,1)S(1)}, u32[]{:S(2)}, u32[]{:S(2)}) collective-permute-start(bf16[4,144,576]{2,1,0:T(8,128)(2,1)S(1)} %shard_map.85), channel_id=1, source_target_pairs={{0,16},{16,128},{128,144},{144,256},{256,272},{272,384},{384,400},... | collective-permute-start | bytes 1990664 | tf_op jit(solution)/shard_map/ppermute | solution.py:408
  46.0 18.7 %all-to-all-start.1 = ((bf16[4,272,576]{2,1,0:T(8,128)(2,1)}), bf16[4,272,576]{2,1,0:T(8,128)(2,1)S(1)}, u32[]{:S(2)}, u32[]{:S(2)}) async-start(bf16[4,272,576]{2,1,0:T(8,128)(2,1)} %shard_map.86), calls=%async_computation.1 | async-start | bytes 2785280 | tf_op jit(solution)/shard_map/all_to_all | solution.py:38
  50.2 94.2 %reduce-scatter.2.cloned.1.call-start = ((), (), s32[]{:S(2)}) async-start(), calls=%async_computation.7 | async-start | bytes 3317760 | tf_op jit(solution)/shard_map/reduce_scatter | solution.py:421
  51.2 18.4 %collective-permute-start.1 = (bf16[4,144,576]{2,1,0:T(8,128)(2,1)}, bf16[4,144,576]{2,1,0:T(8,128)(2,1)}, u32[]{:S(2)}, u32[]{:S(2)}) collective-permute-start(bf16[4,144,576]{2,1,0:T(8,128)(2,1)} %slice.44), channel_id=1, source_target_pairs={{0,16},{16,128},{128,144},{144,256},{256,272},{272,384},{384,400},... | collective-permute-start | bytes 1990664 | tf_op jit(solution)/shard_map/ppermute | solution.py:413
  69.6 2.0 %copy-start.10 = (bf16[768,2304]{1,0:T(8,128)(2,1)S(1)}, bf16[768,2304]{1,0:T(8,128)(2,1)}, u32[]{:S(2)}) copy-start(bf16[768,2304]{1,0:T(8,128)(2,1)} %all-gather.2.cloned.1.call-done.table_ref) | copy-start | bytes 10616836
  82.2 1.3 copy-start.2
  83.5 8.0 %collective-permute-start.2 = (bf16[4,96,2304]{2,1,0:T(8,128)(2,1)}, bf16[4,96,2304]{2,1,0:T(8,128)(2,1)}, u32[]{:S(2)}, u32[]{:S(2)}) collective-permute-start(bf16[4,96,2304]{2,1,0:T(8,128)(2,1)} %get-tuple-element.23), channel_id=1, source_target_pairs={{0,1},{1,0},{2,3},{3,2},{4,5},{5,4},{6,7},{7,6},{8,9},{9,8},{10,11... | collective-permute-start | bytes 5308424 | tf_op jit(solution)/shard_map/ppermute | solution.py:418
  91.5 1.5 copy-start.3
  94.1 10.3 %collective-permute-start.3 = (bf16[96,2304]{1,0:T(8,128)(2,1)S(1)}, bf16[96,2304]{1,0:T(8,128)(2,1)S(1)}, u32[]{:S(2)}, u32[]{:S(2)}) collective-permute-start(bf16[96,2304]{1,0:T(8,128)(2,1)S(1)} %fusion.3), channel_id=1, source_target_pairs={{0,2},{2,4},{4,6},{6,8},{8,10},{10,12},{12,14},{14,0},{1,15},{3,1}... | collective-permute-start | bytes 1327112 | tf_op jit(solution)/shard_map/ppermute | solution.py:429
  105.7 10.2 %collective-permute-start.4 = (bf16[96,2304]{1,0:T(8,128)(2,1)S(1)}, bf16[96,2304]{1,0:T(8,128)(2,1)S(1)}, u32[]{:S(2)}, u32[]{:S(2)}) collective-permute-start(bf16[96,2304]{1,0:T(8,128)(2,1)S(1)} %fusion.2), channel_id=1, source_target_pairs={{0,2},{2,4},{4,6},{6,8},{8,10},{10,12},{12,14},{14,0},{1,15},{3,1}... | collective-permute-start | bytes 1327112 | tf_op jit(solution)/shard_map/ppermute | solution.py:429
  117.1 11.1 %collective-permute-start.5 = (bf16[96,2304]{1,0:T(8,128)(2,1)S(1)}, bf16[96,2304]{1,0:T(8,128)(2,1)}, u32[]{:S(2)}, u32[]{:S(2)}) collective-permute-start(bf16[96,2304]{1,0:T(8,128)(2,1)S(1)} %fusion.1), channel_id=1, source_target_pairs={{0,2},{2,4},{4,6},{6,8},{8,10},{10,12},{12,14},{14,0},{1,15},{3,1}... | collective-permute-start | bytes 1327112 | tf_op jit(solution)/shard_map/ppermute | solution.py:429
  123.7 13.5 %all-to-all-start.3 = ((bf16[4,96,576]{2,1,0:T(8,128)(2,1)}), bf16[4,96,576]{2,1,0:T(8,128)(2,1)S(1)}, u32[]{:S(2)}, u32[]{:S(2)}) async-start(bf16[4,96,576]{2,1,0:T(8,128)(2,1)} %shard_map.91), calls=%async_computation.3 | async-start | bytes 983040 | tf_op jit(solution)/shard_map/all_to_all | solution.py:38
  137.3 6.7 %collective-permute-start.7 = (bf16[48,2304]{1,0:T(8,128)(2,1)S(1)}, bf16[48,2304]{1,0:T(8,128)(2,1)S(1)}, u32[]{:S(2)}, u32[]{:S(2)}) collective-permute-start(bf16[48,2304]{1,0:T(8,128)(2,1)S(1)} %get-tuple-element.36), channel_id=1, source_target_pairs={{1,15},{3,1},{5,3},{7,5},{9,7},{11,9},{13,11},{15,13},{17,31},{19,... | collective-permute-start | bytes 663560 | tf_op jit(solution)/shard_map/ppermute | solution.py:440
  139.2 5.2 %collective-permute-start.6 = (bf16[48,2304]{1,0:T(8,128)(2,1)S(1)}, bf16[48,2304]{1,0:T(8,128)(2,1)S(1)}, u32[]{:S(2)}, u32[]{:S(2)}) collective-permute-start(bf16[48,2304]{1,0:T(8,128)(2,1)S(1)} %get-tuple-element.37), channel_id=1, source_target_pairs={{0,1},{2,3},{4,5},{6,7},{8,9},{10,11},{12,13},{14,15},{1,14},{3,0}... | collective-permute-start | bytes 663560 | tf_op jit(solution)/shard_map/ppermute | solution.py:435
  141.2 15.0 %copy-start.7 = (bf16[12,2304]{1,0:T(8,128)(2,1)S(1)}, bf16[12,2304]{1,0:T(8,128)(2,1)}, u32[]{:S(2)}) copy-start(bf16[12,2304]{1,0:T(8,128)(2,1)} %tokens_ref.3) | copy-start | bytes 165892
  141.2 15.0 %copy-start.9 = (f32[2304]{0:T(1024)S(1)}, f32[2304]{0:T(1024)}, u32[]{:S(2)}) copy-start(f32[2304]{0:T(1024)} %gain_ref.3) | copy-start | bytes 27652
  144.5 1.0 copy-start.5
Sparse Core Ops, SparseCore 0:
  20.4 48.7 all-gather.1
  91.7 44.1 reduce-scatter.1

commit v11 on v10

--- a/solution.py
+++ b/solution.py
@@ -156,31 +156,38 @@
     )(raw)
 
 
-def sort_hidden_kernel(main, tail, rows_each, found_ref, out_ref):
-    blocks, half, _ = out_ref.shape
+def sort_hidden_kernel(main, tail, rows_each, place_ref, found_ref, *refs):
+    outs, got_ref = refs[:-1], refs[-1]
+    blocks = len(outs)
+    half = outs[0].shape[0]
+    me = place_ref[2]
     size = SORTED * rows_each
     order = shuffle(blocks * size, blocks, SORTED, rows_each)
     for g in range(2 * half // size):
         h, at = g * size // half, g * size % half
         rows = slice(g * blocks * size, (g + 1) * blocks * size)
-        for lanes, first, width in (
-            (slice(0, main), h * main, main), (slice(main, main + tail), 2 * main + h * tail, tail)
-        ):
-            got = jnp.dot(order, found_ref[rows, lanes], preferred_element_type=F32).astype(BF16)
-            for x in range(blocks):
-                out_ref[x, at : at + size, first : first + width] = got[x * size : (x + 1) * size]
-
-
-def sort_hidden(found, blocks, rows_each):
+        got = jnp.dot(order, found_ref[rows, :], preferred_element_type=F32)
+        got_ref[...] = got.astype(BF16)
+        for s, out_ref in enumerate(outs):
+            x = lax.rem(me + s, blocks)
+            block = got_ref[pl.ds(pl.multiple_of(x * size, 16), size), :]
+            out_ref[at : at + size, h * main : (h + 1) * main] = block[:, :main]
+            first = 2 * main + h * tail
+            out_ref[at : at + size, first : first + tail] = block[:, main:]
+
+
+def sort_hidden(place, found, blocks, rows_each):
     pool, part = found.shape
     main = part // 128 * 128
+    out = jax.ShapeDtypeStruct((pool // blocks // 2, 2 * part), BF16)
     return pl.pallas_call(
         functools.partial(sort_hidden_kernel, main, part - main, rows_each),
-        out_shape=jax.ShapeDtypeStruct((blocks, pool // blocks // 2, 2 * part), BF16),
-        in_specs=[VMEM],
-        out_specs=VMEM,
+        out_shape=(out,) * blocks,
+        in_specs=[SMEM, VMEM],
+        out_specs=(VMEM,) * blocks,
+        scratch_shapes=[pltpu.VMEM((blocks * SORTED * rows_each, part), BF16)],
         compiler_params=params(16),
-    )(found)
+    )(place, found)
 
 
 def forward_kernel(
@@ -377,8 +384,11 @@
         up_ref[:, start : start + tail] = grad[:, 2 * main + tail :]
 
 
-def spread_kernel(main, tail, got_ref, out_ref):
+def spread_kernel(main, tail, place_ref, *refs):
+    sources, out_ref, got_ref = refs[:-2], refs[-2], refs[-1]
     nx, half, _ = got_ref.shape
+    for s, source in enumerate(sources):
+        got_ref[lax.rem(place_ref[2] - s + nx, nx)] = source[...]
     for q in range(nx):
         start = nx * main + q * tail
         for h in range(2):
@@ -423,12 +433,16 @@
         def term(i):
             return keep[i].astype(F32) + taken[i].astype(F32)
 
-        hidden = exchange(sort_hidden(found, nx, rows), "x")
+        hidden = list(sort_hidden(place, found, nx, rows))
         partial = term(0).astype(BF16)
         for i in range(1, ny // 2):
             partial = lax.ppermute(partial, ("y", "k"), both_ways(ny))
+            if i < nx:
+                hidden[i] = lax.ppermute(hidden[i], "x", ring(nx, i))
+                partial, hidden[i] = lax.optimization_barrier((partial, hidden[i]))
             partial = (partial.astype(F32) + term(i)).astype(BF16)
-        partial, hidden = lax.optimization_barrier((partial, hidden))
+        for i in range(ny // 2, nx):
+            hidden[i] = lax.ppermute(hidden[i], "x", ring(nx, i))
         step = partial.shape[0] // 2
         lower, upper = partial[:step], partial[step:]
         core = lax.axis_index("k")
@@ -444,10 +458,11 @@
         hidden = pl.pallas_call(
             functools.partial(spread_kernel, main, tail),
             out_shape=jax.ShapeDtypeStruct((own_tokens, units), BF16),
-            in_specs=[VMEM],
+            in_specs=[SMEM] + [VMEM] * nx,
             out_specs=VMEM,
+            scratch_shapes=[pltpu.VMEM((nx, own_tokens // 2, pair), BF16)],
             compiler_params=params(8),
-        )(hidden)
+        )(place, *hidden)
         hidden, near, far = lax.optimization_barrier((hidden, near, far))
         last = pl.pallas_call(
             functools.partial(gather_kernel, nx, rows, wide, thin),

time: 167 us -> 165 us (0.988); the launches traced: 164 us -> 164 us
  waiting for transfers between devices: 39.9 us -> 32.4 us
  starting transfers between devices: 53.2 us -> 57.8 us
  blocking collectives: 20.3 us -> 23.1 us
    ppermute x0 -> x3, starting transfers between devices: none -> 11.3 us  [per_device(): hidden[i] = lax.ppermute(hidden[i], 'x', ring(nx, i))]
    ppermute x0 -> x3, waiting for transfers between devices: none -> 11.2 us  [per_device(): hidden[i] = lax.ppermute(hidden[i], 'x', ring(nx, i))]
    ppermute x3, waiting for transfers between devices: 10.5 us -> 0.01 us  [per_device(): partial = lax.ppermute(partial, ('y', 'k'), both_ways(ny))]
    all_to_all x3 -> x2, waiting for transfers between devices: 14.2 us -> 6.43 us  [exchange(): return lax.all_to_all(value, axis, split_axis=0, concat_axis=0, tiled=True)]
    all_to_all x3 -> x2, starting transfers between devices: 12.3 us -> 7.89 us  [exchange(): return lax.all_to_all(value, axis, split_axis=0, concat_axis=0, tiled=True)]
    ppermute x3, starting transfers between devices: 15.5 us -> 11.8 us  [per_device(): partial = lax.ppermute(partial, ('y', 'k'), both_ways(ny))]
    all_to_all x2, blocking collectives: 20.3 us -> 23.1 us  [exchange(): return lax.all_to_all(value, axis, split_axis=0, concat_axis=0, tiled=True)]
    ppermute x1, waiting for transfers between devices: 1.89 us -> 0.01 us  [per_device(): lax.ppermute(upper, ('y', 'k'), [(2 * y + 1, 2 * ((y - 1) % ny) + 1) for...]
  transfers between devices with their start and end apart: 13 -> 15, of which waited for: 8 -> 7; matrix products, arithmetic and copies ran while one was open for 4% -> 3% of each run, Pallas kernels for 6% -> 6%
where the time goes in v11:
time: 165 us; the launch traced here: 164 us
  starting transfers between devices  57.8 us (35%)
  waiting for transfers between devices  32.4 us (20%)
  blocking collectives  23.1 us (14%)
  Pallas kernels  22.7 us (14%)
  between operations  14.3 us (9%)
  local copies, waits for them, and re-layouts  9.08 us (6%)
  other arithmetic  4.76 us (3%)
    all_to_all x2, blocking collectives, exchange(): return lax.all_to_all(value, axis, split_axis=0, concat_axis=0, tiled=True)  23.1 us
    ppermute x3, starting transfers between devices, per_device(): partial = lax.ppermute(partial, ('y', 'k'), both_ways(ny))  11.8 us
    ppermute x3, starting transfers between devices, per_device(): hidden[i] = lax.ppermute(hidden[i], 'x', ring(nx, i))  11.3 us
    ppermute x3, waiting for transfers between devices, per_device(): hidden[i] = lax.ppermute(hidden[i], 'x', ring(nx, i))  11.2 us
    ppermute x1, starting transfers between devices, per_device(): lax.ppermute(pack_weights(nx, gate_weight, up_weight, cut), ('c', 'l', 'k...  10.8 us
    pallas_call x1, Pallas kernels, forward(): pl.pallas_call(functools.partial(forward_kernel, chunk, main, part - main...  10.6 us
    ppermute x1, waiting for transfers between devices, per_device(): lax.ppermute(pack_weights(nx, gate_weight, up_weight, cut), ('c', 'l', 'k...  8.39 us
    all_to_all x2, starting transfers between devices, exchange(): return lax.all_to_all(value, axis, split_axis=0, concat_axis=0, tiled=True)  7.89 us
  transfers between devices with their start and end apart: 15, of which 7 were waited for; matrix products, arithmetic and copies ran while one was open for 3% of the time, Pallas kernels for 6%

profile of v11, /device:TPU:1, one launch (start us, length us, event | category | flops | bytes accessed | tf_op | source)
XLA Modules:
  0.0 164.2 jit_solution(7496653402817989826)
XLA Ops:
  9.1 10.3 %all_to_all.20 = bf16[4,12,2304]{2,1,0:T(8,128)(2,1)S(1)} all-to-all(bf16[4,12,2304]{2,1,0:T(8,128)(2,1)S(1)} %shard_map.84), channel_id=1, replica_groups=mesh['c'=4,'x'=4,'l'=2,'y'=8,'k'=2] {'x'}, dimensions={0} | all-to-all | bytes 442368 | tf_op jit(solution)/shard_map/all_to_all | solution.py:38
  20.3 1.4 shard_map.87
  21.7 3.7 %all-to-all-start.2 = ((bf16[4,288,576]{2,1,0:T(8,128)(2,1)}), bf16[4,288,576]{2,1,0:T(8,128)(2,1)S(1)}, u32[]{:S(2)}, u32[]{:S(2)}) async-start(bf16[4,288,576]{2,1,0:T(8,128)(2,1)} %shard_map.87), calls=%async_computation.2 | async-start | bytes 2949120 | tf_op jit(solution)/shard_map/all_to_all | solution.py:38
  25.6 10.8 %collective-permute-start = (bf16[4,144,576]{2,1,0:T(8,128)(2,1)S(1)}, bf16[4,144,576]{2,1,0:T(8,128)(2,1)S(1)}, u32[]{:S(2)}, u32[]{:S(2)}) collective-permute-start(bf16[4,144,576]{2,1,0:T(8,128)(2,1)S(1)} %shard_map.85), channel_id=1, source_target_pairs={{0,16},{16,128},{128,144},{144,256},{256,272},{272,384},{384,400},... | collective-permute-start | bytes 1990664 | tf_op jit(solution)/shard_map/ppermute | solution.py:418
  36.3 8.4 %collective-permute-done.weights_ref = bf16[4,144,576]{2,1,0:T(8,128)(2,1)S(1)} collective-permute-done((bf16[4,144,576]{2,1,0:T(8,128)(2,1)S(1)}, bf16[4,144,576]{2,1,0:T(8,128)(2,1)S(1)}, u32[]{:S(2)}, u32[]{:S(2)}) %collective-permute-start) | collective-permute-done | bytes 663584 | tf_op jit(solution)/shard_map/ppermute | solution.py:418
  44.7 1.3 shard_map.86
  46.0 4.2 %all-to-all-start.1 = ((bf16[4,272,576]{2,1,0:T(8,128)(2,1)}), bf16[4,272,576]{2,1,0:T(8,128)(2,1)S(1)}, u32[]{:S(2)}, u32[]{:S(2)}) async-start(bf16[4,272,576]{2,1,0:T(8,128)(2,1)} %shard_map.86), calls=%async_computation.1 | async-start | bytes 2785280 | tf_op jit(solution)/shard_map/all_to_all | solution.py:38
  51.2 7.0 %collective-permute-start.1 = (bf16[4,144,576]{2,1,0:T(8,128)(2,1)}, bf16[4,144,576]{2,1,0:T(8,128)(2,1)}, u32[]{:S(2)}, u32[]{:S(2)}) collective-permute-start(bf16[4,144,576]{2,1,0:T(8,128)(2,1)} %slice.44), channel_id=1, source_target_pairs={{0,16},{16,128},{128,144},{144,256},{256,272},{272,384},{384,400},... | collective-permute-start | bytes 1990664 | tf_op jit(solution)/shard_map/ppermute | solution.py:423
  58.3 6.4 %all-to-all-done.1.raw_ref.early_ref = bf16[4,272,576]{2,1,0:T(8,128)(2,1)S(1)} async-done(((bf16[4,272,576]{2,1,0:T(8,128)(2,1)}), bf16[4,272,576]{2,1,0:T(8,128)(2,1)S(1)}, u32[]{:S(2)}, u32[]{:S(2)}) %all-to-all-start.1) | async-done | bytes 1253408 | tf_op jit(solution)/shard_map/all_to_all | solution.py:38
  64.7 4.5 %all-gather.2.cloned.1.call-done.table_ref = bf16[768,2304]{1,0:T(8,128)(2,1)} async-done(((bf16[48,2304]{1,0:T(8,128)(2,1)}), bf16[768,2304]{1,0:T(8,128)(2,1)}) %all-gather.2.cloned.1.call-update) | async-done | bytes 3538960 | tf_op jit(solution)/shard_map/all_gather | solution.py:415
  69.6 2.0 %copy-done.10 = bf16[768,2304]{1,0:T(8,128)(2,1)S(1)} copy-done((bf16[768,2304]{1,0:T(8,128)(2,1)S(1)}, bf16[768,2304]{1,0:T(8,128)(2,1)}, u32[]{:S(2)}) %copy-start.10) | copy-done | bytes 3538968
  71.6 10.6 %shard_map.89 = (bf16[768,288]{1,0:T(8,128)(2,1)S(1)}, bf16[768,576]{1,0:T(8,128)(2,1)S(1)}, bf16[4,96,2304]{2,1,0:T(8,128)(2,1)S(1)}, bf16[4,96,2304]{2,1,0:T(8,128)(2,1)}) custom-call(s32[4]{0:T(128)S(1)} %pad_add_fusion.place_ref, bf16[768,2304]{1,0:T(8,128)(2,1)S(1)} %copy-done.10, bf16[4,288,576]{2,1,0:T(8,128)(2,1)S(1)} %all-to-all-done.2.own_ref, ...), custom_call_target="tpu_custom_call" | custom-call | flops 4076863488 | bytes 9732096 | tf_op jit(solution)/shard_map/pallas_call | solution.py:251
  82.2 1.3 copy-done.2
  83.5 3.6 %collective-permute-start.2 = (bf16[4,96,2304]{2,1,0:T(8,128)(2,1)}, bf16[4,96,2304]{2,1,0:T(8,128)(2,1)}, u32[]{:S(2)}, u32[]{:S(2)}) collective-permute-start(bf16[4,96,2304]{2,1,0:T(8,128)(2,1)} %get-tuple-element.33), channel_id=1, source_target_pairs={{0,1},{1,0},{2,3},{3,2},{4,5},{5,4},{6,7},{7,6},{8,9},{9,8},{10,11... | collective-permute-start | bytes 5308424 | tf_op jit(solution)/shard_map/ppermute | solution.py:428
  87.1 4.3 %shard_map.91 = bf16[2304,576]{1,0:T(8,128)(2,1)} custom-call(bf16[768,2304]{1,0:T(8,128)(2,1)S(1)} %copy-done.10, bf16[768,576]{1,0:T(8,128)(2,1)S(1)} %get-tuple-element.34.cots_ref), custom_call_target="tpu_custom_call" | custom-call | flops 2038431744 | bytes 6193152 | tf_op jit(solution)/shard_map/pallas_call | solution.py:297
  91.5 1.4 copy-done.3
  94.1 5.1 %collective-permute-start.3 = (bf16[96,2304]{1,0:T(8,128)(2,1)S(1)}, bf16[96,2304]{1,0:T(8,128)(2,1)S(1)}, u32[]{:S(2)}, u32[]{:S(2)}) collective-permute-start(bf16[96,2304]{1,0:T(8,128)(2,1)S(1)} %fusion.3), channel_id=1, source_target_pairs={{0,2},{2,4},{4,6},{6,8},{8,10},{10,12},{12,14},{14,0},{1,15},{3,1}... | collective-permute-start | bytes 1327112 | tf_op jit(solution)/shard_map/ppermute | solution.py:439
  100.3 3.6 %collective-permute-start.4 = (bf16[96,576]{1,0:T(8,128)(2,1)S(1)}, bf16[96,576]{1,0:T(8,128)(2,1)S(1)}, u32[]{:S(2)}, u32[]{:S(2)}) collective-permute-start(bf16[96,576]{1,0:T(8,128)(2,1)S(1)} %get-tuple-element.36), channel_id=1, source_target_pairs={{0,32},{32,64},{64,96},{96,0},{1,33},{33,65},{65,97},{97,1},{2,34}... | collective-permute-start | bytes 331784 | tf_op jit(solution)/shard_map/ppermute | solution.py:441
  103.8 3.5 %collective-permute-done.4.refs_1_ = bf16[96,576]{1,0:T(8,128)(2,1)S(1)} collective-permute-done((bf16[96,576]{1,0:T(8,128)(2,1)S(1)}, bf16[96,576]{1,0:T(8,128)(2,1)S(1)}, u32[]{:S(2)}, u32[]{:S(2)}) %collective-permute-start.4) | collective-permute-done | bytes 110624 | tf_op jit(solution)/shard_map/ppermute | solution.py:441
  108.5 3.5 %collective-permute-start.5 = (bf16[96,2304]{1,0:T(8,128)(2,1)S(1)}, bf16[96,2304]{1,0:T(8,128)(2,1)S(1)}, u32[]{:S(2)}, u32[]{:S(2)}) collective-permute-start(bf16[96,2304]{1,0:T(8,128)(2,1)S(1)} %fusion.2), channel_id=1, source_target_pairs={{0,2},{2,4},{4,6},{6,8},{8,10},{10,12},{12,14},{14,0},{1,15},{3,1}... | collective-permute-start | bytes 1327112 | tf_op jit(solution)/shard_map/ppermute | solution.py:439
  112.0 3.9 %collective-permute-start.6 = (bf16[96,576]{1,0:T(8,128)(2,1)S(1)}, bf16[96,576]{1,0:T(8,128)(2,1)S(1)}, u32[]{:S(2)}, u32[]{:S(2)}) collective-permute-start(bf16[96,576]{1,0:T(8,128)(2,1)S(1)} %get-tuple-element.39), channel_id=1, source_target_pairs={{0,64},{32,96},{64,0},{96,32},{1,65},{33,97},{65,1},{97,33},{2,66}... | collective-permute-start | bytes 331784 | tf_op jit(solution)/shard_map/ppermute | solution.py:441
  115.9 4.4 %collective-permute-done.6.refs_2_ = bf16[96,576]{1,0:T(8,128)(2,1)S(1)} collective-permute-done((bf16[96,576]{1,0:T(8,128)(2,1)S(1)}, bf16[96,576]{1,0:T(8,128)(2,1)S(1)}, u32[]{:S(2)}, u32[]{:S(2)}) %collective-permute-start.6) | collective-permute-done | bytes 110624 | tf_op jit(solution)/shard_map/ppermute | solution.py:441
  120.3 1.2 fusion.1
  121.5 3.2 %collective-permute-start.7 = (bf16[96,2304]{1,0:T(8,128)(2,1)S(1)}, bf16[96,2304]{1,0:T(8,128)(2,1)S(1)}, u32[]{:S(2)}, u32[]{:S(2)}) collective-permute-start(bf16[96,2304]{1,0:T(8,128)(2,1)S(1)} %fusion.1), channel_id=1, source_target_pairs={{0,2},{2,4},{4,6},{6,8},{8,10},{10,12},{12,14},{14,0},{1,15},{3,1}... | collective-permute-start | bytes 1327112 | tf_op jit(solution)/shard_map/ppermute | solution.py:439
  124.7 3.9 %collective-permute-start.8 = (bf16[96,576]{1,0:T(8,128)(2,1)S(1)}, bf16[96,576]{1,0:T(8,128)(2,1)S(1)}, u32[]{:S(2)}, u32[]{:S(2)}) collective-permute-start(bf16[96,576]{1,0:T(8,128)(2,1)S(1)} %get-tuple-element.42), channel_id=1, source_target_pairs={{0,96},{32,0},{64,32},{96,64},{1,97},{33,1},{65,33},{97,65},{2,98}... | collective-permute-start | bytes 331784 | tf_op jit(solution)/shard_map/ppermute | solution.py:441
  128.6 3.3 %collective-permute-done.8.refs_3_ = bf16[96,576]{1,0:T(8,128)(2,1)S(1)} collective-permute-done((bf16[96,576]{1,0:T(8,128)(2,1)S(1)}, bf16[96,576]{1,0:T(8,128)(2,1)S(1)}, u32[]{:S(2)}, u32[]{:S(2)}) %collective-permute-start.8) | collective-permute-done | bytes 110624 | tf_op jit(solution)/shard_map/ppermute | solution.py:441
  131.9 1.2 fusion.sums_ref
  133.1 3.5 %collective-permute-start.10 = (bf16[48,2304]{1,0:T(8,128)(2,1)S(1)}, bf16[48,2304]{1,0:T(8,128)(2,1)S(1)}, u32[]{:S(2)}, u32[]{:S(2)}) collective-permute-start(bf16[48,2304]{1,0:T(8,128)(2,1)S(1)} %get-tuple-element.52), channel_id=1, source_target_pairs={{1,15},{3,1},{5,3},{7,5},{9,7},{11,9},{13,11},{15,13},{17,31},{19,... | collective-permute-start | bytes 663560 | tf_op jit(solution)/shard_map/ppermute | solution.py:454
  136.6 1.9 %collective-permute-start.9 = (bf16[48,2304]{1,0:T(8,128)(2,1)S(1)}, bf16[48,2304]{1,0:T(8,128)(2,1)S(1)}, u32[]{:S(2)}, u32[]{:S(2)}) collective-permute-start(bf16[48,2304]{1,0:T(8,128)(2,1)S(1)} %get-tuple-element.53), channel_id=1, source_target_pairs={{0,1},{2,3},{4,5},{6,7},{8,9},{10,11},{12,13},{14,15},{1,14},{3,0}... | collective-permute-start | bytes 663560 | tf_op jit(solution)/shard_map/ppermute | solution.py:449
  138.5 1.5 shard_map.92
  140.0 1.8 %collective-permute-done.9.near_ref = bf16[48,2304]{1,0:T(8,128)(2,1)S(1)} collective-permute-done((bf16[48,2304]{1,0:T(8,128)(2,1)S(1)}, bf16[48,2304]{1,0:T(8,128)(2,1)S(1)}, u32[]{:S(2)}, u32[]{:S(2)}) %collective-permute-start.9) | collective-permute-done | bytes 221216 | tf_op jit(solution)/shard_map/ppermute | solution.py:449
  143.5 12.8 %all_to_all.21.got_ref = bf16[4,120,640]{2,1,0:T(8,128)(2,1)S(1)} all-to-all(bf16[4,120,640]{2,1,0:T(8,128)(2,1)S(1)} %shard_map.93), channel_id=1, replica_groups=mesh['c'=4,'x'=4,'l'=2,'y'=8,'k'=2] {'x'}, dimensions={0} | all-to-all | bytes 1228800 | tf_op jit(solution)/shard_map/all_to_all | solution.py:38
  (43 shorter events, 10.5 us)
Async XLA Ops:
  7.2 13.1 %copy-start.1 = (bf16[288,1152]{1,0:T(8,128)(2,1)S(1)}, bf16[288,1152]{1,0:T(8,128)(2,1)}, u32[]{:S(2)}) copy-start(bf16[288,1152]{1,0:T(8,128)(2,1)} %up_ref.3) | copy-start | bytes 1990660
  7.2 13.1 %copy-start = (bf16[288,1152]{1,0:T(8,128)(2,1)S(1)}, bf16[288,1152]{1,0:T(8,128)(2,1)}, u32[]{:S(2)}) copy-start(bf16[288,1152]{1,0:T(8,128)(2,1)} %gate_ref.3) | copy-start | bytes 1990660
  7.2 62.0 %all-gather.2.cloned.1.call-start = ((), (), s32[]{:S(2)}) async-start(), calls=%async_computation.5 | async-start | bytes 3760128 | tf_op jit(solution)/shard_map/all_gather | solution.py:415
  7.2 1.0 copy-start.6
  8.2 0.7 copy-start.8
  21.7 23.1 %copy-start.4 = (bf16[192,1152]{1,0:T(8,128)(2,1)S(1)}, bf16[192,1152]{1,0:T(8,128)(2,1)}, u32[]{:S(2)}) copy-start(bf16[192,1152]{1,0:T(8,128)(2,1)} %grad_ref.1) | copy-start | bytes 1327108
  21.7 24.3 %all-to-all-start.2 = ((bf16[4,288,576]{2,1,0:T(8,128)(2,1)}), bf16[4,288,576]{2,1,0:T(8,128)(2,1)S(1)}, u32[]{:S(2)}, u32[]{:S(2)}) async-start(bf16[4,288,576]{2,1,0:T(8,128)(2,1)} %shard_map.87), calls=%async_computation.2 | async-start | bytes 2949120 | tf_op jit(solution)/shard_map/all_to_all | solution.py:38
  25.6 19.2 %collective-permute-start = (bf16[4,144,576]{2,1,0:T(8,128)(2,1)S(1)}, bf16[4,144,576]{2,1,0:T(8,128)(2,1)S(1)}, u32[]{:S(2)}, u32[]{:S(2)}) collective-permute-start(bf16[4,144,576]{2,1,0:T(8,128)(2,1)S(1)} %shard_map.85), channel_id=1, source_target_pairs={{0,16},{16,128},{128,144},{144,256},{256,272},{272,384},{384,400},... | collective-permute-start | bytes 1990664 | tf_op jit(solution)/shard_map/ppermute | solution.py:418
  46.0 18.7 %all-to-all-start.1 = ((bf16[4,272,576]{2,1,0:T(8,128)(2,1)}), bf16[4,272,576]{2,1,0:T(8,128)(2,1)S(1)}, u32[]{:S(2)}, u32[]{:S(2)}) async-start(bf16[4,272,576]{2,1,0:T(8,128)(2,1)} %shard_map.86), calls=%async_computation.1 | async-start | bytes 2785280 | tf_op jit(solution)/shard_map/all_to_all | solution.py:38
  50.2 91.6 %reduce-scatter.2.cloned.1.call-start = ((), (), s32[]{:S(2)}) async-start(), calls=%async_computation.6 | async-start | bytes 3317760 | tf_op jit(solution)/shard_map/reduce_scatter | solution.py:431
  51.2 18.4 %collective-permute-start.1 = (bf16[4,144,576]{2,1,0:T(8,128)(2,1)}, bf16[4,144,576]{2,1,0:T(8,128)(2,1)}, u32[]{:S(2)}, u32[]{:S(2)}) collective-permute-start(bf16[4,144,576]{2,1,0:T(8,128)(2,1)} %slice.44), channel_id=1, source_target_pairs={{0,16},{16,128},{128,144},{144,256},{256,272},{272,384},{384,400},... | collective-permute-start | bytes 1990664 | tf_op jit(solution)/shard_map/ppermute | solution.py:423
  69.6 2.0 %copy-start.10 = (bf16[768,2304]{1,0:T(8,128)(2,1)S(1)}, bf16[768,2304]{1,0:T(8,128)(2,1)}, u32[]{:S(2)}) copy-start(bf16[768,2304]{1,0:T(8,128)(2,1)} %all-gather.2.cloned.1.call-done.table_ref) | copy-start | bytes 10616836
  82.2 1.3 copy-start.2
  83.5 8.0 %collective-permute-start.2 = (bf16[4,96,2304]{2,1,0:T(8,128)(2,1)}, bf16[4,96,2304]{2,1,0:T(8,128)(2,1)}, u32[]{:S(2)}, u32[]{:S(2)}) collective-permute-start(bf16[4,96,2304]{2,1,0:T(8,128)(2,1)} %get-tuple-element.33), channel_id=1, source_target_pairs={{0,1},{1,0},{2,3},{3,2},{4,5},{5,4},{6,7},{7,6},{8,9},{9,8},{10,11... | collective-permute-start | bytes 5308424 | tf_op jit(solution)/shard_map/ppermute | solution.py:428
  91.5 1.5 copy-start.3
  94.1 13.2 %collective-permute-start.3 = (bf16[96,2304]{1,0:T(8,128)(2,1)S(1)}, bf16[96,2304]{1,0:T(8,128)(2,1)S(1)}, u32[]{:S(2)}, u32[]{:S(2)}) collective-permute-start(bf16[96,2304]{1,0:T(8,128)(2,1)S(1)} %fusion.3), channel_id=1, source_target_pairs={{0,2},{2,4},{4,6},{6,8},{8,10},{10,12},{12,14},{14,0},{1,15},{3,1}... | collective-permute-start | bytes 1327112 | tf_op jit(solution)/shard_map/ppermute | solution.py:439
  100.3 7.0 %collective-permute-start.4 = (bf16[96,576]{1,0:T(8,128)(2,1)S(1)}, bf16[96,576]{1,0:T(8,128)(2,1)S(1)}, u32[]{:S(2)}, u32[]{:S(2)}) collective-permute-start(bf16[96,576]{1,0:T(8,128)(2,1)S(1)} %get-tuple-element.36), channel_id=1, source_target_pairs={{0,32},{32,64},{64,96},{96,0},{1,33},{33,65},{65,97},{97,1},{2,34}... | collective-permute-start | bytes 331784 | tf_op jit(solution)/shard_map/ppermute | solution.py:441
  108.5 11.8 %collective-permute-start.5 = (bf16[96,2304]{1,0:T(8,128)(2,1)S(1)}, bf16[96,2304]{1,0:T(8,128)(2,1)S(1)}, u32[]{:S(2)}, u32[]{:S(2)}) collective-permute-start(bf16[96,2304]{1,0:T(8,128)(2,1)S(1)} %fusion.2), channel_id=1, source_target_pairs={{0,2},{2,4},{4,6},{6,8},{8,10},{10,12},{12,14},{14,0},{1,15},{3,1}... | collective-permute-start | bytes 1327112 | tf_op jit(solution)/shard_map/ppermute | solution.py:439
  112.0 8.3 %collective-permute-start.6 = (bf16[96,576]{1,0:T(8,128)(2,1)S(1)}, bf16[96,576]{1,0:T(8,128)(2,1)S(1)}, u32[]{:S(2)}, u32[]{:S(2)}) collective-permute-start(bf16[96,576]{1,0:T(8,128)(2,1)S(1)} %get-tuple-element.39), channel_id=1, source_target_pairs={{0,64},{32,96},{64,0},{96,32},{1,65},{33,97},{65,1},{97,33},{2,66}... | collective-permute-start | bytes 331784 | tf_op jit(solution)/shard_map/ppermute | solution.py:441
  121.5 10.4 %collective-permute-start.7 = (bf16[96,2304]{1,0:T(8,128)(2,1)S(1)}, bf16[96,2304]{1,0:T(8,128)(2,1)S(1)}, u32[]{:S(2)}, u32[]{:S(2)}) collective-permute-start(bf16[96,2304]{1,0:T(8,128)(2,1)S(1)} %fusion.1), channel_id=1, source_target_pairs={{0,2},{2,4},{4,6},{6,8},{8,10},{10,12},{12,14},{14,0},{1,15},{3,1}... | collective-permute-start | bytes 1327112 | tf_op jit(solution)/shard_map/ppermute | solution.py:439
  124.7 7.2 %collective-permute-start.8 = (bf16[96,576]{1,0:T(8,128)(2,1)S(1)}, bf16[96,576]{1,0:T(8,128)(2,1)S(1)}, u32[]{:S(2)}, u32[]{:S(2)}) collective-permute-start(bf16[96,576]{1,0:T(8,128)(2,1)S(1)} %get-tuple-element.42), channel_id=1, source_target_pairs={{0,96},{32,0},{64,32},{96,64},{1,97},{33,1},{65,33},{97,65},{2,98}... | collective-permute-start | bytes 331784 | tf_op jit(solution)/shard_map/ppermute | solution.py:441
  133.1 6.9 %collective-permute-start.10 = (bf16[48,2304]{1,0:T(8,128)(2,1)S(1)}, bf16[48,2304]{1,0:T(8,128)(2,1)S(1)}, u32[]{:S(2)}, u32[]{:S(2)}) collective-permute-start(bf16[48,2304]{1,0:T(8,128)(2,1)S(1)} %get-tuple-element.52), channel_id=1, source_target_pairs={{1,15},{3,1},{5,3},{7,5},{9,7},{11,9},{13,11},{15,13},{17,31},{19,... | collective-permute-start | bytes 663560 | tf_op jit(solution)/shard_map/ppermute | solution.py:454
  136.6 5.2 %collective-permute-start.9 = (bf16[48,2304]{1,0:T(8,128)(2,1)S(1)}, bf16[48,2304]{1,0:T(8,128)(2,1)S(1)}, u32[]{:S(2)}, u32[]{:S(2)}) collective-permute-start(bf16[48,2304]{1,0:T(8,128)(2,1)S(1)} %get-tuple-element.53), channel_id=1, source_target_pairs={{0,1},{2,3},{4,5},{6,7},{8,9},{10,11},{12,13},{14,15},{1,14},{3,0}... | collective-permute-start | bytes 663560 | tf_op jit(solution)/shard_map/ppermute | solution.py:449
  138.5 17.7 %copy-start.7 = (bf16[12,2304]{1,0:T(8,128)(2,1)S(1)}, bf16[12,2304]{1,0:T(8,128)(2,1)}, u32[]{:S(2)}) copy-start(bf16[12,2304]{1,0:T(8,128)(2,1)} %tokens_ref.3) | copy-start | bytes 165892
  138.5 17.7 %copy-start.9 = (f32[2304]{0:T(1024)S(1)}, f32[2304]{0:T(1024)}, u32[]{:S(2)}) copy-start(f32[2304]{0:T(1024)} %gain_ref.3) | copy-start | bytes 27652
  141.8 1.0 copy-start.5
Sparse Core Ops, SparseCore 0:
  20.4 48.7 all-gather.1
  91.6 44.1 reduce-scatter.1

commit v12 on v11

--- a/solution.py
+++ b/solution.py
@@ -191,14 +191,16 @@
 
 
 def forward_kernel(
-    chunk, main, tail, place_ref, table_ref, own_ref, early_ref, late_ref, grads_ref,
-    found_ref, cots_ref, keep_ref, give_ref, matrix,
+    chunk, main, tail, place_ref, table_any, own_ref, early_ref, late_ref, grads_ref,
+    found_ref, cots_ref, keep_ref, give_ref, table_ref, matrix, sem,
 ):
     blocks, feats, pair = own_ref.shape
     cut = feats - late_ref.shape[1]
     pool, width = table_ref.shape
     low, core, me = place_ref[0], place_ref[1], place_ref[3]
     chain, step, _ = keep_ref.shape
+    fetch = pltpu.make_async_copy(table_any, table_ref, sem)
+    fetch.start()
     near = low * (width // 2)
     far = (1 - low) * (width // 2)
     for x in range(blocks):
@@ -208,6 +210,7 @@
             (far + x * feats + cut, feats - cut, late_ref[x]),
         ):
             matrix[pl.ds(pl.multiple_of(first, 16), size), :] = rows
+    fetch.wait()
     for first in range(0, pool, chunk):
         rows = slice(first, first + chunk)
         both = jnp.dot(table_ref[rows, :], matrix[...], preferred_element_type=F32)
@@ -256,10 +259,14 @@
             jax.ShapeDtypeStruct((ny // 2, step, width), BF16),
             jax.ShapeDtypeStruct((ny // 2, step, width), BF16),
         ),
-        in_specs=[SMEM, VMEM, VMEM, VMEM, VMEM, VMEM],
+        in_specs=[SMEM, ANY, VMEM, VMEM, VMEM, VMEM],
         out_specs=(VMEM, VMEM, VMEM, VMEM),
-        scratch_shapes=[pltpu.VMEM((width, pair), BF16)],
-        compiler_params=params(32),
+        scratch_shapes=[
+            pltpu.VMEM((pool, width), BF16),
+            pltpu.VMEM((width, pair), BF16),
+            pltpu.SemaphoreType.DMA,
+        ],
+        compiler_params=params(44),
         cost_estimate=pl.CostEstimate(
             flops=4 * pool * width * pair, bytes_accessed=2 * (2 * pool * width + width * pair), transcendentals=0
         ),
@@ -421,7 +428,7 @@
         own = exchange(pack_weights(nx, gate_weight, up_weight, feats), "x")
         early = exchange(pack_grads(nx, early, hidden_grad), "x")
         late = lax.ppermute(own[:, cut:], ("c", "l", "k"), both_ways(nz))
-        table, early = lax.optimization_barrier((table, early))
+        table, early, late = lax.optimization_barrier((table, early, late))
         grads = sort_grads(early, cut, own_tokens, rows)
 
         found, cots, keep, give = forward(place, table, own, early, late, grads, ny, pool)

time: 165 us -> 165 us (level)
  Pallas kernels: 22.7 us -> 24.7 us
  local copies, waits for them, and re-layouts: 9.08 us -> 7.08 us
    all_gather x1, waiting for transfers between devices: 4.48 us -> 2.29 us  [per_device(): table = lax.all_gather(near, ('y', 'k'), axis=0, tiled=True)]
    ppermute x1, waiting for transfers between devices: 0.01 us -> 2.19 us  [per_device(): late = lax.ppermute(own[:, cut:], ('c', 'l', 'k'), both_ways(nz))]
    unnamed x22, local copies, waits for them, and re-layouts: 7.4 us -> 5.4 us
    pallas_call x1, Pallas kernels: 10.6 us -> 12.6 us  [forward(): pl.pallas_call(functools.partial(forward_kernel, chunk, main, part - main...]
  transfers between devices with their start and end apart: 15 -> 15, of which waited for: 7 -> 8; matrix products, arithmetic and copies ran while one was open for 3% -> 3% of each run, Pallas kernels for 6% -> 6%
where the time goes in v12:
time: 165 us; the launch traced here: 164 us
  starting transfers between devices  58.2 us (35%)
  waiting for transfers between devices  32.4 us (20%)
  Pallas kernels  24.7 us (15%)
  blocking collectives  22.6 us (14%)
  between operations  14.3 us (9%)
  local copies, waits for them, and re-layouts  7.08 us (4%)
  other arithmetic  4.76 us (3%)
    all_to_all x2, blocking collectives, exchange(): return lax.all_to_all(value, axis, split_axis=0, concat_axis=0, tiled=True)  22.6 us
    pallas_call x1, Pallas kernels, forward(): pl.pallas_call(functools.partial(forward_kernel, chunk, main, part - main...  12.6 us
    ppermute x3, starting transfers between devices, per_device(): partial = lax.ppermute(partial, ('y', 'k'), both_ways(ny))  11.8 us
    ppermute x3, starting transfers between devices, per_device(): hidden[i] = lax.ppermute(hidden[i], 'x', ring(nx, i))  11.3 us
    ppermute x3, waiting for transfers between devices, per_device(): hidden[i] = lax.ppermute(hidden[i], 'x', ring(nx, i))  11.3 us
    ppermute x1, starting transfers between devices, per_device(): lax.ppermute(pack_weights(nx, gate_weight, up_weight, cut), ('c', 'l', 'k...  10.8 us
    ppermute x1, waiting for transfers between devices, per_device(): lax.ppermute(pack_weights(nx, gate_weight, up_weight, cut), ('c', 'l', 'k...  8.39 us
    all_to_all x2, starting transfers between devices, exchange(): return lax.all_to_all(value, axis, split_axis=0, concat_axis=0, tiled=True)  7.89 us
  transfers between devices with their start and end apart: 15, of which 8 were waited for; matrix products, arithmetic and copies ran while one was open for 3% of the time, Pallas kernels for 6%

profile of v12, /device:TPU:1, one launch (start us, length us, event | category | flops | bytes accessed | tf_op | source)
XLA Modules:
  0.0 164.1 jit_solution(13122101748915023321)
XLA Ops:
  9.1 10.3 %all_to_all.20 = bf16[4,12,2304]{2,1,0:T(8,128)(2,1)S(1)} all-to-all(bf16[4,12,2304]{2,1,0:T(8,128)(2,1)S(1)} %shard_map.84), channel_id=1, replica_groups=mesh['c'=4,'x'=4,'l'=2,'y'=8,'k'=2] {'x'}, dimensions={0} | all-to-all | bytes 442368 | tf_op jit(solution)/shard_map/all_to_all | solution.py:38
  20.3 1.4 shard_map.87
  21.7 3.7 %all-to-all-start.2 = ((bf16[4,288,576]{2,1,0:T(8,128)(2,1)}), bf16[4,288,576]{2,1,0:T(8,128)(2,1)S(1)}, u32[]{:S(2)}, u32[]{:S(2)}) async-start(bf16[4,288,576]{2,1,0:T(8,128)(2,1)} %shard_map.87), calls=%async_computation.2 | async-start | bytes 2949120 | tf_op jit(solution)/shard_map/all_to_all | solution.py:38
  25.6 10.8 %collective-permute-start = (bf16[4,144,576]{2,1,0:T(8,128)(2,1)S(1)}, bf16[4,144,576]{2,1,0:T(8,128)(2,1)S(1)}, u32[]{:S(2)}, u32[]{:S(2)}) collective-permute-start(bf16[4,144,576]{2,1,0:T(8,128)(2,1)S(1)} %shard_map.85), channel_id=1, source_target_pairs={{0,16},{16,128},{128,144},{144,256},{256,272},{272,384},{384,400},... | collective-permute-start | bytes 1990664 | tf_op jit(solution)/shard_map/ppermute | solution.py:425
  36.3 8.4 %collective-permute-done.weights_ref = bf16[4,144,576]{2,1,0:T(8,128)(2,1)S(1)} collective-permute-done((bf16[4,144,576]{2,1,0:T(8,128)(2,1)S(1)}, bf16[4,144,576]{2,1,0:T(8,128)(2,1)S(1)}, u32[]{:S(2)}, u32[]{:S(2)}) %collective-permute-start) | collective-permute-done | bytes 663584 | tf_op jit(solution)/shard_map/ppermute | solution.py:425
  44.7 1.3 shard_map.86
  46.0 4.2 %all-to-all-start.1 = ((bf16[4,272,576]{2,1,0:T(8,128)(2,1)}), bf16[4,272,576]{2,1,0:T(8,128)(2,1)S(1)}, u32[]{:S(2)}, u32[]{:S(2)}) async-start(bf16[4,272,576]{2,1,0:T(8,128)(2,1)} %shard_map.86), calls=%async_computation.1 | async-start | bytes 2785280 | tf_op jit(solution)/shard_map/all_to_all | solution.py:38
  51.2 7.0 %collective-permute-start.1 = (bf16[4,144,576]{2,1,0:T(8,128)(2,1)}, bf16[4,144,576]{2,1,0:T(8,128)(2,1)}, u32[]{:S(2)}, u32[]{:S(2)}) collective-permute-start(bf16[4,144,576]{2,1,0:T(8,128)(2,1)} %slice.44), channel_id=1, source_target_pairs={{0,16},{16,128},{128,144},{144,256},{256,272},{272,384},{384,400},... | collective-permute-start | bytes 1990664 | tf_op jit(solution)/shard_map/ppermute | solution.py:430
  58.3 6.4 %all-to-all-done.1.raw_ref.early_ref = bf16[4,272,576]{2,1,0:T(8,128)(2,1)S(1)} async-done(((bf16[4,272,576]{2,1,0:T(8,128)(2,1)}), bf16[4,272,576]{2,1,0:T(8,128)(2,1)S(1)}, u32[]{:S(2)}, u32[]{:S(2)}) %all-to-all-start.1) | async-done | bytes 1253408 | tf_op jit(solution)/shard_map/all_to_all | solution.py:38
  64.7 2.2 %collective-permute-done.1.late_ref = bf16[4,144,576]{2,1,0:T(8,128)(2,1)} collective-permute-done((bf16[4,144,576]{2,1,0:T(8,128)(2,1)}, bf16[4,144,576]{2,1,0:T(8,128)(2,1)}, u32[]{:S(2)}, u32[]{:S(2)}) %collective-permute-start.1) | collective-permute-done | bytes 663584 | tf_op jit(solution)/shard_map/ppermute | solution.py:430
  66.9 2.3 %all-gather.2.cloned.1.call-done.table_any.table_ref = bf16[768,2304]{1,0:T(8,128)(2,1)} async-done(((bf16[48,2304]{1,0:T(8,128)(2,1)}), bf16[768,2304]{1,0:T(8,128)(2,1)}) %all-gather.2.cloned.1.call-update) | async-done | bytes 3538960 | tf_op jit(solution)/shard_map/all_gather | solution.py:422
  69.6 12.6 %shard_map.89 = (bf16[768,288]{1,0:T(8,128)(2,1)S(1)}, bf16[768,576]{1,0:T(8,128)(2,1)S(1)}, bf16[4,96,2304]{2,1,0:T(8,128)(2,1)S(1)}, bf16[4,96,2304]{2,1,0:T(8,128)(2,1)}) custom-call(s32[4]{0:T(128)S(1)} %pad_add_fusion.place_ref, bf16[768,2304]{1,0:T(8,128)(2,1)} %all-gather.2.cloned.1.call-done.table_any.table_ref, ...), custom_call_target="tpu_custom_call" | custom-call | flops 4076863488 | bytes 9732096 | tf_op jit(solution)/shard_map/pallas_call | solution.py:254
  82.2 1.3 copy-done.2
  83.4 4.0 %collective-permute-start.2 = (bf16[4,96,2304]{2,1,0:T(8,128)(2,1)}, bf16[4,96,2304]{2,1,0:T(8,128)(2,1)}, u32[]{:S(2)}, u32[]{:S(2)}) collective-permute-start(bf16[4,96,2304]{2,1,0:T(8,128)(2,1)} %get-tuple-element.35), channel_id=1, source_target_pairs={{0,1},{1,0},{2,3},{3,2},{4,5},{5,4},{6,7},{7,6},{8,9},{9,8},{10,11... | collective-permute-start | bytes 5308424 | tf_op jit(solution)/shard_map/ppermute | solution.py:435
  87.5 4.4 %shard_map.91 = bf16[2304,576]{1,0:T(8,128)(2,1)} custom-call(bf16[768,2304]{1,0:T(8,128)(2,1)S(1)} %copy-done.10, bf16[768,576]{1,0:T(8,128)(2,1)S(1)} %get-tuple-element.36.cots_ref), custom_call_target="tpu_custom_call" | custom-call | flops 2038431744 | bytes 6193152 | tf_op jit(solution)/shard_map/pallas_call | solution.py:304
  91.9 1.4 copy-done.3
  94.4 5.1 %collective-permute-start.3 = (bf16[96,2304]{1,0:T(8,128)(2,1)S(1)}, bf16[96,2304]{1,0:T(8,128)(2,1)S(1)}, u32[]{:S(2)}, u32[]{:S(2)}) collective-permute-start(bf16[96,2304]{1,0:T(8,128)(2,1)S(1)} %fusion.3), channel_id=1, source_target_pairs={{0,2},{2,4},{4,6},{6,8},{8,10},{10,12},{12,14},{14,0},{1,15},{3,1}... | collective-permute-start | bytes 1327112 | tf_op jit(solution)/shard_map/ppermute | solution.py:446
  100.6 3.6 %collective-permute-start.4 = (bf16[96,576]{1,0:T(8,128)(2,1)S(1)}, bf16[96,576]{1,0:T(8,128)(2,1)S(1)}, u32[]{:S(2)}, u32[]{:S(2)}) collective-permute-start(bf16[96,576]{1,0:T(8,128)(2,1)S(1)} %get-tuple-element.38), channel_id=1, source_target_pairs={{0,32},{32,64},{64,96},{96,0},{1,33},{33,65},{65,97},{97,1},{2,34}... | collective-permute-start | bytes 331784 | tf_op jit(solution)/shard_map/ppermute | solution.py:448
  104.2 3.5 %collective-permute-done.4.refs_1_ = bf16[96,576]{1,0:T(8,128)(2,1)S(1)} collective-permute-done((bf16[96,576]{1,0:T(8,128)(2,1)S(1)}, bf16[96,576]{1,0:T(8,128)(2,1)S(1)}, u32[]{:S(2)}, u32[]{:S(2)}) %collective-permute-start.4) | collective-permute-done | bytes 110624 | tf_op jit(solution)/shard_map/ppermute | solution.py:448
  108.9 3.5 %collective-permute-start.5 = (bf16[96,2304]{1,0:T(8,128)(2,1)S(1)}, bf16[96,2304]{1,0:T(8,128)(2,1)S(1)}, u32[]{:S(2)}, u32[]{:S(2)}) collective-permute-start(bf16[96,2304]{1,0:T(8,128)(2,1)S(1)} %fusion.2), channel_id=1, source_target_pairs={{0,2},{2,4},{4,6},{6,8},{8,10},{10,12},{12,14},{14,0},{1,15},{3,1}... | collective-permute-start | bytes 1327112 | tf_op jit(solution)/shard_map/ppermute | solution.py:446
  112.4 3.9 %collective-permute-start.6 = (bf16[96,576]{1,0:T(8,128)(2,1)S(1)}, bf16[96,576]{1,0:T(8,128)(2,1)S(1)}, u32[]{:S(2)}, u32[]{:S(2)}) collective-permute-start(bf16[96,576]{1,0:T(8,128)(2,1)S(1)} %get-tuple-element.41), channel_id=1, source_target_pairs={{0,64},{32,96},{64,0},{96,32},{1,65},{33,97},{65,1},{97,33},{2,66}... | collective-permute-start | bytes 331784 | tf_op jit(solution)/shard_map/ppermute | solution.py:448
  116.2 4.4 %collective-permute-done.6.refs_2_ = bf16[96,576]{1,0:T(8,128)(2,1)S(1)} collective-permute-done((bf16[96,576]{1,0:T(8,128)(2,1)S(1)}, bf16[96,576]{1,0:T(8,128)(2,1)S(1)}, u32[]{:S(2)}, u32[]{:S(2)}) %collective-permute-start.6) | collective-permute-done | bytes 110624 | tf_op jit(solution)/shard_map/ppermute | solution.py:448
  120.7 1.2 fusion.1
  121.9 3.2 %collective-permute-start.7 = (bf16[96,2304]{1,0:T(8,128)(2,1)S(1)}, bf16[96,2304]{1,0:T(8,128)(2,1)S(1)}, u32[]{:S(2)}, u32[]{:S(2)}) collective-permute-start(bf16[96,2304]{1,0:T(8,128)(2,1)S(1)} %fusion.1), channel_id=1, source_target_pairs={{0,2},{2,4},{4,6},{6,8},{8,10},{10,12},{12,14},{14,0},{1,15},{3,1}... | collective-permute-start | bytes 1327112 | tf_op jit(solution)/shard_map/ppermute | solution.py:446
  125.1 3.8 %collective-permute-start.8 = (bf16[96,576]{1,0:T(8,128)(2,1)S(1)}, bf16[96,576]{1,0:T(8,128)(2,1)S(1)}, u32[]{:S(2)}, u32[]{:S(2)}) collective-permute-start(bf16[96,576]{1,0:T(8,128)(2,1)S(1)} %get-tuple-element.44), channel_id=1, source_target_pairs={{0,96},{32,0},{64,32},{96,64},{1,97},{33,1},{65,33},{97,65},{2,98}... | collective-permute-start | bytes 331784 | tf_op jit(solution)/shard_map/ppermute | solution.py:448
  129.0 3.4 %collective-permute-done.8.refs_3_ = bf16[96,576]{1,0:T(8,128)(2,1)S(1)} collective-permute-done((bf16[96,576]{1,0:T(8,128)(2,1)S(1)}, bf16[96,576]{1,0:T(8,128)(2,1)S(1)}, u32[]{:S(2)}, u32[]{:S(2)}) %collective-permute-start.8) | collective-permute-done | bytes 110624 | tf_op jit(solution)/shard_map/ppermute | solution.py:448
  132.3 1.2 fusion.sums_ref
  133.5 3.4 %collective-permute-start.10 = (bf16[48,2304]{1,0:T(8,128)(2,1)S(1)}, bf16[48,2304]{1,0:T(8,128)(2,1)S(1)}, u32[]{:S(2)}, u32[]{:S(2)}) collective-permute-start(bf16[48,2304]{1,0:T(8,128)(2,1)S(1)} %get-tuple-element.54), channel_id=1, source_target_pairs={{1,15},{3,1},{5,3},{7,5},{9,7},{11,9},{13,11},{15,13},{17,31},{19,... | collective-permute-start | bytes 663560 | tf_op jit(solution)/shard_map/ppermute | solution.py:461
  137.0 1.9 %collective-permute-start.9 = (bf16[48,2304]{1,0:T(8,128)(2,1)S(1)}, bf16[48,2304]{1,0:T(8,128)(2,1)S(1)}, u32[]{:S(2)}, u32[]{:S(2)}) collective-permute-start(bf16[48,2304]{1,0:T(8,128)(2,1)S(1)} %get-tuple-element.55), channel_id=1, source_target_pairs={{0,1},{2,3},{4,5},{6,7},{8,9},{10,11},{12,13},{14,15},{1,14},{3,0}... | collective-permute-start | bytes 663560 | tf_op jit(solution)/shard_map/ppermute | solution.py:456
  138.9 1.5 shard_map.92
  140.4 1.8 %collective-permute-done.9.near_ref = bf16[48,2304]{1,0:T(8,128)(2,1)S(1)} collective-permute-done((bf16[48,2304]{1,0:T(8,128)(2,1)S(1)}, bf16[48,2304]{1,0:T(8,128)(2,1)S(1)}, u32[]{:S(2)}, u32[]{:S(2)}) %collective-permute-start.9) | collective-permute-done | bytes 221216 | tf_op jit(solution)/shard_map/ppermute | solution.py:456
  143.9 12.3 %all_to_all.21.got_ref = bf16[4,120,640]{2,1,0:T(8,128)(2,1)S(1)} all-to-all(bf16[4,120,640]{2,1,0:T(8,128)(2,1)S(1)} %shard_map.93), channel_id=1, replica_groups=mesh['c'=4,'x'=4,'l'=2,'y'=8,'k'=2] {'x'}, dimensions={0} | all-to-all | bytes 1228800 | tf_op jit(solution)/shard_map/all_to_all | solution.py:38
  (43 shorter events, 10.5 us)
Async XLA Ops:
  7.2 13.1 %copy-start.1 = (bf16[288,1152]{1,0:T(8,128)(2,1)S(1)}, bf16[288,1152]{1,0:T(8,128)(2,1)}, u32[]{:S(2)}) copy-start(bf16[288,1152]{1,0:T(8,128)(2,1)} %up_ref.3) | copy-start | bytes 1990660
  7.2 13.1 %copy-start = (bf16[288,1152]{1,0:T(8,128)(2,1)S(1)}, bf16[288,1152]{1,0:T(8,128)(2,1)}, u32[]{:S(2)}) copy-start(bf16[288,1152]{1,0:T(8,128)(2,1)} %gate_ref.3) | copy-start | bytes 1990660
  7.2 62.0 %all-gather.2.cloned.1.call-start = ((), (), s32[]{:S(2)}) async-start(), calls=%async_computation.5 | async-start | bytes 3760128 | tf_op jit(solution)/shard_map/all_gather | solution.py:422
  7.2 1.0 copy-start.6
  8.2 0.7 copy-start.8
  21.7 23.1 %copy-start.4 = (bf16[192,1152]{1,0:T(8,128)(2,1)S(1)}, bf16[192,1152]{1,0:T(8,128)(2,1)}, u32[]{:S(2)}) copy-start(bf16[192,1152]{1,0:T(8,128)(2,1)} %grad_ref.1) | copy-start | bytes 1327108
  21.7 24.3 %all-to-all-start.2 = ((bf16[4,288,576]{2,1,0:T(8,128)(2,1)}), bf16[4,288,576]{2,1,0:T(8,128)(2,1)S(1)}, u32[]{:S(2)}, u32[]{:S(2)}) async-start(bf16[4,288,576]{2,1,0:T(8,128)(2,1)} %shard_map.87), calls=%async_computation.2 | async-start | bytes 2949120 | tf_op jit(solution)/shard_map/all_to_all | solution.py:38
  25.6 19.2 %collective-permute-start = (bf16[4,144,576]{2,1,0:T(8,128)(2,1)S(1)}, bf16[4,144,576]{2,1,0:T(8,128)(2,1)S(1)}, u32[]{:S(2)}, u32[]{:S(2)}) collective-permute-start(bf16[4,144,576]{2,1,0:T(8,128)(2,1)S(1)} %shard_map.85), channel_id=1, source_target_pairs={{0,16},{16,128},{128,144},{144,256},{256,272},{272,384},{384,400},... | collective-permute-start | bytes 1990664 | tf_op jit(solution)/shard_map/ppermute | solution.py:425
  46.0 18.7 %all-to-all-start.1 = ((bf16[4,272,576]{2,1,0:T(8,128)(2,1)}), bf16[4,272,576]{2,1,0:T(8,128)(2,1)S(1)}, u32[]{:S(2)}, u32[]{:S(2)}) async-start(bf16[4,272,576]{2,1,0:T(8,128)(2,1)} %shard_map.86), calls=%async_computation.1 | async-start | bytes 2785280 | tf_op jit(solution)/shard_map/all_to_all | solution.py:38
  50.2 92.0 %reduce-scatter.2.cloned.1.call-start = ((), (), s32[]{:S(2)}) async-start(), calls=%async_computation.6 | async-start | bytes 3317760 | tf_op jit(solution)/shard_map/reduce_scatter | solution.py:438
  51.2 15.7 %collective-permute-start.1 = (bf16[4,144,576]{2,1,0:T(8,128)(2,1)}, bf16[4,144,576]{2,1,0:T(8,128)(2,1)}, u32[]{:S(2)}, u32[]{:S(2)}) collective-permute-start(bf16[4,144,576]{2,1,0:T(8,128)(2,1)} %slice.44), channel_id=1, source_target_pairs={{0,16},{16,128},{128,144},{144,256},{256,272},{272,384},{384,400},... | collective-permute-start | bytes 1990664 | tf_op jit(solution)/shard_map/ppermute | solution.py:430
  69.6 17.9 %copy-start.10 = (bf16[768,2304]{1,0:T(8,128)(2,1)S(1)}, bf16[768,2304]{1,0:T(8,128)(2,1)}, u32[]{:S(2)}) copy-start(bf16[768,2304]{1,0:T(8,128)(2,1)} %all-gather.2.cloned.1.call-done.table_any.table_ref) | copy-start | bytes 10616836
  82.2 1.3 copy-start.2
  83.4 8.4 %collective-permute-start.2 = (bf16[4,96,2304]{2,1,0:T(8,128)(2,1)}, bf16[4,96,2304]{2,1,0:T(8,128)(2,1)}, u32[]{:S(2)}, u32[]{:S(2)}) collective-permute-start(bf16[4,96,2304]{2,1,0:T(8,128)(2,1)} %get-tuple-element.35), channel_id=1, source_target_pairs={{0,1},{1,0},{2,3},{3,2},{4,5},{5,4},{6,7},{7,6},{8,9},{9,8},{10,11... | collective-permute-start | bytes 5308424 | tf_op jit(solution)/shard_map/ppermute | solution.py:435
  91.8 1.5 copy-start.3
  94.4 13.2 %collective-permute-start.3 = (bf16[96,2304]{1,0:T(8,128)(2,1)S(1)}, bf16[96,2304]{1,0:T(8,128)(2,1)S(1)}, u32[]{:S(2)}, u32[]{:S(2)}) collective-permute-start(bf16[96,2304]{1,0:T(8,128)(2,1)S(1)} %fusion.3), channel_id=1, source_target_pairs={{0,2},{2,4},{4,6},{6,8},{8,10},{10,12},{12,14},{14,0},{1,15},{3,1}... | collective-permute-start | bytes 1327112 | tf_op jit(solution)/shard_map/ppermute | solution.py:446
  100.6 7.0 %collective-permute-start.4 = (bf16[96,576]{1,0:T(8,128)(2,1)S(1)}, bf16[96,576]{1,0:T(8,128)(2,1)S(1)}, u32[]{:S(2)}, u32[]{:S(2)}) collective-permute-start(bf16[96,576]{1,0:T(8,128)(2,1)S(1)} %get-tuple-element.38), channel_id=1, source_target_pairs={{0,32},{32,64},{64,96},{96,0},{1,33},{33,65},{65,97},{97,1},{2,34}... | collective-permute-start | bytes 331784 | tf_op jit(solution)/shard_map/ppermute | solution.py:448
  108.9 11.8 %collective-permute-start.5 = (bf16[96,2304]{1,0:T(8,128)(2,1)S(1)}, bf16[96,2304]{1,0:T(8,128)(2,1)S(1)}, u32[]{:S(2)}, u32[]{:S(2)}) collective-permute-start(bf16[96,2304]{1,0:T(8,128)(2,1)S(1)} %fusion.2), channel_id=1, source_target_pairs={{0,2},{2,4},{4,6},{6,8},{8,10},{10,12},{12,14},{14,0},{1,15},{3,1}... | collective-permute-start | bytes 1327112 | tf_op jit(solution)/shard_map/ppermute | solution.py:446
  112.4 8.3 %collective-permute-start.6 = (bf16[96,576]{1,0:T(8,128)(2,1)S(1)}, bf16[96,576]{1,0:T(8,128)(2,1)S(1)}, u32[]{:S(2)}, u32[]{:S(2)}) collective-permute-start(bf16[96,576]{1,0:T(8,128)(2,1)S(1)} %get-tuple-element.41), channel_id=1, source_target_pairs={{0,64},{32,96},{64,0},{96,32},{1,65},{33,97},{65,1},{97,33},{2,66}... | collective-permute-start | bytes 331784 | tf_op jit(solution)/shard_map/ppermute | solution.py:448
  121.9 10.5 %collective-permute-start.7 = (bf16[96,2304]{1,0:T(8,128)(2,1)S(1)}, bf16[96,2304]{1,0:T(8,128)(2,1)S(1)}, u32[]{:S(2)}, u32[]{:S(2)}) collective-permute-start(bf16[96,2304]{1,0:T(8,128)(2,1)S(1)} %fusion.1), channel_id=1, source_target_pairs={{0,2},{2,4},{4,6},{6,8},{8,10},{10,12},{12,14},{14,0},{1,15},{3,1}... | collective-permute-start | bytes 1327112 | tf_op jit(solution)/shard_map/ppermute | solution.py:446
  125.1 7.2 %collective-permute-start.8 = (bf16[96,576]{1,0:T(8,128)(2,1)S(1)}, bf16[96,576]{1,0:T(8,128)(2,1)S(1)}, u32[]{:S(2)}, u32[]{:S(2)}) collective-permute-start(bf16[96,576]{1,0:T(8,128)(2,1)S(1)} %get-tuple-element.44), channel_id=1, source_target_pairs={{0,96},{32,0},{64,32},{96,64},{1,97},{33,1},{65,33},{97,65},{2,98}... | collective-permute-start | bytes 331784 | tf_op jit(solution)/shard_map/ppermute | solution.py:448
  133.5 6.9 %collective-permute-start.10 = (bf16[48,2304]{1,0:T(8,128)(2,1)S(1)}, bf16[48,2304]{1,0:T(8,128)(2,1)S(1)}, u32[]{:S(2)}, u32[]{:S(2)}) collective-permute-start(bf16[48,2304]{1,0:T(8,128)(2,1)S(1)} %get-tuple-element.54), channel_id=1, source_target_pairs={{1,15},{3,1},{5,3},{7,5},{9,7},{11,9},{13,11},{15,13},{17,31},{19,... | collective-permute-start | bytes 663560 | tf_op jit(solution)/shard_map/ppermute | solution.py:461
  137.0 5.2 %collective-permute-start.9 = (bf16[48,2304]{1,0:T(8,128)(2,1)S(1)}, bf16[48,2304]{1,0:T(8,128)(2,1)S(1)}, u32[]{:S(2)}, u32[]{:S(2)}) collective-permute-start(bf16[48,2304]{1,0:T(8,128)(2,1)S(1)} %get-tuple-element.55), channel_id=1, source_target_pairs={{0,1},{2,3},{4,5},{6,7},{8,9},{10,11},{12,13},{14,15},{1,14},{3,0}... | collective-permute-start | bytes 663560 | tf_op jit(solution)/shard_map/ppermute | solution.py:456
  138.9 17.3 %copy-start.7 = (bf16[12,2304]{1,0:T(8,128)(2,1)S(1)}, bf16[12,2304]{1,0:T(8,128)(2,1)}, u32[]{:S(2)}) copy-start(bf16[12,2304]{1,0:T(8,128)(2,1)} %tokens_ref.3) | copy-start | bytes 165892
  138.9 17.2 %copy-start.9 = (f32[2304]{0:T(1024)S(1)}, f32[2304]{0:T(1024)}, u32[]{:S(2)}) copy-start(f32[2304]{0:T(1024)} %gain_ref.3) | copy-start | bytes 27652
  142.2 1.0 copy-start.5
Sparse Core Ops, SparseCore 0:
  20.4 48.7 all-gather.1
  92.0 44.0 reduce-scatter.1

commit v13 on v12

--- a/solution.py
+++ b/solution.py
@@ -192,15 +192,20 @@
 
 def forward_kernel(
     chunk, main, tail, place_ref, table_any, own_ref, early_ref, late_ref, grads_ref,
-    found_ref, cots_ref, keep_ref, give_ref, table_ref, matrix, sem,
+    found_ref, cots_ref, keep_ref, give_ref, table_ref, matrix, sems,
 ):
     blocks, feats, pair = own_ref.shape
     cut = feats - late_ref.shape[1]
     pool, width = table_ref.shape
     low, core, me = place_ref[0], place_ref[1], place_ref[3]
     chain, step, _ = keep_ref.shape
-    fetch = pltpu.make_async_copy(table_any, table_ref, sem)
-    fetch.start()
+    tables = []
+    for first in range(0, pool, chunk):
+        rows = pl.ds(first, chunk)
+        tables.append(
+            pltpu.make_async_copy(table_any.at[rows], table_ref.at[rows], sems.at[first // chunk])
+        )
+        tables[-1].start()
     near = low * (width // 2)
     far = (1 - low) * (width // 2)
     for x in range(blocks):
@@ -210,9 +215,9 @@
             (far + x * feats + cut, feats - cut, late_ref[x]),
         ):
             matrix[pl.ds(pl.multiple_of(first, 16), size), :] = rows
-    fetch.wait()
     for first in range(0, pool, chunk):
         rows = slice(first, first + chunk)
+        tables[first // chunk].wait()
         both = jnp.dot(table_ref[rows, :], matrix[...], preferred_element_type=F32)
         grads = grads_ref[rows, :].astype(F32)
         hidden, gate_cot, up_cot = activate(
@@ -264,7 +269,7 @@
         scratch_shapes=[
             pltpu.VMEM((pool, width), BF16),
             pltpu.VMEM((width, pair), BF16),
-            pltpu.SemaphoreType.DMA,
+            pltpu.SemaphoreType.DMA((pool // chunk,)),
         ],
         compiler_params=params(44),
         cost_estimate=pl.CostEstimate(
@@ -431,7 +436,7 @@
         table, early, late = lax.optimization_barrier((table, early, late))
         grads = sort_grads(early, cut, own_tokens, rows)
 
-        found, cots, keep, give = forward(place, table, own, early, late, grads, ny, pool)
+        found, cots, keep, give = forward(place, table, own, early, late, grads, ny, pool // 2)
         taken = lax.ppermute(give, "k", [(0, 1), (1, 0)])
         grad = gradient(table, cots, nx, nl, nc)
         taken, grad = lax.optimization_barrier((taken, grad))

time: 165 us -> 165 us (level)
  no operation moved by 1% of the time
where the time goes in v13:
time: 165 us; the launch traced here: 164 us
  starting transfers between devices  58.2 us (35%)
  waiting for transfers between devices  32.4 us (20%)
  Pallas kernels  24.6 us (15%)
  blocking collectives  22.9 us (14%)
  between operations  14.3 us (9%)
  local copies, waits for them, and re-layouts  7.08 us (4%)
  other arithmetic  4.76 us (3%)
    all_to_all x2, blocking collectives, exchange(): return lax.all_to_all(value, axis, split_axis=0, concat_axis=0, tiled=True)  22.9 us
    pallas_call x1, Pallas kernels, forward(): pl.pallas_call(functools.partial(forward_kernel, chunk, main, part - main...  12.5 us
    ppermute x3, starting transfers between devices, per_device(): partial = lax.ppermute(partial, ('y', 'k'), both_ways(ny))  11.8 us
    ppermute x3, waiting for transfers between devices, per_device(): hidden[i] = lax.ppermute(hidden[i], 'x', ring(nx, i))  11.3 us
    ppermute x3, starting transfers between devices, per_device(): hidden[i] = lax.ppermute(hidden[i], 'x', ring(nx, i))  11.3 us
    ppermute x1, starting transfers between devices, per_device(): lax.ppermute(pack_weights(nx, gate_weight, up_weight, cut), ('c', 'l', 'k...  10.8 us
    ppermute x1, waiting for transfers between devices, per_device(): lax.ppermute(pack_weights(nx, gate_weight, up_weight, cut), ('c', 'l', 'k...  8.39 us
    all_to_all x2, starting transfers between devices, exchange(): return lax.all_to_all(value, axis, split_axis=0, concat_axis=0, tiled=True)  7.89 us
  transfers between devices with their start and end apart: 15, of which 8 were waited for; matrix products, arithmetic and copies ran while one was open for 3% of the time, Pallas kernels for 6%

profile of v13, /device:TPU:1, one launch (start us, length us, event | category | flops | bytes accessed | tf_op | source)
XLA Modules:
  0.0 164.3 jit_solution(17459311591025732007)
XLA Ops:
  9.1 10.3 %all_to_all.20 = bf16[4,12,2304]{2,1,0:T(8,128)(2,1)S(1)} all-to-all(bf16[4,12,2304]{2,1,0:T(8,128)(2,1)S(1)} %shard_map.84), channel_id=1, replica_groups=mesh['c'=4,'x'=4,'l'=2,'y'=8,'k'=2] {'x'}, dimensions={0} | all-to-all | bytes 442368 | tf_op jit(solution)/shard_map/all_to_all | solution.py:38
  20.3 1.4 shard_map.87
  21.7 3.7 %all-to-all-start.2 = ((bf16[4,288,576]{2,1,0:T(8,128)(2,1)}), bf16[4,288,576]{2,1,0:T(8,128)(2,1)S(1)}, u32[]{:S(2)}, u32[]{:S(2)}) async-start(bf16[4,288,576]{2,1,0:T(8,128)(2,1)} %shard_map.87), calls=%async_computation.2 | async-start | bytes 2949120 | tf_op jit(solution)/shard_map/all_to_all | solution.py:38
  25.6 10.8 %collective-permute-start = (bf16[4,144,576]{2,1,0:T(8,128)(2,1)S(1)}, bf16[4,144,576]{2,1,0:T(8,128)(2,1)S(1)}, u32[]{:S(2)}, u32[]{:S(2)}) collective-permute-start(bf16[4,144,576]{2,1,0:T(8,128)(2,1)S(1)} %shard_map.85), channel_id=1, source_target_pairs={{0,16},{16,128},{128,144},{144,256},{256,272},{272,384},{384,400},... | collective-permute-start | bytes 1990664 | tf_op jit(solution)/shard_map/ppermute | solution.py:430
  36.3 8.4 %collective-permute-done.weights_ref = bf16[4,144,576]{2,1,0:T(8,128)(2,1)S(1)} collective-permute-done((bf16[4,144,576]{2,1,0:T(8,128)(2,1)S(1)}, bf16[4,144,576]{2,1,0:T(8,128)(2,1)S(1)}, u32[]{:S(2)}, u32[]{:S(2)}) %collective-permute-start) | collective-permute-done | bytes 663584 | tf_op jit(solution)/shard_map/ppermute | solution.py:430
  44.7 1.3 shard_map.86
  46.0 4.2 %all-to-all-start.1 = ((bf16[4,272,576]{2,1,0:T(8,128)(2,1)}), bf16[4,272,576]{2,1,0:T(8,128)(2,1)S(1)}, u32[]{:S(2)}, u32[]{:S(2)}) async-start(bf16[4,272,576]{2,1,0:T(8,128)(2,1)} %shard_map.86), calls=%async_computation.1 | async-start | bytes 2785280 | tf_op jit(solution)/shard_map/all_to_all | solution.py:38
  51.2 7.0 %collective-permute-start.1 = (bf16[4,144,576]{2,1,0:T(8,128)(2,1)}, bf16[4,144,576]{2,1,0:T(8,128)(2,1)}, u32[]{:S(2)}, u32[]{:S(2)}) collective-permute-start(bf16[4,144,576]{2,1,0:T(8,128)(2,1)} %slice.44), channel_id=1, source_target_pairs={{0,16},{16,128},{128,144},{144,256},{256,272},{272,384},{384,400},... | collective-permute-start | bytes 1990664 | tf_op jit(solution)/shard_map/ppermute | solution.py:435
  58.3 6.4 %all-to-all-done.1.raw_ref.early_ref = bf16[4,272,576]{2,1,0:T(8,128)(2,1)S(1)} async-done(((bf16[4,272,576]{2,1,0:T(8,128)(2,1)}), bf16[4,272,576]{2,1,0:T(8,128)(2,1)S(1)}, u32[]{:S(2)}, u32[]{:S(2)}) %all-to-all-start.1) | async-done | bytes 1253408 | tf_op jit(solution)/shard_map/all_to_all | solution.py:38
  64.7 2.2 %collective-permute-done.1.late_ref = bf16[4,144,576]{2,1,0:T(8,128)(2,1)} collective-permute-done((bf16[4,144,576]{2,1,0:T(8,128)(2,1)}, bf16[4,144,576]{2,1,0:T(8,128)(2,1)}, u32[]{:S(2)}, u32[]{:S(2)}) %collective-permute-start.1) | collective-permute-done | bytes 663584 | tf_op jit(solution)/shard_map/ppermute | solution.py:435
  66.9 2.3 %all-gather.2.cloned.1.call-done.table_any.table_ref = bf16[768,2304]{1,0:T(8,128)(2,1)} async-done(((bf16[48,2304]{1,0:T(8,128)(2,1)}), bf16[768,2304]{1,0:T(8,128)(2,1)}) %all-gather.2.cloned.1.call-update) | async-done | bytes 3538960 | tf_op jit(solution)/shard_map/all_gather | solution.py:427
  69.6 12.5 %shard_map.89 = (bf16[768,288]{1,0:T(8,128)(2,1)S(1)}, bf16[768,576]{1,0:T(8,128)(2,1)S(1)}, bf16[4,96,2304]{2,1,0:T(8,128)(2,1)S(1)}, bf16[4,96,2304]{2,1,0:T(8,128)(2,1)}) custom-call(s32[4]{0:T(128)S(1)} %pad_add_fusion.place_ref, bf16[768,2304]{1,0:T(8,128)(2,1)} %all-gather.2.cloned.1.call-done.table_any.table_ref, ...), custom_call_target="tpu_custom_call" | custom-call | flops 4076863488 | bytes 9732096 | tf_op jit(solution)/shard_map/pallas_call | solution.py:259
  82.1 1.3 copy-done.2
  83.3 4.0 %collective-permute-start.2 = (bf16[4,96,2304]{2,1,0:T(8,128)(2,1)}, bf16[4,96,2304]{2,1,0:T(8,128)(2,1)}, u32[]{:S(2)}, u32[]{:S(2)}) collective-permute-start(bf16[4,96,2304]{2,1,0:T(8,128)(2,1)} %get-tuple-element.35), channel_id=1, source_target_pairs={{0,1},{1,0},{2,3},{3,2},{4,5},{5,4},{6,7},{7,6},{8,9},{9,8},{10,11... | collective-permute-start | bytes 5308424 | tf_op jit(solution)/shard_map/ppermute | solution.py:440
  87.4 4.4 %shard_map.91 = bf16[2304,576]{1,0:T(8,128)(2,1)} custom-call(bf16[768,2304]{1,0:T(8,128)(2,1)S(1)} %copy-done.10, bf16[768,576]{1,0:T(8,128)(2,1)S(1)} %get-tuple-element.36.cots_ref), custom_call_target="tpu_custom_call" | custom-call | flops 2038431744 | bytes 6193152 | tf_op jit(solution)/shard_map/pallas_call | solution.py:309
  91.8 1.4 copy-done.3
  94.3 5.1 %collective-permute-start.3 = (bf16[96,2304]{1,0:T(8,128)(2,1)S(1)}, bf16[96,2304]{1,0:T(8,128)(2,1)S(1)}, u32[]{:S(2)}, u32[]{:S(2)}) collective-permute-start(bf16[96,2304]{1,0:T(8,128)(2,1)S(1)} %fusion.3), channel_id=1, source_target_pairs={{0,2},{2,4},{4,6},{6,8},{8,10},{10,12},{12,14},{14,0},{1,15},{3,1}... | collective-permute-start | bytes 1327112 | tf_op jit(solution)/shard_map/ppermute | solution.py:451
  100.5 3.6 %collective-permute-start.4 = (bf16[96,576]{1,0:T(8,128)(2,1)S(1)}, bf16[96,576]{1,0:T(8,128)(2,1)S(1)}, u32[]{:S(2)}, u32[]{:S(2)}) collective-permute-start(bf16[96,576]{1,0:T(8,128)(2,1)S(1)} %get-tuple-element.38), channel_id=1, source_target_pairs={{0,32},{32,64},{64,96},{96,0},{1,33},{33,65},{65,97},{97,1},{2,34}... | collective-permute-start | bytes 331784 | tf_op jit(solution)/shard_map/ppermute | solution.py:453
  104.1 3.5 %collective-permute-done.4.refs_1_ = bf16[96,576]{1,0:T(8,128)(2,1)S(1)} collective-permute-done((bf16[96,576]{1,0:T(8,128)(2,1)S(1)}, bf16[96,576]{1,0:T(8,128)(2,1)S(1)}, u32[]{:S(2)}, u32[]{:S(2)}) %collective-permute-start.4) | collective-permute-done | bytes 110624 | tf_op jit(solution)/shard_map/ppermute | solution.py:453
  108.8 3.5 %collective-permute-start.5 = (bf16[96,2304]{1,0:T(8,128)(2,1)S(1)}, bf16[96,2304]{1,0:T(8,128)(2,1)S(1)}, u32[]{:S(2)}, u32[]{:S(2)}) collective-permute-start(bf16[96,2304]{1,0:T(8,128)(2,1)S(1)} %fusion.2), channel_id=1, source_target_pairs={{0,2},{2,4},{4,6},{6,8},{8,10},{10,12},{12,14},{14,0},{1,15},{3,1}... | collective-permute-start | bytes 1327112 | tf_op jit(solution)/shard_map/ppermute | solution.py:451
  112.3 3.9 %collective-permute-start.6 = (bf16[96,576]{1,0:T(8,128)(2,1)S(1)}, bf16[96,576]{1,0:T(8,128)(2,1)S(1)}, u32[]{:S(2)}, u32[]{:S(2)}) collective-permute-start(bf16[96,576]{1,0:T(8,128)(2,1)S(1)} %get-tuple-element.41), channel_id=1, source_target_pairs={{0,64},{32,96},{64,0},{96,32},{1,65},{33,97},{65,1},{97,33},{2,66}... | collective-permute-start | bytes 331784 | tf_op jit(solution)/shard_map/ppermute | solution.py:453
  116.1 4.4 %collective-permute-done.6.refs_2_ = bf16[96,576]{1,0:T(8,128)(2,1)S(1)} collective-permute-done((bf16[96,576]{1,0:T(8,128)(2,1)S(1)}, bf16[96,576]{1,0:T(8,128)(2,1)S(1)}, u32[]{:S(2)}, u32[]{:S(2)}) %collective-permute-start.6) | collective-permute-done | bytes 110624 | tf_op jit(solution)/shard_map/ppermute | solution.py:453
  120.6 1.2 fusion.1
  121.8 3.2 %collective-permute-start.7 = (bf16[96,2304]{1,0:T(8,128)(2,1)S(1)}, bf16[96,2304]{1,0:T(8,128)(2,1)S(1)}, u32[]{:S(2)}, u32[]{:S(2)}) collective-permute-start(bf16[96,2304]{1,0:T(8,128)(2,1)S(1)} %fusion.1), channel_id=1, source_target_pairs={{0,2},{2,4},{4,6},{6,8},{8,10},{10,12},{12,14},{14,0},{1,15},{3,1}... | collective-permute-start | bytes 1327112 | tf_op jit(solution)/shard_map/ppermute | solution.py:451
  125.0 3.8 %collective-permute-start.8 = (bf16[96,576]{1,0:T(8,128)(2,1)S(1)}, bf16[96,576]{1,0:T(8,128)(2,1)S(1)}, u32[]{:S(2)}, u32[]{:S(2)}) collective-permute-start(bf16[96,576]{1,0:T(8,128)(2,1)S(1)} %get-tuple-element.44), channel_id=1, source_target_pairs={{0,96},{32,0},{64,32},{96,64},{1,97},{33,1},{65,33},{97,65},{2,98}... | collective-permute-start | bytes 331784 | tf_op jit(solution)/shard_map/ppermute | solution.py:453
  128.9 3.4 %collective-permute-done.8.refs_3_ = bf16[96,576]{1,0:T(8,128)(2,1)S(1)} collective-permute-done((bf16[96,576]{1,0:T(8,128)(2,1)S(1)}, bf16[96,576]{1,0:T(8,128)(2,1)S(1)}, u32[]{:S(2)}, u32[]{:S(2)}) %collective-permute-start.8) | collective-permute-done | bytes 110624 | tf_op jit(solution)/shard_map/ppermute | solution.py:453
  132.2 1.2 fusion.sums_ref
  133.4 3.4 %collective-permute-start.10 = (bf16[48,2304]{1,0:T(8,128)(2,1)S(1)}, bf16[48,2304]{1,0:T(8,128)(2,1)S(1)}, u32[]{:S(2)}, u32[]{:S(2)}) collective-permute-start(bf16[48,2304]{1,0:T(8,128)(2,1)S(1)} %get-tuple-element.54), channel_id=1, source_target_pairs={{1,15},{3,1},{5,3},{7,5},{9,7},{11,9},{13,11},{15,13},{17,31},{19,... | collective-permute-start | bytes 663560 | tf_op jit(solution)/shard_map/ppermute | solution.py:466
  136.9 1.9 %collective-permute-start.9 = (bf16[48,2304]{1,0:T(8,128)(2,1)S(1)}, bf16[48,2304]{1,0:T(8,128)(2,1)S(1)}, u32[]{:S(2)}, u32[]{:S(2)}) collective-permute-start(bf16[48,2304]{1,0:T(8,128)(2,1)S(1)} %get-tuple-element.55), channel_id=1, source_target_pairs={{0,1},{2,3},{4,5},{6,7},{8,9},{10,11},{12,13},{14,15},{1,14},{3,0}... | collective-permute-start | bytes 663560 | tf_op jit(solution)/shard_map/ppermute | solution.py:461
  138.8 1.5 shard_map.92
  140.3 1.8 %collective-permute-done.9.near_ref = bf16[48,2304]{1,0:T(8,128)(2,1)S(1)} collective-permute-done((bf16[48,2304]{1,0:T(8,128)(2,1)S(1)}, bf16[48,2304]{1,0:T(8,128)(2,1)S(1)}, u32[]{:S(2)}, u32[]{:S(2)}) %collective-permute-start.9) | collective-permute-done | bytes 221216 | tf_op jit(solution)/shard_map/ppermute | solution.py:461
  143.8 12.6 %all_to_all.21.got_ref = bf16[4,120,640]{2,1,0:T(8,128)(2,1)S(1)} all-to-all(bf16[4,120,640]{2,1,0:T(8,128)(2,1)S(1)} %shard_map.93), channel_id=1, replica_groups=mesh['c'=4,'x'=4,'l'=2,'y'=8,'k'=2] {'x'}, dimensions={0} | all-to-all | bytes 1228800 | tf_op jit(solution)/shard_map/all_to_all | solution.py:38
  (43 shorter events, 10.5 us)
Async XLA Ops:
  7.2 13.1 %copy-start.1 = (bf16[288,1152]{1,0:T(8,128)(2,1)S(1)}, bf16[288,1152]{1,0:T(8,128)(2,1)}, u32[]{:S(2)}) copy-start(bf16[288,1152]{1,0:T(8,128)(2,1)} %up_ref.3) | copy-start | bytes 1990660
  7.2 13.1 %copy-start = (bf16[288,1152]{1,0:T(8,128)(2,1)S(1)}, bf16[288,1152]{1,0:T(8,128)(2,1)}, u32[]{:S(2)}) copy-start(bf16[288,1152]{1,0:T(8,128)(2,1)} %gate_ref.3) | copy-start | bytes 1990660
  7.2 62.0 %all-gather.2.cloned.1.call-start = ((), (), s32[]{:S(2)}) async-start(), calls=%async_computation.5 | async-start | bytes 3760128 | tf_op jit(solution)/shard_map/all_gather | solution.py:427
  7.2 1.0 copy-start.6
  8.2 0.7 copy-start.8
  21.7 23.1 %copy-start.4 = (bf16[192,1152]{1,0:T(8,128)(2,1)S(1)}, bf16[192,1152]{1,0:T(8,128)(2,1)}, u32[]{:S(2)}) copy-start(bf16[192,1152]{1,0:T(8,128)(2,1)} %grad_ref.1) | copy-start | bytes 1327108
  21.7 24.3 %all-to-all-start.2 = ((bf16[4,288,576]{2,1,0:T(8,128)(2,1)}), bf16[4,288,576]{2,1,0:T(8,128)(2,1)S(1)}, u32[]{:S(2)}, u32[]{:S(2)}) async-start(bf16[4,288,576]{2,1,0:T(8,128)(2,1)} %shard_map.87), calls=%async_computation.2 | async-start | bytes 2949120 | tf_op jit(solution)/shard_map/all_to_all | solution.py:38
  25.6 19.2 %collective-permute-start = (bf16[4,144,576]{2,1,0:T(8,128)(2,1)S(1)}, bf16[4,144,576]{2,1,0:T(8,128)(2,1)S(1)}, u32[]{:S(2)}, u32[]{:S(2)}) collective-permute-start(bf16[4,144,576]{2,1,0:T(8,128)(2,1)S(1)} %shard_map.85), channel_id=1, source_target_pairs={{0,16},{16,128},{128,144},{144,256},{256,272},{272,384},{384,400},... | collective-permute-start | bytes 1990664 | tf_op jit(solution)/shard_map/ppermute | solution.py:430
  46.0 18.7 %all-to-all-start.1 = ((bf16[4,272,576]{2,1,0:T(8,128)(2,1)}), bf16[4,272,576]{2,1,0:T(8,128)(2,1)S(1)}, u32[]{:S(2)}, u32[]{:S(2)}) async-start(bf16[4,272,576]{2,1,0:T(8,128)(2,1)} %shard_map.86), calls=%async_computation.1 | async-start | bytes 2785280 | tf_op jit(solution)/shard_map/all_to_all | solution.py:38
  50.2 91.9 %reduce-scatter.2.cloned.1.call-start = ((), (), s32[]{:S(2)}) async-start(), calls=%async_computation.6 | async-start | bytes 3317760 | tf_op jit(solution)/shard_map/reduce_scatter | solution.py:443
  51.2 15.7 %collective-permute-start.1 = (bf16[4,144,576]{2,1,0:T(8,128)(2,1)}, bf16[4,144,576]{2,1,0:T(8,128)(2,1)}, u32[]{:S(2)}, u32[]{:S(2)}) collective-permute-start(bf16[4,144,576]{2,1,0:T(8,128)(2,1)} %slice.44), channel_id=1, source_target_pairs={{0,16},{16,128},{128,144},{144,256},{256,272},{272,384},{384,400},... | collective-permute-start | bytes 1990664 | tf_op jit(solution)/shard_map/ppermute | solution.py:435
  69.6 17.8 %copy-start.10 = (bf16[768,2304]{1,0:T(8,128)(2,1)S(1)}, bf16[768,2304]{1,0:T(8,128)(2,1)}, u32[]{:S(2)}) copy-start(bf16[768,2304]{1,0:T(8,128)(2,1)} %all-gather.2.cloned.1.call-done.table_any.table_ref) | copy-start | bytes 10616836
  82.1 1.3 copy-start.2
  83.3 8.4 %collective-permute-start.2 = (bf16[4,96,2304]{2,1,0:T(8,128)(2,1)}, bf16[4,96,2304]{2,1,0:T(8,128)(2,1)}, u32[]{:S(2)}, u32[]{:S(2)}) collective-permute-start(bf16[4,96,2304]{2,1,0:T(8,128)(2,1)} %get-tuple-element.35), channel_id=1, source_target_pairs={{0,1},{1,0},{2,3},{3,2},{4,5},{5,4},{6,7},{7,6},{8,9},{9,8},{10,11... | collective-permute-start | bytes 5308424 | tf_op jit(solution)/shard_map/ppermute | solution.py:440
  91.7 1.5 copy-start.3
  94.3 13.2 %collective-permute-start.3 = (bf16[96,2304]{1,0:T(8,128)(2,1)S(1)}, bf16[96,2304]{1,0:T(8,128)(2,1)S(1)}, u32[]{:S(2)}, u32[]{:S(2)}) collective-permute-start(bf16[96,2304]{1,0:T(8,128)(2,1)S(1)} %fusion.3), channel_id=1, source_target_pairs={{0,2},{2,4},{4,6},{6,8},{8,10},{10,12},{12,14},{14,0},{1,15},{3,1}... | collective-permute-start | bytes 1327112 | tf_op jit(solution)/shard_map/ppermute | solution.py:451
  100.5 7.0 %collective-permute-start.4 = (bf16[96,576]{1,0:T(8,128)(2,1)S(1)}, bf16[96,576]{1,0:T(8,128)(2,1)S(1)}, u32[]{:S(2)}, u32[]{:S(2)}) collective-permute-start(bf16[96,576]{1,0:T(8,128)(2,1)S(1)} %get-tuple-element.38), channel_id=1, source_target_pairs={{0,32},{32,64},{64,96},{96,0},{1,33},{33,65},{65,97},{97,1},{2,34}... | collective-permute-start | bytes 331784 | tf_op jit(solution)/shard_map/ppermute | solution.py:453
  108.8 11.8 %collective-permute-start.5 = (bf16[96,2304]{1,0:T(8,128)(2,1)S(1)}, bf16[96,2304]{1,0:T(8,128)(2,1)S(1)}, u32[]{:S(2)}, u32[]{:S(2)}) collective-permute-start(bf16[96,2304]{1,0:T(8,128)(2,1)S(1)} %fusion.2), channel_id=1, source_target_pairs={{0,2},{2,4},{4,6},{6,8},{8,10},{10,12},{12,14},{14,0},{1,15},{3,1}... | collective-permute-start | bytes 1327112 | tf_op jit(solution)/shard_map/ppermute | solution.py:451
  112.3 8.3 %collective-permute-start.6 = (bf16[96,576]{1,0:T(8,128)(2,1)S(1)}, bf16[96,576]{1,0:T(8,128)(2,1)S(1)}, u32[]{:S(2)}, u32[]{:S(2)}) collective-permute-start(bf16[96,576]{1,0:T(8,128)(2,1)S(1)} %get-tuple-element.41), channel_id=1, source_target_pairs={{0,64},{32,96},{64,0},{96,32},{1,65},{33,97},{65,1},{97,33},{2,66}... | collective-permute-start | bytes 331784 | tf_op jit(solution)/shard_map/ppermute | solution.py:453
  121.8 10.4 %collective-permute-start.7 = (bf16[96,2304]{1,0:T(8,128)(2,1)S(1)}, bf16[96,2304]{1,0:T(8,128)(2,1)S(1)}, u32[]{:S(2)}, u32[]{:S(2)}) collective-permute-start(bf16[96,2304]{1,0:T(8,128)(2,1)S(1)} %fusion.1), channel_id=1, source_target_pairs={{0,2},{2,4},{4,6},{6,8},{8,10},{10,12},{12,14},{14,0},{1,15},{3,1}... | collective-permute-start | bytes 1327112 | tf_op jit(solution)/shard_map/ppermute | solution.py:451
  125.0 7.2 %collective-permute-start.8 = (bf16[96,576]{1,0:T(8,128)(2,1)S(1)}, bf16[96,576]{1,0:T(8,128)(2,1)S(1)}, u32[]{:S(2)}, u32[]{:S(2)}) collective-permute-start(bf16[96,576]{1,0:T(8,128)(2,1)S(1)} %get-tuple-element.44), channel_id=1, source_target_pairs={{0,96},{32,0},{64,32},{96,64},{1,97},{33,1},{65,33},{97,65},{2,98}... | collective-permute-start | bytes 331784 | tf_op jit(solution)/shard_map/ppermute | solution.py:453
  133.4 6.9 %collective-permute-start.10 = (bf16[48,2304]{1,0:T(8,128)(2,1)S(1)}, bf16[48,2304]{1,0:T(8,128)(2,1)S(1)}, u32[]{:S(2)}, u32[]{:S(2)}) collective-permute-start(bf16[48,2304]{1,0:T(8,128)(2,1)S(1)} %get-tuple-element.54), channel_id=1, source_target_pairs={{1,15},{3,1},{5,3},{7,5},{9,7},{11,9},{13,11},{15,13},{17,31},{19,... | collective-permute-start | bytes 663560 | tf_op jit(solution)/shard_map/ppermute | solution.py:466
  136.9 5.2 %collective-permute-start.9 = (bf16[48,2304]{1,0:T(8,128)(2,1)S(1)}, bf16[48,2304]{1,0:T(8,128)(2,1)S(1)}, u32[]{:S(2)}, u32[]{:S(2)}) collective-permute-start(bf16[48,2304]{1,0:T(8,128)(2,1)S(1)} %get-tuple-element.55), channel_id=1, source_target_pairs={{0,1},{2,3},{4,5},{6,7},{8,9},{10,11},{12,13},{14,15},{1,14},{3,0}... | collective-permute-start | bytes 663560 | tf_op jit(solution)/shard_map/ppermute | solution.py:461
  138.8 17.6 %copy-start.7 = (bf16[12,2304]{1,0:T(8,128)(2,1)S(1)}, bf16[12,2304]{1,0:T(8,128)(2,1)}, u32[]{:S(2)}) copy-start(bf16[12,2304]{1,0:T(8,128)(2,1)} %tokens_ref.3) | copy-start | bytes 165892
  138.8 17.6 %copy-start.9 = (f32[2304]{0:T(1024)S(1)}, f32[2304]{0:T(1024)}, u32[]{:S(2)}) copy-start(f32[2304]{0:T(1024)} %gain_ref.3) | copy-start | bytes 27652
  142.1 1.0 copy-start.5
Sparse Core Ops, SparseCore 0:
  20.4 48.7 all-gather.1
  91.9 44.2 reduce-scatter.1
